TPU v7x, 256 devices: a whole 4x4x8 slice. The times are simulated.
256 devices in a mesh: seq: 128 (over z, x, y_hi, core), rep: 2 (over y_lo).
Axes of the slice: x: 4, y: 4 (y_hi: 2, y_lo: 2; y = y_hi * 2 + y_lo), z: 8, core: 2. Of those that a mesh axis runs over, the one named last changes fastest.
Arguments:
- hidden_in: bfloat16 [2, 16384, 1536], P('rep', 'seq'), may hold values from -24 to 24
- upstream: bfloat16 [2, 16384, 1536], P('rep', 'seq'), may hold values from -6 to 6
- out_weight: bfloat16 [1536, 1536], P(('seq', 'rep')), may hold values from -0.15625 to 0.15625
- conv_kernel: bfloat16 [31, 1536], replicated, may hold values from -1 to 1
- durations: int32 [2, 1024], P('rep', 'seq'), may hold values from 1 to 31, as said below
Outputs:
- frame_grad: bfloat16 [2, 16384, 1536], P('rep', 'seq')
- gloss_grad: float32 [2, 1024, 1536], P('rep', 'seq')
- weight_grad: float32 [1536, 1536], P(('seq', 'rep'))
- kernel_grad: float32 [31, 1536], replicated
Inputs may be any that keep to these rules, and one draw needn't show every extreme that they name: In each broadcast the durations sum to 16384. The first frame of a gloss block of 8 rows lies at or after the first frame of the same index's frames and less than 16 frames after it.
All inputs are finite; a program needn't handle non-finite values.
Results may differ from a plain program's by a relative error of at most 0.005.
Values may be sent and summed in bfloat16 or wider, within the bound.
No kernel may reach another device: no remote copies, remote signals or barrier semaphores. Data moves between devices by JAX's collectives and lax.ppermute only.
A program may use at most 64 MiB of HBM per device.

v0:
```python
import math

import jax
import jax.numpy as jnp
from jax import lax
from jax.sharding import PartitionSpec as P


def padded_2(block, sides, width):
    for axis, dim in sides:
        count = lax.axis_size(axis)
        forward = [(i, i + 1) for i in range(count - 1)]
        backward = [(target, source) for source, target in forward]
        low = lax.ppermute(
            lax.slice_in_dim(block, block.shape[dim] - width, None, axis=dim), axis, forward
        )
        high = lax.ppermute(lax.slice_in_dim(block, 0, width, axis=dim), axis, backward)
        block = jnp.concatenate([low, block, high], axis=dim)
    return block


def prefix(value, axis, join, neutral):
    count, mine = (lax.axis_size(axis), lax.axis_index(axis))
    pieces = lax.all_gather(value, axis)
    subtotal = jnp.full_like(value, 0) + jnp.asarray(neutral, value.dtype)

    def lap(position, subtotal):
        longer = join(subtotal, pieces[position])
        return jnp.where(position < mine, longer, subtotal)

    return lax.fori_loop(0, count - 1, lap, subtotal)


def shifted(shard, axis, by):
    peers = lax.axis_size(axis)
    pairs = [(i, i + by) for i in range(peers) if 0 <= i + by < peers]
    return lax.ppermute(shard, axis, pairs)


def covers(positions, starts, ends):
    inside = (positions[None, :] >= starts[:, None]) & (positions[None, :] < ends[:, None])
    return inside.astype(jnp.bfloat16)


def body(hidden_in, upstream, out_weight, conv_kernel, durations):
    frame_count = hidden_in.shape[1]
    gloss_count = durations.shape[1]
    taps = conv_kernel.shape[0]
    half_width = taps // 2
    kernel_f = conv_kernel.astype(jnp.float32)
    scaling = 1.0 / math.sqrt(lax.axis_size("rep") * lax.axis_size("seq") * frame_count)
    grad_out = upstream[0]
    padded = padded_2(hidden_in, (("seq", 1),), half_width)[0]
    conv_out = jnp.zeros((frame_count, hidden_in.shape[2]), jnp.float32)
    for kernel_tap in range(taps):
        conv_out = conv_out + kernel_f[kernel_tap] * padded[
            kernel_tap : kernel_tap + frame_count
        ].astype(jnp.float32)
    activated = jax.nn.silu(conv_out).astype(jnp.bfloat16)
    grad_act = lax.dot_general(
        grad_out,
        lax.all_gather(out_weight, ("seq", "rep"), axis=0, tiled=True),
        (((1,), (1,)), ((), ())),
        preferred_element_type=jnp.float32,
    )
    sigmoid_a = jax.nn.sigmoid(conv_out)
    grad_conv = (grad_act * sigmoid_a * (1.0 + conv_out * (1.0 - sigmoid_a))).astype(jnp.bfloat16)
    padded_grad = padded_2(grad_conv[None], (("seq", 1),), half_width)[0]
    frame_sum = jnp.zeros_like(conv_out)
    for kernel_tap in range(taps):
        begin = 2 * half_width - kernel_tap
        frame_sum = frame_sum + kernel_f[kernel_tap] * padded_grad[
            begin : begin + frame_count
        ].astype(jnp.float32)
    frame_grad = frame_sum.astype(jnp.bfloat16)
    conv_grad_f = grad_conv.astype(jnp.float32)
    tap_rows = [
        jnp.sum(
            conv_grad_f * padded[kernel_tap : kernel_tap + frame_count].astype(jnp.float32), axis=0
        )
        for kernel_tap in range(taps)
    ]
    kernel_grad = lax.psum(jnp.stack(tap_rows) * scaling, ("seq", "rep"))
    weight_grad = lax.psum_scatter(
        lax.dot_general(
            activated, grad_out, (((0,), (0,)), ((), ())), preferred_element_type=jnp.float32
        )
        * scaling,
        ("seq", "rep"),
        scatter_dimension=0,
        tiled=True,
    )
    lengths = durations[0]
    block_total = jnp.sum(lengths).reshape(1)
    block_start = prefix(
        block_total, "seq", lambda earlier, later: earlier + later, jnp.zeros((1,), jnp.int32)
    )[0]
    own_ends = block_start + jnp.cumsum(lengths)
    own_starts = own_ends - lengths
    anchor = lax.axis_index("seq") * frame_count
    positions = anchor + lax.iota(jnp.int32, frame_count)
    starts_all = jnp.concatenate((own_starts, anchor.reshape(1)))
    ends_all = jnp.concatenate((own_ends, block_start.reshape(1)))
    partial_sums = jnp.dot(
        covers(positions, starts_all, ends_all), frame_grad, preferred_element_type=jnp.float32
    )
    received = shifted(partial_sums[gloss_count:], "seq", -1)
    gloss_grad = jnp.concatenate(
        (partial_sums[: gloss_count - 1], partial_sums[gloss_count - 1 : gloss_count] + received), 0
    )
    return (frame_grad[None], gloss_grad[None], weight_grad, kernel_grad)


def solution(mesh):
    in_specs = (
        P("rep", "seq", None),
        P("rep", "seq", None),
        P(("seq", "rep"), None),
        P(),
        P("rep", "seq"),
    )
    out_specs = (P("rep", "seq", None), P("rep", "seq", None), P(("seq", "rep"), None), P())
    return jax.shard_map(body, mesh=mesh, in_specs=in_specs, out_specs=out_specs, check_vma=False)
```

profile of v0, /device:TPU:1, one launch (start us, length us, event | category | flops | bytes accessed | tf_op | source)
XLA Modules:
  0.0 1897.8 jit_solution(10318307794654139285)
XLA Ops:
  8.8 5.1 collective-permute-start.1
  14.0 3.0 collective-permute-start
  20.4 12.4 convolution_multiply_fusion
  32.8 716.0 %fusion = f32[8,1536]{1,0:T(8,128)S(1)} fusion(f32[1536,1536]{1,0:T(8,128)} %convolution_multiply_fusion), kind=kCustom, calls=%all-reduce-scatter | all-reduce-scatter fusion | flops 3145729 | bytes 9486336
  748.8 1.4 collective-permute-start.67
  750.2 12.9 collective-permute-start.66
  764.4 5.6 collective-permute-start.68
  785.8 16.6 collective-permute-start.52
  802.4 5.9 collective-permute-start.51
  809.6 1.6 collective-permute-start.49
  811.3 2.8 collective-permute-start.48
  814.1 4.4 collective-permute-start.47
  818.5 4.4 collective-permute-start.46
  829.5 5.1 collective-permute-start.40
  834.5 2.2 collective-permute-start.39
  836.7 1.9 collective-permute-start.38
  838.7 1.8 collective-permute-start.37
  840.5 2.0 collective-permute-start.36
  842.5 5.9 collective-permute-start.35
  848.4 13.1 collective-permute-start.34
  861.6 13.1 collective-permute-start.33
  874.7 13.1 collective-permute-start.32
  887.9 13.1 collective-permute-start.31
  901.0 13.1 collective-permute-start.30
  914.1 13.1 collective-permute-start.29
  927.3 13.1 collective-permute-start.28
  940.4 13.1 collective-permute-start.27
  953.6 13.1 collective-permute-start.26
  966.7 13.1 collective-permute-start.25
  982.5 21.9 %all-reduce = s32[128]{0:T(128)} all-reduce(s32[128]{0:T(128)S(1)} %dynamic-update-slice), channel_id=1, replica_groups=mesh['seq'=128,'rep'=2] {'seq'}, use_global_device_ids=true, to_apply=%add | all-reduce | flops 128 | bytes 1024
  1004.4 12.0 collective-permute-start.24
  1016.4 13.1 collective-permute-start.23
  1029.6 13.7 collective-permute-start.22
  1043.3 13.1 collective-permute-start.21
  1056.4 13.1 collective-permute-start.20
  1069.6 248.9 %while.13 = (s32[]{:T(128)}, s32[1]{0:T(128)}, s32[]{:T(128)}, s32[128,1]{0,1:T(1,128)}, s32[]{:T(128)}) while((s32[]{:T(128)}, s32[1]{0:T(128)}, s32[]{:T(128)}, s32[128,1]{0,1:T(1,128)}, s32[]{:T(128)}) %tuple.102), condition=%wide.region_2.3_spmd, body=%wide.region_1.2_spmd.sunk | while | flops 5 | bytes 115 | solution.py:31
  1319.8 13.1 collective-permute-start.19
  1333.0 13.1 collective-permute-start.18
  1346.1 13.1 collective-permute-start.17
  1359.3 13.1 collective-permute-start.16
  1372.4 13.1 collective-permute-start.15
  1386.7 12.5 collective-permute-start.14
  1399.3 13.1 collective-permute-start.13
  1412.4 13.1 collective-permute-start.12
  1425.6 13.1 collective-permute-start.11
  1438.7 13.1 collective-permute-start.10
  1453.1 13.7 collective-permute-start.9
  1466.8 13.1 collective-permute-start.8
  1480.0 13.2 collective-permute-start.7
  1493.1 4.5 collective-permute-start.6
  1497.6 11.6 collective-permute-start.5
  1509.9 2.7 collective-permute-done.5
  1512.6 97.1 %concatenate.86 = f32[518,1536]{1,0:T(8,128)} concatenate(f32[6,1536]{1,0:T(8,128)S(1)} %collective-permute-done.68, f32[8,1536]{1,0:T(8,128)S(1)} %collective-permute-done.67, f32[8,1536]{1,0:T(8,128)S(1)} %collective-permute-done.66, f32[8,1536]{1,0:T(8,128)S(1)} %collective-permute-done.65, f32[8,1536]{1,0:T(8,128)S(1)} %collective-permute-done.64, ...), dimensions={0} | concatenate | bytes 6365184
  1609.9 1.6 constant_dynamic-slice_fusion.1
  1611.5 8.4 reshape.674
  1620.2 7.9 fusion.199
  1630.5 3.7 collective-permute-start.3
  1634.3 2.1 collective-permute-start.2
  1637.7 3.5 collective-permute-done.2
  1641.2 3.4 fusion.294
  1644.6 1.9 collective-permute-start.4
  1646.5 4.4 fusion.217
  1651.7 237.7 %all-reduce.5.cloned.1.call-done = f32[31,1536]{1,0:T(8,128)} async-done(((f32[31,1536]{1,0:T(8,128)}), f32[31,1536]{1,0:T(8,128)}) %all-reduce.5.cloned.1.call-update) | async-done | bytes 190480 | tf_op jit(solution)/shard_map/psum | solution.py:83
  1889.3 1.6 copy.20
  (417 shorter events, 204.7 us)
Async XLA Ops:
  7.2 1604.3 %all-gather.3.cloned.1.call-start = ((), (), s32[]{:S(2)}) async-start(), calls=%async_computation.1 | async-start | bytes 6316032 | tf_op jit(solution)/shard_map/all_gather | solution.py:62
  7.9 1881.4 %all-reduce.5.cloned.1.call-start = ((), (), s32[]{:S(2)}) async-start(), calls=%async_computation | async-start | bytes 393216 | tf_op jit(solution)/shard_map/psum | solution.py:83
  8.8 10.9 collective-permute-start.1
  748.8 23.9 %collective-permute-start.67 = (f32[8,1536]{1,0:T(8,128)S(1)}, f32[8,1536]{1,0:T(8,128)S(1)}, u32[]{:S(2)}, u32[]{:S(2)}) collective-permute-start(f32[8,1536]{1,0:T(8,128)S(1)} %fusion), channel_id=1, source_target_pairs={{0,63},{1,64},{2,65},{3,66},{4,67},{5,68},{6,69},{7,70},{8,71},{9,... | collective-permute-start | bytes 147464
  750.2 23.7 %collective-permute-start.66 = (f32[8,1536]{1,0:T(8,128)S(1)}, f32[8,1536]{1,0:T(8,128)S(1)}, u32[]{:S(2)}, u32[]{:S(2)}) collective-permute-start(f32[8,1536]{1,0:T(8,128)S(1)} %fusion), channel_id=1, source_target_pairs={{0,62},{1,63},{2,64},{3,65},{4,66},{5,67},{6,68},{7,69},{8,70},{9,... | collective-permute-start | bytes 147464
  763.1 12.2 collective-permute-start.65
  764.4 7.0 collective-permute-start.68
  771.4 6.5 collective-permute-start.63
  772.7 6.5 collective-permute-start.62
  775.3 6.5 collective-permute-start.60
  776.6 6.5 collective-permute-start.59
  780.5 21.9 %collective-permute-start.56 = (f32[8,1536]{1,0:T(8,128)S(1)}, f32[8,1536]{1,0:T(8,128)S(1)}, u32[]{:S(2)}, u32[]{:S(2)}) collective-permute-start(f32[8,1536]{1,0:T(8,128)S(1)} %fusion), channel_id=1, source_target_pairs={{0,52},{1,53},{2,54},{3,55},{4,56},{5,57},{6,58},{7,59},{8,60},{9,... | collective-permute-start | bytes 147464
  781.8 26.5 %collective-permute-start.55 = (f32[8,1536]{1,0:T(8,128)S(1)}, f32[8,1536]{1,0:T(8,128)S(1)}, u32[]{:S(2)}, u32[]{:S(2)}) collective-permute-start(f32[8,1536]{1,0:T(8,128)S(1)} %fusion), channel_id=1, source_target_pairs={{0,51},{1,52},{2,53},{3,54},{4,55},{5,56},{6,57},{7,58},{8,59},{9,... | collective-permute-start | bytes 147464
  783.2 26.5 %collective-permute-start.54 = (f32[8,1536]{1,0:T(8,128)S(1)}, f32[8,1536]{1,0:T(8,128)S(1)}, u32[]{:S(2)}, u32[]{:S(2)}) collective-permute-start(f32[8,1536]{1,0:T(8,128)S(1)} %fusion), channel_id=1, source_target_pairs={{0,50},{1,51},{2,52},{3,53},{4,54},{5,55},{6,56},{7,57},{8,58},{9,... | collective-permute-start | bytes 147464
  784.5 26.8 %collective-permute-start.53 = (f32[8,1536]{1,0:T(8,128)S(1)}, f32[8,1536]{1,0:T(8,128)S(1)}, u32[]{:S(2)}, u32[]{:S(2)}) collective-permute-start(f32[8,1536]{1,0:T(8,128)S(1)} %fusion), channel_id=1, source_target_pairs={{0,49},{1,50},{2,51},{3,52},{4,53},{5,54},{6,55},{7,56},{8,57},{9,... | collective-permute-start | bytes 147464
  785.8 28.3 %collective-permute-start.52 = (f32[8,1536]{1,0:T(8,128)S(1)}, f32[8,1536]{1,0:T(8,128)S(1)}, u32[]{:S(2)}, u32[]{:S(2)}) collective-permute-start(f32[8,1536]{1,0:T(8,128)S(1)} %fusion), channel_id=1, source_target_pairs={{0,48},{1,49},{2,50},{3,51},{4,52},{5,53},{6,54},{7,55},{8,56},{9,... | collective-permute-start | bytes 147464
  802.4 16.0 collective-permute-start.51
  808.3 14.6 collective-permute-start.50
  809.6 14.6 collective-permute-start.49
  811.3 14.2 collective-permute-start.48
  814.1 12.8 collective-permute-start.47
  818.5 9.7 collective-permute-start.46
  824.2 10.3 collective-permute-start.44
  825.5 11.2 collective-permute-start.43
  826.8 11.8 collective-permute-start.42
  828.2 12.3 collective-permute-start.41
  829.5 13.1 collective-permute-start.40
  834.5 13.9 collective-permute-start.39
  836.7 24.8 %collective-permute-start.38 = (f32[8,1536]{1,0:T(8,128)S(1)}, f32[8,1536]{1,0:T(8,128)S(1)}, u32[]{:S(2)}, u32[]{:S(2)}) collective-permute-start(f32[8,1536]{1,0:T(8,128)S(1)} %fusion), channel_id=1, source_target_pairs={{0,34},{1,35},{2,36},{3,37},{4,38},{5,39},{6,40},{7,41},{8,42},{9,... | collective-permute-start | bytes 147464
  838.7 36.0 %collective-permute-start.37 = (f32[8,1536]{1,0:T(8,128)S(1)}, f32[8,1536]{1,0:T(8,128)S(1)}, u32[]{:S(2)}, u32[]{:S(2)}) collective-permute-start(f32[8,1536]{1,0:T(8,128)S(1)} %fusion), channel_id=1, source_target_pairs={{0,33},{1,34},{2,35},{3,36},{4,37},{5,38},{6,39},{7,40},{8,41},{9,... | collective-permute-start | bytes 147464
  840.5 47.4 %collective-permute-start.36 = (f32[8,1536]{1,0:T(8,128)S(1)}, f32[8,1536]{1,0:T(8,128)S(1)}, u32[]{:S(2)}, u32[]{:S(2)}) collective-permute-start(f32[8,1536]{1,0:T(8,128)S(1)} %fusion), channel_id=1, source_target_pairs={{0,32},{1,33},{2,34},{3,35},{4,36},{5,37},{6,38},{7,39},{8,40},{9,... | collective-permute-start | bytes 147464
  842.5 58.5 %collective-permute-start.35 = (f32[8,1536]{1,0:T(8,128)S(1)}, f32[8,1536]{1,0:T(8,128)S(1)}, u32[]{:S(2)}, u32[]{:S(2)}) collective-permute-start(f32[8,1536]{1,0:T(8,128)S(1)} %fusion), channel_id=1, source_target_pairs={{0,31},{1,32},{2,33},{3,34},{4,35},{5,36},{6,37},{7,38},{8,39},{9,... | collective-permute-start | bytes 147464
  848.4 65.7 %collective-permute-start.34 = (f32[8,1536]{1,0:T(8,128)S(1)}, f32[8,1536]{1,0:T(8,128)S(1)}, u32[]{:S(2)}, u32[]{:S(2)}) collective-permute-start(f32[8,1536]{1,0:T(8,128)S(1)} %fusion), channel_id=1, source_target_pairs={{0,30},{1,31},{2,32},{3,33},{4,34},{5,35},{6,36},{7,37},{8,38},{9,... | collective-permute-start | bytes 147464
  861.6 65.7 %collective-permute-start.33 = (f32[8,1536]{1,0:T(8,128)S(1)}, f32[8,1536]{1,0:T(8,128)S(1)}, u32[]{:S(2)}, u32[]{:S(2)}) collective-permute-start(f32[8,1536]{1,0:T(8,128)S(1)} %fusion), channel_id=1, source_target_pairs={{0,29},{1,30},{2,31},{3,32},{4,33},{5,34},{6,35},{7,36},{8,37},{9,... | collective-permute-start | bytes 147464
  874.7 65.7 %collective-permute-start.32 = (f32[8,1536]{1,0:T(8,128)S(1)}, f32[8,1536]{1,0:T(8,128)S(1)}, u32[]{:S(2)}, u32[]{:S(2)}) collective-permute-start(f32[8,1536]{1,0:T(8,128)S(1)} %fusion), channel_id=1, source_target_pairs={{0,28},{1,29},{2,30},{3,31},{4,32},{5,33},{6,34},{7,35},{8,36},{9,... | collective-permute-start | bytes 147464
  887.9 65.7 %collective-permute-start.31 = (f32[8,1536]{1,0:T(8,128)S(1)}, f32[8,1536]{1,0:T(8,128)S(1)}, u32[]{:S(2)}, u32[]{:S(2)}) collective-permute-start(f32[8,1536]{1,0:T(8,128)S(1)} %fusion), channel_id=1, source_target_pairs={{0,27},{1,28},{2,29},{3,30},{4,31},{5,32},{6,33},{7,34},{8,35},{9,... | collective-permute-start | bytes 147464
  901.0 65.7 %collective-permute-start.30 = (f32[8,1536]{1,0:T(8,128)S(1)}, f32[8,1536]{1,0:T(8,128)S(1)}, u32[]{:S(2)}, u32[]{:S(2)}) collective-permute-start(f32[8,1536]{1,0:T(8,128)S(1)} %fusion), channel_id=1, source_target_pairs={{0,26},{1,27},{2,28},{3,29},{4,30},{5,31},{6,32},{7,33},{8,34},{9,... | collective-permute-start | bytes 147464
  914.1 90.3 %collective-permute-start.29 = (f32[8,1536]{1,0:T(8,128)S(1)}, f32[8,1536]{1,0:T(8,128)S(1)}, u32[]{:S(2)}, u32[]{:S(2)}) collective-permute-start(f32[8,1536]{1,0:T(8,128)S(1)} %fusion), channel_id=1, source_target_pairs={{0,25},{1,26},{2,27},{3,28},{4,29},{5,30},{6,31},{7,32},{8,33},{9,... | collective-permute-start | bytes 147464
  927.3 89.1 %collective-permute-start.28 = (f32[8,1536]{1,0:T(8,128)S(1)}, f32[8,1536]{1,0:T(8,128)S(1)}, u32[]{:S(2)}, u32[]{:S(2)}) collective-permute-start(f32[8,1536]{1,0:T(8,128)S(1)} %fusion), channel_id=1, source_target_pairs={{0,24},{1,25},{2,26},{3,27},{4,28},{5,29},{6,30},{7,31},{8,32},{9,... | collective-permute-start | bytes 147464
  940.4 89.1 %collective-permute-start.27 = (f32[8,1536]{1,0:T(8,128)S(1)}, f32[8,1536]{1,0:T(8,128)S(1)}, u32[]{:S(2)}, u32[]{:S(2)}) collective-permute-start(f32[8,1536]{1,0:T(8,128)S(1)} %fusion), channel_id=1, source_target_pairs={{0,23},{1,24},{2,25},{3,26},{4,27},{5,28},{6,29},{7,30},{8,31},{9,... | collective-permute-start | bytes 147464
  953.6 89.7 %collective-permute-start.26 = (f32[8,1536]{1,0:T(8,128)S(1)}, f32[8,1536]{1,0:T(8,128)S(1)}, u32[]{:S(2)}, u32[]{:S(2)}) collective-permute-start(f32[8,1536]{1,0:T(8,128)S(1)} %fusion), channel_id=1, source_target_pairs={{0,22},{1,23},{2,24},{3,25},{4,26},{5,27},{6,28},{7,29},{8,30},{9,... | collective-permute-start | bytes 147464
  966.7 89.7 %collective-permute-start.25 = (f32[8,1536]{1,0:T(8,128)S(1)}, f32[8,1536]{1,0:T(8,128)S(1)}, u32[]{:S(2)}, u32[]{:S(2)}) collective-permute-start(f32[8,1536]{1,0:T(8,128)S(1)} %fusion), channel_id=1, source_target_pairs={{0,21},{1,22},{2,23},{3,24},{4,25},{5,26},{6,27},{7,28},{8,29},{9,... | collective-permute-start | bytes 147464
  1004.4 315.4 %collective-permute-start.24 = (f32[8,1536]{1,0:T(8,128)S(1)}, f32[8,1536]{1,0:T(8,128)S(1)}, u32[]{:S(2)}, u32[]{:S(2)}) collective-permute-start(f32[8,1536]{1,0:T(8,128)S(1)} %fusion), channel_id=1, source_target_pairs={{0,20},{1,21},{2,22},{3,23},{4,24},{5,25},{6,26},{7,27},{8,28},{9,... | collective-permute-start | bytes 147464
  1016.4 316.5 %collective-permute-start.23 = (f32[8,1536]{1,0:T(8,128)S(1)}, f32[8,1536]{1,0:T(8,128)S(1)}, u32[]{:S(2)}, u32[]{:S(2)}) collective-permute-start(f32[8,1536]{1,0:T(8,128)S(1)} %fusion), channel_id=1, source_target_pairs={{0,19},{1,20},{2,21},{3,22},{4,23},{5,24},{6,25},{7,26},{8,27},{9,... | collective-permute-start | bytes 147464
  1029.6 316.5 %collective-permute-start.22 = (f32[8,1536]{1,0:T(8,128)S(1)}, f32[8,1536]{1,0:T(8,128)}, u32[]{:S(2)}, u32[]{:S(2)}) collective-permute-start(f32[8,1536]{1,0:T(8,128)S(1)} %fusion), channel_id=1, source_target_pairs={{0,18},{1,19},{2,20},{3,21},{4,22},{5,23},{6,24},{7,25},{8,26},{9,... | collective-permute-start | bytes 147464
  1043.3 316.0 %collective-permute-start.21 = (f32[8,1536]{1,0:T(8,128)S(1)}, f32[8,1536]{1,0:T(8,128)}, u32[]{:S(2)}, u32[]{:S(2)}) collective-permute-start(f32[8,1536]{1,0:T(8,128)S(1)} %fusion), channel_id=1, source_target_pairs={{0,17},{1,18},{2,19},{3,20},{4,21},{5,22},{6,23},{7,24},{8,25},{9,... | collective-permute-start | bytes 147464
  1056.4 316.0 %collective-permute-start.20 = (f32[8,1536]{1,0:T(8,128)S(1)}, f32[8,1536]{1,0:T(8,128)}, u32[]{:S(2)}, u32[]{:S(2)}) collective-permute-start(f32[8,1536]{1,0:T(8,128)S(1)} %fusion), channel_id=1, source_target_pairs={{0,16},{1,17},{2,18},{3,19},{4,20},{5,21},{6,22},{7,23},{8,24},{9,... | collective-permute-start | bytes 147464
  1319.8 66.9 %collective-permute-start.19 = (f32[8,1536]{1,0:T(8,128)S(1)}, f32[8,1536]{1,0:T(8,128)}, u32[]{:S(2)}, u32[]{:S(2)}) collective-permute-start(f32[8,1536]{1,0:T(8,128)S(1)} %fusion), channel_id=1, source_target_pairs={{0,15},{1,16},{2,17},{3,18},{4,19},{5,20},{6,21},{7,22},{8,23},{9,... | collective-permute-start | bytes 147464
  1333.0 66.3 %collective-permute-start.18 = (f32[8,1536]{1,0:T(8,128)S(1)}, f32[8,1536]{1,0:T(8,128)}, u32[]{:S(2)}, u32[]{:S(2)}) collective-permute-start(f32[8,1536]{1,0:T(8,128)S(1)} %fusion), channel_id=1, source_target_pairs={{0,14},{1,15},{2,16},{3,17},{4,18},{5,19},{6,20},{7,21},{8,22},{9,... | collective-permute-start | bytes 147464
  1346.1 66.3 %collective-permute-start.17 = (f32[8,1536]{1,0:T(8,128)S(1)}, f32[8,1536]{1,0:T(8,128)}, u32[]{:S(2)}, u32[]{:S(2)}) collective-permute-start(f32[8,1536]{1,0:T(8,128)S(1)} %fusion), channel_id=1, source_target_pairs={{0,13},{1,14},{2,15},{3,16},{4,17},{5,18},{6,19},{7,20},{8,21},{9,... | collective-permute-start | bytes 147464
  1359.3 66.3 %collective-permute-start.16 = (f32[8,1536]{1,0:T(8,128)S(1)}, f32[8,1536]{1,0:T(8,128)}, u32[]{:S(2)}, u32[]{:S(2)}) collective-permute-start(f32[8,1536]{1,0:T(8,128)S(1)} %fusion), channel_id=1, source_target_pairs={{0,12},{1,13},{2,14},{3,15},{4,16},{5,17},{6,18},{7,19},{8,20},{9,... | collective-permute-start | bytes 147464
  1372.4 66.3 %collective-permute-start.15 = (f32[8,1536]{1,0:T(8,128)S(1)}, f32[8,1536]{1,0:T(8,128)}, u32[]{:S(2)}, u32[]{:S(2)}) collective-permute-start(f32[8,1536]{1,0:T(8,128)S(1)} %fusion), channel_id=1, source_target_pairs={{0,11},{1,12},{2,13},{3,14},{4,15},{5,16},{6,17},{7,18},{8,19},{9,... | collective-permute-start | bytes 147464
  1386.7 66.4 %collective-permute-start.14 = (f32[8,1536]{1,0:T(8,128)S(1)}, f32[8,1536]{1,0:T(8,128)S(1)}, u32[]{:S(2)}, u32[]{:S(2)}) collective-permute-start(f32[8,1536]{1,0:T(8,128)S(1)} %fusion), channel_id=1, source_target_pairs={{0,10},{1,11},{2,12},{3,13},{4,14},{5,15},{6,16},{7,17},{8,18},{9,... | collective-permute-start | bytes 147464
  1399.3 67.6 %collective-permute-start.13 = (f32[8,1536]{1,0:T(8,128)S(1)}, f32[8,1536]{1,0:T(8,128)S(1)}, u32[]{:S(2)}, u32[]{:S(2)}) collective-permute-start(f32[8,1536]{1,0:T(8,128)S(1)} %fusion), channel_id=1, source_target_pairs={{0,9},{1,10},{2,11},{3,12},{4,13},{5,14},{6,15},{7,16},{8,17},{9,1... | collective-permute-start | bytes 147464
  1412.4 67.6 %collective-permute-start.12 = (f32[8,1536]{1,0:T(8,128)S(1)}, f32[8,1536]{1,0:T(8,128)S(1)}, u32[]{:S(2)}, u32[]{:S(2)}) collective-permute-start(f32[8,1536]{1,0:T(8,128)S(1)} %fusion), channel_id=1, source_target_pairs={{0,8},{1,9},{2,10},{3,11},{4,12},{5,13},{6,14},{7,15},{8,16},{9,17... | collective-permute-start | bytes 147464
  1425.6 67.6 %collective-permute-start.11 = (f32[8,1536]{1,0:T(8,128)S(1)}, f32[8,1536]{1,0:T(8,128)S(1)}, u32[]{:S(2)}, u32[]{:S(2)}) collective-permute-start(f32[8,1536]{1,0:T(8,128)S(1)} %fusion), channel_id=1, source_target_pairs={{0,7},{1,8},{2,9},{3,10},{4,11},{5,12},{6,13},{7,14},{8,15},{9,16}... | collective-permute-start | bytes 147464
  1438.7 58.9 %collective-permute-start.10 = (f32[8,1536]{1,0:T(8,128)S(1)}, f32[8,1536]{1,0:T(8,128)S(1)}, u32[]{:S(2)}, u32[]{:S(2)}) collective-permute-start(f32[8,1536]{1,0:T(8,128)S(1)} %fusion), channel_id=1, source_target_pairs={{0,6},{1,7},{2,8},{3,9},{4,10},{5,11},{6,12},{7,13},{8,14},{9,15},... | collective-permute-start | bytes 147464
  1453.1 56.7 %collective-permute-start.9 = (f32[8,1536]{1,0:T(8,128)S(1)}, f32[8,1536]{1,0:T(8,128)}, u32[]{:S(2)}, u32[]{:S(2)}) collective-permute-start(f32[8,1536]{1,0:T(8,128)S(1)} %fusion), channel_id=1, source_target_pairs={{0,5},{1,6},{2,7},{3,8},{4,9},{5,10},{6,11},{7,12},{8,13},{9,14},{... | collective-permute-start | bytes 147464
  1466.8 43.0 %collective-permute-start.8 = (f32[8,1536]{1,0:T(8,128)S(1)}, f32[8,1536]{1,0:T(8,128)}, u32[]{:S(2)}, u32[]{:S(2)}) collective-permute-start(f32[8,1536]{1,0:T(8,128)S(1)} %fusion), channel_id=1, source_target_pairs={{0,4},{1,5},{2,6},{3,7},{4,8},{5,9},{6,10},{7,11},{8,12},{9,13},{1... | collective-permute-start | bytes 147464
  1480.0 29.9 %collective-permute-start.7 = (f32[8,1536]{1,0:T(8,128)S(1)}, f32[8,1536]{1,0:T(8,128)}, u32[]{:S(2)}, u32[]{:S(2)}) collective-permute-start(f32[8,1536]{1,0:T(8,128)S(1)} %fusion), channel_id=1, source_target_pairs={{0,3},{1,4},{2,5},{3,6},{4,7},{5,8},{6,9},{7,10},{8,11},{9,12},{10... | collective-permute-start | bytes 147464
  1493.1 16.7 collective-permute-start.6
  1497.6 14.9 collective-permute-start.5
  1630.5 7.2 collective-permute-start.3
  1634.3 6.9 collective-permute-start.2
  (79 other events, 3374.9 us)
Sparse Core Ops, SparseCore 0:
  9.9 726.1 all-gather.2
  1637.8 251.4 all-reduce.4
where the time goes:
time: 1910 us; the launch traced here: 1900 us
  blocking collectives  738 us (39%)
  starting transfers between devices  498 us (26%)
  local copies, waits for them, and re-layouts  278 us (15%)
  waiting for transfers between devices  245 us (13%)
  loops' own time  84.9 us (4%)
  matrix products  23.6 us (1%)
    unnamed x2, blocking collectives  738 us
    unnamed x64, starting transfers between devices  482 us
    psum x1, waiting for transfers between devices, body(): kernel_grad = lax.psum(jnp.stack(tap_rows) * scaling, ('seq', 'rep'))  238 us
    dynamic_slice x127, local copies, waits for them, and re-layouts, lap(): longer = join(subtotal, pieces[position])  164 us
    unnamed x153, local copies, waits for them, and re-layouts  112 us
    another operation x1, loops' own time, prefix(): return lax.fori_loop(0, count - 1, lap, subtotal)  84.9 us
  transfers between devices with their start and end apart: 71, of which 4 were waited for; matrix products, arithmetic and copies ran while one was open for 53% of the time, Pallas kernels for 0%

commit v1 on v0

v1 whole, which is shorter than its diff:
```python
import math

import jax
import jax.numpy as jnp
import numpy as np
from jax import lax
from jax.sharding import Mesh
from jax.sharding import PartitionSpec as P

AXES = ("z", "x", "yh", "core", "rep")
SIZES = (8, 4, 2, 2, 2)
GROUP = ("yh", "core")
PLANE = ("x", "rep")
QUARTERS = 4
BLOCK = 6
PAD = 56
LEFT_H, RIGHT_H = 32, 48
LEFT_U, RIGHT_U = 16, 32
SWAP = [(0, 1), (1, 0)]
BF = jnp.bfloat16
F32 = jnp.float32


def placement():
    out = np.zeros((384, 8 * PAD), np.float32)
    for zl in range(2):
        for x in range(4):
            for q in range(4):
                for rep in range(2):
                    for r in range(BLOCK):
                        row = (((zl * 4 + x) * 4 + q) * 2 + rep) * BLOCK + r
                        out[row, (x * 2 + rep) * PAD + (q * 2 + zl) * BLOCK + r] = 1
    return out


def turned():
    pairs = []
    for zq in range(4):
        for zl in range(2):
            for q in range(4):
                pairs.append(((zq * 2 + zl) * 4 + q, (q * 2 + zl) * 4 + zq))
    return pairs


def ordered(mine, other, first):
    return jnp.where(first, jnp.stack((mine, other)), jnp.stack((other, mine)))


def half(value, index, axis):
    size = value.shape[axis] // 2
    return lax.dynamic_slice_in_dim(value, index * size, size, axis)


def split_out(value, axis, dim, index):
    got = lax.ppermute(half(value, 1 - index, dim), axis, SWAP)
    return ordered(half(value, index, dim), got, index == 0)


def body(hidden_in, upstream, out_weight, conv_kernel, durations):
    taps = conv_kernel.shape[0]
    width = taps // 2
    yh, core = lax.axis_index("yh"), lax.axis_index("core")
    rep = lax.axis_index("rep")
    quarter = yh * 2 + core
    place = lax.axis_index("z") * 4 + lax.axis_index("x")
    frames = 4 * hidden_in.shape[1]
    scaling = 1.0 / math.sqrt(2 * 128 * hidden_in.shape[1])
    channels = 384

    lengths = ordered(durations[0], lax.ppermute(durations[0], "yh", SWAP), yh == 0)
    lengths = jnp.swapaxes(
        ordered(lengths, lax.ppermute(lengths, "core", SWAP), core == 0), 0, 1
    ).reshape(4, -1)
    totals = jnp.sum(lengths, axis=1)

    rows = lax.ppermute(out_weight, ("z", "yh", "core"), turned())
    note = jnp.zeros((2, 1536), BF).at[0, :4].set(totals.astype(BF))
    rows = jnp.concatenate((rows, note), axis=0)
    rows = lax.all_to_all(
        jnp.broadcast_to(rows[None], (8,) + rows.shape), "z", 0, 0, tiled=True
    )
    note = jnp.zeros((PAD - 48, 1536), BF).at[0, :32].set(rows[:, 6, :4].reshape(32))
    rows = jnp.concatenate((rows[:, :BLOCK].reshape(48, 1536), note), axis=0)
    rows = lax.all_to_all(
        jnp.broadcast_to(rows[None], (8,) + rows.shape), PLANE, 0, 0, tiled=True
    )
    notes = rows[:, 48, :32].reshape(4, 2, 8, 4).astype(F32)
    notes = jnp.where(rep == 0, notes[:, 0], notes[:, 1])
    spread = jnp.asarray(placement(), BF)
    weights = jnp.dot(
        spread, rows.reshape(8 * PAD, 1536), preferred_element_type=F32
    ).astype(BF)

    hidden = split_out(hidden_in[0], "yh", 1, yh)
    hidden = split_out(hidden, "core", 2, core)
    hidden = jnp.swapaxes(hidden, 0, 1).reshape(frames, channels)
    grads = ordered(upstream[0], lax.ppermute(upstream[0], "yh", SWAP), yh == 0)
    grads = ordered(grads, lax.ppermute(grads, "core", SWAP), core == 0)
    grads = jnp.swapaxes(grads, 0, 1).reshape(frames, 1536)
    forward = [(i, i + 1) for i in range(31)]
    backward = [(i + 1, i) for i in range(31)]
    ring = ("z", "x")
    hidden_ext = jnp.concatenate(
        (
            lax.ppermute(hidden[-LEFT_H:], ring, forward),
            hidden,
            lax.ppermute(hidden[:RIGHT_H], ring, backward),
        )
    ).astype(F32)
    grads_ext = jnp.concatenate(
        (
            lax.ppermute(grads[-LEFT_U:], ring, forward),
            grads,
            lax.ppermute(grads[:RIGHT_U], ring, backward),
        )
    )
    kernel_f = lax.dynamic_slice_in_dim(
        conv_kernel, quarter * channels, channels, 1
    ).astype(F32)

    wide = frames + LEFT_U + RIGHT_U
    conv_out = jnp.zeros((wide, channels), F32)
    for k in range(taps):
        begin = LEFT_H - LEFT_U + k - width
        conv_out = conv_out + kernel_f[k] * hidden_ext[begin : begin + wide]
    sig = jax.nn.sigmoid(conv_out)
    activated = (conv_out * sig)[LEFT_U : LEFT_U + frames].astype(BF)
    slope = sig * (1.0 + conv_out * (1.0 - sig))
    activated = jnp.dot(activated, spread, preferred_element_type=F32).astype(BF)
    weight_part = lax.dot_general(
        activated, grads, (((0,), (0,)), ((), ())), preferred_element_type=F32
    ).astype(BF)

    grad_act = lax.dot_general(
        grads_ext, weights, (((1,), (1,)), ((), ())), preferred_element_type=F32
    )
    grad_conv = (grad_act * slope).astype(BF).astype(F32)
    longer = frames + 16
    frame_sum = jnp.zeros((longer, channels), F32)
    for k in range(taps):
        begin = LEFT_U + width - k
        frame_sum = frame_sum + kernel_f[k] * grad_conv[begin : begin + longer]
    frame_grad = frame_sum.astype(BF)
    own_grad = grad_conv[LEFT_U : LEFT_U + frames]
    tap_rows = [
        jnp.sum(
            own_grad * hidden_ext[LEFT_H + k - width : LEFT_H + k - width + frames],
            axis=0,
        )
        for k in range(taps)
    ]
    tap_rows = jnp.stack(tap_rows + [jnp.zeros_like(tap_rows[0])]).reshape(8, 1536)

    high = tap_rows.astype(BF)
    low = (tap_rows - high.astype(F32)).astype(BF)
    parts = weight_part.reshape(8, PAD, 1536)
    parts = jnp.concatenate(
        (parts[:, :48], high[:, None], low[:, None], parts[:, 50:]), axis=1
    )
    parts = lax.all_to_all(parts, PLANE, 0, 0, tiled=True)
    parts = jnp.sum(parts.astype(F32), axis=0)
    taps_part = parts[48] + parts[49]
    high = taps_part.astype(BF)
    low = (taps_part - high.astype(F32)).astype(BF)
    parts = jnp.concatenate(
        (
            parts[:48].astype(BF).reshape(8, BLOCK, 1536),
            jnp.broadcast_to(high, (8, 1, 1536)),
            jnp.broadcast_to(low, (8, 1, 1536)),
        ),
        axis=1,
    )
    parts = lax.all_to_all(parts, "z", 0, 0, tiled=True)
    parts = jnp.sum(parts.astype(F32), axis=0) * scaling
    weight_grad = lax.ppermute(
        parts[:BLOCK], ("z", "yh", "core"), [(b, a) for a, b in turned()]
    )
    taps_sum = (parts[6] + parts[7])[None]
    taps_all = lax.all_to_all(
        jnp.broadcast_to(taps_sum, (32, 1536)), ("x", "yh", "core", "rep"), 0, 0, tiled=True
    )
    taps_all = taps_all.reshape(4, 4, 2, 4, channels)
    kernel_grad = taps_all.transpose(0, 2, 3, 1, 4).reshape(32, 1536)[:taps]

    order = lax.iota(jnp.int32, 8)[None, :] * 4 + lax.iota(jnp.int32, 4)[:, None]
    before = jnp.sum(jnp.where(order < place, jnp.sum(notes, axis=2), 0.0))
    start = before.astype(jnp.int32) - place * frames
    ends = start + jnp.cumsum(lengths.reshape(-1))
    starts = ends - lengths.reshape(-1)
    at = lax.iota(jnp.int32, longer)
    covers = (at[None] >= starts[:, None]) & (at[None] < ends[:, None])
    gloss = jnp.dot(covers.astype(BF), frame_grad, preferred_element_type=F32)

    def back(value):
        value = value.reshape(2, 2, -1, channels)
        kept = lax.dynamic_index_in_dim(value, core, 1, False)
        got = lax.ppermute(
            lax.dynamic_index_in_dim(value, 1 - core, 1, False), "core", SWAP
        )
        value = jnp.where(
            core == 0,
            jnp.concatenate((kept, got), axis=2),
            jnp.concatenate((got, kept), axis=2),
        )
        kept = lax.dynamic_index_in_dim(value, yh, 0, False)
        got = lax.ppermute(
            lax.dynamic_index_in_dim(value, 1 - yh, 0, False), "yh", SWAP
        )
        return jnp.where(
            yh == 0,
            jnp.concatenate((kept, got), axis=1),
            jnp.concatenate((got, kept), axis=1),
        )

    return (
        back(frame_grad[:frames])[None],
        back(gloss)[None],
        weight_grad,
        kernel_grad,
    )


def solution(mesh):
    fine = Mesh(mesh.devices.reshape(SIZES), AXES)
    seq = ("z", "x", "yh", "core")
    rows = P(seq + ("rep",), None)
    in_specs = (P("rep", seq, None), P("rep", seq, None), rows, P(), P("rep", seq))
    out_specs = (P("rep", seq, None), P("rep", seq, None), rows, P())
    return jax.shard_map(
        body, mesh=fine, in_specs=in_specs, out_specs=out_specs, check_vma=False
    )
```

time: 1910 us -> 146 us (0.08)
  blocking collectives: 738 us -> 0 us
  starting transfers between devices: 498 us -> 79.3 us
  local copies, waits for them, and re-layouts: 278 us -> 12.1 us
  waiting for transfers between devices: 245 us -> 23.7 us
  loops' own time: 84.9 us -> 0 us
    unnamed x2 -> x0, blocking collectives: 738 us -> none
    unnamed x64 -> x0, starting transfers between devices: 482 us -> none
    psum x1 -> x0, waiting for transfers between devices: 238 us -> none  [body(): kernel_grad = lax.psum(jnp.stack(tap_rows) * scaling, ('seq', 'rep'))]
    dynamic_slice x127 -> x3, local copies, waits for them, and re-layouts: 164 us -> 1.1 us  [the longest x1 1.05 us: half(): return lax.dynamic_slice_in_dim(value, index * size, size, axis)]
    unnamed x153 -> x136, local copies, waits for them, and re-layouts: 112 us -> 1.59 us
    another operation x1 -> x0, loops' own time: 84.9 us -> none  [prefix(): return lax.fori_loop(0, count - 1, lap, subtotal)]
    ppermute x5 -> x16, starting transfers between devices: 15.9 us -> 51.2 us  [the longest x2 10.6 us: back(): lax.ppermute(lax.dynamic_index_in_dim(value, 1 - yh, 0, False), 'yh', SWAP)]
    all_to_all x0 -> x5, starting transfers between devices: none -> 28 us  [the longest x1 7.14 us: body(): parts = lax.all_to_all(parts, 'z', 0, 0, tiled=True)]
  transfers between devices with their start and end apart: 71 -> 21, of which waited for: 4 -> 7; matrix products, arithmetic and copies ran while one was open for 53% -> 20% of each run, Pallas kernels for 0% -> 0%
where the time goes in v1:
time: 146 us; the launch traced here: 145 us
  starting transfers between devices  79.3 us (54%)
  waiting for transfers between devices  23.7 us (16%)
  other arithmetic  20.1 us (14%)
  local copies, waits for them, and re-layouts  12.1 us (8%)
  matrix products  7.45 us (5%)
  between operations  2.95 us (2%)
    ppermute x2, starting transfers between devices, back(): lax.ppermute(lax.dynamic_index_in_dim(value, 1 - yh, 0, False), 'yh', SWAP)  10.6 us
    all_to_all x1, waiting for transfers between devices, body(): lax.all_to_all(jnp.broadcast_to(taps_sum, (32, 1536)), ('x', 'yh', 'core'...  7.32 us
    all_to_all x1, starting transfers between devices, body(): parts = lax.all_to_all(parts, 'z', 0, 0, tiled=True)  7.14 us
    all_to_all x1, starting transfers between devices, body(): parts = lax.all_to_all(parts, PLANE, 0, 0, tiled=True)  6.88 us
    ppermute x2, starting transfers between devices, split_out(): got = lax.ppermute(half(value, 1 - index, dim), axis, SWAP)  6.76 us
    all_to_all x1, starting transfers between devices, body(): lax.all_to_all(jnp.broadcast_to(taps_sum, (32, 1536)), ('x', 'yh', 'core'...  6.22 us
    all_to_all x1, waiting for transfers between devices, body(): lax.all_to_all(jnp.broadcast_to(rows[None], (8,) + rows.shape), 'z', 0, 0...  6.19 us
    ppermute x1, starting transfers between devices, body(): lax.ppermute(parts[:BLOCK], ('z', 'yh', 'core'), [(b, a) for a, b in turn...  5.83 us
  transfers between devices with their start and end apart: 21, of which 7 were waited for; matrix products, arithmetic and copies ran while one was open for 20% of the time, Pallas kernels for 0%

profile of v1, /device:TPU:1, one launch (start us, length us, event | category | flops | bytes accessed | tf_op | source)
XLA Modules:
  0.0 145.5 jit_solution(9021816661691964669)
XLA Ops:
  0.6 3.8 %collective-permute-start.5 = (s32[8]{0:T(128)}, s32[8]{0:T(128)S(1)}, u32[]{:S(2)}, u32[]{:S(2)}) collective-permute-start(s32[8]{0:T(128)} %bitcast.88), channel_id=1, source_target_pairs={{0,4},{4,0},{1,5},{5,1},{2,6},{6,2},{3,7},{7,3},{8,12},{12,8},{9,1... | collective-permute-start | bytes 104 | tf_op jit(solution)/shard_map/ppermute | solution.py:70
  4.5 5.7 %collective-permute-start.4 = (bf16[6,1536]{1,0:T(8,128)(2,1)}, bf16[6,1536]{1,0:T(8,128)(2,1)S(1)}, u32[]{:S(2)}, u32[]{:S(2)}) collective-permute-start(bf16[6,1536]{1,0:T(8,128)(2,1)} %param.12), channel_id=1, source_target_pairs={{0,0},{2,64},{4,128},{6,192},{32,32},{34,96},{36,160},{38,224},{64... | collective-permute-start | bytes 55304 | tf_op jit(solution)/shard_map/ppermute | solution.py:76
  10.2 1.1 constant_dynamic-slice_fusion.3
  11.3 5.8 %collective-permute-start.7 = (bf16[128,768]{1,0:T(8,128)(2,1)S(1)}, bf16[128,768]{1,0:T(8,128)(2,1)S(1)}, u32[]{:S(2)}, u32[]{:S(2)}) collective-permute-start(bf16[128,768]{1,0:T(8,128)(2,1)S(1)} %get-tuple-element.107), channel_id=1, source_target_pairs={{0,4},{4,0},{1,5},{5,1},{2,6},{6,2},{3,7},{7,3},{8,12},{12,8},{9,1... | collective-permute-start | bytes 589832 | tf_op jit(solution)/shard_map/ppermute | solution.py:55
  17.2 0.7 dynamic-slice_convert_fusion
  18.4 0.7 add_select_fusion.2
  19.1 1.6 %collective-permute-start.6 = (s32[2,8]{1,0:T(2,128)S(1)}, s32[2,8]{1,0:T(2,128)S(1)}, u32[]{:S(2)}, u32[]{:S(2)}) collective-permute-start(s32[2,8]{1,0:T(2,128)S(1)} %add_select_fusion.2), channel_id=1, source_target_pairs={{0,2},{2,0},{1,3},{3,1},{4,6},{6,4},{5,7},{7,5},{8,10},{10,8},{9,1... | collective-permute-start | bytes 200 | tf_op jit(solution)/shard_map/ppermute | solution.py:72
  20.8 0.7 add_select_fusion.1
  21.6 0.1 fusion.128
  21.9 0.7 broadcast_in_dim.13
  22.6 3.4 %all-to-all-start = ((bf16[8,8,1536]{2,1,0:T(8,128)(2,1)}), bf16[8,8,1536]{2,1,0:T(8,128)(2,1)S(1)}, u32[]{:S(2)}, u32[]{:S(2)}) async-start(bf16[8,8,1536]{2,1,0:T(8,128)(2,1)} %broadcast_in_dim.13), calls=%async_computation | async-start | bytes 393216 | tf_op jit(solution)/shard_map/all_to_all | solution.py:79
  26.0 0.5 iota_multiply_fusion
  26.6 0.7 reshape.409
  27.5 1.0 collective-permute-start.8
  28.5 6.2 %all-to-all-done = bf16[8,8,1536]{2,1,0:T(8,128)(2,1)S(1)} async-done(((bf16[8,8,1536]{2,1,0:T(8,128)(2,1)}), bf16[8,8,1536]{2,1,0:T(8,128)(2,1)S(1)}, u32[]{:S(2)}, u32[]{:S(2)}) %all-to-all-start) | async-done | bytes 196640 | tf_op jit(solution)/shard_map/all_to_all | solution.py:79
  34.9 1.2 broadcast_in_dim.14
  36.1 4.4 %all-to-all-start.1 = ((bf16[8,56,1536]{2,1,0:T(8,128)(2,1)}), bf16[8,56,1536]{2,1,0:T(8,128)(2,1)}, u32[]{:S(2)}, u32[]{:S(2)}) async-start(bf16[8,56,1536]{2,1,0:T(8,128)(2,1)} %broadcast_in_dim.14), calls=%async_computation.1 | async-start | bytes 2752512 | tf_op jit(solution)/shard_map/all_to_all | solution.py:84
  40.6 3.2 %collective-permute-start.9 = (bf16[32,384]{1,0:T(8,128)(2,1)S(1)}, bf16[32,384]{1,0:T(8,128)(2,1)S(1)}, u32[]{:S(2)}, u32[]{:S(2)}) collective-permute-start(bf16[32,384]{1,0:T(8,128)(2,1)S(1)} %slice.650), channel_id=1, source_target_pairs={{0,8},{8,16},{16,24},{24,32},{32,40},{40,48},{48,56},{56,64},{64,7... | collective-permute-start | bytes 73736 | tf_op jit(solution)/shard_map/ppermute | solution.py:105
  43.9 1.3 collective-permute-start.10
  45.2 0.1 maximum_select_fusion.1
  45.3 3.6 %collective-permute-start.1 = (bf16[2,128,1536]{2,1,0:T(8,128)(2,1)S(1)}, bf16[2,128,1536]{2,1,0:T(8,128)(2,1)S(1)}, u32[]{:S(2)}, u32[]{:S(2)}) collective-permute-start(bf16[2,128,1536]{2,1,0:T(8,128)(2,1)S(1)} %maximum_select_fusion.1), channel_id=1, source_target_pairs={{0,2},{2,0},{1,3},{3,1},{4,6},{6,4},{5,7},{7,5},{8,10},{10,8},{9,1... | collective-permute-start | bytes 2359304 | tf_op jit(solution)/shard_map/ppermute | solution.py:98
  49.0 0.1 fusion.108
  49.1 4.2 %collective-permute-done.9 = bf16[32,384]{1,0:T(8,128)(2,1)S(1)} collective-permute-done((bf16[32,384]{1,0:T(8,128)(2,1)S(1)}, bf16[32,384]{1,0:T(8,128)(2,1)S(1)}, u32[]{:S(2)}, u32[]{:S(2)}) %collective-permute-start.9) | collective-permute-done | bytes 24608 | tf_op jit(solution)/shard_map/ppermute | solution.py:105
  53.3 2.2 %collective-permute-done.10 = bf16[48,384]{1,0:T(8,128)(2,1)S(1)} collective-permute-done((bf16[48,384]{1,0:T(8,128)(2,1)S(1)}, bf16[48,384]{1,0:T(8,128)(2,1)S(1)}, u32[]{:S(2)}, u32[]{:S(2)}) %collective-permute-start.10) | collective-permute-done | bytes 36896 | tf_op jit(solution)/shard_map/ppermute | solution.py:107
  55.9 4.3 %add_divide_fusion = (f32[560,384]{1,0:T(8,128)}, f32[560,384]{1,0:T(8,128)S(1)}) fusion(f32[592,384]{1,0:T(8,128)S(1)} %maximum_convert_fusion, f32[384]{0:T(512)S(1)} %get-tuple-element.60, f32[384]{0:T(512)S(1)} %get-tuple-element.61, f32[384]{0:T(512)S(1)} %get-tuple-element.62, f32[384]{0:T(512)S(1)} %get-tuple-element.63, ...), kind=kLoop, calls=%fused_computation.76 | loop fusion | flops 13762560 | bytes 28432896 | tf_op jit(solution)/shard_map/div | solution.py:126
  60.1 0.3 maximum_select_fusion
  60.4 0.6 slice.646
  61.0 0.6 slice.647
  61.7 2.6 %collective-permute-start.2 = (bf16[16,1536]{1,0:T(8,128)(2,1)}, bf16[16,1536]{1,0:T(8,128)(2,1)}, u32[]{:S(2)}, u32[]{:S(2)}) collective-permute-start(bf16[16,1536]{1,0:T(8,128)(2,1)} %slice.646), channel_id=1, source_target_pairs={{0,8},{8,16},{16,24},{24,32},{32,40},{40,48},{48,56},{56,64},{64,7... | collective-permute-start | bytes 147464 | tf_op jit(solution)/shard_map/ppermute | solution.py:112
  64.3 1.5 %collective-permute-start.3 = (bf16[32,1536]{1,0:T(8,128)(2,1)}, bf16[32,1536]{1,0:T(8,128)(2,1)}, u32[]{:S(2)}, u32[]{:S(2)}) collective-permute-start(bf16[32,1536]{1,0:T(8,128)(2,1)} %slice.647), channel_id=1, source_target_pairs={{8,0},{16,8},{24,16},{32,24},{40,32},{48,40},{56,48},{64,56},{72,6... | collective-permute-start | bytes 294920 | tf_op jit(solution)/shard_map/ppermute | solution.py:114
  65.8 3.5 %convolution_convert_fusion = bf16[448,1536]{1,0:T(8,128)(2,1)} fusion(bf16[512,1536]{1,0:T(8,128)(2,1)S(1)} %bitcast.65, bf16[384,448]{1,0:T(8,128)(2,1)} %constant.126.clone, f32[560,384]{1,0:T(8,128)} %get-tuple-element.92, f32[560,384]{1,0:T(8,128)S(1)} %get-tuple-element.93), kind=kOutput, calls=%fused_computation | convolution fusion | flops 882114560 | bytes 4915200 | tf_op jit(solution)/shard_map/dot_general | solution.py:130
  69.3 1.0 slice.783
  70.2 2.4 %slice.750 = bf16[8,48,1536]{2,1,0:T(8,128)(2,1)} slice(bf16[8,56,1536]{2,1,0:T(8,128)(2,1)} %bitcast.68), slice={[0:8], [0:48], [0:1536]} | slice | bytes 2359296 | tf_op jit(solution)/shard_map/slice | solution.py:158
  72.6 3.7 %fusion.12 = f32[560,384]{1,0:T(8,128)S(1)} fusion(bf16[32,1536]{1,0:T(8,128)(2,1)} %collective-permute-done.3, bf16[512,1536]{1,0:T(8,128)(2,1)S(1)} %bitcast.66, bf16[16,1536]{1,0:T(8,128)(2,1)} %collective-permute-done.2, bf16[448,1536]{1,0:T(8,128)(2,1)} %bitcast.16, bf16[384,448]{1,0:T(8,128)(2,1)} %constant.126.clone, f32[560,384]{1,0:T(8,128)} %copy-done.1), kind=kOutput, calls=%fused_computation.14 | convolution fusion | flops 1196986368 | bytes 5160960 | tf_op jit(solution)/shard_map/dot_general | solution.py:134
  76.4 0.9 fusion.76
  77.2 0.8 fusion.93
  78.1 1.1 fusion.84
  79.5 0.1 stack.240
  79.8 1.3 pad_maximum_fusion
  81.4 6.9 %all-to-all-start.2 = ((bf16[8,56,1536]{2,1,0:T(8,128)(2,1)}), bf16[8,56,1536]{2,1,0:T(8,128)(2,1)S(1)}, u32[]{:S(2)}, u32[]{:S(2)}) async-start(bf16[8,56,1536]{2,1,0:T(8,128)(2,1)} %pad_maximum_fusion), calls=%async_computation.2 | async-start | bytes 2752512 | tf_op jit(solution)/shard_map/all_to_all | solution.py:160
  88.6 3.2 %fusion.46 = bf16[528,384]{1,0:T(8,128)(2,1)S(1)} fusion(f32[560,384]{1,0:T(8,128)S(1)} %fusion.12, f32[384]{0:T(512)S(1)} %copy-done.6, f32[384]{0:T(512)S(1)} %copy-done.8, f32[384]{0:T(512)S(1)} %copy-done.10, f32[384]{0:T(512)S(1)} %copy-done.12, f32[384]{0:T(512)S(1)} %copy-done.14, f32[384]{0:T(512)S(1)} %copy-done.16, f32[384]{0:T(512)S(1)} %copy-done.18, ...), kind=kLoop, calls=%fused_computation.79 | loop fusion | flops 12570624 | bytes 25594368 | tf_op jit(solution)/shard_map/convert_element_type | solution.py:143
  91.8 0.7 fusion.124
  92.7 0.6 select_reduce_fusion
  94.0 0.1 add_reduce_fusion
  94.2 0.2 fusion.115
  94.4 4.4 %collective-permute-start.13 = (f32[2,8,384]{2,1,0:T(8,128)S(1)}, f32[2,8,384]{2,1,0:T(8,128)S(1)}, u32[]{:S(2)}, u32[]{:S(2)}) collective-permute-start(f32[2,8,384]{2,1,0:T(8,128)S(1)} %get-tuple-element.113), channel_id=1, source_target_pairs={{0,2},{2,0},{1,3},{3,1},{4,6},{6,4},{5,7},{7,5},{8,10},{10,8},{9,1... | collective-permute-start | bytes 73736 | tf_op jit(solution)/shard_map/ppermute | solution.py:197
  98.9 0.1 collective-permute-start.11
  99.0 0.7 collective-permute-done.13
  99.7 5.6 %collective-permute-start.14 = (f32[8,768]{1,0:T(8,128)S(1)}, f32[8,768]{1,0:T(8,128)S(1)}, u32[]{:S(2)}, u32[]{:S(2)}) collective-permute-start(f32[8,768]{1,0:T(8,128)S(1)} %get-tuple-element.111), channel_id=1, source_target_pairs={{0,4},{4,0},{1,5},{5,1},{2,6},{6,2},{3,7},{7,3},{8,12},{12,8},{9,1... | collective-permute-start | bytes 73736 | tf_op jit(solution)/shard_map/ppermute | solution.py:206
  105.3 0.2 convert_reduce_fusion
  105.7 0.8 pad_maximum_fusion.1
  106.6 7.1 %all-to-all-start.3 = ((bf16[8,8,1536]{2,1,0:T(8,128)(2,1)}), bf16[8,8,1536]{2,1,0:T(8,128)(2,1)S(1)}, u32[]{:S(2)}, u32[]{:S(2)}) async-start(bf16[8,8,1536]{2,1,0:T(8,128)(2,1)} %pad_maximum_fusion.1), calls=%async_computation.3 | async-start | bytes 393216 | tf_op jit(solution)/shard_map/all_to_all | solution.py:173
  113.7 0.6 maximum_select_fusion.7
  114.4 0.1 maximum_select_fusion.4
  114.5 5.0 %collective-permute-start.12 = (bf16[128,768]{1,0:T(8,128)(2,1)S(1)}, bf16[128,768]{1,0:T(8,128)(2,1)S(1)}, u32[]{:S(2)}, u32[]{:S(2)}) collective-permute-start(bf16[128,768]{1,0:T(8,128)(2,1)S(1)} %get-tuple-element.101), channel_id=1, source_target_pairs={{0,4},{4,0},{1,5},{5,1},{2,6},{6,2},{3,7},{7,3},{8,12},{12,8},{9,1... | collective-permute-start | bytes 589832 | tf_op jit(solution)/shard_map/ppermute | solution.py:206
  119.5 3.0 %all-to-all-done.3 = bf16[8,8,1536]{2,1,0:T(8,128)(2,1)S(1)} async-done(((bf16[8,8,1536]{2,1,0:T(8,128)(2,1)}), bf16[8,8,1536]{2,1,0:T(8,128)(2,1)S(1)}, u32[]{:S(2)}, u32[]{:S(2)}) %all-to-all-start.3) | async-done | bytes 196640 | tf_op jit(solution)/shard_map/all_to_all | solution.py:173
  122.5 5.8 %collective-permute-start.15 = (f32[6,1536]{1,0:T(8,128)S(1)}, f32[6,1536]{1,0:T(8,128)S(1)}, u32[]{:S(2)}, u32[]{:S(2)}) collective-permute-start(f32[6,1536]{1,0:T(8,128)S(1)} %bitcast.86), channel_id=1, source_target_pairs={{0,0},{64,2},{128,4},{192,6},{32,32},{96,34},{160,36},{224,38},{2,... | collective-permute-start | bytes 110600 | tf_op jit(solution)/shard_map/ppermute | solution.py:175
  128.4 0.8 broadcast_in_dim.18
  129.1 6.2 %all-to-all-start.4 = ((f32[32,1,1536]{2,1,0:T(1,128)}), f32[32,1,1536]{2,1,0:T(1,128)S(1)}, u32[]{:S(2)}, u32[]{:S(2)}) async-start(f32[32,1,1536]{2,1,0:T(1,128)} %broadcast_in_dim.18), calls=%async_computation.4 | async-start | bytes 393216 | tf_op jit(solution)/shard_map/all_to_all | solution.py:179
  135.4 0.8 maximum_select_fusion.5
  136.2 7.3 %all-to-all-done.4 = f32[32,1,1536]{2,1,0:T(1,128)S(1)} async-done(((f32[32,1,1536]{2,1,0:T(1,128)}), f32[32,1,1536]{2,1,0:T(1,128)S(1)}, u32[]{:S(2)}, u32[]{:S(2)}) %all-to-all-start.4) | async-done | bytes 196640 | tf_op jit(solution)/shard_map/all_to_all | solution.py:179
  143.5 0.5 reduce.42
  144.1 0.7 copy.45
  144.8 0.6 copy.47
  (224 shorter events, 2.3 us)
Async XLA Ops:
  0.6 17.8 %collective-permute-start.5 = (s32[8]{0:T(128)}, s32[8]{0:T(128)S(1)}, u32[]{:S(2)}, u32[]{:S(2)}) collective-permute-start(s32[8]{0:T(128)} %bitcast.88), channel_id=1, source_target_pairs={{0,4},{4,0},{1,5},{5,1},{2,6},{6,2},{3,7},{7,3},{8,12},{12,8},{9,1... | collective-permute-start | bytes 104 | tf_op jit(solution)/shard_map/ppermute | solution.py:70
  4.5 17.5 %collective-permute-start.4 = (bf16[6,1536]{1,0:T(8,128)(2,1)}, bf16[6,1536]{1,0:T(8,128)(2,1)S(1)}, u32[]{:S(2)}, u32[]{:S(2)}) collective-permute-start(bf16[6,1536]{1,0:T(8,128)(2,1)} %param.12), channel_id=1, source_target_pairs={{0,0},{2,64},{4,128},{6,192},{32,32},{34,96},{36,160},{38,224},{64... | collective-permute-start | bytes 55304 | tf_op jit(solution)/shard_map/ppermute | solution.py:76
  11.3 16.1 %collective-permute-start.7 = (bf16[128,768]{1,0:T(8,128)(2,1)S(1)}, bf16[128,768]{1,0:T(8,128)(2,1)S(1)}, u32[]{:S(2)}, u32[]{:S(2)}) collective-permute-start(bf16[128,768]{1,0:T(8,128)(2,1)S(1)} %get-tuple-element.107), channel_id=1, source_target_pairs={{0,4},{4,0},{1,5},{5,1},{2,6},{6,2},{3,7},{7,3},{8,12},{12,8},{9,1... | collective-permute-start | bytes 589832 | tf_op jit(solution)/shard_map/ppermute | solution.py:55
  17.1 28.1 %collective-permute-start = (bf16[128,1536]{1,0:T(8,128)(2,1)}, bf16[128,1536]{1,0:T(8,128)(2,1)S(1)}, u32[]{:S(2)}, u32[]{:S(2)}) collective-permute-start(bf16[128,1536]{1,0:T(8,128)(2,1)} %bitcast.73), channel_id=1, source_target_pairs={{0,4},{4,0},{1,5},{5,1},{2,6},{6,2},{3,7},{7,3},{8,12},{12,8},{9,1... | collective-permute-start | bytes 1179656 | tf_op jit(solution)/shard_map/ppermute | solution.py:97
  18.0 37.6 %copy-start.41 = (f32[384]{0:T(512)}, f32[384]{0:T(512)S(1)}, u32[]{:S(2)}) copy-start(f32[384]{0:T(512)S(1)} %get-tuple-element.78) | copy-start | bytes 4612
  18.0 37.6 %copy-start.43 = (f32[384]{0:T(512)}, f32[384]{0:T(512)S(1)}, u32[]{:S(2)}) copy-start(f32[384]{0:T(512)S(1)} %get-tuple-element.79) | copy-start | bytes 4612
  18.0 37.6 %copy-start.45 = (f32[384]{0:T(512)}, f32[384]{0:T(512)S(1)}, u32[]{:S(2)}) copy-start(f32[384]{0:T(512)S(1)} %get-tuple-element.80) | copy-start | bytes 4612
  18.0 37.6 %copy-start.47 = (f32[384]{0:T(512)}, f32[384]{0:T(512)S(1)}, u32[]{:S(2)}) copy-start(f32[384]{0:T(512)S(1)} %get-tuple-element.81) | copy-start | bytes 4612
  18.0 37.6 %copy-start.49 = (f32[384]{0:T(512)}, f32[384]{0:T(512)S(1)}, u32[]{:S(2)}) copy-start(f32[384]{0:T(512)S(1)} %get-tuple-element.82) | copy-start | bytes 4612
  18.0 37.6 %copy-start.51 = (f32[384]{0:T(512)}, f32[384]{0:T(512)S(1)}, u32[]{:S(2)}) copy-start(f32[384]{0:T(512)S(1)} %get-tuple-element.83) | copy-start | bytes 4612
  18.0 37.6 %copy-start.53 = (f32[384]{0:T(512)}, f32[384]{0:T(512)S(1)}, u32[]{:S(2)}) copy-start(f32[384]{0:T(512)S(1)} %get-tuple-element.84) | copy-start | bytes 4612
  18.0 37.6 %copy-start.55 = (f32[384]{0:T(512)}, f32[384]{0:T(512)S(1)}, u32[]{:S(2)}) copy-start(f32[384]{0:T(512)S(1)} %get-tuple-element.85) | copy-start | bytes 4612
  18.1 37.6 %copy-start.57 = (f32[384]{0:T(512)}, f32[384]{0:T(512)S(1)}, u32[]{:S(2)}) copy-start(f32[384]{0:T(512)S(1)} %get-tuple-element.86) | copy-start | bytes 4612
  18.1 37.6 %copy-start.59 = (f32[384]{0:T(512)}, f32[384]{0:T(512)S(1)}, u32[]{:S(2)}) copy-start(f32[384]{0:T(512)S(1)} %get-tuple-element.87) | copy-start | bytes 4612
  18.1 37.6 %copy-start.61 = (f32[384]{0:T(512)}, f32[384]{0:T(512)S(1)}, u32[]{:S(2)}) copy-start(f32[384]{0:T(512)S(1)} %get-tuple-element.88) | copy-start | bytes 4612
  18.1 37.6 %copy-start.63 = (f32[384]{0:T(512)}, f32[384]{0:T(512)S(1)}, u32[]{:S(2)}) copy-start(f32[384]{0:T(512)S(1)} %get-tuple-element.89) | copy-start | bytes 4612
  18.2 37.5 %copy-start.3 = (f32[384]{0:T(512)}, f32[384]{0:T(512)S(1)}, u32[]{:S(2)}) copy-start(f32[384]{0:T(512)S(1)} %get-tuple-element.59) | copy-start | bytes 4612
  18.2 37.5 %copy-start.5 = (f32[384]{0:T(512)}, f32[384]{0:T(512)S(1)}, u32[]{:S(2)}) copy-start(f32[384]{0:T(512)S(1)} %get-tuple-element.60) | copy-start | bytes 4612
  18.2 37.5 %copy-start.7 = (f32[384]{0:T(512)}, f32[384]{0:T(512)S(1)}, u32[]{:S(2)}) copy-start(f32[384]{0:T(512)S(1)} %get-tuple-element.61) | copy-start | bytes 4612
  18.2 37.5 %copy-start.9 = (f32[384]{0:T(512)}, f32[384]{0:T(512)S(1)}, u32[]{:S(2)}) copy-start(f32[384]{0:T(512)S(1)} %get-tuple-element.62) | copy-start | bytes 4612
  18.2 37.5 %copy-start.11 = (f32[384]{0:T(512)}, f32[384]{0:T(512)S(1)}, u32[]{:S(2)}) copy-start(f32[384]{0:T(512)S(1)} %get-tuple-element.63) | copy-start | bytes 4612
  18.2 37.5 %copy-start.13 = (f32[384]{0:T(512)}, f32[384]{0:T(512)S(1)}, u32[]{:S(2)}) copy-start(f32[384]{0:T(512)S(1)} %get-tuple-element.64) | copy-start | bytes 4612
  18.3 37.5 %copy-start.15 = (f32[384]{0:T(512)}, f32[384]{0:T(512)S(1)}, u32[]{:S(2)}) copy-start(f32[384]{0:T(512)S(1)} %get-tuple-element.65) | copy-start | bytes 4612
  18.3 37.5 %copy-start.17 = (f32[384]{0:T(512)}, f32[384]{0:T(512)S(1)}, u32[]{:S(2)}) copy-start(f32[384]{0:T(512)S(1)} %get-tuple-element.66) | copy-start | bytes 4612
  18.3 37.5 %copy-start.19 = (f32[384]{0:T(512)}, f32[384]{0:T(512)S(1)}, u32[]{:S(2)}) copy-start(f32[384]{0:T(512)S(1)} %get-tuple-element.67) | copy-start | bytes 4612
  18.3 37.5 %copy-start.21 = (f32[384]{0:T(512)}, f32[384]{0:T(512)S(1)}, u32[]{:S(2)}) copy-start(f32[384]{0:T(512)S(1)} %get-tuple-element.68) | copy-start | bytes 4612
  18.3 37.5 %copy-start.23 = (f32[384]{0:T(512)}, f32[384]{0:T(512)S(1)}, u32[]{:S(2)}) copy-start(f32[384]{0:T(512)S(1)} %get-tuple-element.69) | copy-start | bytes 4612
  18.3 37.5 %copy-start.25 = (f32[384]{0:T(512)}, f32[384]{0:T(512)S(1)}, u32[]{:S(2)}) copy-start(f32[384]{0:T(512)S(1)} %get-tuple-element.70) | copy-start | bytes 4612
  18.3 37.5 %copy-start.27 = (f32[384]{0:T(512)}, f32[384]{0:T(512)S(1)}, u32[]{:S(2)}) copy-start(f32[384]{0:T(512)S(1)} %get-tuple-element.71) | copy-start | bytes 4612
  18.3 37.5 %copy-start.29 = (f32[384]{0:T(512)}, f32[384]{0:T(512)S(1)}, u32[]{:S(2)}) copy-start(f32[384]{0:T(512)S(1)} %get-tuple-element.72) | copy-start | bytes 4612
  18.3 37.5 %copy-start.31 = (f32[384]{0:T(512)}, f32[384]{0:T(512)S(1)}, u32[]{:S(2)}) copy-start(f32[384]{0:T(512)S(1)} %get-tuple-element.73) | copy-start | bytes 4612
  18.3 37.5 %copy-start.33 = (f32[384]{0:T(512)}, f32[384]{0:T(512)S(1)}, u32[]{:S(2)}) copy-start(f32[384]{0:T(512)S(1)} %get-tuple-element.74) | copy-start | bytes 4612
  18.4 37.5 %copy-start.35 = (f32[384]{0:T(512)}, f32[384]{0:T(512)S(1)}, u32[]{:S(2)}) copy-start(f32[384]{0:T(512)S(1)} %get-tuple-element.75) | copy-start | bytes 4612
  18.4 37.5 %copy-start.37 = (f32[384]{0:T(512)}, f32[384]{0:T(512)S(1)}, u32[]{:S(2)}) copy-start(f32[384]{0:T(512)S(1)} %get-tuple-element.76) | copy-start | bytes 4612
  18.4 37.5 %copy-start.39 = (f32[384]{0:T(512)}, f32[384]{0:T(512)S(1)}, u32[]{:S(2)}) copy-start(f32[384]{0:T(512)S(1)} %get-tuple-element.77) | copy-start | bytes 4612
  19.1 2.4 %collective-permute-start.6 = (s32[2,8]{1,0:T(2,128)S(1)}, s32[2,8]{1,0:T(2,128)S(1)}, u32[]{:S(2)}, u32[]{:S(2)}) collective-permute-start(s32[2,8]{1,0:T(2,128)S(1)} %add_select_fusion.2), channel_id=1, source_target_pairs={{0,2},{2,0},{1,3},{3,1},{4,6},{6,4},{5,7},{7,5},{8,10},{10,8},{9,1... | collective-permute-start | bytes 200 | tf_op jit(solution)/shard_map/ppermute | solution.py:72
  22.6 12.0 %all-to-all-start = ((bf16[8,8,1536]{2,1,0:T(8,128)(2,1)}), bf16[8,8,1536]{2,1,0:T(8,128)(2,1)S(1)}, u32[]{:S(2)}, u32[]{:S(2)}) async-start(bf16[8,8,1536]{2,1,0:T(8,128)(2,1)} %broadcast_in_dim.13), calls=%async_computation | async-start | bytes 393216 | tf_op jit(solution)/shard_map/all_to_all | solution.py:79
  27.5 13.0 %collective-permute-start.8 = (bf16[2,128,384]{2,1,0:T(8,128)(2,1)S(1)}, bf16[2,128,384]{2,1,0:T(8,128)(2,1)S(1)}, u32[]{:S(2)}, u32[]{:S(2)}) collective-permute-start(bf16[2,128,384]{2,1,0:T(8,128)(2,1)S(1)} %get-tuple-element.105), channel_id=1, source_target_pairs={{0,2},{2,0},{1,3},{3,1},{4,6},{6,4},{5,7},{7,5},{8,10},{10,8},{9,1... | collective-permute-start | bytes 589832 | tf_op jit(solution)/shard_map/ppermute | solution.py:55
  36.1 9.1 %copy-start.2 = (bf16[1,128,1536]{2,1,0:T(8,128)(2,1)S(1)}, bf16[1,128,1536]{2,1,0:T(8,128)(2,1)}, u32[]{:S(2)}) copy-start(bf16[1,128,1536]{2,1,0:T(8,128)(2,1)} %param.11) | copy-start | bytes 1179652
  36.1 36.6 %all-to-all-start.1 = ((bf16[8,56,1536]{2,1,0:T(8,128)(2,1)}), bf16[8,56,1536]{2,1,0:T(8,128)(2,1)}, u32[]{:S(2)}, u32[]{:S(2)}) async-start(bf16[8,56,1536]{2,1,0:T(8,128)(2,1)} %broadcast_in_dim.14), calls=%async_computation.1 | async-start | bytes 2752512 | tf_op jit(solution)/shard_map/all_to_all | solution.py:84
  40.6 12.7 %collective-permute-start.9 = (bf16[32,384]{1,0:T(8,128)(2,1)S(1)}, bf16[32,384]{1,0:T(8,128)(2,1)S(1)}, u32[]{:S(2)}, u32[]{:S(2)}) collective-permute-start(bf16[32,384]{1,0:T(8,128)(2,1)S(1)} %slice.650), channel_id=1, source_target_pairs={{0,8},{8,16},{16,24},{24,32},{32,40},{40,48},{48,56},{56,64},{64,7... | collective-permute-start | bytes 73736 | tf_op jit(solution)/shard_map/ppermute | solution.py:105
  43.9 11.6 %collective-permute-start.10 = (bf16[48,384]{1,0:T(8,128)(2,1)S(1)}, bf16[48,384]{1,0:T(8,128)(2,1)S(1)}, u32[]{:S(2)}, u32[]{:S(2)}) collective-permute-start(bf16[48,384]{1,0:T(8,128)(2,1)S(1)} %slice.651), channel_id=1, source_target_pairs={{8,0},{16,8},{24,16},{32,24},{40,32},{48,40},{56,48},{64,56},{72,6... | collective-permute-start | bytes 110600 | tf_op jit(solution)/shard_map/ppermute | solution.py:107
  45.3 14.8 %collective-permute-start.1 = (bf16[2,128,1536]{2,1,0:T(8,128)(2,1)S(1)}, bf16[2,128,1536]{2,1,0:T(8,128)(2,1)S(1)}, u32[]{:S(2)}, u32[]{:S(2)}) collective-permute-start(bf16[2,128,1536]{2,1,0:T(8,128)(2,1)S(1)} %maximum_select_fusion.1), channel_id=1, source_target_pairs={{0,2},{2,0},{1,3},{3,1},{4,6},{6,4},{5,7},{7,5},{8,10},{10,8},{9,1... | collective-permute-start | bytes 2359304 | tf_op jit(solution)/shard_map/ppermute | solution.py:98
  60.1 12.5 %copy-start.1 = (f32[560,384]{1,0:T(8,128)}, f32[560,384]{1,0:T(8,128)S(1)}, u32[]{:S(2)}) copy-start(f32[560,384]{1,0:T(8,128)S(1)} %get-tuple-element.93) | copy-start | bytes 2580484
  61.7 10.9 %collective-permute-start.2 = (bf16[16,1536]{1,0:T(8,128)(2,1)}, bf16[16,1536]{1,0:T(8,128)(2,1)}, u32[]{:S(2)}, u32[]{:S(2)}) collective-permute-start(bf16[16,1536]{1,0:T(8,128)(2,1)} %slice.646), channel_id=1, source_target_pairs={{0,8},{8,16},{16,24},{24,32},{32,40},{40,48},{48,56},{56,64},{64,7... | collective-permute-start | bytes 147464 | tf_op jit(solution)/shard_map/ppermute | solution.py:112
  64.3 8.3 %collective-permute-start.3 = (bf16[32,1536]{1,0:T(8,128)(2,1)}, bf16[32,1536]{1,0:T(8,128)(2,1)}, u32[]{:S(2)}, u32[]{:S(2)}) collective-permute-start(bf16[32,1536]{1,0:T(8,128)(2,1)} %slice.647), channel_id=1, source_target_pairs={{8,0},{16,8},{24,16},{32,24},{40,32},{48,40},{56,48},{64,56},{72,6... | collective-permute-start | bytes 294920 | tf_op jit(solution)/shard_map/ppermute | solution.py:114
  81.1 7.2 %copy-start.12 = (f32[384]{0:T(512)S(1)}, f32[384]{0:T(512)}, u32[]{:S(2)}) copy-start(f32[384]{0:T(512)} %copy-done.11) | copy-start | bytes 4612
  81.1 7.2 %copy-start.14 = (f32[384]{0:T(512)S(1)}, f32[384]{0:T(512)}, u32[]{:S(2)}) copy-start(f32[384]{0:T(512)} %copy-done.13) | copy-start | bytes 4612
  81.1 7.2 %copy-start.16 = (f32[384]{0:T(512)S(1)}, f32[384]{0:T(512)}, u32[]{:S(2)}) copy-start(f32[384]{0:T(512)} %copy-done.15) | copy-start | bytes 4612
  81.1 7.2 %copy-start.18 = (f32[384]{0:T(512)S(1)}, f32[384]{0:T(512)}, u32[]{:S(2)}) copy-start(f32[384]{0:T(512)} %copy-done.17) | copy-start | bytes 4612
  81.1 7.2 %copy-start.20 = (f32[384]{0:T(512)S(1)}, f32[384]{0:T(512)}, u32[]{:S(2)}) copy-start(f32[384]{0:T(512)} %copy-done.19) | copy-start | bytes 4612
  81.1 7.2 %copy-start.22 = (f32[384]{0:T(512)S(1)}, f32[384]{0:T(512)}, u32[]{:S(2)}) copy-start(f32[384]{0:T(512)} %copy-done.21) | copy-start | bytes 4612
  81.2 7.2 %copy-start.24 = (f32[384]{0:T(512)S(1)}, f32[384]{0:T(512)}, u32[]{:S(2)}) copy-start(f32[384]{0:T(512)} %copy-done.23) | copy-start | bytes 4612
  81.2 7.2 %copy-start.26 = (f32[384]{0:T(512)S(1)}, f32[384]{0:T(512)}, u32[]{:S(2)}) copy-start(f32[384]{0:T(512)} %copy-done.25) | copy-start | bytes 4612
  81.2 7.2 %copy-start.28 = (f32[384]{0:T(512)S(1)}, f32[384]{0:T(512)}, u32[]{:S(2)}) copy-start(f32[384]{0:T(512)} %copy-done.27) | copy-start | bytes 4612
  81.2 7.2 %copy-start.30 = (f32[384]{0:T(512)S(1)}, f32[384]{0:T(512)}, u32[]{:S(2)}) copy-start(f32[384]{0:T(512)} %copy-done.29) | copy-start | bytes 4612
  81.4 24.0 %all-to-all-start.2 = ((bf16[8,56,1536]{2,1,0:T(8,128)(2,1)}), bf16[8,56,1536]{2,1,0:T(8,128)(2,1)S(1)}, u32[]{:S(2)}, u32[]{:S(2)}) async-start(bf16[8,56,1536]{2,1,0:T(8,128)(2,1)} %pad_maximum_fusion), calls=%async_computation.2 | async-start | bytes 2752512 | tf_op jit(solution)/shard_map/all_to_all | solution.py:160
  94.4 5.3 %collective-permute-start.13 = (f32[2,8,384]{2,1,0:T(8,128)S(1)}, f32[2,8,384]{2,1,0:T(8,128)S(1)}, u32[]{:S(2)}, u32[]{:S(2)}) collective-permute-start(f32[2,8,384]{2,1,0:T(8,128)S(1)} %get-tuple-element.113), channel_id=1, source_target_pairs={{0,2},{2,0},{1,3},{3,1},{4,6},{6,4},{5,7},{7,5},{8,10},{10,8},{9,1... | collective-permute-start | bytes 73736 | tf_op jit(solution)/shard_map/ppermute | solution.py:197
  98.9 15.4 %collective-permute-start.11 = (bf16[2,128,384]{2,1,0:T(8,128)(2,1)S(1)}, bf16[2,128,384]{2,1,0:T(8,128)(2,1)S(1)}, u32[]{:S(2)}, u32[]{:S(2)}) collective-permute-start(bf16[2,128,384]{2,1,0:T(8,128)(2,1)S(1)} %get-tuple-element.103), channel_id=1, source_target_pairs={{0,2},{2,0},{1,3},{3,1},{4,6},{6,4},{5,7},{7,5},{8,10},{10,8},{9,1... | collective-permute-start | bytes 589832 | tf_op jit(solution)/shard_map/ppermute | solution.py:197
  99.7 14.0 %collective-permute-start.14 = (f32[8,768]{1,0:T(8,128)S(1)}, f32[8,768]{1,0:T(8,128)S(1)}, u32[]{:S(2)}, u32[]{:S(2)}) collective-permute-start(f32[8,768]{1,0:T(8,128)S(1)} %get-tuple-element.111), channel_id=1, source_target_pairs={{0,4},{4,0},{1,5},{5,1},{2,6},{6,2},{3,7},{7,3},{8,12},{12,8},{9,1... | collective-permute-start | bytes 73736 | tf_op jit(solution)/shard_map/ppermute | solution.py:206
  106.6 15.9 %all-to-all-start.3 = ((bf16[8,8,1536]{2,1,0:T(8,128)(2,1)}), bf16[8,8,1536]{2,1,0:T(8,128)(2,1)S(1)}, u32[]{:S(2)}, u32[]{:S(2)}) async-start(bf16[8,8,1536]{2,1,0:T(8,128)(2,1)} %pad_maximum_fusion.1), calls=%async_computation.3 | async-start | bytes 393216 | tf_op jit(solution)/shard_map/all_to_all | solution.py:173
  114.5 20.9 %collective-permute-start.12 = (bf16[128,768]{1,0:T(8,128)(2,1)S(1)}, bf16[128,768]{1,0:T(8,128)(2,1)S(1)}, u32[]{:S(2)}, u32[]{:S(2)}) collective-permute-start(bf16[128,768]{1,0:T(8,128)(2,1)S(1)} %get-tuple-element.101), channel_id=1, source_target_pairs={{0,4},{4,0},{1,5},{5,1},{2,6},{6,2},{3,7},{7,3},{8,12},{12,8},{9,1... | collective-permute-start | bytes 589832 | tf_op jit(solution)/shard_map/ppermute | solution.py:206
  122.5 13.7 %collective-permute-start.15 = (f32[6,1536]{1,0:T(8,128)S(1)}, f32[6,1536]{1,0:T(8,128)S(1)}, u32[]{:S(2)}, u32[]{:S(2)}) collective-permute-start(f32[6,1536]{1,0:T(8,128)S(1)} %bitcast.86), channel_id=1, source_target_pairs={{0,0},{64,2},{128,4},{192,6},{32,32},{96,34},{160,36},{224,38},{2,... | collective-permute-start | bytes 110600 | tf_op jit(solution)/shard_map/ppermute | solution.py:175
  129.1 14.4 %all-to-all-start.4 = ((f32[32,1,1536]{2,1,0:T(1,128)}), f32[32,1,1536]{2,1,0:T(1,128)S(1)}, u32[]{:S(2)}, u32[]{:S(2)}) async-start(f32[32,1,1536]{2,1,0:T(1,128)} %broadcast_in_dim.18), calls=%async_computation.4 | async-start | bytes 393216 | tf_op jit(solution)/shard_map/all_to_all | solution.py:179
  (24 other events, 162.4 us)

commit v2 on v1

v2 whole, which is shorter than its diff:
```python
import math

import jax
import jax.numpy as jnp
import numpy as np
from jax import lax
from jax.experimental import pallas as pl
from jax.experimental.pallas import tpu as pltpu
from jax.sharding import Mesh
from jax.sharding import PartitionSpec as P

AXES = ("z", "x", "yh", "core", "rep")
SIZES = (8, 4, 2, 2, 2)
GROUP = ("yh", "core")
PLANE = ("x", "rep")
QUARTERS = 4
BLOCK = 6
PAD = 56
LEFT_H, RIGHT_H = 32, 48
LEFT_U, RIGHT_U = 16, 32
FRAMES, CHANNELS, TAPS = 512, 384, 31
WIDE = FRAMES + LEFT_U + RIGHT_U
LONG = FRAMES + 16
SWAP = [(0, 1), (1, 0)]
BF = jnp.bfloat16
F32 = jnp.float32


def placement(pad):
    out = np.zeros((CHANNELS, 8 * pad), np.float32)
    for zl in range(2):
        for x in range(4):
            for q in range(4):
                for rep in range(2):
                    for r in range(BLOCK):
                        row = (((zl * 4 + x) * 4 + q) * 2 + rep) * BLOCK + r
                        out[row, (x * 2 + rep) * pad + (q * 2 + zl) * BLOCK + r] = 1
    return jnp.asarray(out, BF)


def turned():
    pairs = []
    for zq in range(4):
        for zl in range(2):
            for q in range(4):
                pairs.append(((zq * 2 + zl) * 4 + q, (q * 2 + zl) * 4 + zq))
    return pairs


def ordered(mine, other, first):
    return jnp.where(first, jnp.stack((mine, other)), jnp.stack((other, mine)))


def half(value, index, axis):
    size = value.shape[axis] // 2
    return lax.dynamic_slice_in_dim(value, index * size, size, axis)


def lanes(tile):
    return slice(tile * 128, tile * 128 + 128)


def assemble(hidden, upstream, across, beside, out):
    yh, core = lax.axis_index("yh"), lax.axis_index("core")
    quarter = pl.ds(pl.multiple_of((yh * 2 + core) * CHANNELS, 128), CHANNELS)
    part = pl.ds(pl.multiple_of(core * CHANNELS, 128), CHANNELS)
    own = yh * 2 + core
    out[own, :, :CHANNELS] = hidden[:, quarter]
    out[own, :, CHANNELS:] = upstream[...]
    far = (1 - yh) * 2 + core
    out[far, :, :CHANNELS] = across[:, part]
    out[far, :, CHANNELS:] = across[:, 2 * CHANNELS :]
    out[yh * 2 + 1 - core] = beside[0]
    out[(1 - yh) * 2 + 1 - core] = beside[1]


def convolve(frames, left, right, kernel, order, slope, hidden, parts, active):
    hidden[:LEFT_H] = left[:, :CHANNELS].astype(F32)
    hidden[LEFT_H : LEFT_H + FRAMES] = frames[:, :CHANNELS].astype(F32)
    hidden[LEFT_H + FRAMES :] = right[:, :CHANNELS].astype(F32)
    rows = 80
    for tile in range(CHANNELS // 128):

        def chunk(c, _, tile=tile):
            base = pl.multiple_of(c * rows, 8)
            total = jnp.zeros((rows, 128), F32)
            window = hidden[pl.ds(base, rows + 32), lanes(tile)]
            for b in range(8):
                slab = window[b : b + rows + 24]
                for a in range(4):
                    k = 8 * a + b - 1
                    if 0 <= k < TAPS:
                        total += kernel[k : k + 1, lanes(tile)] * slab[8 * a : 8 * a + rows]
            sig = jax.nn.sigmoid(total)
            slope[pl.ds(base, rows), lanes(tile)] = sig * (1.0 + total * (1.0 - sig))
            active[pl.ds(base, rows), lanes(tile)] = total * sig
            return 0

        lax.fori_loop(0, WIDE // rows, chunk, 0)
    acts = active[LEFT_U : LEFT_U + FRAMES].astype(BF)
    acts = jnp.dot(acts, order[...], preferred_element_type=F32).astype(BF)
    product = lax.dot_general(
        acts,
        frames[:, CHANNELS:],
        (((0,), (0,)), ((), ())),
        preferred_element_type=F32,
    ).astype(BF)
    for s in range(8):
        parts[s] = product[48 * s : 48 * s + 48]


def backward(
    gathered, spread, frames, left, right, slope, hidden, kernel,
    frame_grad, taps, grad_conv, frame_sum, sums,
):
    weights = jnp.dot(spread[...], gathered[...], preferred_element_type=F32).astype(BF)

    def gradient(upstream, begin, count):
        value = lax.dot_general(
            upstream, weights, (((1,), (1,)), ((), ())), preferred_element_type=F32
        )
        value = (value * slope[begin : begin + count]).astype(BF)
        grad_conv[begin : begin + count] = value.astype(F32)

    gradient(left[LEFT_H - LEFT_U :, CHANNELS:], 0, LEFT_U)
    gradient(frames[:, CHANNELS:], LEFT_U, FRAMES)
    gradient(right[:RIGHT_U, CHANNELS:], LEFT_U + FRAMES, RIGHT_U)
    rows, span = 88, 128
    sums[...] = jnp.zeros_like(sums)
    for tile in range(CHANNELS // 128):

        def chunk(c, _, tile=tile):
            base = pl.multiple_of(c * rows, 8)
            total = jnp.zeros((rows, 128), F32)
            window = grad_conv[pl.ds(base, rows + 32), lanes(tile)]
            for b in range(8):
                slab = window[b : b + rows + 24]
                for a in range(4):
                    k = TAPS - 8 * a - b
                    if 0 <= k < TAPS:
                        total += kernel[k : k + 1, lanes(tile)] * slab[8 * a : 8 * a + rows]
            frame_sum[pl.ds(base, rows), lanes(tile)] = total
            return 0

        lax.fori_loop(0, LONG // rows, chunk, 0)

        def piece(c, _, tile=tile):
            base = pl.multiple_of(c * span, 8)
            grads = grad_conv[pl.ds(base + LEFT_U, span), lanes(tile)]
            window = hidden[pl.ds(base + LEFT_U, span + 32), lanes(tile)]
            for b in range(8):
                slab = window[b : b + span + 24]
                for a in range(4):
                    k = 8 * a + b - 1
                    if 0 <= k < TAPS:
                        terms = grads * slab[8 * a : 8 * a + span]
                        sums[k, :, lanes(tile)] += jnp.sum(
                            terms.reshape(span // 8, 8, 128), axis=0
                        )
            return 0

        lax.fori_loop(0, FRAMES // span, piece, 0)
    frame_grad[...] = frame_sum[...].astype(BF)
    for k in range(TAPS + 1):
        at = (k % 4) * CHANNELS
        taps[k // 4 : k // 4 + 1, at : at + CHANNELS] = jnp.sum(sums[k], axis=0, keepdims=True)


def call(kernel, outs, scratch, flops, *args):
    shapes = [jax.ShapeDtypeStruct(shape, dtype) for shape, dtype in outs]
    size = sum(math.prod(s.shape) * s.dtype.itemsize for s in list(args) + shapes)
    return pl.pallas_call(
        kernel,
        out_shape=shapes,
        scratch_shapes=[pltpu.VMEM(shape, dtype) for shape, dtype in scratch],
        compiler_params=pltpu.CompilerParams(vmem_limit_bytes=40 * 2**20),
        cost_estimate=pl.CostEstimate(
            flops=flops, bytes_accessed=size, transcendentals=0
        ),
    )(*args)


def body(hidden_in, upstream, out_weight, conv_kernel, durations):
    yh, core = lax.axis_index("yh"), lax.axis_index("core")
    rep = lax.axis_index("rep")
    quarter = yh * 2 + core
    place = lax.axis_index("z") * 4 + lax.axis_index("x")
    scaling = 1.0 / math.sqrt(2 * 128 * hidden_in.shape[1])

    lengths = ordered(durations[0], lax.ppermute(durations[0], "yh", SWAP), yh == 0)
    lengths = jnp.swapaxes(
        ordered(lengths, lax.ppermute(lengths, "core", SWAP), core == 0), 0, 1
    ).reshape(4, -1)
    totals = jnp.sum(lengths, axis=1)

    rows = lax.ppermute(out_weight, ("z", "yh", "core"), turned())
    note = jnp.zeros((2, 1536), BF).at[0, :4].set(totals.astype(BF))
    rows = jnp.concatenate((rows, note), axis=0)
    rows = lax.all_to_all(
        jnp.broadcast_to(rows[None], (8,) + rows.shape), "z", 0, 0, tiled=True
    )
    note = jnp.zeros((PAD - 48, 1536), BF).at[0, :32].set(rows[:, 6, :4].reshape(32))
    rows = jnp.concatenate((rows[:, :BLOCK].reshape(48, 1536), note), axis=0)
    rows = lax.all_to_all(
        jnp.broadcast_to(rows[None], (8,) + rows.shape), PLANE, 0, 0, tiled=True
    )
    notes = rows[:, 48, :32].reshape(4, 2, 8, 4).astype(F32)
    notes = jnp.where(rep == 0, notes[:, 0], notes[:, 1])

    hidden, grads = hidden_in[0], upstream[0]
    across = jnp.concatenate((half(hidden, 1 - yh, 1), grads), axis=1)
    across = lax.ppermute(across, "yh", SWAP)
    beside = jnp.stack(
        (
            jnp.concatenate((half(half(hidden, yh, 1), 1 - core, 1), grads), axis=1),
            jnp.concatenate(
                (half(across[:, : 2 * CHANNELS], 1 - core, 1), across[:, 2 * CHANNELS :]),
                axis=1,
            ),
        )
    )
    beside = lax.ppermute(beside, "core", SWAP)
    [frames] = call(
        assemble, [((4, 128, CHANNELS + 1536), BF)], [], 0, hidden, grads, across, beside
    )
    frames = frames.reshape(FRAMES, CHANNELS + 1536)
    ring = ("z", "x")
    left = lax.ppermute(frames[-LEFT_H:], ring, [(i, i + 1) for i in range(31)])
    right = lax.ppermute(frames[:RIGHT_H], ring, [(i + 1, i) for i in range(31)])
    kernel_f = lax.dynamic_slice_in_dim(
        jnp.pad(conv_kernel, ((0, 1), (0, 0))), quarter * CHANNELS, CHANNELS, 1
    ).astype(F32)

    slope, hidden_f, parts = call(
        convolve,
        [((WIDE, CHANNELS), F32), ((LEFT_H + FRAMES + RIGHT_H, CHANNELS), F32), ((8, 48, 1536), BF)],
        [((WIDE, CHANNELS), F32)],
        800_000_000,
        frames, left, right, kernel_f, placement(48),
    )
    parts = lax.all_to_all(parts, PLANE, 0, 0, tiled=True)
    parts = jnp.sum(parts.astype(F32), axis=0).astype(BF)

    frame_grad, tap_rows = call(
        backward,
        [((LONG, CHANNELS), BF), ((8, 1536), F32)],
        [((WIDE, CHANNELS), F32), ((LONG, CHANNELS), F32), ((TAPS + 1, 8, CHANNELS), F32)],
        1_400_000_000,
        rows.reshape(8 * PAD, 1536), placement(PAD), frames, left, right, slope, hidden_f, kernel_f,
    )

    taps_part = lax.all_to_all(tap_rows, PLANE, 0, 0, tiled=True)
    taps_part = jnp.sum(taps_part, axis=0)
    high = taps_part.astype(BF)
    low = (taps_part - high.astype(F32)).astype(BF)
    parts = jnp.concatenate(
        (
            parts.reshape(8, BLOCK, 1536),
            jnp.broadcast_to(high, (8, 1, 1536)),
            jnp.broadcast_to(low, (8, 1, 1536)),
        ),
        axis=1,
    )
    parts = lax.all_to_all(parts, "z", 0, 0, tiled=True)
    parts = jnp.sum(parts.astype(F32), axis=0) * scaling
    weight_grad = lax.ppermute(
        parts[:BLOCK], ("z", "yh", "core"), [(b, a) for a, b in turned()]
    )
    taps_sum = (parts[6] + parts[7])[None]
    taps_all = lax.all_to_all(
        jnp.broadcast_to(taps_sum, (32, 1536)), ("x", "yh", "core", "rep"), 0, 0, tiled=True
    )
    taps_all = taps_all.reshape(4, 4, 2, 4, CHANNELS)
    kernel_grad = taps_all.transpose(0, 2, 3, 1, 4).reshape(32, 1536)[:TAPS]

    order = lax.iota(jnp.int32, 8)[None, :] * 4 + lax.iota(jnp.int32, 4)[:, None]
    before = jnp.sum(jnp.where(order < place, jnp.sum(notes, axis=2), 0.0))
    start = before.astype(jnp.int32) - place * FRAMES
    ends = start + jnp.cumsum(lengths.reshape(-1))
    starts = ends - lengths.reshape(-1)
    at = lax.iota(jnp.int32, LONG)
    covers = (at[None] >= starts[:, None]) & (at[None] < ends[:, None])
    gloss = jnp.dot(covers.astype(BF), frame_grad, preferred_element_type=F32)

    def back(value):
        value = value.reshape(2, 2, -1, CHANNELS)
        kept = lax.dynamic_index_in_dim(value, core, 1, False)
        got = lax.ppermute(
            lax.dynamic_index_in_dim(value, 1 - core, 1, False), "core", SWAP
        )
        value = jnp.where(
            core == 0,
            jnp.concatenate((kept, got), axis=2),
            jnp.concatenate((got, kept), axis=2),
        )
        kept = lax.dynamic_index_in_dim(value, yh, 0, False)
        got = lax.ppermute(
            lax.dynamic_index_in_dim(value, 1 - yh, 0, False), "yh", SWAP
        )
        return jnp.where(
            yh == 0,
            jnp.concatenate((kept, got), axis=1),
            jnp.concatenate((got, kept), axis=1),
        )

    return (
        back(frame_grad[:FRAMES])[None],
        back(gloss)[None],
        weight_grad,
        kernel_grad,
    )


def solution(mesh):
    fine = Mesh(mesh.devices.reshape(SIZES), AXES)
    seq = ("z", "x", "yh", "core")
    rows = P(seq + ("rep",), None)
    in_specs = (P("rep", seq, None), P("rep", seq, None), rows, P(), P("rep", seq))
    out_specs = (P("rep", seq, None), P("rep", seq, None), rows, P())
    return jax.shard_map(
        body, mesh=fine, in_specs=in_specs, out_specs=out_specs, check_vma=False
    )
```

time: 146 us -> 152 us (1.041)
  waiting for transfers between devices: 23.7 us -> 45.5 us
  starting transfers between devices: 79.3 us -> 61.3 us
  Pallas kernels: 0 us -> 16.6 us
  other arithmetic: 20.1 us -> 7.53 us
  matrix products: 7.45 us -> 0.24 us
  local copies, waits for them, and re-layouts: 12.1 us -> 17.7 us
    pallas_call x0 -> x3, Pallas kernels: none -> 16.6 us  [call(): pl.pallas_call(kernel, out_shape=shapes, scratch_shapes=[pltpu.VMEM(shape...]
    ppermute x2, starting transfers between devices: 10.6 us -> 0.28 us  [back(): lax.ppermute(lax.dynamic_index_in_dim(value, 1 - yh, 0, False), 'yh', SWAP)]
    all_to_all x1, waiting for transfers between devices: 0.01 us -> 10.3 us  [body(): parts = lax.all_to_all(parts, PLANE, 0, 0, tiled=True)]
    unnamed x136 -> x34, local copies, waits for them, and re-layouts: 1.59 us -> 9.97 us
    dot_general x2 -> x0, matrix products: 7.21 us -> none  [the longest x1 3.74 us: body(): lax.dot_general(grads_ext, weights, (((1,), (1,)), ((), ())), preferred_e...]
    all_to_all x0 -> x1, starting transfers between devices: none -> 5.77 us  [body(): taps_part = lax.all_to_all(tap_rows, PLANE, 0, 0, tiled=True)]
    ppermute x8 -> x4, starting transfers between devices: 19.1 us -> 14.1 us  [the longest x1 5.8 us: body(): across = lax.ppermute(across, 'yh', SWAP)]
    all_to_all x1, waiting for transfers between devices: 2.96 us -> 7.71 us  [body(): parts = lax.all_to_all(parts, 'z', 0, 0, tiled=True)]
  transfers between devices with their start and end apart: 21 -> 18, of which waited for: 7 -> 10; matrix products, arithmetic and copies ran while one was open for 20% -> 9% of each run, Pallas kernels for 0% -> 0%
where the time goes in v2:
time: 152 us; the launch traced here: 151 us
  starting transfers between devices  61.3 us (40%)
  waiting for transfers between devices  45.5 us (30%)
  local copies, waits for them, and re-layouts  17.7 us (12%)
  Pallas kernels  16.6 us (11%)
  other arithmetic  7.53 us (5%)
  between operations  1.71 us (1%)
    pallas_call x3, Pallas kernels, call(): pl.pallas_call(kernel, out_shape=shapes, scratch_shapes=[pltpu.VMEM(shape...  16.6 us
    all_to_all x1, waiting for transfers between devices, body(): parts = lax.all_to_all(parts, PLANE, 0, 0, tiled=True)  10.3 us
    unnamed x34, local copies, waits for them, and re-layouts  9.97 us
    all_to_all x1, waiting for transfers between devices, body(): parts = lax.all_to_all(parts, 'z', 0, 0, tiled=True)  7.71 us
    all_to_all x1, waiting for transfers between devices, body(): lax.all_to_all(jnp.broadcast_to(rows[None], (8,) + rows.shape), 'z', 0, 0...  7.57 us
    all_to_all x1, waiting for transfers between devices, body(): lax.all_to_all(jnp.broadcast_to(taps_sum, (32, 1536)), ('x', 'yh', 'core'...  7.32 us
    all_to_all x1, starting transfers between devices, body(): lax.all_to_all(jnp.broadcast_to(taps_sum, (32, 1536)), ('x', 'yh', 'core'...  6.17 us
    ppermute x1, starting transfers between devices, body(): lax.ppermute(parts[:BLOCK], ('z', 'yh', 'core'), [(b, a) for a, b in turn...  6.03 us
  transfers between devices with their start and end apart: 18, of which 10 were waited for; matrix products, arithmetic and copies ran while one was open for 9% of the time, Pallas kernels for 0%

profile of v2, /device:TPU:1, one launch (start us, length us, event | category | flops | bytes accessed | tf_op | source)
XLA Modules:
  0.0 150.5 jit_solution(7596580859455914377)
XLA Ops:
  0.6 3.8 %collective-permute-start.1 = (s32[8]{0:T(128)}, s32[8]{0:T(128)S(1)}, u32[]{:S(2)}, u32[]{:S(2)}) collective-permute-start(s32[8]{0:T(128)} %bitcast.64), channel_id=1, source_target_pairs={{0,4},{4,0},{1,5},{5,1},{2,6},{6,2},{3,7},{7,3},{8,12},{12,8},{9,1... | collective-permute-start | bytes 104 | tf_op jit(solution)/shard_map/ppermute | solution.py:190
  4.5 5.7 %collective-permute-start = (bf16[6,1536]{1,0:T(8,128)(2,1)}, bf16[6,1536]{1,0:T(8,128)(2,1)S(1)}, u32[]{:S(2)}, u32[]{:S(2)}) collective-permute-start(bf16[6,1536]{1,0:T(8,128)(2,1)} %param.13), channel_id=1, source_target_pairs={{0,0},{2,64},{4,128},{6,192},{32,32},{34,96},{36,160},{38,224},{64... | collective-permute-start | bytes 55304 | tf_op jit(solution)/shard_map/ppermute | solution.py:196
  10.2 1.0 dynamic-slice_bitcast_fusion.3
  11.2 1.0 pad_maximum_fusion.1
  12.3 5.8 %collective-permute-start.3 = (bf16[128,2304]{1,0:T(8,128)(2,1)S(1)}, bf16[128,2304]{1,0:T(8,128)(2,1)S(1)}, u32[]{:S(2)}, u32[]{:S(2)}) collective-permute-start(bf16[128,2304]{1,0:T(8,128)(2,1)S(1)} %pad_maximum_fusion.1), channel_id=1, source_target_pairs={{0,4},{4,0},{1,5},{5,1},{2,6},{6,2},{3,7},{7,3},{8,12},{12,8},{9,1... | collective-permute-start | bytes 1769480 | tf_op jit(solution)/shard_map/ppermute | solution.py:212
  18.1 1.7 %collective-permute-start.2 = (s32[2,8]{1,0:T(2,128)S(1)}, s32[2,8]{1,0:T(2,128)S(1)}, u32[]{:S(2)}, u32[]{:S(2)}) collective-permute-start(s32[2,8]{1,0:T(2,128)S(1)} %add_select_fusion.2), channel_id=1, source_target_pairs={{0,2},{2,0},{1,3},{3,1},{4,6},{6,4},{5,7},{7,5},{8,10},{10,8},{9,1... | collective-permute-start | bytes 200 | tf_op jit(solution)/shard_map/ppermute | solution.py:192
  19.7 0.8 collective-permute-done.2
  20.6 0.1 fusion.14
  20.7 0.1 copy.31
  20.9 0.7 broadcast_in_dim.13
  21.6 3.4 %all-to-all-start = ((bf16[8,8,1536]{2,1,0:T(8,128)(2,1)}), bf16[8,8,1536]{2,1,0:T(8,128)(2,1)S(1)}, u32[]{:S(2)}, u32[]{:S(2)}) async-start(bf16[8,8,1536]{2,1,0:T(8,128)(2,1)} %broadcast_in_dim.13), calls=%async_computation | async-start | bytes 393216 | tf_op jit(solution)/shard_map/all_to_all | solution.py:199
  25.0 1.0 dynamic-slice_bitcast_fusion.4
  26.1 7.6 %all-to-all-done = bf16[8,8,1536]{2,1,0:T(8,128)(2,1)S(1)} async-done(((bf16[8,8,1536]{2,1,0:T(8,128)(2,1)}), bf16[8,8,1536]{2,1,0:T(8,128)(2,1)S(1)}, u32[]{:S(2)}, u32[]{:S(2)}) %all-to-all-start) | async-done | bytes 196640 | tf_op jit(solution)/shard_map/all_to_all | solution.py:199
  33.9 1.2 broadcast_in_dim.14
  35.1 4.1 %all-to-all-start.1 = ((bf16[8,56,1536]{2,1,0:T(8,128)(2,1)}), bf16[8,56,1536]{2,1,0:T(8,128)(2,1)S(1)}, u32[]{:S(2)}, u32[]{:S(2)}) async-start(bf16[8,56,1536]{2,1,0:T(8,128)(2,1)} %broadcast_in_dim.14), calls=%async_computation.1 | async-start | bytes 2752512 | tf_op jit(solution)/shard_map/all_to_all | solution.py:204
  39.3 0.7 copy-done.2
  40.0 1.0 pad_maximum_fusion
  41.1 3.3 %collective-permute-start.4 = (bf16[2,128,1920]{2,1,0:T(8,128)(2,1)}, bf16[2,128,1920]{2,1,0:T(8,128)(2,1)S(1)}, u32[]{:S(2)}, u32[]{:S(2)}) collective-permute-start(bf16[2,128,1920]{2,1,0:T(8,128)(2,1)} %pad_maximum_fusion), channel_id=1, source_target_pairs={{0,2},{2,0},{1,3},{3,1},{4,6},{6,4},{5,7},{7,5},{8,10},{10,8},{9,1... | collective-permute-start | bytes 2949128 | tf_op jit(solution)/shard_map/ppermute | solution.py:222
  44.4 0.5 iota_multiply_fusion
  45.1 0.7 reduce-window.7
  45.8 1.0 collective-permute-done.4.beside
  46.8 0.9 copy-done.8
  47.7 1.0 copy-done.1
  48.7 1.1 copy-done.3
  49.8 1.0 copy-done.6
  50.8 1.2 copy-done.9
  52.0 0.2 shard_map.102
  52.2 0.7 slice.92
  52.8 0.7 slice.93
  53.5 3.6 %collective-permute-start.5 = (bf16[32,1920]{1,0:T(8,128)(2,1)}, bf16[32,1920]{1,0:T(8,128)(2,1)S(1)}, u32[]{:S(2)}, u32[]{:S(2)}) collective-permute-start(bf16[32,1920]{1,0:T(8,128)(2,1)} %slice.92), channel_id=1, source_target_pairs={{0,8},{8,16},{16,24},{24,32},{32,40},{40,48},{48,56},{56,64},{64,7... | collective-permute-start | bytes 368648 | tf_op jit(solution)/shard_map/ppermute | solution.py:228
  57.1 1.3 collective-permute-start.6
  58.6 1.1 collective-permute-done.5.left
  59.8 5.1 %collective-permute-done.6.right = bf16[48,1920]{1,0:T(8,128)(2,1)} collective-permute-done((bf16[48,1920]{1,0:T(8,128)(2,1)}, bf16[48,1920]{1,0:T(8,128)(2,1)}, u32[]{:S(2)}, u32[]{:S(2)}) %collective-permute-start.6) | collective-permute-done | bytes 184352 | tf_op jit(solution)/shard_map/ppermute | solution.py:229
  64.9 1.0 copy-done.11
  65.9 6.9 %shard_map.103 = (f32[560,384]{1,0:T(8,128)S(1)}, f32[592,384]{1,0:T(8,128)S(1)}, bf16[8,48,1536]{2,1,0:T(8,128)(2,1)S(1)}) custom-call(bf16[512,1920]{1,0:T(8,128)(2,1)S(1)} %bitcast.47, bf16[32,1920]{1,0:T(8,128)(2,1)S(1)} %collective-permute-done.5.left, bf16[48,1920]{1,0:T(8,128)(2,1)} %collective-permute-done.6.right, f32[32,384]{1,0:T(8,128)S(1)} %fusion.9.kernel, ...), custom_call_target="tpu_custom_call" | custom-call | flops 800000000 | bytes 5566464 | tf_op jit(solution)/shard_map/pallas_call | solution.py:172
  72.8 1.0 copy-done.7
  73.8 9.6 %shard_map.104 = (bf16[528,384]{1,0:T(8,128)(2,1)S(1)}, f32[8,1536]{1,0:T(8,128)S(1)}) custom-call(bf16[448,1536]{1,0:T(8,128)(2,1)S(1)} %bitcast.49, bf16[384,448]{1,0:T(8,128)(2,1)S(1)} %copy-done.10, bf16[512,1920]{1,0:T(8,128)(2,1)S(1)} %bitcast.48, bf16[32,1920]{1,0:T(8,128)(2,1)S(1)} %collective-permute-done.5.left, ...), custom_call_target="tpu_custom_call" | custom-call | flops 1400000000 | bytes 6266880 | tf_op jit(solution)/shard_map/pallas_call | solution.py:172
  83.4 0.8 copy-done.4
  84.1 0.7 copy.35
  84.8 5.8 %all-to-all-start.3 = ((f32[8,1,1536]{2,1,0:T(1,128)}), f32[8,1,1536]{2,1,0:T(1,128)S(1)}, u32[]{:S(2)}, u32[]{:S(2)}) async-start(f32[8,1,1536]{2,1,0:T(1,128)} %copy.35), calls=%async_computation.3 | async-start | bytes 98304 | tf_op jit(solution)/shard_map/all_to_all | solution.py:252
  90.6 0.6 select_reduce_fusion
  91.8 3.8 %all-to-all-done.3 = f32[8,1,1536]{2,1,0:T(1,128)S(1)} async-done(((f32[8,1,1536]{2,1,0:T(1,128)}), f32[8,1,1536]{2,1,0:T(1,128)S(1)}, u32[]{:S(2)}, u32[]{:S(2)}) %all-to-all-start.3) | async-done | bytes 49184 | tf_op jit(solution)/shard_map/all_to_all | solution.py:252
  95.6 3.7 %all-to-all-start.2 = ((bf16[8,48,1536]{2,1,0:T(8,128)(2,1)}), bf16[8,48,1536]{2,1,0:T(8,128)(2,1)S(1)}, u32[]{:S(2)}, u32[]{:S(2)}) async-start(bf16[8,48,1536]{2,1,0:T(8,128)(2,1)} %copy-done.7), calls=%async_computation.2 | async-start | bytes 2359296 | tf_op jit(solution)/shard_map/all_to_all | solution.py:241
  99.4 0.1 add_reduce_fusion
  99.5 0.2 fusion.3
  99.8 3.0 %collective-permute-start.9 = (f32[2,8,384]{2,1,0:T(8,128)S(1)}, f32[2,8,384]{2,1,0:T(8,128)S(1)}, u32[]{:S(2)}, u32[]{:S(2)}) collective-permute-start(f32[2,8,384]{2,1,0:T(8,128)S(1)} %get-tuple-element.49), channel_id=1, source_target_pairs={{0,2},{2,0},{1,3},{3,1},{4,6},{6,4},{5,7},{7,5},{8,10},{10,8},{9,1... | collective-permute-start | bytes 73736 | tf_op jit(solution)/shard_map/ppermute | solution.py:288
  102.9 0.1 collective-permute-start.7
  103.0 0.7 collective-permute-done.9
  103.7 0.1 collective-permute-start.10
  103.9 10.3 %all-to-all-done.2 = bf16[8,48,1536]{2,1,0:T(8,128)(2,1)S(1)} async-done(((bf16[8,48,1536]{2,1,0:T(8,128)(2,1)}), bf16[8,48,1536]{2,1,0:T(8,128)(2,1)S(1)}, u32[]{:S(2)}, u32[]{:S(2)}) %all-to-all-start.2) | async-done | bytes 1179680 | tf_op jit(solution)/shard_map/all_to_all | solution.py:241
  114.2 0.2 reduce_sum.60
  114.5 0.8 pad_maximum_fusion.2
  115.3 3.4 %all-to-all-start.4 = ((bf16[8,8,1536]{2,1,0:T(8,128)(2,1)}), bf16[8,8,1536]{2,1,0:T(8,128)(2,1)S(1)}, u32[]{:S(2)}, u32[]{:S(2)}) async-start(bf16[8,8,1536]{2,1,0:T(8,128)(2,1)} %pad_maximum_fusion.2), calls=%async_computation.4 | async-start | bytes 393216 | tf_op jit(solution)/shard_map/all_to_all | solution.py:264
  118.7 0.6 maximum_select_fusion.3
  119.5 0.2 collective-permute-start.8
  119.7 7.7 %all-to-all-done.4 = bf16[8,8,1536]{2,1,0:T(8,128)(2,1)S(1)} async-done(((bf16[8,8,1536]{2,1,0:T(8,128)(2,1)}), bf16[8,8,1536]{2,1,0:T(8,128)(2,1)S(1)}, u32[]{:S(2)}, u32[]{:S(2)}) %all-to-all-start.4) | async-done | bytes 196640 | tf_op jit(solution)/shard_map/all_to_all | solution.py:264
  127.4 6.0 %collective-permute-start.11 = (f32[6,1536]{1,0:T(8,128)S(1)}, f32[6,1536]{1,0:T(8,128)S(1)}, u32[]{:S(2)}, u32[]{:S(2)}) collective-permute-start(f32[6,1536]{1,0:T(8,128)S(1)} %bitcast.62), channel_id=1, source_target_pairs={{0,0},{64,2},{128,4},{192,6},{32,32},{96,34},{160,36},{224,38},{2,... | collective-permute-start | bytes 110600 | tf_op jit(solution)/shard_map/ppermute | solution.py:266
  133.5 0.8 broadcast_in_dim.18
  134.3 6.2 %all-to-all-start.5 = ((f32[32,1,1536]{2,1,0:T(1,128)}), f32[32,1,1536]{2,1,0:T(1,128)S(1)}, u32[]{:S(2)}, u32[]{:S(2)}) async-start(f32[32,1,1536]{2,1,0:T(1,128)} %broadcast_in_dim.18), calls=%async_computation.5 | async-start | bytes 393216 | tf_op jit(solution)/shard_map/all_to_all | solution.py:270
  140.5 0.8 maximum_select_fusion.1
  141.3 7.3 %all-to-all-done.5 = f32[32,1,1536]{2,1,0:T(1,128)S(1)} async-done(((f32[32,1,1536]{2,1,0:T(1,128)}), f32[32,1,1536]{2,1,0:T(1,128)S(1)}, u32[]{:S(2)}, u32[]{:S(2)}) %all-to-all-start.5) | async-done | bytes 196640 | tf_op jit(solution)/shard_map/all_to_all | solution.py:270
  148.6 0.5 reduce.12
  149.2 0.7 copy.37
  149.9 0.6 copy.39
  (70 shorter events, 1.5 us)
Async XLA Ops:
  0.6 17.4 %copy-start.14 = (s32[1,8]{1,0:T(1,128)S(1)}, s32[1,8]{1,0:T(1,128)}, u32[]{:S(2)}) copy-start(s32[1,8]{1,0:T(1,128)} %param.15) | copy-start | bytes 100
  0.6 17.4 %collective-permute-start.1 = (s32[8]{0:T(128)}, s32[8]{0:T(128)S(1)}, u32[]{:S(2)}, u32[]{:S(2)}) collective-permute-start(s32[8]{0:T(128)} %bitcast.64), channel_id=1, source_target_pairs={{0,4},{4,0},{1,5},{5,1},{2,6},{6,2},{3,7},{7,3},{8,12},{12,8},{9,1... | collective-permute-start | bytes 104 | tf_op jit(solution)/shard_map/ppermute | solution.py:190
  4.5 16.4 %collective-permute-start = (bf16[6,1536]{1,0:T(8,128)(2,1)}, bf16[6,1536]{1,0:T(8,128)(2,1)S(1)}, u32[]{:S(2)}, u32[]{:S(2)}) collective-permute-start(bf16[6,1536]{1,0:T(8,128)(2,1)} %param.13), channel_id=1, source_target_pairs={{0,0},{2,64},{4,128},{6,192},{32,32},{34,96},{36,160},{38,224},{64... | collective-permute-start | bytes 55304 | tf_op jit(solution)/shard_map/ppermute | solution.py:196
  10.2 15.8 %copy-start = (bf16[1,128,1536]{2,1,0:T(8,128)(2,1)S(1)}, bf16[1,128,1536]{2,1,0:T(8,128)(2,1)}, u32[]{:S(2)}) copy-start(bf16[1,128,1536]{2,1,0:T(8,128)(2,1)} %param.12) | copy-start | bytes 1179652
  12.3 26.9 %collective-permute-start.3 = (bf16[128,2304]{1,0:T(8,128)(2,1)S(1)}, bf16[128,2304]{1,0:T(8,128)(2,1)S(1)}, u32[]{:S(2)}, u32[]{:S(2)}) collective-permute-start(bf16[128,2304]{1,0:T(8,128)(2,1)S(1)} %pad_maximum_fusion.1), channel_id=1, source_target_pairs={{0,4},{4,0},{1,5},{5,1},{2,6},{6,2},{3,7},{7,3},{8,12},{12,8},{9,1... | collective-permute-start | bytes 1769480 | tf_op jit(solution)/shard_map/ppermute | solution.py:212
  18.1 2.5 %collective-permute-start.2 = (s32[2,8]{1,0:T(2,128)S(1)}, s32[2,8]{1,0:T(2,128)S(1)}, u32[]{:S(2)}, u32[]{:S(2)}) collective-permute-start(s32[2,8]{1,0:T(2,128)S(1)} %add_select_fusion.2), channel_id=1, source_target_pairs={{0,2},{2,0},{1,3},{3,1},{4,6},{6,4},{5,7},{7,5},{8,10},{10,8},{9,1... | collective-permute-start | bytes 200 | tf_op jit(solution)/shard_map/ppermute | solution.py:192
  21.6 12.0 %all-to-all-start = ((bf16[8,8,1536]{2,1,0:T(8,128)(2,1)}), bf16[8,8,1536]{2,1,0:T(8,128)(2,1)S(1)}, u32[]{:S(2)}, u32[]{:S(2)}) async-start(bf16[8,8,1536]{2,1,0:T(8,128)(2,1)} %broadcast_in_dim.13), calls=%async_computation | async-start | bytes 393216 | tf_op jit(solution)/shard_map/all_to_all | solution.py:199
  35.1 23.4 %all-to-all-start.1 = ((bf16[8,56,1536]{2,1,0:T(8,128)(2,1)}), bf16[8,56,1536]{2,1,0:T(8,128)(2,1)S(1)}, u32[]{:S(2)}, u32[]{:S(2)}) async-start(bf16[8,56,1536]{2,1,0:T(8,128)(2,1)} %broadcast_in_dim.14), calls=%async_computation.1 | async-start | bytes 2752512 | tf_op jit(solution)/shard_map/all_to_all | solution.py:204
  39.2 0.8 copy-start.2
  40.0 4.9 %copy-start.12 = (bf16[31,1536]{1,0:T(8,128)(2,1)S(1)}, bf16[31,1536]{1,0:T(8,128)(2,1)}, u32[]{:S(2)}) copy-start(bf16[31,1536]{1,0:T(8,128)(2,1)} %param.14) | copy-start | bytes 285700
  41.1 5.7 %collective-permute-start.4 = (bf16[2,128,1920]{2,1,0:T(8,128)(2,1)}, bf16[2,128,1920]{2,1,0:T(8,128)(2,1)S(1)}, u32[]{:S(2)}, u32[]{:S(2)}) collective-permute-start(bf16[2,128,1920]{2,1,0:T(8,128)(2,1)} %pad_maximum_fusion), channel_id=1, source_target_pairs={{0,2},{2,0},{1,3},{3,1},{4,6},{6,4},{5,7},{7,5},{8,10},{10,8},{9,1... | collective-permute-start | bytes 2949128 | tf_op jit(solution)/shard_map/ppermute | solution.py:222
  46.8 0.9 copy-start.8
  47.7 1.0 copy-start.1
  48.7 1.1 copy-start.3
  49.8 1.0 copy-start.6
  50.8 1.2 copy-start.9
  53.5 6.3 %collective-permute-start.5 = (bf16[32,1920]{1,0:T(8,128)(2,1)}, bf16[32,1920]{1,0:T(8,128)(2,1)S(1)}, u32[]{:S(2)}, u32[]{:S(2)}) collective-permute-start(bf16[32,1920]{1,0:T(8,128)(2,1)} %slice.92), channel_id=1, source_target_pairs={{0,8},{8,16},{16,24},{24,32},{32,40},{40,48},{48,56},{56,64},{64,7... | collective-permute-start | bytes 368648 | tf_op jit(solution)/shard_map/ppermute | solution.py:228
  57.1 7.7 %collective-permute-start.6 = (bf16[48,1920]{1,0:T(8,128)(2,1)}, bf16[48,1920]{1,0:T(8,128)(2,1)}, u32[]{:S(2)}, u32[]{:S(2)}) collective-permute-start(bf16[48,1920]{1,0:T(8,128)(2,1)} %slice.93), channel_id=1, source_target_pairs={{8,0},{16,8},{24,16},{32,24},{40,32},{48,40},{56,48},{64,56},{72,6... | collective-permute-start | bytes 552968 | tf_op jit(solution)/shard_map/ppermute | solution.py:229
  58.6 15.1 %copy-start.10 = (bf16[384,448]{1,0:T(8,128)(2,1)S(1)}, bf16[384,448]{1,0:T(8,128)(2,1)}, u32[]{:S(2)}) copy-start(bf16[384,448]{1,0:T(8,128)(2,1)} %constant.142.clone.spread) | copy-start | bytes 1032196
  64.9 1.0 copy-start.11
  72.8 1.0 copy-start.7
  73.8 16.8 %copy-start.15 = (s32[8]{0:T(128)S(1)}, s32[8]{0:T(128)}, u32[]{:S(2)}) copy-start(s32[8]{0:T(128)} %iota_multiply_fusion) | copy-start | bytes 100
  83.3 0.8 copy-start.4
  84.8 10.9 %all-to-all-start.3 = ((f32[8,1,1536]{2,1,0:T(1,128)}), f32[8,1,1536]{2,1,0:T(1,128)S(1)}, u32[]{:S(2)}, u32[]{:S(2)}) async-start(f32[8,1,1536]{2,1,0:T(1,128)} %copy.35), calls=%async_computation.3 | async-start | bytes 98304 | tf_op jit(solution)/shard_map/all_to_all | solution.py:252
  95.6 3.7 %copy-start.13 = (s32[32,1]{1,0:T(8,128)S(1)}, s32[32,1]{1,0:T(8,128)}, u32[]{:S(2)}) copy-start(s32[32,1]{1,0:T(8,128)} %reduce-window.7) | copy-start | bytes 388
  95.6 3.8 %copy-start.5 = (bf16[528,384]{1,0:T(8,128)(2,1)S(1)}, bf16[528,384]{1,0:T(8,128)(2,1)}, u32[]{:S(2)}) copy-start(bf16[528,384]{1,0:T(8,128)(2,1)} %copy-done.4) | copy-start | bytes 1216516
  95.6 18.5 %all-to-all-start.2 = ((bf16[8,48,1536]{2,1,0:T(8,128)(2,1)}), bf16[8,48,1536]{2,1,0:T(8,128)(2,1)S(1)}, u32[]{:S(2)}, u32[]{:S(2)}) async-start(bf16[8,48,1536]{2,1,0:T(8,128)(2,1)} %copy-done.7), calls=%async_computation.2 | async-start | bytes 2359296 | tf_op jit(solution)/shard_map/all_to_all | solution.py:241
  99.8 3.9 %collective-permute-start.9 = (f32[2,8,384]{2,1,0:T(8,128)S(1)}, f32[2,8,384]{2,1,0:T(8,128)S(1)}, u32[]{:S(2)}, u32[]{:S(2)}) collective-permute-start(f32[2,8,384]{2,1,0:T(8,128)S(1)} %get-tuple-element.49), channel_id=1, source_target_pairs={{0,2},{2,0},{1,3},{3,1},{4,6},{6,4},{5,7},{7,5},{8,10},{10,8},{9,1... | collective-permute-start | bytes 73736 | tf_op jit(solution)/shard_map/ppermute | solution.py:288
  102.9 16.5 %collective-permute-start.7 = (bf16[2,128,384]{2,1,0:T(8,128)(2,1)S(1)}, bf16[2,128,384]{2,1,0:T(8,128)(2,1)S(1)}, u32[]{:S(2)}, u32[]{:S(2)}) collective-permute-start(bf16[2,128,384]{2,1,0:T(8,128)(2,1)S(1)} %get-tuple-element.45), channel_id=1, source_target_pairs={{0,2},{2,0},{1,3},{3,1},{4,6},{6,4},{5,7},{7,5},{8,10},{10,8},{9,1... | collective-permute-start | bytes 589832 | tf_op jit(solution)/shard_map/ppermute | solution.py:288
  103.7 15.0 %collective-permute-start.10 = (f32[8,768]{1,0:T(8,128)S(1)}, f32[8,768]{1,0:T(8,128)S(1)}, u32[]{:S(2)}, u32[]{:S(2)}) collective-permute-start(f32[8,768]{1,0:T(8,128)S(1)} %get-tuple-element.47), channel_id=1, source_target_pairs={{0,4},{4,0},{1,5},{5,1},{2,6},{6,2},{3,7},{7,3},{8,12},{12,8},{9,1... | collective-permute-start | bytes 73736 | tf_op jit(solution)/shard_map/ppermute | solution.py:297
  115.3 12.0 %all-to-all-start.4 = ((bf16[8,8,1536]{2,1,0:T(8,128)(2,1)}), bf16[8,8,1536]{2,1,0:T(8,128)(2,1)S(1)}, u32[]{:S(2)}, u32[]{:S(2)}) async-start(bf16[8,8,1536]{2,1,0:T(8,128)(2,1)} %pad_maximum_fusion.2), calls=%async_computation.4 | async-start | bytes 393216 | tf_op jit(solution)/shard_map/all_to_all | solution.py:264
  119.5 20.9 %collective-permute-start.8 = (bf16[128,768]{1,0:T(8,128)(2,1)S(1)}, bf16[128,768]{1,0:T(8,128)(2,1)S(1)}, u32[]{:S(2)}, u32[]{:S(2)}) collective-permute-start(bf16[128,768]{1,0:T(8,128)(2,1)S(1)} %get-tuple-element.43), channel_id=1, source_target_pairs={{0,4},{4,0},{1,5},{5,1},{2,6},{6,2},{3,7},{7,3},{8,12},{12,8},{9,1... | collective-permute-start | bytes 589832 | tf_op jit(solution)/shard_map/ppermute | solution.py:297
  127.4 13.9 %collective-permute-start.11 = (f32[6,1536]{1,0:T(8,128)S(1)}, f32[6,1536]{1,0:T(8,128)S(1)}, u32[]{:S(2)}, u32[]{:S(2)}) collective-permute-start(f32[6,1536]{1,0:T(8,128)S(1)} %bitcast.62), channel_id=1, source_target_pairs={{0,0},{64,2},{128,4},{192,6},{32,32},{96,34},{160,36},{224,38},{2,... | collective-permute-start | bytes 110600 | tf_op jit(solution)/shard_map/ppermute | solution.py:266
  134.3 14.4 %all-to-all-start.5 = ((f32[32,1,1536]{2,1,0:T(1,128)}), f32[32,1,1536]{2,1,0:T(1,128)S(1)}, u32[]{:S(2)}, u32[]{:S(2)}) async-start(f32[32,1,1536]{2,1,0:T(1,128)} %broadcast_in_dim.18), calls=%async_computation.5 | async-start | bytes 393216 | tf_op jit(solution)/shard_map/all_to_all | solution.py:270

commit v3 on v2

v3 whole, which is shorter than its diff:
```python
import math

import jax
import jax.numpy as jnp
import numpy as np
from jax import lax
from jax.experimental import pallas as pl
from jax.experimental.pallas import tpu as pltpu
from jax.sharding import Mesh
from jax.sharding import PartitionSpec as P

AXES = ("z", "x", "yh", "core", "rep")
SIZES = (8, 4, 2, 2, 2)
GROUP = ("yh", "core")
PLANE = ("x", "rep")
QUARTERS = 4
BLOCK = 6
PLANE_ROWS = 48
EXTRA = 128
EDGE, AFTER = 16, 32
FRAMES, CHANNELS, TAPS = 512, 384, 31
LONG = FRAMES + EDGE
SWAP = [(0, 1), (1, 0)]
BF = jnp.bfloat16
F32 = jnp.float32


def placement():
    out = np.zeros((CHANNELS, CHANNELS), np.float32)
    for zl in range(2):
        for x in range(4):
            for q in range(4):
                for rep in range(2):
                    for r in range(BLOCK):
                        row = (((zl * 4 + x) * 4 + q) * 2 + rep) * BLOCK + r
                        out[row, (x * 2 + rep) * PLANE_ROWS + (q * 2 + zl) * BLOCK + r] = 1
    return jnp.asarray(out, BF)


def turned():
    pairs = []
    for zq in range(4):
        for zl in range(2):
            for q in range(4):
                pairs.append(((zq * 2 + zl) * 4 + q, (q * 2 + zl) * 4 + zq))
    return pairs


def ordered(mine, other, first):
    return jnp.where(first, jnp.stack((mine, other)), jnp.stack((other, mine)))


def half(value, index, axis):
    size = value.shape[axis] // 2
    return lax.dynamic_slice_in_dim(value, index * size, size, axis)


def lanes(tile):
    return slice(tile * 128, tile * 128 + 128)


def begin(pairs, sems):
    copies = [pltpu.make_async_copy(a, b, sems.at[i]) for i, (a, b) in enumerate(pairs)]
    for copy in copies:
        copy.start()
    return copies


def finish(copies):
    for copy in copies:
        copy.wait()


def spread(weights, durations, slot, out, got, lengths, block, sems):
    finish(begin([(weights, got), (durations, lengths)], sems))
    lane = lax.broadcasted_iota(jnp.int32, (1, 1536), 1)
    total = jnp.sum(lengths[...].astype(F32), axis=1, keepdims=True)
    note = jnp.where(lane == lax.axis_index("z"), jnp.broadcast_to(total, (1, 1536)), 0.0)
    rows = [got[...].astype(F32), note, jnp.zeros((1, 1536), F32)]
    block[...] = jnp.concatenate(rows, axis=0).astype(BF)
    finish(begin([(block, out.at[peer]) for peer in range(8)], sems))


def pack(gathered, slot, across, upstream, plane, rows, got, block, sems):
    finish(begin([(gathered, got)], sems))
    note = jnp.zeros((8, EXTRA), F32)
    for z in range(8):
        block_z = got[z].astype(F32)
        rows[BLOCK * z : BLOCK * z + BLOCK] = block_z[:BLOCK]
        note += jnp.broadcast_to(block_z[BLOCK : BLOCK + 1, :EXTRA], (8, EXTRA))
    block[:, :1536] = rows[...].astype(BF)
    block[:, 1536:] = jnp.concatenate([note] * (PLANE_ROWS // 8), axis=0).astype(BF)
    finish(begin([(block, plane.at[peer]) for peer in range(8)], sems))


def group_grads(sources, grads):
    yh, core = lax.axis_index("yh"), lax.axis_index("core")
    places = [yh * 2 + core, 2 - 2 * yh + core, yh * 2 + 1 - core, 3 - 2 * yh - core]
    return [(source, grads.at[place]) for source, place in zip(sources, places)]


def convolve(
    own, slot, across, slot_across, beside, up_0, up_1, up_2, up_3, kernel, order, slope, hidden, parts,
    grads, frames, weights, turn, v_slope, v_hidden, v_parts, active, sems,
):
    yh, core = lax.axis_index("yh"), lax.axis_index("core")
    part = pl.ds(pl.multiple_of(core * CHANNELS, 128), CHANNELS)
    mine = pl.ds(pl.multiple_of((yh * 2 + core) * CHANNELS, 128), CHANNELS)
    needed = begin(
        [
            (own.at[:, mine], frames.at[yh * 2 + core, pl.ds(0, 128)]),
            (slot.at[:, mine], frames.at[yh * 2 + core, pl.ds(128, EDGE)]),
            (across.at[:, part], frames.at[(1 - yh) * 2 + core, pl.ds(0, 128)]),
            (slot_across.at[:, part], frames.at[(1 - yh) * 2 + core, pl.ds(128, EDGE)]),
            (beside.at[0], frames.at[yh * 2 + 1 - core]),
            (beside.at[1], frames.at[(1 - yh) * 2 + 1 - core]),
            (kernel, weights),
        ],
        sems,
    )
    later = begin(
        group_grads((up_0, up_1, up_2, up_3), grads) + [(order, turn)], sems.at[pl.ds(8, 5)]
    )
    finish(needed)
    v_hidden[:EDGE] = frames[0, 128:].astype(F32)
    for b in range(4):
        v_hidden[EDGE + 128 * b : EDGE + 128 * b + 128] = frames[b, :128].astype(F32)
    v_hidden[EDGE + FRAMES :] = frames[3, 128:].astype(F32)
    rows = 128
    for tile in range(CHANNELS // 128):

        def chunk(c, _, tile=tile):
            base = pl.multiple_of(c * rows, 8)
            total = jnp.zeros((rows, 128), F32)
            window = v_hidden[pl.ds(base, rows + 32), lanes(tile)]
            for b in range(8):
                slab = window[b : b + rows + 24]
                for a in range(4):
                    k = 8 * a + b - 1
                    if 0 <= k < TAPS:
                        total += weights[k : k + 1, lanes(tile)] * slab[8 * a : 8 * a + rows]
            sig = jax.nn.sigmoid(total)
            v_slope[pl.ds(base, rows), lanes(tile)] = sig * (1.0 + total * (1.0 - sig))
            active[pl.ds(base, rows), lanes(tile)] = total * sig
            return 0

        lax.fori_loop(0, FRAMES // rows, chunk, 0)
    out = begin([(v_slope, slope), (v_hidden, hidden)], sems)
    finish(later)
    acts = active[...].astype(BF)
    acts = jnp.dot(acts, turn[...], preferred_element_type=F32).astype(BF)
    product = lax.dot_general(
        acts,
        grads[...].reshape(FRAMES, 1536),
        (((0,), (0,)), ((), ())),
        preferred_element_type=F32,
    ).astype(BF)
    for s in range(8):
        v_parts[s] = product[PLANE_ROWS * s : PLANE_ROWS * (s + 1)]
    finish(begin([(v_parts, parts.at[:, :, pl.ds(0, 1536)])], sems.at[pl.ds(2, 1)]))
    finish(out)


def backward(
    gathered, spread, up_0, up_1, up_2, up_3, slope, hidden, parts,
    grad_conv, head, tail, message,
    got, turn, grads, v_slope, v_hidden, v_grad, v_grad_f, v_taps, sums, sems,
):
    needed = begin(
        [(gathered.at[s, :, pl.ds(0, 1536)], got.at[s]) for s in range(8)]
        + [(spread, turn)],
        sems,
    )
    later = begin(group_grads((up_0, up_1, up_2, up_3), grads), sems.at[pl.ds(9, 4)])
    last = begin([(slope, v_slope), (hidden, v_hidden)], sems.at[pl.ds(13, 2)])
    finish(needed)
    weights = jnp.dot(
        turn[...], got[...].reshape(CHANNELS, 1536), preferred_element_type=F32
    ).astype(BF)
    finish(later)
    value = lax.dot_general(
        grads[...].reshape(FRAMES, 1536),
        weights,
        (((1,), (1,)), ((), ())),
        preferred_element_type=F32,
    )
    finish(last)
    value = (value * v_slope[...]).astype(BF)
    v_grad[...] = value
    v_grad_f[...] = value.astype(F32)
    out = begin(
        [
            (v_grad, grad_conv),
            (v_grad.at[pl.ds(0, AFTER)], head),
            (v_grad.at[pl.ds(FRAMES - EDGE, EDGE)], tail),
        ],
        sems,
    )
    span = 128
    sums[...] = jnp.zeros_like(sums)
    for tile in range(CHANNELS // 128):

        def piece(c, _, tile=tile):
            base = pl.multiple_of(c * span, 8)
            terms = v_grad_f[pl.ds(base, span), lanes(tile)]
            window = v_hidden[pl.ds(base, span + 32), lanes(tile)]
            for b in range(8):
                slab = window[b : b + span + 24]
                for a in range(4):
                    k = 8 * a + b - 1
                    if 0 <= k < TAPS:
                        sums[k, :, lanes(tile)] += jnp.sum(
                            (terms * slab[8 * a : 8 * a + span]).reshape(span // 8, 8, 128),
                            axis=0,
                        )
            return 0

        lax.fori_loop(0, FRAMES // span, piece, 0)
    for s in range(8):
        rows = [
            jnp.sum(sums[4 * s + t, :, lanes(tile)], axis=0, keepdims=True)
            for t in range(4)
            for tile in range(CHANNELS // 128)
        ]
        rows = jnp.concatenate(rows, axis=0)
        high = rows.astype(BF).astype(F32)
        rows = [high, rows - high, jnp.zeros((PLANE_ROWS - 24, 128), F32)]
        v_taps[s] = jnp.concatenate(rows, axis=0).astype(BF)
    finish(begin([(v_taps, message.at[:, :, pl.ds(1536, EXTRA)])], sems.at[pl.ds(3, 1)]))
    finish(out)


def transposed(
    grad_conv, before, after, kernel, frame_grad, v_grad, edge, rest, weights, wide, total_f, v_out, sems,
):
    finish(
        begin([(grad_conv, v_grad), (before, edge), (after, rest), (kernel, weights)], sems)
    )
    wide[:EDGE] = edge[...].astype(F32)
    wide[EDGE : EDGE + FRAMES] = v_grad[...].astype(F32)
    wide[EDGE + FRAMES :] = rest[...].astype(F32)
    rows = 88
    for tile in range(CHANNELS // 128):

        def chunk(c, _, tile=tile):
            base = pl.multiple_of(c * rows, 8)
            total = jnp.zeros((rows, 128), F32)
            window = wide[pl.ds(base, rows + 32), lanes(tile)]
            for b in range(8):
                slab = window[b : b + rows + 24]
                for a in range(4):
                    k = TAPS - 8 * a - b
                    if 0 <= k < TAPS:
                        total += weights[k : k + 1, lanes(tile)] * slab[8 * a : 8 * a + rows]
            total_f[pl.ds(base, rows), lanes(tile)] = total
            return 0

        lax.fori_loop(0, LONG // rows, chunk, 0)
    v_out[...] = total_f[...].astype(BF)
    finish(begin([(v_out, frame_grad)], sems))


def pack_z(parts, out, v_parts, v_sum, v_out, sems):
    finish(begin([(parts, v_parts)], sems))
    v_sum[...] = jnp.sum(v_parts[...].astype(F32), axis=0)
    taps = v_sum[:12, 1536:] + v_sum[12:24, 1536:]
    taps = jnp.concatenate([taps[j : j + 1] for j in range(12)], axis=1)
    high = taps.astype(BF).astype(F32)
    for z in range(8):
        rows = [v_sum[BLOCK * z : BLOCK * z + BLOCK, :1536], high, taps - high]
        v_out[z] = jnp.concatenate(rows, axis=0).astype(BF)
    finish(begin([(v_out, out)], sems))


def unpack_z(got, weights, taps, v_got, v_weights, v_taps, sems):
    finish(begin([(got, v_got)], sems))
    total = v_got[0].astype(F32)
    for z in range(1, 8):
        total += v_got[z].astype(F32)
    total = total * (1.0 / math.sqrt(2 * 16384))
    v_weights[...] = total[:BLOCK]
    for peer in range(32):
        v_taps[peer] = total[6:7] + total[7:8]
    finish(begin([(v_taps, taps), (v_weights, weights)], sems))


def arrange(got, out, v_got, v_out, sems):
    finish(begin([(got, v_got)], sems))
    for x in range(4):
        for q in range(4):
            for rep in range(2):
                for t in range(4):
                    k = (x * 2 + rep) * 4 + t
                    if k < TAPS:
                        v_out[k : k + 1, q * CHANNELS : q * CHANNELS + CHANNELS] = v_got[
                            (x * 4 + q) * 2 + rep, :, t * CHANNELS : t * CHANNELS + CHANNELS
                        ]
    finish(begin([(v_out, out)], sems))


def call(kernel, outs, scratch, flops, *args, alias=None):
    shapes = [jax.ShapeDtypeStruct(shape, dtype) for shape, dtype in outs]
    size = sum(math.prod(s.shape) * s.dtype.itemsize for s in list(args) + shapes)
    return pl.pallas_call(
        kernel,
        out_shape=shapes,
        in_specs=[pl.BlockSpec(memory_space=pltpu.HBM)] * len(args),
        out_specs=[pl.BlockSpec(memory_space=pltpu.HBM)] * len(shapes),
        scratch_shapes=[pltpu.VMEM(shape, dtype) for shape, dtype in scratch]
        + [pltpu.SemaphoreType.DMA((16,))],
        input_output_aliases=alias or {},
        compiler_params=pltpu.CompilerParams(vmem_limit_bytes=(56 if flops else 12) * 2**20),
        cost_estimate=pl.CostEstimate(
            flops=flops, bytes_accessed=size, transcendentals=0
        ),
    )(*args)


def body(hidden_in, upstream, out_weight, conv_kernel, durations):
    yh, core = lax.axis_index("yh"), lax.axis_index("core")
    rep = lax.axis_index("rep")
    z, x = lax.axis_index("z"), lax.axis_index("x")
    quarter = yh * 2 + core
    place = z * 4 + x
    hidden, grads = hidden_in[0], upstream[0]

    rows = lax.ppermute(out_weight, ("z", "yh", "core"), turned())
    ends = [(4 * i + 3, 4 * i + 4) for i in range(31)]
    slot = lax.ppermute(
        jnp.where(quarter == 0, hidden[:EDGE], hidden[128 - EDGE :]),
        ("z", "x", "yh", "core"),
        ends + [(b, a) for a, b in ends],
    )
    [rows] = call(
        spread,
        [((8, 8, 1536), BF)],
        [((BLOCK, 1536), BF), ((1, 8), jnp.int32), ((8, 1536), BF)],
        0,
        rows, durations, slot,
    )
    rows = lax.all_to_all(rows, "z", 0, 0, tiled=True)
    across = lax.ppermute(half(hidden, 1 - yh, 1), "yh", SWAP)
    up_1 = lax.ppermute(grads, "yh", SWAP)
    up_2 = lax.ppermute(grads, "core", SWAP)
    slot_across = lax.ppermute(half(slot, 1 - yh, 1), "yh", SWAP)
    up_3 = lax.ppermute(up_1, "core", SWAP)
    ups = (grads, up_1, up_2, up_3)
    near = jnp.concatenate((half(hidden, yh, 1), half(slot, yh, 1)), axis=0)
    far = jnp.concatenate((across, slot_across), axis=0)
    beside = half(jnp.stack((near, far)), 1 - core, 2)
    beside = lax.ppermute(beside, "core", SWAP)
    [plane] = call(
        pack,
        [((8, PLANE_ROWS, 1536 + EXTRA), BF)],
        [((PLANE_ROWS, 1536), F32), ((8, 8, 1536), BF), ((PLANE_ROWS, 1536 + EXTRA), BF)],
        0,
        rows, slot_across, across, up_1,
    )
    rows = lax.all_to_all(plane, PLANE, 0, 0, tiled=True)
    ring = ("z", "x")
    up, down = [(i, i + 1) for i in range(31)], [(i + 1, i) for i in range(31)]
    kernel_f = lax.dynamic_slice_in_dim(
        jnp.pad(conv_kernel, ((0, 1), (0, 0))), quarter * CHANNELS, CHANNELS, 1
    ).astype(F32)
    square = ((CHANNELS, CHANNELS), BF)
    frames_f = ((FRAMES, CHANNELS), F32)
    wide_f = ((FRAMES + 2 * EDGE, CHANNELS), F32)
    all_grads = ((4, 128, 1536), BF)
    sent = ((8, PLANE_ROWS, 1536), BF)
    message = ((8, PLANE_ROWS, 1536 + EXTRA), BF)
    kernel_shape = ((TAPS + 1, CHANNELS), F32)
    slope, hidden_f, parts = call(
        convolve,
        [frames_f, wide_f, message],
        [
            all_grads, ((4, 128 + EDGE, CHANNELS), BF), kernel_shape, square, frames_f, wide_f, sent, frames_f,
        ],
        800_000_000,
        hidden, slot, across, slot_across, beside, *ups, kernel_f, placement(),
    )
    grad_conv, head, tail, parts = call(
        backward,
        [
            ((FRAMES, CHANNELS), BF), ((AFTER, CHANNELS), BF), ((EDGE, CHANNELS), BF), message,
        ],
        [
            sent, square, all_grads, frames_f, wide_f, ((FRAMES, CHANNELS), BF), frames_f,
            ((8, PLANE_ROWS, EXTRA), BF), ((TAPS + 1, 8, CHANNELS), F32),
        ],
        1_400_000_000,
        rows, placement(), *ups, slope, hidden_f, parts,
        alias={8: 3},
    )

    parts = lax.all_to_all(parts, PLANE, 0, 0, tiled=True)
    [parts] = call(
        pack_z,
        [((8, 8, 1536), BF)],
        [message, ((PLANE_ROWS, 1536 + EXTRA), F32), ((8, 8, 1536), BF)],
        0,
        parts,
    )
    parts = lax.all_to_all(parts, "z", 0, 0, tiled=True)
    weight_grad, taps_all = call(
        unpack_z,
        [((BLOCK, 1536), F32), ((32, 1, 1536), F32)],
        [((8, 8, 1536), BF), ((BLOCK, 1536), F32), ((32, 1, 1536), F32)],
        0,
        parts,
    )
    taps_all = lax.all_to_all(
        taps_all, ("x", "yh", "core", "rep"), 0, 0, tiled=True
    )
    weight_grad = lax.ppermute(
        weight_grad, ("z", "yh", "core"), [(b, a) for a, b in turned()]
    )
    [kernel_grad] = call(
        arrange,
        [((TAPS, 1536), F32)],
        [((32, 1, 1536), F32), ((TAPS, 1536), F32)],
        0,
        taps_all,
    )

    [frame_grad] = call(
        transposed,
        [((LONG, CHANNELS), BF)],
        [
            ((FRAMES, CHANNELS), BF), ((EDGE, CHANNELS), BF), ((AFTER, CHANNELS), BF),
            kernel_shape, ((FRAMES + EDGE + AFTER, CHANNELS), F32), ((LONG, CHANNELS), F32),
            ((LONG, CHANNELS), BF),
        ],
        200_000_000,
        grad_conv, lax.ppermute(tail, ring, up), lax.ppermute(head, ring, down), kernel_f,
    )
    notes = rows[:, 0, 1536:1544].reshape(4, 2, 8).astype(F32)
    notes = jnp.where(rep == 0, notes[:, 0], notes[:, 1])
    order = lax.iota(jnp.int32, 8)[None, :] * 4 + lax.iota(jnp.int32, 4)[:, None]
    earlier = jnp.sum(jnp.where(order < place, notes, 0.0)).astype(jnp.int32)
    known = jnp.concatenate((durations[0], jnp.full((8,), earlier)))
    known = jnp.stack(
        [known]
        + [lax.ppermute(known, GROUP, [(i, i ^ k) for i in range(4)]) for k in (1, 2, 3)]
    )
    start = jnp.sum(known[:, 8]) - place * FRAMES
    blocks = quarter ^ lax.iota(jnp.int32, 4)
    lengths = jnp.sum(
        jnp.where(blocks[None] == lax.iota(jnp.int32, 4)[:, None], 1, 0)[:, :, None]
        * known[None, :, :8],
        axis=1,
    ).reshape(-1)
    ends = start + jnp.cumsum(lengths)
    starts = ends - lengths
    at = lax.iota(jnp.int32, LONG)
    covers = (at[None] >= starts[:, None]) & (at[None] < ends[:, None])
    gloss = jnp.dot(covers.astype(BF), frame_grad, preferred_element_type=F32)

    def back(value):
        value = value.reshape(2, 2, -1, CHANNELS)
        kept = lax.dynamic_index_in_dim(value, core, 1, False)
        got = lax.ppermute(
            lax.dynamic_index_in_dim(value, 1 - core, 1, False), "core", SWAP
        )
        value = jnp.where(
            core == 0,
            jnp.concatenate((kept, got), axis=2),
            jnp.concatenate((got, kept), axis=2),
        )
        kept = lax.dynamic_index_in_dim(value, yh, 0, False)
        got = lax.ppermute(
            lax.dynamic_index_in_dim(value, 1 - yh, 0, False), "yh", SWAP
        )
        return jnp.where(
            yh == 0,
            jnp.concatenate((kept, got), axis=1),
            jnp.concatenate((got, kept), axis=1),
        )

    return (
        back(frame_grad[:FRAMES])[None],
        back(gloss)[None],
        weight_grad,
        kernel_grad,
    )


def solution(mesh):
    fine = Mesh(mesh.devices.reshape(SIZES), AXES)
    seq = ("z", "x", "yh", "core")
    rows = P(seq + ("rep",), None)
    in_specs = (P("rep", seq, None), P("rep", seq, None), rows, P(), P("rep", seq))
    out_specs = (P("rep", seq, None), P("rep", seq, None), rows, P())
    return jax.shard_map(
        body, mesh=fine, in_specs=in_specs, out_specs=out_specs, check_vma=False
    )
```

time: 152 us -> 141 us (0.928)
  the two profiles are of different devices: /device:TPU:1 before, /device:TPU:22 now
where the time goes in v3:
time: 141 us; the launch traced here: 140 us
  starting transfers between devices  68.4 us (49%)
  waiting for transfers between devices  33.2 us (24%)
  Pallas kernels  26.2 us (19%)
  other arithmetic  4.8 us (3%)
  local copies, waits for them, and re-layouts  4.08 us (3%)
  between operations  2.34 us (2%)
    pallas_call x8, Pallas kernels, call(): pl.pallas_call(kernel, out_shape=shapes, in_specs=[pl.BlockSpec(memory_sp...  26.2 us
    ppermute x1, waiting for transfers between devices, body(): lax.ppermute(weight_grad, ('z', 'yh', 'core'), [(b, a) for a, b in turned...  8.99 us
    all_to_all x1, starting transfers between devices, body(): lax.all_to_all(taps_all, ('x', 'yh', 'core', 'rep'), 0, 0, tiled=True)  8.89 us
    ppermute x1, starting transfers between devices, body(): rows = lax.ppermute(out_weight, ('z', 'yh', 'core'), turned())  8.55 us
    all_to_all x1, waiting for transfers between devices, body(): parts = lax.all_to_all(parts, 'z', 0, 0, tiled=True)  6.65 us
    all_to_all x1, starting transfers between devices, body(): parts = lax.all_to_all(parts, 'z', 0, 0, tiled=True)  6.05 us
    all_to_all x1, starting transfers between devices, body(): rows = lax.all_to_all(plane, PLANE, 0, 0, tiled=True)  5.85 us
    ppermute x1, waiting for transfers between devices, body(): slot_across = lax.ppermute(half(slot, 1 - yh, 1), 'yh', SWAP)  5.21 us
  transfers between devices with their start and end apart: 23, of which 10 were waited for; matrix products, arithmetic and copies ran while one was open for 4% of the time, Pallas kernels for 17%

profile of v3, /device:TPU:22, one launch (start us, length us, event | category | flops | bytes accessed | tf_op | source)
XLA Modules:
  0.0 140.4 jit_solution(14700199152672261021)
XLA Ops:
  0.6 0.8 select_bitcast_fusion
  1.5 0.7 collective-permute-start.1
  2.1 4.6 %collective-permute-start.4 = (bf16[128,1536]{1,0:T(8,128)(2,1)}, bf16[128,1536]{1,0:T(8,128)(2,1)S(1)}, u32[]{:S(2)}, u32[]{:S(2)}) collective-permute-start(bf16[128,1536]{1,0:T(8,128)(2,1)} %bitcast.42), channel_id=1, source_target_pairs={{0,4},{4,0},{1,5},{5,1},{2,6},{6,2},{3,7},{7,3},{8,12},{12,8},{9,1... | collective-permute-start | bytes 1179656 | tf_op jit(solution)/shard_map/ppermute | solution.py:343
  6.7 8.6 %collective-permute-start = (bf16[6,1536]{1,0:T(8,128)(2,1)}, bf16[6,1536]{1,0:T(8,128)(2,1)S(1)}, u32[]{:S(2)}, u32[]{:S(2)}) collective-permute-start(bf16[6,1536]{1,0:T(8,128)(2,1)} %param.9), channel_id=1, source_target_pairs={{0,0},{2,64},{4,128},{6,192},{32,32},{34,96},{36,160},{38,224},{64... | collective-permute-start | bytes 55304 | tf_op jit(solution)/shard_map/ppermute | solution.py:327
  15.3 3.7 %collective-permute-done.weights = bf16[6,1536]{1,0:T(8,128)(2,1)S(1)} collective-permute-done((bf16[6,1536]{1,0:T(8,128)(2,1)}, bf16[6,1536]{1,0:T(8,128)(2,1)S(1)}, u32[]{:S(2)}, u32[]{:S(2)}) %collective-permute-start) | collective-permute-done | bytes 18464 | tf_op jit(solution)/shard_map/ppermute | solution.py:327
  18.9 0.7 copy-done.4
  19.6 0.9 shard_map.102
  20.5 3.6 %all-to-all-start = ((bf16[8,8,1536]{2,1,0:T(8,128)(2,1)}), bf16[8,8,1536]{2,1,0:T(8,128)(2,1)S(1)}, u32[]{:S(2)}, u32[]{:S(2)}) async-start(bf16[8,8,1536]{2,1,0:T(8,128)(2,1)} %shard_map.102), calls=%async_computation | async-start | bytes 393216 | tf_op jit(solution)/shard_map/all_to_all | solution.py:341
  24.2 1.0 dynamic-slice_bitcast_fusion.3
  25.2 5.0 %collective-permute-start.3 = (bf16[128,768]{1,0:T(8,128)(2,1)S(1)}, bf16[128,768]{1,0:T(8,128)(2,1)S(1)}, u32[]{:S(2)}, u32[]{:S(2)}) collective-permute-start(bf16[128,768]{1,0:T(8,128)(2,1)S(1)} %get-tuple-element.27), channel_id=1, source_target_pairs={{0,4},{4,0},{1,5},{5,1},{2,6},{6,2},{3,7},{7,3},{8,12},{12,8},{9,1... | collective-permute-start | bytes 589832 | tf_op jit(solution)/shard_map/ppermute | solution.py:342
  30.2 0.1 collective-permute-start.2
  30.3 5.2 %collective-permute-done.2.slot.slot_across = bf16[16,768]{1,0:T(8,128)(2,1)S(1)} collective-permute-done((bf16[16,768]{1,0:T(8,128)(2,1)S(1)}, bf16[16,768]{1,0:T(8,128)(2,1)S(1)}, u32[]{:S(2)}, u32[]{:S(2)}) %collective-permute-start.2) | collective-permute-done | bytes 24608 | tf_op jit(solution)/shard_map/ppermute | solution.py:345
  35.5 0.2 all-to-all-done.gathered
  35.8 1.5 %shard_map.103 = bf16[8,48,1664]{2,1,0:T(8,128)(2,1)} custom-call(bf16[8,8,1536]{2,1,0:T(8,128)(2,1)S(1)} %all-to-all-done.gathered, bf16[16,768]{1,0:T(8,128)(2,1)S(1)} %collective-permute-done.2.slot.slot_across, bf16[128,768]{1,0:T(8,128)(2,1)S(1)} %collective-permute-done.3.across, bf16[128,1536]{1,0:T(8,128)(2,1)S(1)} %collective-permute-done.4.upstream.up_1), custom_call_target="tpu_custom_call" | custom-call | bytes 2088960 | tf_op jit(solution)/shard_map/pallas_call | solution.py:304
  37.3 0.0 copy-start.7
  37.3 0.0 copy-start.10
  37.3 5.8 %all-to-all-start.1 = ((bf16[8,48,1664]{2,1,0:T(8,128)(2,1)}), bf16[8,48,1664]{2,1,0:T(8,128)(2,1)S(1)}, u32[]{:S(2)}, u32[]{:S(2)}) async-start(bf16[8,48,1664]{2,1,0:T(8,128)(2,1)} %shard_map.103), calls=%async_computation.1 | async-start | bytes 2555904 | tf_op jit(solution)/shard_map/all_to_all | solution.py:359
  43.2 0.6 fusion.6.kernel
  43.9 0.6 collective-permute-start.6
  44.5 0.1 collective-permute-start.7
  44.6 0.2 collective-permute-done.5.up_2
  44.9 1.2 collective-permute-done.7.beside
  46.1 0.7 copy-done.13
  46.8 0.1 copy-done.9
  46.9 7.7 %shard_map.104 = (f32[512,384]{1,0:T(8,128)}, f32[544,384]{1,0:T(8,128)}, bf16[8,48,1664]{2,1,0:T(8,128)(2,1)}) custom-call(bf16[128,1536]{1,0:T(8,128)(2,1)} %bitcast.41, bf16[16,1536]{1,0:T(8,128)(2,1)} %copy-done.2, bf16[128,768]{1,0:T(8,128)(2,1)} %copy-done.1, bf16[16,768]{1,0:T(8,128)(2,1)} %copy-done.3, bf16[2,144,384]{2,1,0:T(8,128)(2,1)} %copy-done.13, ...), custom_call_target="tpu_custom_call" | custom-call | flops 800000000 | bytes 5701632 | tf_op jit(solution)/shard_map/pallas_call | solution.py:304
  54.6 4.2 %all-to-all-done.1.gathered = bf16[8,48,1664]{2,1,0:T(8,128)(2,1)S(1)} async-done(((bf16[8,48,1664]{2,1,0:T(8,128)(2,1)}), bf16[8,48,1664]{2,1,0:T(8,128)(2,1)S(1)}, u32[]{:S(2)}, u32[]{:S(2)}) %all-to-all-start.1) | async-done | bytes 1277984 | tf_op jit(solution)/shard_map/all_to_all | solution.py:359
  58.8 0.7 select_reduce_fusion
  60.2 0.1 collective-permute-start.12
  60.3 2.0 %collective-permute-start.13 = (s32[16]{0:T(128)S(1)}, s32[16]{0:T(128)S(1)}, u32[]{:S(2)}, u32[]{:S(2)}) collective-permute-start(s32[16]{0:T(128)S(1)} %concatenate.72), channel_id=1, source_target_pairs={{0,4},{2,6},{4,0},{6,2},{1,5},{3,7},{5,1},{7,3},{8,12},{10,14},{12... | collective-permute-start | bytes 200 | tf_op jit(solution)/shard_map/ppermute | solution.py:443
  62.2 1.4 collective-permute-start.14
  63.6 6.4 %shard_map.105 = (bf16[512,384]{1,0:T(8,128)(2,1)}, bf16[32,384]{1,0:T(8,128)(2,1)}, bf16[16,384]{1,0:T(8,128)(2,1)}, bf16[8,48,1664]{2,1,0:T(8,128)(2,1)}) custom-call(bf16[8,48,1664]{2,1,0:T(8,128)(2,1)} %copy-done.6, bf16[384,384]{1,0:T(8,128)(2,1)} %constant.74.clone.order.spread, bf16[128,1536]{1,0:T(8,128)(2,1)} %bitcast.44, ...), custom_call_target="tpu_custom_call", output_to_operand_aliasing={{3}: (8, {})} | custom-call | flops 1400000000 | bytes 7753728 | tf_op jit(solution)/shard_map/pallas_call | solution.py:304
  70.1 2.8 %collective-permute-start.9 = (bf16[32,384]{1,0:T(8,128)(2,1)}, bf16[32,384]{1,0:T(8,128)(2,1)S(1)}, u32[]{:S(2)}, u32[]{:S(2)}) collective-permute-start(bf16[32,384]{1,0:T(8,128)(2,1)} %get-tuple-element.18), channel_id=1, source_target_pairs={{8,0},{16,8},{24,16},{32,24},{40,32},{48,40},{56,48},{64,56},{72,6... | collective-permute-start | bytes 73736 | tf_op jit(solution)/shard_map/ppermute | solution.py:434
  72.8 5.2 %collective-permute-start.8 = (bf16[16,384]{1,0:T(8,128)(2,1)}, bf16[16,384]{1,0:T(8,128)(2,1)S(1)}, u32[]{:S(2)}, u32[]{:S(2)}) collective-permute-start(bf16[16,384]{1,0:T(8,128)(2,1)} %get-tuple-element.17), channel_id=1, source_target_pairs={{0,8},{8,16},{16,24},{24,32},{32,40},{40,48},{48,56},{56,64},{64,7... | collective-permute-start | bytes 36872 | tf_op jit(solution)/shard_map/ppermute | solution.py:434
  78.0 5.2 %all-to-all-start.2 = ((bf16[8,48,1664]{2,1,0:T(8,128)(2,1)}), bf16[8,48,1664]{2,1,0:T(8,128)(2,1)S(1)}, u32[]{:S(2)}, u32[]{:S(2)}) async-start(bf16[8,48,1664]{2,1,0:T(8,128)(2,1)} %get-tuple-element.19), calls=%async_computation.2 | async-start | bytes 2555904 | tf_op jit(solution)/shard_map/all_to_all | solution.py:395
  83.2 0.1 multiply_reduce_fusion
  83.3 0.1 reshape.190
  83.4 0.1 reduce-window.7
  83.5 0.7 slice_reduce_fusion
  84.8 0.1 add_reduce_fusion
  84.9 0.1 reshape.187
  85.0 0.0 copy-start.12
  85.1 0.6 copy-done.12
  85.6 0.0 copy-done.11
  85.7 6.1 %shard_map.106 = bf16[528,384]{1,0:T(8,128)(2,1)} custom-call(bf16[512,384]{1,0:T(8,128)(2,1)} %get-tuple-element.16.grad_conv, bf16[16,384]{1,0:T(8,128)(2,1)} %copy-done.12, bf16[32,384]{1,0:T(8,128)(2,1)} %copy-done.11, f32[32,384]{1,0:T(8,128)} %fusion.6.kernel), custom_call_target="tpu_custom_call" | custom-call | flops 200000000 | bytes 884736 | tf_op jit(solution)/shard_map/pallas_call | solution.py:304
  91.7 1.3 fusion.2
  93.1 0.3 collective-permute-start.15
  93.4 0.1 dynamic-slice_bitcast_fusion.2
  93.4 0.6 collective-permute-start.10
  94.0 0.6 collective-permute-done.15
  94.5 2.3 %collective-permute-start.16 = (f32[8,768]{1,0:T(8,128)S(1)}, f32[8,768]{1,0:T(8,128)S(1)}, u32[]{:S(2)}, u32[]{:S(2)}) collective-permute-start(f32[8,768]{1,0:T(8,128)S(1)} %get-tuple-element.29), channel_id=1, source_target_pairs={{0,4},{4,0},{1,5},{5,1},{2,6},{6,2},{3,7},{7,3},{8,12},{12,8},{9,1... | collective-permute-start | bytes 73736 | tf_op jit(solution)/shard_map/ppermute | solution.py:470
  96.8 2.2 %all-to-all-done.2.parts = bf16[8,48,1664]{2,1,0:T(8,128)(2,1)S(1)} async-done(((bf16[8,48,1664]{2,1,0:T(8,128)(2,1)}), bf16[8,48,1664]{2,1,0:T(8,128)(2,1)S(1)}, u32[]{:S(2)}, u32[]{:S(2)}) %all-to-all-start.2) | async-done | bytes 1277984 | tf_op jit(solution)/shard_map/all_to_all | solution.py:395
  99.0 1.5 %shard_map.107 = bf16[8,8,1536]{2,1,0:T(8,128)(2,1)} custom-call(bf16[8,48,1664]{2,1,0:T(8,128)(2,1)S(1)} %all-to-all-done.2.parts), custom_call_target="tpu_custom_call" | custom-call | bytes 1474560 | tf_op jit(solution)/shard_map/pallas_call | solution.py:304
  100.5 6.1 %all-to-all-start.3 = ((bf16[8,8,1536]{2,1,0:T(8,128)(2,1)}), bf16[8,8,1536]{2,1,0:T(8,128)(2,1)S(1)}, u32[]{:S(2)}, u32[]{:S(2)}) async-start(bf16[8,8,1536]{2,1,0:T(8,128)(2,1)} %shard_map.107), calls=%async_computation.3 | async-start | bytes 393216 | tf_op jit(solution)/shard_map/all_to_all | solution.py:403
  106.6 0.1 maximum_select_fusion
  106.7 2.3 %collective-permute-start.11 = (bf16[128,768]{1,0:T(8,128)(2,1)S(1)}, bf16[128,768]{1,0:T(8,128)(2,1)S(1)}, u32[]{:S(2)}, u32[]{:S(2)}) collective-permute-start(bf16[128,768]{1,0:T(8,128)(2,1)S(1)} %get-tuple-element.23), channel_id=1, source_target_pairs={{0,4},{4,0},{1,5},{5,1},{2,6},{6,2},{3,7},{7,3},{8,12},{12,8},{9,1... | collective-permute-start | bytes 589832 | tf_op jit(solution)/shard_map/ppermute | solution.py:470
  109.1 0.6 maximum_select_fusion.3
  109.7 6.7 %all-to-all-done.3.got = bf16[8,8,1536]{2,1,0:T(8,128)(2,1)S(1)} async-done(((bf16[8,8,1536]{2,1,0:T(8,128)(2,1)}), bf16[8,8,1536]{2,1,0:T(8,128)(2,1)S(1)}, u32[]{:S(2)}, u32[]{:S(2)}) %all-to-all-start.3) | async-done | bytes 196640 | tf_op jit(solution)/shard_map/all_to_all | solution.py:403
  116.4 1.1 shard_map.108
  117.5 8.9 %all-to-all-start.4 = ((f32[32,1,1536]{2,1,0:T(1,128)}), f32[32,1,1536]{2,1,0:T(1,128)S(1)}, u32[]{:S(2)}, u32[]{:S(2)}) async-start(f32[32,1,1536]{2,1,0:T(1,128)} %get-tuple-element.21), calls=%async_computation.4 | async-start | bytes 393216 | tf_op jit(solution)/shard_map/all_to_all | solution.py:411
  126.4 2.4 %collective-permute-start.17 = (f32[6,1536]{1,0:T(8,128)S(1)}, f32[6,1536]{1,0:T(8,128)S(1)}, u32[]{:S(2)}, u32[]{:S(2)}) collective-permute-start(f32[6,1536]{1,0:T(8,128)S(1)} %get-tuple-element.20), channel_id=1, source_target_pairs={{0,0},{64,2},{128,4},{192,6},{32,32},{96,34},{160,36},{224,38},{2,... | collective-permute-start | bytes 110600 | tf_op jit(solution)/shard_map/ppermute | solution.py:414
  128.8 0.8 maximum_select_fusion.1
  129.7 9.0 %collective-permute-done.17 = f32[6,1536]{1,0:T(8,128)S(1)} collective-permute-done((f32[6,1536]{1,0:T(8,128)S(1)}, f32[6,1536]{1,0:T(8,128)S(1)}, u32[]{:S(2)}, u32[]{:S(2)}) %collective-permute-start.17) | collective-permute-done | bytes 36896 | tf_op jit(solution)/shard_map/ppermute | solution.py:414
  138.7 1.1 shard_map.109
  139.8 0.6 copy.17
  (53 shorter events, 0.3 us)
Async XLA Ops:
  1.5 17.5 %collective-permute-start.1 = (bf16[16,1536]{1,0:T(8,128)(2,1)S(1)}, bf16[16,1536]{1,0:T(8,128)(2,1)S(1)}, u32[]{:S(2)}, u32[]{:S(2)}) collective-permute-start(bf16[16,1536]{1,0:T(8,128)(2,1)S(1)} %select_bitcast_fusion), channel_id=1, source_target_pairs={{6,8},{14,16},{22,24},{30,32},{38,40},{46,48},{54,56},{62,64},{70,... | collective-permute-start | bytes 147464 | tf_op jit(solution)/shard_map/ppermute | solution.py:329
  2.1 33.6 %collective-permute-start.4 = (bf16[128,1536]{1,0:T(8,128)(2,1)}, bf16[128,1536]{1,0:T(8,128)(2,1)S(1)}, u32[]{:S(2)}, u32[]{:S(2)}) collective-permute-start(bf16[128,1536]{1,0:T(8,128)(2,1)} %bitcast.42), channel_id=1, source_target_pairs={{0,4},{4,0},{1,5},{5,1},{2,6},{6,2},{3,7},{7,3},{8,12},{12,8},{9,1... | collective-permute-start | bytes 1179656 | tf_op jit(solution)/shard_map/ppermute | solution.py:343
  6.7 12.2 %collective-permute-start = (bf16[6,1536]{1,0:T(8,128)(2,1)}, bf16[6,1536]{1,0:T(8,128)(2,1)S(1)}, u32[]{:S(2)}, u32[]{:S(2)}) collective-permute-start(bf16[6,1536]{1,0:T(8,128)(2,1)} %param.9), channel_id=1, source_target_pairs={{0,0},{2,64},{4,128},{6,192},{32,32},{34,96},{36,160},{38,224},{64... | collective-permute-start | bytes 55304 | tf_op jit(solution)/shard_map/ppermute | solution.py:327
  18.9 0.7 copy-start.4
  19.6 17.7 %copy-start.2 = (bf16[16,1536]{1,0:T(8,128)(2,1)}, bf16[16,1536]{1,0:T(8,128)(2,1)S(1)}, u32[]{:S(2)}) copy-start(bf16[16,1536]{1,0:T(8,128)(2,1)S(1)} %collective-permute-done.1.slot) | copy-start | bytes 147460
  20.5 15.2 %all-to-all-start = ((bf16[8,8,1536]{2,1,0:T(8,128)(2,1)}), bf16[8,8,1536]{2,1,0:T(8,128)(2,1)S(1)}, u32[]{:S(2)}, u32[]{:S(2)}) async-start(bf16[8,8,1536]{2,1,0:T(8,128)(2,1)} %shard_map.102), calls=%async_computation | async-start | bytes 393216 | tf_op jit(solution)/shard_map/all_to_all | solution.py:341
  25.2 10.3 %collective-permute-start.3 = (bf16[128,768]{1,0:T(8,128)(2,1)S(1)}, bf16[128,768]{1,0:T(8,128)(2,1)S(1)}, u32[]{:S(2)}, u32[]{:S(2)}) collective-permute-start(bf16[128,768]{1,0:T(8,128)(2,1)S(1)} %get-tuple-element.27), channel_id=1, source_target_pairs={{0,4},{4,0},{1,5},{5,1},{2,6},{6,2},{3,7},{7,3},{8,12},{12,8},{9,1... | collective-permute-start | bytes 589832 | tf_op jit(solution)/shard_map/ppermute | solution.py:342
  30.2 5.3 %collective-permute-start.2 = (bf16[16,768]{1,0:T(8,128)(2,1)S(1)}, bf16[16,768]{1,0:T(8,128)(2,1)S(1)}, u32[]{:S(2)}, u32[]{:S(2)}) collective-permute-start(bf16[16,768]{1,0:T(8,128)(2,1)S(1)} %get-tuple-element.33), channel_id=1, source_target_pairs={{0,4},{4,0},{1,5},{5,1},{2,6},{6,2},{3,7},{7,3},{8,12},{12,8},{9,1... | collective-permute-start | bytes 73736 | tf_op jit(solution)/shard_map/ppermute | solution.py:345
  35.5 8.9 %copy-start.3 = (bf16[16,768]{1,0:T(8,128)(2,1)}, bf16[16,768]{1,0:T(8,128)(2,1)S(1)}, u32[]{:S(2)}) copy-start(bf16[16,768]{1,0:T(8,128)(2,1)S(1)} %collective-permute-done.2.slot.slot_across) | copy-start | bytes 73732
  35.5 8.9 %copy-start.1 = (bf16[128,768]{1,0:T(8,128)(2,1)}, bf16[128,768]{1,0:T(8,128)(2,1)S(1)}, u32[]{:S(2)}) copy-start(bf16[128,768]{1,0:T(8,128)(2,1)S(1)} %collective-permute-done.3.across) | copy-start | bytes 589828
  35.8 8.1 %copy-start = (bf16[128,1536]{1,0:T(8,128)(2,1)}, bf16[128,1536]{1,0:T(8,128)(2,1)S(1)}, u32[]{:S(2)}) copy-start(bf16[128,1536]{1,0:T(8,128)(2,1)S(1)} %collective-permute-done.4.upstream.up_1) | copy-start | bytes 1179652
  37.3 5.9 %copy-start.7 = (bf16[1,128,1536]{2,1,0:T(8,128)(2,1)S(1)}, bf16[1,128,1536]{2,1,0:T(8,128)(2,1)}, u32[]{:S(2)}) copy-start(bf16[1,128,1536]{2,1,0:T(8,128)(2,1)} %param.8) | copy-start | bytes 1179652
  37.3 5.9 %copy-start.10 = (bf16[31,1536]{1,0:T(8,128)(2,1)S(1)}, bf16[31,1536]{1,0:T(8,128)(2,1)}, u32[]{:S(2)}) copy-start(bf16[31,1536]{1,0:T(8,128)(2,1)} %param.10) | copy-start | bytes 285700
  37.3 21.4 %all-to-all-start.1 = ((bf16[8,48,1664]{2,1,0:T(8,128)(2,1)}), bf16[8,48,1664]{2,1,0:T(8,128)(2,1)S(1)}, u32[]{:S(2)}, u32[]{:S(2)}) async-start(bf16[8,48,1664]{2,1,0:T(8,128)(2,1)} %shard_map.103), calls=%async_computation.1 | async-start | bytes 2555904 | tf_op jit(solution)/shard_map/all_to_all | solution.py:359
  43.2 1.7 %collective-permute-start.5 = (bf16[128,1536]{1,0:T(8,128)(2,1)S(1)}, bf16[128,1536]{1,0:T(8,128)(2,1)S(1)}, u32[]{:S(2)}, u32[]{:S(2)}) collective-permute-start(bf16[128,1536]{1,0:T(8,128)(2,1)S(1)} %bitcast.45), channel_id=1, source_target_pairs={{0,2},{2,0},{1,3},{3,1},{4,6},{6,4},{5,7},{7,5},{8,10},{10,8},{9,1... | collective-permute-start | bytes 1179656 | tf_op jit(solution)/shard_map/ppermute | solution.py:344
  43.9 2.2 %collective-permute-start.6 = (bf16[128,1536]{1,0:T(8,128)(2,1)S(1)}, bf16[128,1536]{1,0:T(8,128)(2,1)S(1)}, u32[]{:S(2)}, u32[]{:S(2)}) collective-permute-start(bf16[128,1536]{1,0:T(8,128)(2,1)S(1)} %collective-permute-done.4.upstream.up_1), channel_id=1, source_target_pairs={{0,2},{2,0},{1,3},{3,1},{4,6},{6,4},{5,7},{7,5},{8,10},{10,8},{9,1... | collective-permute-start | bytes 1179656 | tf_op jit(solution)/shard_map/ppermute | solution.py:346
  44.5 1.6 %collective-permute-start.7 = (bf16[2,144,384]{2,1,0:T(8,128)(2,1)S(1)}, bf16[2,144,384]{2,1,0:T(8,128)(2,1)S(1)}, u32[]{:S(2)}, u32[]{:S(2)}) collective-permute-start(bf16[2,144,384]{2,1,0:T(8,128)(2,1)S(1)} %fusion), channel_id=1, source_target_pairs={{0,2},{2,0},{1,3},{3,1},{4,6},{6,4},{5,7},{7,5},{8,10},{10,8},{9,1... | collective-permute-start | bytes 663560 | tf_op jit(solution)/shard_map/ppermute | solution.py:351
  44.9 1.2 copy-start.8
  46.1 0.7 copy-start.13
  46.1 0.8 copy-start.9
  46.9 13.2 %copy-start.5 = (s32[1,8]{1,0:T(1,128)S(1)}, s32[1,8]{1,0:T(1,128)}, u32[]{:S(2)}) copy-start(s32[1,8]{1,0:T(1,128)} %durations.1) | copy-start | bytes 100
  58.8 4.9 %copy-start.6 = (bf16[8,48,1664]{2,1,0:T(8,128)(2,1)}, bf16[8,48,1664]{2,1,0:T(8,128)(2,1)S(1)}, u32[]{:S(2)}) copy-start(bf16[8,48,1664]{2,1,0:T(8,128)(2,1)S(1)} %all-to-all-done.1.gathered) | copy-start | bytes 3833860
  60.2 23.1 %collective-permute-start.12 = (s32[16]{0:T(128)S(1)}, s32[16]{0:T(128)S(1)}, u32[]{:S(2)}, u32[]{:S(2)}) collective-permute-start(s32[16]{0:T(128)S(1)} %concatenate.72), channel_id=1, source_target_pairs={{0,2},{2,0},{4,6},{6,4},{1,3},{3,1},{5,7},{7,5},{8,10},{10,8},{12,... | collective-permute-start | bytes 200 | tf_op jit(solution)/shard_map/ppermute | solution.py:443
  60.3 23.0 %collective-permute-start.13 = (s32[16]{0:T(128)S(1)}, s32[16]{0:T(128)S(1)}, u32[]{:S(2)}, u32[]{:S(2)}) collective-permute-start(s32[16]{0:T(128)S(1)} %concatenate.72), channel_id=1, source_target_pairs={{0,4},{2,6},{4,0},{6,2},{1,5},{3,7},{5,1},{7,3},{8,12},{10,14},{12... | collective-permute-start | bytes 200 | tf_op jit(solution)/shard_map/ppermute | solution.py:443
  62.2 21.0 %collective-permute-start.14 = (s32[16]{0:T(128)S(1)}, s32[16]{0:T(128)S(1)}, u32[]{:S(2)}, u32[]{:S(2)}) collective-permute-start(s32[16]{0:T(128)S(1)} %concatenate.72), channel_id=1, source_target_pairs={{0,6},{2,4},{4,2},{6,0},{1,7},{3,5},{5,3},{7,1},{8,14},{10,12},{12... | collective-permute-start | bytes 200 | tf_op jit(solution)/shard_map/ppermute | solution.py:443
  70.1 15.0 %collective-permute-start.9 = (bf16[32,384]{1,0:T(8,128)(2,1)}, bf16[32,384]{1,0:T(8,128)(2,1)S(1)}, u32[]{:S(2)}, u32[]{:S(2)}) collective-permute-start(bf16[32,384]{1,0:T(8,128)(2,1)} %get-tuple-element.18), channel_id=1, source_target_pairs={{8,0},{16,8},{24,16},{32,24},{40,32},{48,40},{56,48},{64,56},{72,6... | collective-permute-start | bytes 73736 | tf_op jit(solution)/shard_map/ppermute | solution.py:434
  72.8 12.2 %collective-permute-start.8 = (bf16[16,384]{1,0:T(8,128)(2,1)}, bf16[16,384]{1,0:T(8,128)(2,1)S(1)}, u32[]{:S(2)}, u32[]{:S(2)}) collective-permute-start(bf16[16,384]{1,0:T(8,128)(2,1)} %get-tuple-element.17), channel_id=1, source_target_pairs={{0,8},{8,16},{16,24},{24,32},{32,40},{40,48},{48,56},{56,64},{64,7... | collective-permute-start | bytes 36872 | tf_op jit(solution)/shard_map/ppermute | solution.py:434
  78.0 21.0 %all-to-all-start.2 = ((bf16[8,48,1664]{2,1,0:T(8,128)(2,1)}), bf16[8,48,1664]{2,1,0:T(8,128)(2,1)S(1)}, u32[]{:S(2)}, u32[]{:S(2)}) async-start(bf16[8,48,1664]{2,1,0:T(8,128)(2,1)} %get-tuple-element.19), calls=%async_computation.2 | async-start | bytes 2555904 | tf_op jit(solution)/shard_map/all_to_all | solution.py:395
  85.0 0.6 copy-start.12
  85.1 0.6 copy-start.11
  91.7 1.6 %slice-start = ((bf16[528,384]{1,0:T(8,128)(2,1)}), bf16[512,384]{1,0:T(8,128)(2,1)S(1)}, s32[]{:S(2)}) async-start(bf16[528,384]{1,0:T(8,128)(2,1)} %shard_map.106), calls=%async_computation.5 | async-start | bytes 786432 | tf_op jit(solution)/shard_map/slice | solution.py:480
  93.1 1.5 %collective-permute-start.15 = (f32[2,8,384]{2,1,0:T(8,128)S(1)}, f32[2,8,384]{2,1,0:T(8,128)S(1)}, u32[]{:S(2)}, u32[]{:S(2)}) collective-permute-start(f32[2,8,384]{2,1,0:T(8,128)S(1)} %get-tuple-element.31), channel_id=1, source_target_pairs={{0,2},{2,0},{1,3},{3,1},{4,6},{6,4},{5,7},{7,5},{8,10},{10,8},{9,1... | collective-permute-start | bytes 73736 | tf_op jit(solution)/shard_map/ppermute | solution.py:461
  93.4 13.2 %collective-permute-start.10 = (bf16[2,128,384]{2,1,0:T(8,128)(2,1)S(1)}, bf16[2,128,384]{2,1,0:T(8,128)(2,1)S(1)}, u32[]{:S(2)}, u32[]{:S(2)}) collective-permute-start(bf16[2,128,384]{2,1,0:T(8,128)(2,1)S(1)} %get-tuple-element.25), channel_id=1, source_target_pairs={{0,2},{2,0},{1,3},{3,1},{4,6},{6,4},{5,7},{7,5},{8,10},{10,8},{9,1... | collective-permute-start | bytes 589832 | tf_op jit(solution)/shard_map/ppermute | solution.py:461
  94.5 14.6 %collective-permute-start.16 = (f32[8,768]{1,0:T(8,128)S(1)}, f32[8,768]{1,0:T(8,128)S(1)}, u32[]{:S(2)}, u32[]{:S(2)}) collective-permute-start(f32[8,768]{1,0:T(8,128)S(1)} %get-tuple-element.29), channel_id=1, source_target_pairs={{0,4},{4,0},{1,5},{5,1},{2,6},{6,2},{3,7},{7,3},{8,12},{12,8},{9,1... | collective-permute-start | bytes 73736 | tf_op jit(solution)/shard_map/ppermute | solution.py:470
  100.5 15.8 %all-to-all-start.3 = ((bf16[8,8,1536]{2,1,0:T(8,128)(2,1)}), bf16[8,8,1536]{2,1,0:T(8,128)(2,1)S(1)}, u32[]{:S(2)}, u32[]{:S(2)}) async-start(bf16[8,8,1536]{2,1,0:T(8,128)(2,1)} %shard_map.107), calls=%async_computation.3 | async-start | bytes 393216 | tf_op jit(solution)/shard_map/all_to_all | solution.py:403
  106.7 22.1 %collective-permute-start.11 = (bf16[128,768]{1,0:T(8,128)(2,1)S(1)}, bf16[128,768]{1,0:T(8,128)(2,1)S(1)}, u32[]{:S(2)}, u32[]{:S(2)}) collective-permute-start(bf16[128,768]{1,0:T(8,128)(2,1)S(1)} %get-tuple-element.23), channel_id=1, source_target_pairs={{0,4},{4,0},{1,5},{5,1},{2,6},{6,2},{3,7},{7,3},{8,12},{12,8},{9,1... | collective-permute-start | bytes 589832 | tf_op jit(solution)/shard_map/ppermute | solution.py:470
  117.5 21.2 %all-to-all-start.4 = ((f32[32,1,1536]{2,1,0:T(1,128)}), f32[32,1,1536]{2,1,0:T(1,128)S(1)}, u32[]{:S(2)}, u32[]{:S(2)}) async-start(f32[32,1,1536]{2,1,0:T(1,128)} %get-tuple-element.21), calls=%async_computation.4 | async-start | bytes 393216 | tf_op jit(solution)/shard_map/all_to_all | solution.py:411
  126.4 12.3 %collective-permute-start.17 = (f32[6,1536]{1,0:T(8,128)S(1)}, f32[6,1536]{1,0:T(8,128)S(1)}, u32[]{:S(2)}, u32[]{:S(2)}) collective-permute-start(f32[6,1536]{1,0:T(8,128)S(1)} %get-tuple-element.20), channel_id=1, source_target_pairs={{0,0},{64,2},{128,4},{192,6},{32,32},{96,34},{160,36},{224,38},{2,... | collective-permute-start | bytes 110600 | tf_op jit(solution)/shard_map/ppermute | solution.py:414

commit v4 on v3

v4 whole, which is shorter than its diff:
```python
import math

import jax
import jax.numpy as jnp
import numpy as np
from jax import lax
from jax.experimental import pallas as pl
from jax.experimental.pallas import tpu as pltpu
from jax.sharding import Mesh
from jax.sharding import PartitionSpec as P

AXES = ("z", "x", "yh", "core", "rep")
SIZES = (8, 4, 2, 2, 2)
GROUP = ("yh", "core")
PLANE = ("x", "rep")
QUARTERS = 4
BLOCK = 6
PLANE_ROWS = 48
EXTRA = 128
FRAMES, CHANNELS, TAPS = 512, 384, 31
EDGE_H, EDGE_U, SPILL = 48, 32, 16
LEFT_H, LEFT_U = 32, 16
WIDE = FRAMES + LEFT_U + EDGE_U
LONG = FRAMES + SPILL
SHARE = 128 + EDGE_H + 2 * EDGE_U
HANDED = 128 + EDGE_H + 4 * EDGE_U
BACK = 128 + SPILL + 16
SWAP = [(0, 1), (1, 0)]
BF = jnp.bfloat16
F32 = jnp.float32


def placement():
    out = np.zeros((CHANNELS, CHANNELS), np.float32)
    for zl in range(2):
        for x in range(4):
            for q in range(4):
                for rep in range(2):
                    for r in range(BLOCK):
                        row = (((zl * 4 + x) * 4 + q) * 2 + rep) * BLOCK + r
                        out[row, (x * 2 + rep) * PLANE_ROWS + (q * 2 + zl) * BLOCK + r] = 1
    return jnp.asarray(out, BF)


def turned():
    pairs = []
    for zq in range(4):
        for zl in range(2):
            for q in range(4):
                pairs.append(((zq * 2 + zl) * 4 + q, (q * 2 + zl) * 4 + zq))
    return pairs


def lanes(tile):
    return slice(tile * 128, tile * 128 + 128)


def begin(pairs, sems):
    copies = [pltpu.make_async_copy(a, b, sems.at[i]) for i, (a, b) in enumerate(pairs)]
    for copy in copies:
        copy.start()
    return copies


def finish(copies):
    for copy in copies:
        copy.wait()


def spread(weights, durations, slot, hidden, out, share, got, lengths, block, v_share, sems):
    yh = lax.axis_index("yh")
    other = pl.ds(pl.multiple_of((1 - yh) * 2 * CHANNELS, 128), 2 * CHANNELS)
    up = pl.ds(EDGE_H, EDGE_U)
    taken = begin(
        [
            (hidden.at[:, other], v_share.at[pl.ds(0, 128)]),
            (slot.at[pl.ds(0, EDGE_H), other], v_share.at[pl.ds(128, EDGE_H)]),
            (slot.at[up, pl.ds(0, 768)], v_share.at[pl.ds(128 + EDGE_H, EDGE_U)]),
            (slot.at[up, pl.ds(768, 768)], v_share.at[pl.ds(128 + EDGE_H + EDGE_U, EDGE_U)]),
        ],
        sems.at[pl.ds(9, 4)],
    )
    finish(begin([(weights, got), (durations, lengths)], sems))
    lane = lax.broadcasted_iota(jnp.int32, (1, 1536), 1)
    total = jnp.sum(lengths[...].astype(F32), axis=1, keepdims=True)
    note = jnp.where(lane == lax.axis_index("z"), jnp.broadcast_to(total, (1, 1536)), 0.0)
    rows = [got[...].astype(F32), note, jnp.zeros((1, 1536), F32)]
    block[...] = jnp.concatenate(rows, axis=0).astype(BF)
    finish(taken)
    given = begin([(v_share, share)], sems.at[pl.ds(9, 1)])
    finish(begin([(block, out.at[peer]) for peer in range(8)], sems))
    finish(given)


def pack(
    gathered, hidden, slot, across, upstream, plane, beside, rows, got, block, v_beside, sems
):
    yh, core = lax.axis_index("yh"), lax.axis_index("core")
    other = pl.ds(pl.multiple_of((yh * 2 + 1 - core) * CHANNELS, 128), CHANNELS)
    part = pl.ds(pl.multiple_of((1 - core) * CHANNELS, 128), CHANNELS)
    first = begin([(gathered, got)], sems)
    ups = 128 + EDGE_H
    moves = [
        (hidden.at[:, other], v_beside.at[0, pl.ds(0, 128)]),
        (slot.at[pl.ds(0, EDGE_H), other], v_beside.at[0, pl.ds(128, EDGE_H)]),
        (across.at[pl.ds(0, ups), part], v_beside.at[1, pl.ds(0, ups)]),
    ]
    for i in range(4):
        cut = pl.ds((i % 2) * CHANNELS, CHANNELS)
        row = pl.ds(ups + EDGE_U * i, EDGE_U)
        wide = pl.ds(i * CHANNELS, CHANNELS)
        moves.append((slot.at[pl.ds(EDGE_H, EDGE_U), wide], v_beside.at[0, row]))
        moves.append((across.at[pl.ds(ups + EDGE_U * (i // 2), EDGE_U), cut], v_beside.at[1, row]))
    moves = begin(moves, sems.at[pl.ds(1, 11)])
    finish(first)
    note = jnp.zeros((8, EXTRA), F32)
    for z in range(8):
        block_z = got[z].astype(F32)
        rows[BLOCK * z : BLOCK * z + BLOCK] = block_z[:BLOCK]
        note += jnp.broadcast_to(block_z[BLOCK : BLOCK + 1, :EXTRA], (8, EXTRA))
    block[:, :1536] = rows[...].astype(BF)
    block[:, 1536:] = jnp.concatenate([note] * (PLANE_ROWS // 8), axis=0).astype(BF)
    sent = begin([(block, plane.at[peer]) for peer in range(8)], sems.at[pl.ds(12, 8)])
    finish(moves)
    handed = begin([(v_beside, beside)], sems)
    finish(sent)
    finish(handed)


def group_grads(sources, grads):
    yh, core = lax.axis_index("yh"), lax.axis_index("core")
    places = [yh * 2 + core, 2 - 2 * yh + core, yh * 2 + 1 - core, 3 - 2 * yh - core]
    return [(source, grads.at[place]) for source, place in zip(sources, places)]


def convolve(
    own, slot, across, beside, up_0, up_1, up_2, up_3, kernel, order, slope, hidden, parts,
    grads, frames, weights, turn, v_slope, v_hidden, v_parts, active, sems,
):
    yh, core = lax.axis_index("yh"), lax.axis_index("core")
    part = pl.ds(pl.multiple_of(core * CHANNELS, 128), CHANNELS)
    mine = pl.ds(pl.multiple_of((yh * 2 + core) * CHANNELS, 128), CHANNELS)
    block = pl.ds(0, 128 + EDGE_H)
    needed = begin(
        [
            (own.at[:, mine], frames.at[yh * 2 + core, pl.ds(0, 128)]),
            (slot.at[pl.ds(0, EDGE_H), mine], frames.at[yh * 2 + core, pl.ds(128, EDGE_H)]),
            (across.at[block, part], frames.at[(1 - yh) * 2 + core]),
            (beside.at[0, block], frames.at[yh * 2 + 1 - core]),
            (beside.at[1, block], frames.at[(1 - yh) * 2 + 1 - core]),
            (kernel, weights),
        ],
        sems,
    )
    later = begin(
        group_grads((up_0, up_1, up_2, up_3), grads) + [(order, turn)], sems.at[pl.ds(8, 5)]
    )
    finish(needed)
    v_hidden[:LEFT_H] = frames[0, 128 + EDGE_H - LEFT_H :].astype(F32)
    for b in range(4):
        v_hidden[LEFT_H + 128 * b : LEFT_H + 128 * b + 128] = frames[b, :128].astype(F32)
    v_hidden[LEFT_H + FRAMES :] = frames[3, 128:].astype(F32)
    rows = 112
    for tile in range(CHANNELS // 128):

        def chunk(c, _, tile=tile):
            base = pl.multiple_of(c * rows, 8)
            total = jnp.zeros((rows, 128), F32)
            window = v_hidden[pl.ds(base, rows + 32), lanes(tile)]
            for b in range(8):
                slab = window[b : b + rows + 24]
                for a in range(4):
                    k = 8 * a + b - 1
                    if 0 <= k < TAPS:
                        total += weights[k : k + 1, lanes(tile)] * slab[8 * a : 8 * a + rows]
            sig = jax.nn.sigmoid(total)
            v_slope[pl.ds(base, rows), lanes(tile)] = sig * (1.0 + total * (1.0 - sig))
            active[pl.ds(base, rows), lanes(tile)] = total * sig
            return 0

        lax.fori_loop(0, WIDE // rows, chunk, 0)
    out = begin([(v_slope, slope), (v_hidden, hidden)], sems)
    finish(later)
    acts = active[LEFT_U : LEFT_U + FRAMES].astype(BF)
    acts = jnp.dot(acts, turn[...], preferred_element_type=F32).astype(BF)
    product = lax.dot_general(
        acts,
        grads[...].reshape(FRAMES, 1536),
        (((0,), (0,)), ((), ())),
        preferred_element_type=F32,
    ).astype(BF)
    for s in range(8):
        v_parts[s] = product[PLANE_ROWS * s : PLANE_ROWS * (s + 1)]
    finish(begin([(v_parts, parts.at[:, :, pl.ds(0, 1536)])], sems.at[pl.ds(2, 1)]))
    finish(out)


def backward(
    gathered, spread, up_0, up_1, up_2, up_3, slope, hidden, parts,
    grad_conv, projection, message,
    got, turn, grads, v_slope, v_hidden, v_grad, v_grad_f, v_taps, sums, v_weights, sems,
):
    needed = begin(
        [(gathered.at[s, :, pl.ds(0, 1536)], got.at[s]) for s in range(8)]
        + [(spread, turn)],
        sems,
    )
    later = begin(group_grads((up_0, up_1, up_2, up_3), grads), sems.at[pl.ds(9, 4)])
    last = begin(
        [(slope.at[pl.ds(LEFT_U, FRAMES)], v_slope), (hidden, v_hidden)], sems.at[pl.ds(13, 2)]
    )
    finish(needed)
    weights = jnp.dot(
        turn[...], got[...].reshape(CHANNELS, 1536), preferred_element_type=F32
    ).astype(BF)
    v_weights[...] = weights
    finish(later)
    value = lax.dot_general(
        grads[...].reshape(FRAMES, 1536),
        weights,
        (((1,), (1,)), ((), ())),
        preferred_element_type=F32,
    )
    finish(last)
    value = (value * v_slope[...]).astype(BF)
    v_grad[...] = value
    v_grad_f[...] = value.astype(F32)
    out = begin([(v_grad, grad_conv), (v_weights, projection)], sems)
    span = 128
    sums[...] = jnp.zeros_like(sums)
    for tile in range(CHANNELS // 128):

        def piece(c, _, tile=tile):
            base = pl.multiple_of(c * span, 8)
            terms = v_grad_f[pl.ds(base, span), lanes(tile)]
            window = v_hidden[pl.ds(base + LEFT_U, span + 32), lanes(tile)]
            for b in range(8):
                slab = window[b : b + span + 24]
                for a in range(4):
                    k = 8 * a + b - 1
                    if 0 <= k < TAPS:
                        sums[k, :, lanes(tile)] += jnp.sum(
                            (terms * slab[8 * a : 8 * a + span]).reshape(span // 8, 8, 128),
                            axis=0,
                        )
            return 0

        lax.fori_loop(0, FRAMES // span, piece, 0)
    for s in range(8):
        rows = [
            jnp.sum(sums[4 * s + t, :, lanes(tile)], axis=0, keepdims=True)
            for t in range(4)
            for tile in range(CHANNELS // 128)
        ]
        rows = jnp.concatenate(rows, axis=0)
        high = rows.astype(BF).astype(F32)
        rows = [high, rows - high, jnp.zeros((PLANE_ROWS - 24, 128), F32)]
        v_taps[s] = jnp.concatenate(rows, axis=0).astype(BF)
    finish(begin([(v_taps, message.at[:, :, pl.ds(1536, EXTRA)])], sems.at[pl.ds(3, 1)]))
    finish(out)


def transposed(
    grad_conv, projection, slope, slot, across, beside, kernel, gathered, lengths,
    kept, given, v_grad, v_weights, v_slope, ups, weights, notes, v_lengths, wide, total_f,
    v_kept, v_given, sems,
):
    yh, core = lax.axis_index("yh"), lax.axis_index("core")
    far = 128 + EDGE_H
    edges = [(slot.at[pl.ds(EDGE_H, EDGE_U)], ups.at[yh * 2 + core])]
    for i in range(2):
        edges.append(
            (
                across.at[pl.ds(far + EDGE_U * i, EDGE_U)],
                ups.at[(1 - yh) * 2 + core, :, pl.ds(768 * i, 768)],
            )
        )
    for i in range(4):
        row, cut = pl.ds(far + EDGE_U * i, EDGE_U), pl.ds(CHANNELS * i, CHANNELS)
        edges.append((beside.at[0, row], ups.at[yh * 2 + 1 - core, :, cut]))
        edges.append((beside.at[1, row], ups.at[(1 - yh) * 2 + 1 - core, :, cut]))
    edges += [
        (projection, v_weights),
        (slope.at[pl.ds(0, LEFT_U)], v_slope.at[pl.ds(0, LEFT_U)]),
        (slope.at[pl.ds(LEFT_U + FRAMES, EDGE_U)], v_slope.at[pl.ds(LEFT_U, EDGE_U)]),
        (grad_conv, v_grad),
        (kernel, weights),
        (gathered.at[:, pl.ds(0, 16), pl.ds(1536, EXTRA)], notes),
        (lengths, v_lengths),
    ]
    finish(begin(edges, sems))
    rows = jnp.concatenate([ups[0, EDGE_U - LEFT_U :], ups[3]], axis=0)
    value = lax.dot_general(
        rows, v_weights[...], (((1,), (1,)), ((), ())), preferred_element_type=F32
    )
    value = (value * v_slope[...]).astype(BF).astype(F32)
    wide[:LEFT_U] = value[:LEFT_U]
    wide[LEFT_U : LEFT_U + FRAMES] = v_grad[...].astype(F32)
    wide[LEFT_U + FRAMES :] = value[LEFT_U:]
    rows = 88
    for tile in range(CHANNELS // 128):

        def chunk(c, _, tile=tile):
            base = pl.multiple_of(c * rows, 8)
            total = jnp.zeros((rows, 128), F32)
            window = wide[pl.ds(base, rows + 32), lanes(tile)]
            for b in range(8):
                slab = window[b : b + rows + 24]
                for a in range(4):
                    k = TAPS - 8 * a - b
                    if 0 <= k < TAPS:
                        total += weights[k : k + 1, lanes(tile)] * slab[8 * a : 8 * a + rows]
            total_f[pl.ds(base, rows), lanes(tile)] = total
            return 0

        lax.fori_loop(0, LONG // rows, chunk, 0)
    place = lax.axis_index("z") * 4 + lax.axis_index("x")
    lane = lax.broadcasted_iota(jnp.int32, (8, EXTRA), 1)
    before = jnp.zeros((8, EXTRA), F32)
    for peer in range(8):
        earlier = (lane * 4 + peer // 2 < place) & (lax.axis_index("rep") == peer % 2) & (lane < 8)
        before += jnp.where(earlier, notes[peer, :8].astype(F32), 0.0)
    before = jnp.broadcast_to(jnp.sum(before, axis=1, keepdims=True), (8, CHANNELS))
    high = before.astype(BF).astype(F32)
    block = jnp.broadcast_to(jnp.sum(v_lengths[...], axis=1, keepdims=True), (8, CHANNELS))
    note = jnp.concatenate([high[:1], before[:1] - high[:1], block[:1], block[:5], block], axis=0)
    for row in range(2):
        for out, side in ((v_kept, core), (v_given, 1 - core)):
            begin_row = pl.multiple_of((row * 2 + side) * 128, 128)
            out[row, : 128 + SPILL] = total_f[pl.ds(begin_row, 128 + SPILL)].astype(BF)
            out[row, 128 + SPILL :] = note.astype(BF)
    finish(begin([(v_kept, kept), (v_given, given)], sems))


def settle(kept, got, far, lengths, frame_grad, gloss, frames, notes, v_lengths, v_gloss, sems):
    yh, core = lax.axis_index("yh"), lax.axis_index("core")
    sources = [(kept.at[yh], yh, core), (got.at[yh], yh, 1 - core)]
    sources += [(far.at[0], 1 - yh, core), (far.at[1], 1 - yh, 1 - core)]
    moves = [(lengths, v_lengths)]
    for source, a, b in sources:
        cut = pl.ds(pl.multiple_of((a * 2 + b) * CHANNELS, 128), CHANNELS)
        moves.append((source.at[pl.ds(0, 128 + SPILL)], frames.at[:, cut]))
        moves.append((source.at[pl.ds(128 + SPILL, 16)], notes.at[a * 2 + b]))
    finish(begin(moves, sems))
    out = begin([(frames.at[pl.ds(0, 128)], frame_grad)], sems)
    mine = yh * 2 + core
    place = lax.axis_index("z") * 4 + lax.axis_index("x")
    start = jnp.zeros((1, EXTRA), F32)
    for q in range(4):
        note = notes[q, :, :EXTRA].astype(F32)
        start += note[0:1] + note[1:2] + jnp.where(q < mine, note[2:3], 0.0)
    start = start[:, :1] - (place * FRAMES + mine * 128).astype(F32)
    gloss_id = lax.broadcasted_iota(jnp.int32, (8, EXTRA), 0)
    lane = lax.broadcasted_iota(jnp.int32, (8, EXTRA), 1)
    length = v_lengths[...]
    first = jnp.sum(jnp.where(lane < gloss_id, length, 0.0), axis=1, keepdims=True) + start
    last = first + jnp.sum(jnp.where(lane == gloss_id, length, 0.0), axis=1, keepdims=True)
    at = lax.broadcasted_iota(jnp.int32, (8, 128 + SPILL), 1).astype(F32)
    covers = jnp.where((at >= first) & (at < last), 1.0, 0.0).astype(BF)
    v_gloss[...] = jnp.dot(covers, frames[...], preferred_element_type=F32)
    finish(begin([(v_gloss, gloss)], sems.at[pl.ds(1, 1)]))
    finish(out)


def pack_z(parts, out, v_parts, v_sum, v_out, sems):
    finish(begin([(parts, v_parts)], sems))
    v_sum[...] = jnp.sum(v_parts[...].astype(F32), axis=0)
    taps = v_sum[:12, 1536:] + v_sum[12:24, 1536:]
    taps = jnp.concatenate([taps[j : j + 1] for j in range(12)], axis=1)
    high = taps.astype(BF).astype(F32)
    for z in range(8):
        rows = [v_sum[BLOCK * z : BLOCK * z + BLOCK, :1536], high, taps - high]
        v_out[z] = jnp.concatenate(rows, axis=0).astype(BF)
    finish(begin([(v_out, out)], sems))


def unpack_z(got, weights, taps, v_got, v_weights, v_taps, sems):
    finish(begin([(got, v_got)], sems))
    total = v_got[0].astype(F32)
    for z in range(1, 8):
        total += v_got[z].astype(F32)
    total = total * (1.0 / math.sqrt(2 * 16384))
    v_weights[...] = total[:BLOCK]
    for peer in range(32):
        v_taps[peer] = total[6:7] + total[7:8]
    finish(begin([(v_taps, taps), (v_weights, weights)], sems))


def arrange(got, out, v_got, v_out, sems):
    finish(begin([(got, v_got)], sems))
    for x in range(4):
        for q in range(4):
            for rep in range(2):
                for t in range(4):
                    k = (x * 2 + rep) * 4 + t
                    if k < TAPS:
                        v_out[k : k + 1, q * CHANNELS : q * CHANNELS + CHANNELS] = v_got[
                            (x * 4 + q) * 2 + rep, :, t * CHANNELS : t * CHANNELS + CHANNELS
                        ]
    finish(begin([(v_out, out)], sems))


def call(kernel, outs, scratch, flops, *args, alias=None):
    shapes = [jax.ShapeDtypeStruct(shape, dtype) for shape, dtype in outs]
    size = sum(math.prod(s.shape) * s.dtype.itemsize for s in list(args) + shapes)
    return pl.pallas_call(
        kernel,
        out_shape=shapes,
        in_specs=[pl.BlockSpec(memory_space=pltpu.HBM)] * len(args),
        out_specs=[pl.BlockSpec(memory_space=pltpu.HBM)] * len(shapes),
        scratch_shapes=[pltpu.VMEM(shape, dtype) for shape, dtype in scratch]
        + [pltpu.SemaphoreType.DMA((20,))],
        input_output_aliases=alias or {},
        compiler_params=pltpu.CompilerParams(vmem_limit_bytes=(56 if flops else 16) * 2**20),
        cost_estimate=pl.CostEstimate(
            flops=flops, bytes_accessed=size, transcendentals=0
        ),
    )(*args)


def body(hidden_in, upstream, out_weight, conv_kernel, durations):
    yh, core = lax.axis_index("yh"), lax.axis_index("core")
    quarter = yh * 2 + core
    hidden, grads = hidden_in[0], upstream[0]
    lengths = jnp.broadcast_to(
        jnp.pad(durations.astype(F32), ((0, 0), (0, EXTRA - durations.shape[1]))), (8, EXTRA)
    )

    ends = [(4 * i + 3, 4 * i + 4) for i in range(31)]
    slot = lax.ppermute(
        jnp.where(
            quarter == 0,
            jnp.concatenate((hidden[:EDGE_H], grads[:EDGE_U])),
            jnp.concatenate((hidden[128 - EDGE_H :], grads[128 - EDGE_U :])),
        ),
        ("z", "x", "yh", "core"),
        ends + [(b, a) for a, b in ends],
    )
    rows = lax.ppermute(out_weight, ("z", "yh", "core"), turned())
    rows, share = call(
        spread,
        [((8, 8, 1536), BF), ((SHARE, 768), BF)],
        [((BLOCK, 1536), BF), ((1, 8), jnp.int32), ((8, 1536), BF), ((SHARE, 768), BF)],
        0,
        rows, durations, slot, hidden,
    )
    rows = lax.all_to_all(rows, "z", 0, 0, tiled=True)
    across = lax.ppermute(share, "yh", SWAP)
    up_1 = lax.ppermute(grads, "yh", SWAP)
    up_2 = lax.ppermute(grads, "core", SWAP)
    up_3 = lax.ppermute(up_1, "core", SWAP)
    ups = (grads, up_1, up_2, up_3)
    plane, beside = call(
        pack,
        [((8, PLANE_ROWS, 1536 + EXTRA), BF), ((2, HANDED, CHANNELS), BF)],
        [
            ((PLANE_ROWS, 1536), F32), ((8, 8, 1536), BF), ((PLANE_ROWS, 1536 + EXTRA), BF),
            ((2, HANDED, CHANNELS), BF),
        ],
        0,
        rows, hidden, slot, across, up_1,
    )
    rows = lax.all_to_all(plane, PLANE, 0, 0, tiled=True)
    beside = lax.ppermute(beside, "core", SWAP)
    kernel_f = lax.dynamic_slice_in_dim(
        jnp.pad(conv_kernel, ((0, 1), (0, 0))), quarter * CHANNELS, CHANNELS, 1
    ).astype(F32)
    square = ((CHANNELS, CHANNELS), BF)
    frames_f = ((FRAMES, CHANNELS), F32)
    wide_f = ((LEFT_H + FRAMES + EDGE_H, CHANNELS), F32)
    slope_f = ((WIDE, CHANNELS), F32)
    all_grads = ((4, 128, 1536), BF)
    sent = ((8, PLANE_ROWS, 1536), BF)
    message = ((8, PLANE_ROWS, 1536 + EXTRA), BF)
    kernel_shape = ((TAPS + 1, CHANNELS), F32)
    slope, hidden_f, parts = call(
        convolve,
        [slope_f, wide_f, message],
        [
            all_grads, ((4, 128 + EDGE_H, CHANNELS), BF), kernel_shape, square, slope_f, wide_f,
            sent, slope_f,
        ],
        800_000_000,
        hidden, slot, across, beside, *ups, kernel_f, placement(),
    )
    grad_conv, projection, parts = call(
        backward,
        [
            ((FRAMES, CHANNELS), BF), ((CHANNELS, 1536), BF), message,
        ],
        [
            sent, square, all_grads, frames_f, wide_f, ((FRAMES, CHANNELS), BF), frames_f,
            ((8, PLANE_ROWS, EXTRA), BF), ((TAPS + 1, 8, CHANNELS), F32),
            ((CHANNELS, 1536), BF),
        ],
        1_400_000_000,
        rows, placement(), *ups, slope, hidden_f, parts,
        alias={8: 2},
    )

    parts = lax.all_to_all(parts, PLANE, 0, 0, tiled=True)
    [parts] = call(
        pack_z,
        [((8, 8, 1536), BF)],
        [message, ((PLANE_ROWS, 1536 + EXTRA), F32), ((8, 8, 1536), BF)],
        0,
        parts,
    )
    parts = lax.all_to_all(parts, "z", 0, 0, tiled=True)
    weight_grad, taps_all = call(
        unpack_z,
        [((BLOCK, 1536), F32), ((32, 1, 1536), F32)],
        [((8, 8, 1536), BF), ((BLOCK, 1536), F32), ((32, 1, 1536), F32)],
        0,
        parts,
    )
    taps_all = lax.all_to_all(
        taps_all, ("x", "yh", "core", "rep"), 0, 0, tiled=True
    )
    weight_grad = lax.ppermute(
        weight_grad, ("z", "yh", "core"), [(b, a) for a, b in turned()]
    )
    [kernel_grad] = call(
        arrange,
        [((TAPS, 1536), F32)],
        [((32, 1, 1536), F32), ((TAPS, 1536), F32)],
        0,
        taps_all,
    )

    back = ((2, BACK, CHANNELS), BF)
    kept, given = call(
        transposed,
        [back, back],
        [
            ((FRAMES, CHANNELS), BF), ((CHANNELS, 1536), BF), ((LEFT_U + EDGE_U, CHANNELS), F32),
            ((4, EDGE_U, 1536), BF), kernel_shape, ((8, 16, EXTRA), BF), ((8, EXTRA), F32),
            slope_f, ((LONG, CHANNELS), F32), back, back,
        ],
        200_000_000,
        grad_conv, projection, slope, slot, across, beside, kernel_f, rows, lengths,
    )
    got = lax.ppermute(given, "core", SWAP)
    far = jnp.stack(
        [lax.dynamic_index_in_dim(part, 1 - yh, 0, False) for part in (kept, got)]
    )
    far = lax.ppermute(far, "yh", SWAP)
    frame_grad, gloss = call(
        settle,
        [((128, 1536), BF), ((8, 1536), F32)],
        [
            ((128 + SPILL, 1536), BF), ((4, 16, CHANNELS), BF), ((8, EXTRA), F32),
            ((8, 1536), F32),
        ],
        0,
        kept, got, far, lengths,
    )
    return (frame_grad[None], gloss[None], weight_grad, kernel_grad)


def solution(mesh):
    fine = Mesh(mesh.devices.reshape(SIZES), AXES)
    seq = ("z", "x", "yh", "core")
    rows = P(seq + ("rep",), None)
    in_specs = (P("rep", seq, None), P("rep", seq, None), rows, P(), P("rep", seq))
    out_specs = (P("rep", seq, None), P("rep", seq, None), rows, P())
    return jax.shard_map(
        body, mesh=fine, in_specs=in_specs, out_specs=out_specs, check_vma=False
    )
```

time: 141 us -> 127 us (0.901)
  the two profiles are of different devices: /device:TPU:22 before, /device:TPU:16 now
where the time goes in v4:
time: 127 us; the launch traced here: 126 us
  starting transfers between devices  45.5 us (36%)
  waiting for transfers between devices  44.6 us (35%)
  Pallas kernels  29.7 us (23%)
  local copies, waits for them, and re-layouts  4.85 us (4%)
    pallas_call x9, Pallas kernels, call(): pl.pallas_call(kernel, out_shape=shapes, in_specs=[pl.BlockSpec(memory_sp...  29.7 us
    ppermute x1, starting transfers between devices, body(): rows = lax.ppermute(out_weight, ('z', 'yh', 'core'), turned())  12.4 us
    all_to_all x1, starting transfers between devices, body(): rows = lax.all_to_all(rows, 'z', 0, 0, tiled=True)  10.5 us
    all_to_all x1, waiting for transfers between devices, body(): rows = lax.all_to_all(rows, 'z', 0, 0, tiled=True)  9.76 us
    all_to_all x1, waiting for transfers between devices, body(): parts = lax.all_to_all(parts, 'z', 0, 0, tiled=True)  9.57 us
    all_to_all x1, waiting for transfers between devices, body(): parts = lax.all_to_all(parts, PLANE, 0, 0, tiled=True)  8.94 us
    ppermute x1, waiting for transfers between devices, body(): lax.ppermute(weight_grad, ('z', 'yh', 'core'), [(b, a) for a, b in turned...  8.84 us
    all_to_all x1, starting transfers between devices, body(): lax.all_to_all(taps_all, ('x', 'yh', 'core', 'rep'), 0, 0, tiled=True)  4.97 us
  transfers between devices with their start and end apart: 15, of which 8 were waited for; matrix products, arithmetic and copies ran while one was open for 1% of the time, Pallas kernels for 16%

profile of v4, /device:TPU:16, one launch (start us, length us, event | category | flops | bytes accessed | tf_op | source)
XLA Modules:
  0.0 126.5 jit_solution(14357629659311460817)
XLA Ops:
  0.6 0.0 copy-start
  0.6 0.0 copy-start.7
  0.7 0.0 copy-start.12
  0.7 0.0 copy-start.6
  0.7 1.1 slice_bitcast_fusion
  1.8 1.0 slice_bitcast_fusion.2
  2.7 0.1 maximum_select_fusion
  2.8 0.7 collective-permute-start.1
  3.5 0.0 copy-done.7
  3.5 2.2 %collective-permute-start.3 = (bf16[128,1536]{1,0:T(8,128)(2,1)S(1)}, bf16[128,1536]{1,0:T(8,128)(2,1)S(1)}, u32[]{:S(2)}, u32[]{:S(2)}) collective-permute-start(bf16[128,1536]{1,0:T(8,128)(2,1)S(1)} %bitcast.19), channel_id=1, source_target_pairs={{0,4},{4,0},{1,5},{5,1},{2,6},{6,2},{3,7},{7,3},{8,12},{12,8},{9,1... | collective-permute-start | bytes 1179656 | tf_op jit(solution)/shard_map/ppermute | solution.py:449
  5.6 0.0 copy-done.12
  5.6 12.4 %collective-permute-start = (bf16[6,1536]{1,0:T(8,128)(2,1)S(1)}, bf16[6,1536]{1,0:T(8,128)(2,1)S(1)}, u32[]{:S(2)}, u32[]{:S(2)}) collective-permute-start(bf16[6,1536]{1,0:T(8,128)(2,1)S(1)} %copy-done.12), channel_id=1, source_target_pairs={{0,0},{2,64},{4,128},{6,192},{32,32},{34,96},{36,160},{38,224},{64... | collective-permute-start | bytes 55304 | tf_op jit(solution)/shard_map/ppermute | solution.py:439
  18.1 1.9 %collective-permute-done.weights = bf16[6,1536]{1,0:T(8,128)(2,1)S(1)} collective-permute-done((bf16[6,1536]{1,0:T(8,128)(2,1)S(1)}, bf16[6,1536]{1,0:T(8,128)(2,1)S(1)}, u32[]{:S(2)}, u32[]{:S(2)}) %collective-permute-start) | collective-permute-done | bytes 18464 | tf_op jit(solution)/shard_map/ppermute | solution.py:439
  20.0 0.0 collective-permute-done.1.slot
  20.0 0.0 copy-done
  20.0 0.0 copy-done.6
  20.0 1.2 shard_map.102
  21.3 0.1 collective-permute-start.2
  21.4 10.5 %all-to-all-start = ((bf16[8,8,1536]{2,1,0:T(8,128)(2,1)}), bf16[8,8,1536]{2,1,0:T(8,128)(2,1)S(1)}, u32[]{:S(2)}, u32[]{:S(2)}) async-start(bf16[8,8,1536]{2,1,0:T(8,128)(2,1)} %get-tuple-element.20), calls=%async_computation | async-start | bytes 393216 | tf_op jit(solution)/shard_map/all_to_all | solution.py:447
  31.8 0.0 collective-permute-done.3.upstream.up_1
  31.8 0.0 copy-start.2
  31.9 9.8 %all-to-all-done.gathered = bf16[8,8,1536]{2,1,0:T(8,128)(2,1)S(1)} async-done(((bf16[8,8,1536]{2,1,0:T(8,128)(2,1)}), bf16[8,8,1536]{2,1,0:T(8,128)(2,1)S(1)}, u32[]{:S(2)}, u32[]{:S(2)}) %all-to-all-start) | async-done | bytes 196640 | tf_op jit(solution)/shard_map/all_to_all | solution.py:447
  41.6 0.0 collective-permute-done.2.across
  41.6 1.6 %shard_map.103 = (bf16[8,48,1664]{2,1,0:T(8,128)(2,1)}, bf16[2,304,384]{2,1,0:T(8,128)(2,1)S(1)}) custom-call(bf16[8,8,1536]{2,1,0:T(8,128)(2,1)S(1)} %all-to-all-done.gathered, bf16[128,1536]{1,0:T(8,128)(2,1)S(1)} %bitcast.16, bf16[80,1536]{1,0:T(8,128)(2,1)S(1)} %collective-permute-done.1.slot, bf16[240,768]{1,0:T(8,128)(2,1)S(1)} %collective-permute-done.2.across, ...), custom_call_target="tpu_custom_call" | custom-call | bytes 3342336 | tf_op jit(solution)/shard_map/pallas_call | solution.py:406
  43.3 0.0 copy-done.1
  43.3 0.0 copy-start.11
  43.3 0.0 copy-done.3
  43.3 4.4 %all-to-all-start.1 = ((bf16[8,48,1664]{2,1,0:T(8,128)(2,1)}), bf16[8,48,1664]{2,1,0:T(8,128)(2,1)}, u32[]{:S(2)}, u32[]{:S(2)}) async-start(bf16[8,48,1664]{2,1,0:T(8,128)(2,1)} %get-tuple-element.22), calls=%async_computation.1 | async-start | bytes 2555904 | tf_op jit(solution)/shard_map/all_to_all | solution.py:463
  47.7 0.1 collective-permute-start.6
  47.8 0.5 collective-permute-start.4
  48.3 0.0 copy-done.2
  48.3 0.1 collective-permute-start.5
  48.4 0.0 copy-done.11
  48.4 0.6 fusion.kernel
  49.0 1.1 collective-permute-done.4.up_2
  50.2 0.6 collective-permute-done.5.up_3
  50.8 0.0 collective-permute-done.6.beside
  50.8 0.2 copy-done.9
  50.9 0.6 copy-done.10
  51.5 0.8 copy-done.8
  52.3 8.1 %shard_map.104 = (f32[560,384]{1,0:T(8,128)}, f32[592,384]{1,0:T(8,128)}, bf16[8,48,1664]{2,1,0:T(8,128)(2,1)}) custom-call(bf16[128,1536]{1,0:T(8,128)(2,1)} %bitcast.14, bf16[80,1536]{1,0:T(8,128)(2,1)} %copy-done.1, bf16[240,768]{1,0:T(8,128)(2,1)} %copy-done.3, bf16[2,304,384]{2,1,0:T(8,128)(2,1)} %copy-done.8, bf16[128,1536]{1,0:T(8,128)(2,1)} %bitcast.17, ...), custom_call_target="tpu_custom_call" | custom-call | flops 800000000 | bytes 6438912 | tf_op jit(solution)/shard_map/pallas_call | solution.py:406
  60.4 3.9 %all-to-all-done.1.gathered = bf16[8,48,1664]{2,1,0:T(8,128)(2,1)} async-done(((bf16[8,48,1664]{2,1,0:T(8,128)(2,1)}), bf16[8,48,1664]{2,1,0:T(8,128)(2,1)}, u32[]{:S(2)}, u32[]{:S(2)}) %all-to-all-start.1) | async-done | bytes 1277984 | tf_op jit(solution)/shard_map/all_to_all | solution.py:463
  64.3 6.5 %shard_map.105 = (bf16[512,384]{1,0:T(8,128)(2,1)}, bf16[384,1536]{1,0:T(8,128)(2,1)}, bf16[8,48,1664]{2,1,0:T(8,128)(2,1)}) custom-call(bf16[8,48,1664]{2,1,0:T(8,128)(2,1)} %all-to-all-done.1.gathered, bf16[384,384]{1,0:T(8,128)(2,1)} %constant.32.clone.order.spread, bf16[128,1536]{1,0:T(8,128)(2,1)} %bitcast.18, ...), custom_call_target="tpu_custom_call", output_to_operand_aliasing={{2}: (8, {})} | custom-call | flops 1400000000 | bytes 9043968 | tf_op jit(solution)/shard_map/pallas_call | solution.py:406
  70.8 3.6 %all-to-all-start.2 = ((bf16[8,48,1664]{2,1,0:T(8,128)(2,1)}), bf16[8,48,1664]{2,1,0:T(8,128)(2,1)S(1)}, u32[]{:S(2)}, u32[]{:S(2)}) async-start(bf16[8,48,1664]{2,1,0:T(8,128)(2,1)} %get-tuple-element.33), calls=%async_computation.2 | async-start | bytes 2555904 | tf_op jit(solution)/shard_map/all_to_all | solution.py:501
  74.4 0.6 broadcast_in_dim.14.lengths
  75.0 7.2 %shard_map.106 = (bf16[2,160,384]{2,1,0:T(8,128)(2,1)}, bf16[2,160,384]{2,1,0:T(8,128)(2,1)}) custom-call(bf16[512,384]{1,0:T(8,128)(2,1)} %get-tuple-element.27.grad_conv, bf16[384,1536]{1,0:T(8,128)(2,1)} %get-tuple-element.28.projection, f32[560,384]{1,0:T(8,128)} %get-tuple-element.24.slope, bf16[80,1536]{1,0:T(8,128)(2,1)} %copy-done.1, ...), custom_call_target="tpu_custom_call" | custom-call | flops 200000000 | bytes 5337088 | tf_op jit(solution)/shard_map/pallas_call | solution.py:406
  82.2 0.0 copy-start.4
  82.2 0.1 collective-permute-start.7
  82.3 8.9 %all-to-all-done.2.parts = bf16[8,48,1664]{2,1,0:T(8,128)(2,1)S(1)} async-done(((bf16[8,48,1664]{2,1,0:T(8,128)(2,1)}), bf16[8,48,1664]{2,1,0:T(8,128)(2,1)S(1)}, u32[]{:S(2)}, u32[]{:S(2)}) %all-to-all-start.2) | async-done | bytes 1277984 | tf_op jit(solution)/shard_map/all_to_all | solution.py:501
  91.2 1.5 %shard_map.108 = bf16[8,8,1536]{2,1,0:T(8,128)(2,1)} custom-call(bf16[8,48,1664]{2,1,0:T(8,128)(2,1)S(1)} %all-to-all-done.2.parts), custom_call_target="tpu_custom_call" | custom-call | bytes 1474560 | tf_op jit(solution)/shard_map/pallas_call | solution.py:406
  92.8 0.0 copy-start.5
  92.8 3.7 %all-to-all-start.3 = ((bf16[8,8,1536]{2,1,0:T(8,128)(2,1)}), bf16[8,8,1536]{2,1,0:T(8,128)(2,1)S(1)}, u32[]{:S(2)}, u32[]{:S(2)}) async-start(bf16[8,8,1536]{2,1,0:T(8,128)(2,1)} %shard_map.108), calls=%async_computation.3 | async-start | bytes 393216 | tf_op jit(solution)/shard_map/all_to_all | solution.py:509
  96.5 0.0 collective-permute-done.7.got
  96.6 0.1 collective-permute-start.8
  96.7 9.6 %all-to-all-done.3.got = bf16[8,8,1536]{2,1,0:T(8,128)(2,1)S(1)} async-done(((bf16[8,8,1536]{2,1,0:T(8,128)(2,1)}), bf16[8,8,1536]{2,1,0:T(8,128)(2,1)S(1)}, u32[]{:S(2)}, u32[]{:S(2)}) %all-to-all-start.3) | async-done | bytes 196640 | tf_op jit(solution)/shard_map/all_to_all | solution.py:509
  106.3 1.1 shard_map.109
  107.4 5.0 %all-to-all-start.4 = ((f32[32,1,1536]{2,1,0:T(1,128)}), f32[32,1,1536]{2,1,0:T(1,128)S(1)}, u32[]{:S(2)}, u32[]{:S(2)}) async-start(f32[32,1,1536]{2,1,0:T(1,128)} %get-tuple-element.35), calls=%async_computation.4 | async-start | bytes 393216 | tf_op jit(solution)/shard_map/all_to_all | solution.py:517
  112.4 2.1 %collective-permute-start.9 = (f32[6,1536]{1,0:T(8,128)S(1)}, f32[6,1536]{1,0:T(8,128)S(1)}, u32[]{:S(2)}, u32[]{:S(2)}) collective-permute-start(f32[6,1536]{1,0:T(8,128)S(1)} %get-tuple-element.34), channel_id=1, source_target_pairs={{0,0},{64,2},{128,4},{192,6},{32,32},{96,34},{160,36},{224,38},{2,... | collective-permute-start | bytes 110600 | tf_op jit(solution)/shard_map/ppermute | solution.py:520
  114.5 0.0 collective-permute-done.8.far
  114.6 1.3 %shard_map.107 = (bf16[128,1536]{1,0:T(8,128)(2,1)}, f32[8,1536]{1,0:T(8,128)}) custom-call(bf16[2,160,384]{2,1,0:T(8,128)(2,1)S(1)} %copy-done.4, bf16[2,160,384]{2,1,0:T(8,128)(2,1)S(1)} %collective-permute-done.7.got, bf16[2,160,384]{2,1,0:T(8,128)(2,1)S(1)} %collective-permute-done.8.far, f32[8,128]{1,0:T(8,128)S(1)} %copy-done.5), custom_call_target="tpu_custom_call" | custom-call | bytes 1183744 | tf_op jit(solution)/shard_map/pallas_call | solution.py:406
  115.8 8.8 %collective-permute-done.9 = f32[6,1536]{1,0:T(8,128)S(1)} collective-permute-done((f32[6,1536]{1,0:T(8,128)S(1)}, f32[6,1536]{1,0:T(8,128)S(1)}, u32[]{:S(2)}, u32[]{:S(2)}) %collective-permute-start.9) | collective-permute-done | bytes 36896 | tf_op jit(solution)/shard_map/ppermute | solution.py:520
  124.7 0.0 all-to-all-done.4.got
  124.7 1.1 shard_map.110
  125.8 0.6 copy.14
  (12 shorter events, 0.1 us)
Async XLA Ops:
  0.6 19.4 %copy-start = (bf16[1,128,1536]{2,1,0:T(8,128)(2,1)S(1)}, bf16[1,128,1536]{2,1,0:T(8,128)(2,1)}, u32[]{:S(2)}) copy-start(bf16[1,128,1536]{2,1,0:T(8,128)(2,1)} %param.7) | copy-start | bytes 1179652
  0.6 2.8 %copy-start.7 = (bf16[1,128,1536]{2,1,0:T(8,128)(2,1)S(1)}, bf16[1,128,1536]{2,1,0:T(8,128)(2,1)}, u32[]{:S(2)}) copy-start(bf16[1,128,1536]{2,1,0:T(8,128)(2,1)} %param.8) | copy-start | bytes 1179652
  0.7 5.0 %copy-start.12 = (bf16[6,1536]{1,0:T(8,128)(2,1)S(1)}, bf16[6,1536]{1,0:T(8,128)(2,1)}, u32[]{:S(2)}) copy-start(bf16[6,1536]{1,0:T(8,128)(2,1)} %param.9) | copy-start | bytes 55300
  0.7 19.3 %copy-start.6 = (s32[1,8]{1,0:T(1,128)S(1)}, s32[1,8]{1,0:T(1,128)}, u32[]{:S(2)}) copy-start(s32[1,8]{1,0:T(1,128)} %durations.1) | copy-start | bytes 100
  2.8 17.2 %collective-permute-start.1 = (bf16[80,1536]{1,0:T(8,128)(2,1)S(1)}, bf16[80,1536]{1,0:T(8,128)(2,1)S(1)}, u32[]{:S(2)}, u32[]{:S(2)}) collective-permute-start(bf16[80,1536]{1,0:T(8,128)(2,1)S(1)} %maximum_select_fusion), channel_id=1, source_target_pairs={{6,8},{14,16},{22,24},{30,32},{38,40},{46,48},{54,56},{62,64},{70,... | collective-permute-start | bytes 737288 | tf_op jit(solution)/shard_map/ppermute | solution.py:430
  3.5 28.4 %collective-permute-start.3 = (bf16[128,1536]{1,0:T(8,128)(2,1)S(1)}, bf16[128,1536]{1,0:T(8,128)(2,1)S(1)}, u32[]{:S(2)}, u32[]{:S(2)}) collective-permute-start(bf16[128,1536]{1,0:T(8,128)(2,1)S(1)} %bitcast.19), channel_id=1, source_target_pairs={{0,4},{4,0},{1,5},{5,1},{2,6},{6,2},{3,7},{7,3},{8,12},{12,8},{9,1... | collective-permute-start | bytes 1179656 | tf_op jit(solution)/shard_map/ppermute | solution.py:449
  5.6 14.3 %collective-permute-start = (bf16[6,1536]{1,0:T(8,128)(2,1)S(1)}, bf16[6,1536]{1,0:T(8,128)(2,1)S(1)}, u32[]{:S(2)}, u32[]{:S(2)}) collective-permute-start(bf16[6,1536]{1,0:T(8,128)(2,1)S(1)} %copy-done.12), channel_id=1, source_target_pairs={{0,0},{2,64},{4,128},{6,192},{32,32},{34,96},{36,160},{38,224},{64... | collective-permute-start | bytes 55304 | tf_op jit(solution)/shard_map/ppermute | solution.py:439
  20.0 23.3 %copy-start.1 = (bf16[80,1536]{1,0:T(8,128)(2,1)}, bf16[80,1536]{1,0:T(8,128)(2,1)S(1)}, u32[]{:S(2)}) copy-start(bf16[80,1536]{1,0:T(8,128)(2,1)S(1)} %collective-permute-done.1.slot) | copy-start | bytes 737284
  21.3 20.4 %collective-permute-start.2 = (bf16[240,768]{1,0:T(8,128)(2,1)S(1)}, bf16[240,768]{1,0:T(8,128)(2,1)S(1)}, u32[]{:S(2)}, u32[]{:S(2)}) collective-permute-start(bf16[240,768]{1,0:T(8,128)(2,1)S(1)} %get-tuple-element.21), channel_id=1, source_target_pairs={{0,4},{4,0},{1,5},{5,1},{2,6},{6,2},{3,7},{7,3},{8,12},{12,8},{9,1... | collective-permute-start | bytes 1105928 | tf_op jit(solution)/shard_map/ppermute | solution.py:448
  21.4 20.3 %all-to-all-start = ((bf16[8,8,1536]{2,1,0:T(8,128)(2,1)}), bf16[8,8,1536]{2,1,0:T(8,128)(2,1)S(1)}, u32[]{:S(2)}, u32[]{:S(2)}) async-start(bf16[8,8,1536]{2,1,0:T(8,128)(2,1)} %get-tuple-element.20), calls=%async_computation | async-start | bytes 393216 | tf_op jit(solution)/shard_map/all_to_all | solution.py:447
  31.8 16.5 %copy-start.2 = (bf16[128,1536]{1,0:T(8,128)(2,1)}, bf16[128,1536]{1,0:T(8,128)(2,1)S(1)}, u32[]{:S(2)}) copy-start(bf16[128,1536]{1,0:T(8,128)(2,1)S(1)} %collective-permute-done.3.upstream.up_1) | copy-start | bytes 1179652
  41.6 1.7 %copy-start.3 = (bf16[240,768]{1,0:T(8,128)(2,1)}, bf16[240,768]{1,0:T(8,128)(2,1)S(1)}, u32[]{:S(2)}) copy-start(bf16[240,768]{1,0:T(8,128)(2,1)S(1)} %collective-permute-done.2.across) | copy-start | bytes 1105924
  43.3 5.1 %copy-start.11 = (bf16[31,1536]{1,0:T(8,128)(2,1)S(1)}, bf16[31,1536]{1,0:T(8,128)(2,1)}, u32[]{:S(2)}) copy-start(bf16[31,1536]{1,0:T(8,128)(2,1)} %param.10) | copy-start | bytes 285700
  43.3 21.0 %all-to-all-start.1 = ((bf16[8,48,1664]{2,1,0:T(8,128)(2,1)}), bf16[8,48,1664]{2,1,0:T(8,128)(2,1)}, u32[]{:S(2)}, u32[]{:S(2)}) async-start(bf16[8,48,1664]{2,1,0:T(8,128)(2,1)} %get-tuple-element.22), calls=%async_computation.1 | async-start | bytes 2555904 | tf_op jit(solution)/shard_map/all_to_all | solution.py:463
  47.7 3.0 %collective-permute-start.6 = (bf16[2,304,384]{2,1,0:T(8,128)(2,1)S(1)}, bf16[2,304,384]{2,1,0:T(8,128)(2,1)S(1)}, u32[]{:S(2)}, u32[]{:S(2)}) collective-permute-start(bf16[2,304,384]{2,1,0:T(8,128)(2,1)S(1)} %get-tuple-element.23), channel_id=1, source_target_pairs={{0,2},{2,0},{1,3},{3,1},{4,6},{6,4},{5,7},{7,5},{8,10},{10,8},{9,1... | collective-permute-start | bytes 1400840 | tf_op jit(solution)/shard_map/ppermute | solution.py:464
  47.8 2.4 %collective-permute-start.4 = (bf16[128,1536]{1,0:T(8,128)(2,1)S(1)}, bf16[128,1536]{1,0:T(8,128)(2,1)S(1)}, u32[]{:S(2)}, u32[]{:S(2)}) collective-permute-start(bf16[128,1536]{1,0:T(8,128)(2,1)S(1)} %bitcast.20), channel_id=1, source_target_pairs={{0,2},{2,0},{1,3},{3,1},{4,6},{6,4},{5,7},{7,5},{8,10},{10,8},{9,1... | collective-permute-start | bytes 1179656 | tf_op jit(solution)/shard_map/ppermute | solution.py:450
  48.3 2.4 %collective-permute-start.5 = (bf16[128,1536]{1,0:T(8,128)(2,1)S(1)}, bf16[128,1536]{1,0:T(8,128)(2,1)S(1)}, u32[]{:S(2)}, u32[]{:S(2)}) collective-permute-start(bf16[128,1536]{1,0:T(8,128)(2,1)S(1)} %collective-permute-done.3.upstream.up_1), channel_id=1, source_target_pairs={{0,2},{2,0},{1,3},{3,1},{4,6},{6,4},{5,7},{7,5},{8,10},{10,8},{9,1... | collective-permute-start | bytes 1179656 | tf_op jit(solution)/shard_map/ppermute | solution.py:451
  50.2 0.7 copy-start.9
  50.8 0.7 copy-start.10
  51.5 0.8 copy-start.8
  70.8 20.5 %all-to-all-start.2 = ((bf16[8,48,1664]{2,1,0:T(8,128)(2,1)}), bf16[8,48,1664]{2,1,0:T(8,128)(2,1)S(1)}, u32[]{:S(2)}, u32[]{:S(2)}) async-start(bf16[8,48,1664]{2,1,0:T(8,128)(2,1)} %get-tuple-element.33), calls=%async_computation.2 | async-start | bytes 2555904 | tf_op jit(solution)/shard_map/all_to_all | solution.py:501
  82.2 14.3 %copy-start.4 = (bf16[2,160,384]{2,1,0:T(8,128)(2,1)S(1)}, bf16[2,160,384]{2,1,0:T(8,128)(2,1)}, u32[]{:S(2)}) copy-start(bf16[2,160,384]{2,1,0:T(8,128)(2,1)} %get-tuple-element.29.kept) | copy-start | bytes 737284
  82.2 14.3 %collective-permute-start.7 = (bf16[2,160,384]{2,1,0:T(8,128)(2,1)}, bf16[2,160,384]{2,1,0:T(8,128)(2,1)S(1)}, u32[]{:S(2)}, u32[]{:S(2)}) collective-permute-start(bf16[2,160,384]{2,1,0:T(8,128)(2,1)} %get-tuple-element.30), channel_id=1, source_target_pairs={{0,2},{2,0},{1,3},{3,1},{4,6},{6,4},{5,7},{7,5},{8,10},{10,8},{9,1... | collective-permute-start | bytes 737288 | tf_op jit(solution)/shard_map/ppermute | solution.py:543
  92.8 21.8 %copy-start.5 = (f32[8,128]{1,0:T(8,128)S(1)}, f32[8,128]{1,0:T(8,128)}, u32[]{:S(2)}) copy-start(f32[8,128]{1,0:T(8,128)} %broadcast_in_dim.14.lengths) | copy-start | bytes 12292
  92.8 13.5 %all-to-all-start.3 = ((bf16[8,8,1536]{2,1,0:T(8,128)(2,1)}), bf16[8,8,1536]{2,1,0:T(8,128)(2,1)S(1)}, u32[]{:S(2)}, u32[]{:S(2)}) async-start(bf16[8,8,1536]{2,1,0:T(8,128)(2,1)} %shard_map.108), calls=%async_computation.3 | async-start | bytes 393216 | tf_op jit(solution)/shard_map/all_to_all | solution.py:509
  96.6 17.9 %collective-permute-start.8 = (bf16[2,160,384]{2,1,0:T(8,128)(2,1)S(1)}, bf16[2,160,384]{2,1,0:T(8,128)(2,1)S(1)}, u32[]{:S(2)}, u32[]{:S(2)}) collective-permute-start(bf16[2,160,384]{2,1,0:T(8,128)(2,1)S(1)} %pad_maximum_fusion), channel_id=1, source_target_pairs={{0,4},{4,0},{1,5},{5,1},{2,6},{6,2},{3,7},{7,3},{8,12},{12,8},{9,1... | collective-permute-start | bytes 737288 | tf_op jit(solution)/shard_map/ppermute | solution.py:547
  107.4 17.3 %all-to-all-start.4 = ((f32[32,1,1536]{2,1,0:T(1,128)}), f32[32,1,1536]{2,1,0:T(1,128)S(1)}, u32[]{:S(2)}, u32[]{:S(2)}) async-start(f32[32,1,1536]{2,1,0:T(1,128)} %get-tuple-element.35), calls=%async_computation.4 | async-start | bytes 393216 | tf_op jit(solution)/shard_map/all_to_all | solution.py:517
  112.4 12.3 %collective-permute-start.9 = (f32[6,1536]{1,0:T(8,128)S(1)}, f32[6,1536]{1,0:T(8,128)S(1)}, u32[]{:S(2)}, u32[]{:S(2)}) collective-permute-start(f32[6,1536]{1,0:T(8,128)S(1)} %get-tuple-element.34), channel_id=1, source_target_pairs={{0,0},{64,2},{128,4},{192,6},{32,32},{96,34},{160,36},{224,38},{2,... | collective-permute-start | bytes 110600 | tf_op jit(solution)/shard_map/ppermute | solution.py:520

commit v5 on v4

v5 whole, which is shorter than its diff:
```python
import math

import jax
import jax.numpy as jnp
import numpy as np
from jax import lax
from jax.experimental import pallas as pl
from jax.experimental.pallas import tpu as pltpu
from jax.sharding import Mesh
from jax.sharding import PartitionSpec as P

AXES = ("z", "x", "yh", "core", "rep")
SIZES = (8, 4, 2, 2, 2)
GROUP = ("yh", "core")
PLANE = ("x", "yh", "core", "rep")
QUARTERS = 4
BLOCK = 6
EXTRA = 128
MEMBERS, ROWS = 32, 24
MESSAGE = MEMBERS * ROWS
FRAMES, CHANNELS, TAPS = 512, 384, 31
EDGE_H, EDGE_U, SPILL = 48, 32, 16
LEFT_H, LEFT_U = 32, 16
WIDE = FRAMES + LEFT_U + EDGE_U
LONG = FRAMES + SPILL
SHARE = EDGE_H + 2 * EDGE_U
HANDED = 128 + EDGE_H + 4 * EDGE_U
BACK = 128 + SPILL
SWAP = [(0, 1), (1, 0)]
BF = jnp.bfloat16
F32 = jnp.float32


def placement(side):
    out = np.zeros((CHANNELS, MESSAGE), np.float32)
    for zl in range(2):
        for member in range(MEMBERS):
            for r in range(BLOCK):
                row = (zl * MEMBERS + member) * BLOCK + r
                out[row, member * ROWS + 12 * side + zl * BLOCK + r] = 1
    return jnp.asarray(out, BF)


def lanes(tile):
    return slice(tile * 128, tile * 128 + 128)


def begin(pairs, sems):
    copies = [pltpu.make_async_copy(a, b, sems.at[i]) for i, (a, b) in enumerate(pairs)]
    for copy in copies:
        copy.start()
    return copies


def finish(copies):
    for copy in copies:
        copy.wait()


def spread(
    weights, durations, hidden, upstream, out, share, edge,
    got, lengths, block, v_share, v_edge, sems,
):
    yh, core = lax.axis_index("yh"), lax.axis_index("core")
    other = pl.ds(pl.multiple_of((1 - yh) * 768, 128), 768)
    last = (yh + core) // 2
    from_h = pl.ds(pl.multiple_of(last * (128 - EDGE_H), 16), EDGE_H)
    from_u = pl.ds(pl.multiple_of(last * (128 - EDGE_U), 16), EDGE_U)
    taken = begin(
        [
            (hidden.at[:, other], v_share.at[pl.ds(0, 128)]),
            (upstream.at[:, pl.ds(0, 768)], v_share.at[pl.ds(128, 128)]),
            (upstream.at[:, pl.ds(768, 768)], v_share.at[pl.ds(256, 128)]),
            (hidden.at[from_h], v_edge.at[pl.ds(0, EDGE_H)]),
            (upstream.at[from_u], v_edge.at[pl.ds(EDGE_H, EDGE_U)]),
        ],
        sems.at[pl.ds(9, 5)],
    )
    finish(begin([(weights, got), (durations, lengths)], sems))
    lane = lax.broadcasted_iota(jnp.int32, (1, 1536), 1)
    total = jnp.sum(lengths[...].astype(F32), axis=1, keepdims=True)
    note = jnp.where(lane == lax.axis_index("z"), jnp.broadcast_to(total, (1, 1536)), 0.0)
    rows = [got[...].astype(F32), note, jnp.zeros((1, 1536), F32)]
    block[...] = jnp.concatenate(rows, axis=0).astype(BF)
    sent = begin([(block, out.at[peer]) for peer in range(8)], sems)
    finish(taken)
    finish(begin([(v_share, share), (v_edge, edge)], sems.at[pl.ds(9, 2)]))
    finish(sent)


def lend(slot, out, v_out, sems):
    other = pl.ds(pl.multiple_of((1 - lax.axis_index("yh")) * 768, 128), 768)
    up = pl.ds(EDGE_H, EDGE_U)
    finish(
        begin(
            [
                (slot.at[pl.ds(0, EDGE_H), other], v_out.at[pl.ds(0, EDGE_H)]),
                (slot.at[up, pl.ds(0, 768)], v_out.at[pl.ds(EDGE_H, EDGE_U)]),
                (slot.at[up, pl.ds(768, 768)], v_out.at[pl.ds(EDGE_H + EDGE_U, EDGE_U)]),
            ],
            sems,
        )
    )
    finish(begin([(v_out, out)], sems))


def pack(gathered, plane, rows, got, block, sems):
    finish(begin([(gathered, got)], sems))
    note = jnp.zeros((8, EXTRA), F32)
    for z in range(8):
        block_z = got[z].astype(F32)
        at = ROWS * (z // 2) + BLOCK * (z % 2)
        rows[at : at + BLOCK, :768] = block_z[:BLOCK, :768]
        rows[at + 12 : at + 12 + BLOCK, :768] = block_z[:BLOCK, 768:]
        note += jnp.broadcast_to(block_z[BLOCK : BLOCK + 1, :EXTRA], (8, EXTRA))
    rows[:, 768:] = jnp.concatenate([note] * (ROWS // 2), axis=0)
    for q in range(4):
        block[q] = rows[ROWS * q : ROWS * q + ROWS].astype(BF)
    finish(begin([(block.at[(j // 2) % 4], plane.at[j]) for j in range(MEMBERS)], sems))


def relay(hidden, slot, across, lent, beside, v_beside, sems):
    yh, core = lax.axis_index("yh"), lax.axis_index("core")
    other = pl.ds(pl.multiple_of((yh * 2 + 1 - core) * CHANNELS, 128), CHANNELS)
    part = pl.ds(pl.multiple_of((1 - core) * CHANNELS, 128), CHANNELS)
    ups = 128 + EDGE_H
    edge = pl.ds(0, EDGE_H)
    moves = [
        (hidden.at[:, other], v_beside.at[0, pl.ds(0, 128)]),
        (slot.at[edge, other], v_beside.at[0, pl.ds(128, EDGE_H)]),
        (across.at[pl.ds(0, 128), part], v_beside.at[1, pl.ds(0, 128)]),
        (lent.at[edge, part], v_beside.at[1, pl.ds(128, EDGE_H)]),
    ]
    for i in range(4):
        cut = pl.ds((i % 2) * CHANNELS, CHANNELS)
        row = pl.ds(ups + EDGE_U * i, EDGE_U)
        wide = pl.ds(i * CHANNELS, CHANNELS)
        moves.append((slot.at[pl.ds(EDGE_H, EDGE_U), wide], v_beside.at[0, row]))
        moves.append((lent.at[pl.ds(EDGE_H + EDGE_U * (i // 2), EDGE_U), cut], v_beside.at[1, row]))
    finish(begin(moves, sems))
    finish(begin([(v_beside, beside)], sems))


def group_grads(upstream, across, beside, beyond, grads):
    yh, core = lax.axis_index("yh"), lax.axis_index("core")
    moves = [(upstream, grads.at[yh * 2 + core]), (beside, grads.at[yh * 2 + 1 - core])]
    for source, place in ((across, 2 - 2 * yh + core), (beyond, 3 - 2 * yh - core)):
        for i in range(2):
            rows, cut = pl.ds(128 + 128 * i, 128), pl.ds(768 * i, 768)
            moves.append((source.at[rows], grads.at[place, :, cut]))
    return moves


def convolve(
    own, slot, across, lent, beside, upstream, up_beside, beyond, kernel, low, high,
    slope, hidden, parts,
    grads, frames, weights, v_low, v_high, v_slope, v_hidden, v_parts, active, sems,
):
    yh, core = lax.axis_index("yh"), lax.axis_index("core")
    part = pl.ds(pl.multiple_of(core * CHANNELS, 128), CHANNELS)
    mine = pl.ds(pl.multiple_of((yh * 2 + core) * CHANNELS, 128), CHANNELS)
    block = pl.ds(0, 128 + EDGE_H)
    needed = begin(
        [
            (own.at[:, mine], frames.at[yh * 2 + core, pl.ds(0, 128)]),
            (slot.at[pl.ds(0, EDGE_H), mine], frames.at[yh * 2 + core, pl.ds(128, EDGE_H)]),
            (across.at[pl.ds(0, 128), part], frames.at[(1 - yh) * 2 + core, pl.ds(0, 128)]),
            (lent.at[pl.ds(0, EDGE_H), part], frames.at[(1 - yh) * 2 + core, pl.ds(128, EDGE_H)]),
            (beside.at[0, block], frames.at[yh * 2 + 1 - core]),
            (beside.at[1, block], frames.at[(1 - yh) * 2 + 1 - core]),
            (kernel, weights),
        ],
        sems,
    )
    later = begin(
        group_grads(upstream, across, up_beside, beyond, grads) + [(low, v_low), (high, v_high)],
        sems.at[pl.ds(8, 8)],
    )
    finish(needed)
    v_hidden[:LEFT_H] = frames[0, 128 + EDGE_H - LEFT_H :].astype(F32)
    for b in range(4):
        v_hidden[LEFT_H + 128 * b : LEFT_H + 128 * b + 128] = frames[b, :128].astype(F32)
    v_hidden[LEFT_H + FRAMES :] = frames[3, 128:].astype(F32)
    rows = 112
    for tile in range(CHANNELS // 128):

        def chunk(c, _, tile=tile):
            base = pl.multiple_of(c * rows, 8)
            total = jnp.zeros((rows, 128), F32)
            window = v_hidden[pl.ds(base, rows + 32), lanes(tile)]
            for b in range(8):
                slab = window[b : b + rows + 24]
                for a in range(4):
                    k = 8 * a + b - 1
                    if 0 <= k < TAPS:
                        total += weights[k : k + 1, lanes(tile)] * slab[8 * a : 8 * a + rows]
            sig = jax.nn.sigmoid(total)
            v_slope[pl.ds(base, rows), lanes(tile)] = sig * (1.0 + total * (1.0 - sig))
            active[pl.ds(base, rows), lanes(tile)] = total * sig
            return 0

        lax.fori_loop(0, WIDE // rows, chunk, 0)
    out = begin([(v_slope, slope), (v_hidden, hidden)], sems)
    finish(later)
    acts = active[LEFT_U : LEFT_U + FRAMES].astype(BF)
    product = jnp.zeros((MESSAGE, 768), F32)
    for side, spot in enumerate((v_low, v_high)):
        columns = jnp.dot(acts, spot[...], preferred_element_type=F32).astype(BF)
        product += lax.dot_general(
            columns,
            grads[:, :, 768 * side : 768 * side + 768].reshape(FRAMES, 768),
            (((0,), (0,)), ((), ())),
            preferred_element_type=F32,
        )
    for j in range(MEMBERS):
        v_parts[j] = product[ROWS * j : ROWS * j + ROWS].astype(BF)
    finish(begin([(v_parts, parts.at[:, :, pl.ds(0, 768)])], sems.at[pl.ds(2, 1)]))
    finish(out)


def backward(
    gathered, low, high, upstream, across, up_beside, beyond, slope, hidden, parts,
    grad_conv, projection, message,
    got, v_low, v_high, grads, v_slope, v_hidden, v_grad, v_grad_f, v_taps, sums, v_weights, sems,
):
    needed = begin(
        [(gathered.at[:, :, pl.ds(0, 768)], got), (low, v_low), (high, v_high)], sems
    )
    later = begin(
        group_grads(upstream, across, up_beside, beyond, grads), sems.at[pl.ds(5, 6)]
    )
    last = begin(
        [(slope.at[pl.ds(LEFT_U, FRAMES)], v_slope), (hidden, v_hidden)], sems.at[pl.ds(13, 2)]
    )
    finish(needed)
    rows = got[...].reshape(MESSAGE, 768)
    for side, spot in enumerate((v_low, v_high)):
        v_weights[:, 768 * side : 768 * side + 768] = jnp.dot(
            spot[...], rows, preferred_element_type=F32
        ).astype(BF)
    finish(later)
    value = lax.dot_general(
        grads[...].reshape(FRAMES, 1536),
        v_weights[...],
        (((1,), (1,)), ((), ())),
        preferred_element_type=F32,
    )
    finish(last)
    value = (value * v_slope[...]).astype(BF)
    v_grad[...] = value
    v_grad_f[...] = value.astype(F32)
    out = begin([(v_grad, grad_conv), (v_weights, projection)], sems)
    span = 128
    sums[...] = jnp.zeros_like(sums)
    for tile in range(CHANNELS // 128):

        def piece(c, _, tile=tile):
            base = pl.multiple_of(c * span, 8)
            terms = v_grad_f[pl.ds(base, span), lanes(tile)]
            window = v_hidden[pl.ds(base + LEFT_U, span + 32), lanes(tile)]
            for b in range(8):
                slab = window[b : b + span + 24]
                for a in range(4):
                    k = 8 * a + b - 1
                    if 0 <= k < TAPS:
                        sums[k, :, lanes(tile)] += jnp.sum(
                            (terms * slab[8 * a : 8 * a + span]).reshape(span // 8, 8, 128),
                            axis=0,
                        )
            return 0

        lax.fori_loop(0, FRAMES // span, piece, 0)
    for j in range(MEMBERS):
        rows = [
            jnp.sum(sums[j, :, lanes(tile)], axis=0, keepdims=True)
            for tile in range(CHANNELS // 128)
        ]
        rows = jnp.concatenate(rows, axis=0)
        high_part = rows.astype(BF).astype(F32)
        rows = [high_part, rows - high_part, jnp.zeros((ROWS - 6, 128), F32)]
        v_taps[j] = jnp.concatenate(rows, axis=0).astype(BF)
    finish(begin([(v_taps, message.at[:, :, pl.ds(768, EXTRA)])], sems.at[pl.ds(3, 1)]))
    finish(out)


def transposed(
    grad_conv, projection, slope, slot, lent, beside, kernel,
    kept, given, v_grad, v_weights, v_slope, ups, weights, wide, total_f, v_kept, v_given, sems,
):
    yh, core = lax.axis_index("yh"), lax.axis_index("core")
    far = 128 + EDGE_H
    edges = [(slot.at[pl.ds(EDGE_H, EDGE_U)], ups.at[yh * 2 + core])]
    for i in range(2):
        edges.append(
            (
                lent.at[pl.ds(EDGE_H + EDGE_U * i, EDGE_U)],
                ups.at[(1 - yh) * 2 + core, :, pl.ds(768 * i, 768)],
            )
        )
    for i in range(4):
        row, cut = pl.ds(far + EDGE_U * i, EDGE_U), pl.ds(CHANNELS * i, CHANNELS)
        edges.append((beside.at[0, row], ups.at[yh * 2 + 1 - core, :, cut]))
        edges.append((beside.at[1, row], ups.at[(1 - yh) * 2 + 1 - core, :, cut]))
    edges += [
        (projection, v_weights),
        (slope.at[pl.ds(0, LEFT_U)], v_slope.at[pl.ds(0, LEFT_U)]),
        (slope.at[pl.ds(LEFT_U + FRAMES, EDGE_U)], v_slope.at[pl.ds(LEFT_U, EDGE_U)]),
        (grad_conv, v_grad),
        (kernel, weights),
    ]
    finish(begin(edges, sems))
    rows = jnp.concatenate([ups[0, EDGE_U - LEFT_U :], ups[3]], axis=0)
    value = lax.dot_general(
        rows, v_weights[...], (((1,), (1,)), ((), ())), preferred_element_type=F32
    )
    value = (value * v_slope[...]).astype(BF).astype(F32)
    wide[:LEFT_U] = value[:LEFT_U]
    wide[LEFT_U : LEFT_U + FRAMES] = v_grad[...].astype(F32)
    wide[LEFT_U + FRAMES :] = value[LEFT_U:]
    rows = 88
    for tile in range(CHANNELS // 128):

        def chunk(c, _, tile=tile):
            base = pl.multiple_of(c * rows, 8)
            total = jnp.zeros((rows, 128), F32)
            window = wide[pl.ds(base, rows + 32), lanes(tile)]
            for b in range(8):
                slab = window[b : b + rows + 24]
                for a in range(4):
                    k = TAPS - 8 * a - b
                    if 0 <= k < TAPS:
                        total += weights[k : k + 1, lanes(tile)] * slab[8 * a : 8 * a + rows]
            total_f[pl.ds(base, rows), lanes(tile)] = total
            return 0

        lax.fori_loop(0, LONG // rows, chunk, 0)
    for row in range(2):
        for out, side in ((v_kept, core), (v_given, 1 - core)):
            begin_row = pl.multiple_of((row * 2 + side) * 128, 128)
            out[row] = total_f[pl.ds(begin_row, BACK)].astype(BF)
    finish(begin([(v_kept, kept), (v_given, given)], sems))


def settle(
    kept, got, far, gathered, lengths, frame_grad, gloss, frames, notes, v_lengths, v_gloss, sems
):
    yh, core = lax.axis_index("yh"), lax.axis_index("core")
    sources = [(kept.at[yh], yh, core), (got.at[yh], yh, 1 - core)]
    sources += [(far.at[0], 1 - yh, core), (far.at[1], 1 - yh, 1 - core)]
    moves = [(lengths, v_lengths), (gathered.at[:, pl.ds(0, 16), pl.ds(768, EXTRA)], notes)]
    for source, a, b in sources:
        cut = pl.ds(pl.multiple_of((a * 2 + b) * CHANNELS, 128), CHANNELS)
        moves.append((source, frames.at[:, cut]))
    finish(begin(moves, sems))
    out = begin([(frames.at[pl.ds(0, 128)], frame_grad)], sems)
    mine = yh * 2 + core
    place = lax.axis_index("z") * 4 + lax.axis_index("x")
    lane = lax.broadcasted_iota(jnp.int32, (8, EXTRA), 1)
    start = jnp.zeros((8, EXTRA), F32)
    for member in range(MEMBERS):
        block = lane * 16 + member // 2
        earlier = (block < place * 4 + mine) & (lane < 8) & (lax.axis_index("rep") == member % 2)
        start += jnp.where(earlier, notes[member, :8].astype(F32), 0.0)
    start = jnp.sum(start, axis=1, keepdims=True) - (place * FRAMES + mine * 128).astype(F32)
    gloss_id = lax.broadcasted_iota(jnp.int32, (8, EXTRA), 0)
    length = v_lengths[...]
    first = jnp.sum(jnp.where(lane < gloss_id, length, 0.0), axis=1, keepdims=True) + start
    last = first + jnp.sum(jnp.where(lane == gloss_id, length, 0.0), axis=1, keepdims=True)
    at = lax.broadcasted_iota(jnp.int32, (8, 128 + SPILL), 1).astype(F32)
    covers = jnp.where((at >= first) & (at < last), 1.0, 0.0).astype(BF)
    v_gloss[...] = jnp.dot(covers, frames[...], preferred_element_type=F32)
    finish(begin([(v_gloss, gloss)], sems.at[pl.ds(1, 1)]))
    finish(out)


def pack_z(parts, out, v_parts, v_out, sems):
    finish(begin([(parts, v_parts)], sems))
    sums = []
    for q in range(4):
        total = jnp.zeros((ROWS, 896), F32)
        for x in range(4):
            for rep in range(2):
                total += v_parts[(x * 4 + q) * 2 + rep].astype(F32)
        sums.append(total)
    taps = [total[:3, 768:] + total[3:6, 768:] for total in sums]
    taps = jnp.concatenate([t[j : j + 1] for t in taps for j in range(3)], axis=1)
    high = taps.astype(BF).astype(F32)
    for z in range(8):
        at = BLOCK * (z % 2)
        halves = [sums[z // 2][at + 12 * side : at + 12 * side + BLOCK, :768] for side in range(2)]
        rows = [jnp.concatenate(halves, axis=1), high, taps - high]
        v_out[z] = jnp.concatenate(rows, axis=0).astype(BF)
    finish(begin([(v_out, out)], sems))


def unpack_z(got, weights, taps, v_got, v_weights, v_taps, sems):
    finish(begin([(got, v_got)], sems))
    total = v_got[0].astype(F32)
    for z in range(1, 8):
        total += v_got[z].astype(F32)
    total = total * (1.0 / math.sqrt(2 * 16384))
    v_weights[...] = total[:BLOCK]
    for peer in range(MEMBERS):
        v_taps[peer] = total[6:7] + total[7:8]
    finish(begin([(v_taps, taps), (v_weights, weights)], sems))


def arrange(got, out, v_got, v_out, sems):
    finish(begin([(got, v_got)], sems))
    for k in range(TAPS):
        v_out[k : k + 1] = v_got[k]
    finish(begin([(v_out, out)], sems))


def call(kernel, outs, scratch, megabytes, *args, alias=None, flops=200_000_000):
    shapes = [jax.ShapeDtypeStruct(shape, dtype) for shape, dtype in outs]
    size = sum(math.prod(s.shape) * s.dtype.itemsize for s in list(args) + shapes)
    return pl.pallas_call(
        kernel,
        out_shape=shapes,
        in_specs=[pl.BlockSpec(memory_space=pltpu.HBM)] * len(args),
        out_specs=[pl.BlockSpec(memory_space=pltpu.HBM)] * len(shapes),
        scratch_shapes=[pltpu.VMEM(shape, dtype) for shape, dtype in scratch]
        + [pltpu.SemaphoreType.DMA((48,))],
        input_output_aliases=alias or {},
        compiler_params=pltpu.CompilerParams(vmem_limit_bytes=megabytes * 2**20),
        cost_estimate=pl.CostEstimate(
            flops=flops, bytes_accessed=size, transcendentals=0
        ),
    )(*args)


def body(hidden_in, upstream, out_weight, conv_kernel, durations):
    yh, core = lax.axis_index("yh"), lax.axis_index("core")
    quarter = yh * 2 + core
    hidden, grads = hidden_in[0], upstream[0]
    lengths = jnp.broadcast_to(
        jnp.pad(durations.astype(F32), ((0, 0), (0, EXTRA - durations.shape[1]))), (8, EXTRA)
    )

    rows, share, edge = call(
        spread,
        [((8, 8, 1536), BF), ((384, 768), BF), ((EDGE_H + EDGE_U, 1536), BF)],
        [
            ((BLOCK, 1536), BF), ((1, 8), jnp.int32), ((8, 1536), BF), ((384, 768), BF),
            ((EDGE_H + EDGE_U, 1536), BF),
        ],
        56,
        out_weight, durations, hidden, grads,
    )
    ends = [(4 * i + 3, 4 * i + 4) for i in range(31)]
    slot = lax.ppermute(edge, ("z", "x", "yh", "core"), ends + [(b, a) for a, b in ends])
    rows = lax.all_to_all(rows, "z", 0, 0, tiled=True)
    across = lax.ppermute(share, "yh", SWAP)
    up_beside = lax.ppermute(grads, "core", SWAP)
    beyond = lax.ppermute(across, "core", SWAP)
    [lent] = call(lend, [((SHARE, 768), BF)], [((SHARE, 768), BF)], 16, slot)
    lent = lax.ppermute(lent, "yh", SWAP)
    message = ((MEMBERS, ROWS, 768 + EXTRA), BF)
    [plane] = call(
        pack,
        [message],
        [((4 * ROWS, 768 + EXTRA), F32), ((8, 8, 1536), BF), ((4, ROWS, 768 + EXTRA), BF)],
        56,
        rows,
    )
    handed = ((2, HANDED, CHANNELS), BF)
    [beside] = call(relay, [handed], [handed], 16, hidden, slot, across, lent, flops=30_000_000_000)
    rows = lax.all_to_all(plane, PLANE, 0, 0, tiled=True)
    beside = lax.ppermute(beside, "core", SWAP)
    kernel_f = lax.dynamic_slice_in_dim(
        jnp.pad(conv_kernel, ((0, 1), (0, 0))), quarter * CHANNELS, CHANNELS, 1
    ).astype(F32)
    spot = ((CHANNELS, MESSAGE), BF)
    low, high = placement(0), placement(1)
    frames_f = ((FRAMES, CHANNELS), F32)
    wide_f = ((LEFT_H + FRAMES + EDGE_H, CHANNELS), F32)
    slope_f = ((WIDE, CHANNELS), F32)
    all_grads = ((4, 128, 1536), BF)
    sent = ((MEMBERS, ROWS, 768), BF)
    kernel_shape = ((TAPS + 1, CHANNELS), F32)
    slope, hidden_f, parts = call(
        convolve,
        [slope_f, wide_f, message],
        [
            all_grads, ((4, 128 + EDGE_H, CHANNELS), BF), kernel_shape, spot, spot, slope_f, wide_f,
            sent, slope_f,
        ],
        56,
        hidden, slot, across, lent, beside, grads, up_beside, beyond, kernel_f, low, high,
    )
    grad_conv, projection, parts = call(
        backward,
        [
            ((FRAMES, CHANNELS), BF), ((CHANNELS, 1536), BF), message,
        ],
        [
            sent, spot, spot, all_grads, frames_f, wide_f, ((FRAMES, CHANNELS), BF), frames_f,
            ((MEMBERS, ROWS, EXTRA), BF), ((TAPS + 1, 8, CHANNELS), F32),
            ((CHANNELS, 1536), BF),
        ],
        56,
        rows, low, high, grads, across, up_beside, beyond, slope, hidden_f, parts,
        alias={9: 2},
    )

    parts = lax.all_to_all(parts, PLANE, 0, 0, tiled=True)
    [parts] = call(
        pack_z,
        [((8, 8, 1536), BF)],
        [message, ((8, 8, 1536), BF)],
        16,
        parts,
    )
    parts = lax.all_to_all(parts, "z", 0, 0, tiled=True)
    weight_grad, taps_all = call(
        unpack_z,
        [((BLOCK, 1536), F32), ((32, 1, 1536), F32)],
        [((8, 8, 1536), BF), ((BLOCK, 1536), F32), ((32, 1, 1536), F32)],
        16,
        parts,
    )
    taps_all = lax.all_to_all(taps_all, PLANE, 0, 0, tiled=True)
    [kernel_grad] = call(
        arrange,
        [((TAPS, 1536), F32)],
        [((32, 1, 1536), F32), ((TAPS, 1536), F32)],
        16,
        taps_all,
    )

    back = ((2, BACK, CHANNELS), BF)
    kept, given = call(
        transposed,
        [back, back],
        [
            ((FRAMES, CHANNELS), BF), ((CHANNELS, 1536), BF), ((LEFT_U + EDGE_U, CHANNELS), F32),
            ((4, EDGE_U, 1536), BF), kernel_shape,
            slope_f, ((LONG, CHANNELS), F32), back, back,
        ],
        56,
        grad_conv, projection, slope, slot, lent, beside, kernel_f,
    )
    got = lax.ppermute(given, "core", SWAP)
    far = jnp.stack(
        [lax.dynamic_index_in_dim(part, 1 - yh, 0, False) for part in (kept, got)]
    )
    far = lax.ppermute(far, "yh", SWAP)
    frame_grad, gloss = call(
        settle,
        [((128, 1536), BF), ((8, 1536), F32)],
        [
            ((BACK, 1536), BF), ((MEMBERS, 16, EXTRA), BF), ((8, EXTRA), F32),
            ((8, 1536), F32),
        ],
        16,
        kept, got, far, rows, lengths,
    )
    return (frame_grad[None], gloss[None], weight_grad, kernel_grad)


def solution(mesh):
    fine = Mesh(mesh.devices.reshape(SIZES), AXES)
    seq = ("z", "x", "yh", "core")
    rows = P(seq + ("rep",), None)
    in_specs = (P("rep", seq, None), P("rep", seq, None), rows, P(), P("rep", seq))
    out_specs = (P("rep", seq, None), P("rep", seq, None), rows, P())
    return jax.shard_map(
        body, mesh=fine, in_specs=in_specs, out_specs=out_specs, check_vma=False
    )
```

time: 127 us -> 124 us (0.976)
  the two profiles are of different devices: /device:TPU:16 before, /device:TPU:1 now
where the time goes in v5:
time: 124 us; the launch traced here: 123 us
  starting transfers between devices  47.5 us (38%)
  Pallas kernels  36.5 us (29%)
  waiting for transfers between devices  34 us (27%)
  local copies, waits for them, and re-layouts  2.73 us (2%)
  other arithmetic  1.39 us (1%)
    pallas_call x11, Pallas kernels, call(): pl.pallas_call(kernel, out_shape=shapes, in_specs=[pl.BlockSpec(memory_sp...  36.5 us
    all_to_all x1, waiting for transfers between devices, body(): parts = lax.all_to_all(parts, PLANE, 0, 0, tiled=True)  12.4 us
    all_to_all x1, starting transfers between devices, body(): rows = lax.all_to_all(plane, PLANE, 0, 0, tiled=True)  10.1 us
    all_to_all x1, starting transfers between devices, body(): rows = lax.all_to_all(rows, 'z', 0, 0, tiled=True)  8.2 us
    all_to_all x1, starting transfers between devices, body(): taps_all = lax.all_to_all(taps_all, PLANE, 0, 0, tiled=True)  6.8 us
    all_to_all x1, waiting for transfers between devices, body(): taps_all = lax.all_to_all(taps_all, PLANE, 0, 0, tiled=True)  6.68 us
    all_to_all x1, waiting for transfers between devices, body(): parts = lax.all_to_all(parts, 'z', 0, 0, tiled=True)  6.6 us
    ppermute x1, starting transfers between devices, body(): lent = lax.ppermute(lent, 'yh', SWAP)  6.1 us
  transfers between devices with their start and end apart: 13, of which 6 were waited for; matrix products, arithmetic and copies ran while one was open for 1% of the time, Pallas kernels for 21%

profile of v5, /device:TPU:1, one launch (start us, length us, event | category | flops | bytes accessed | tf_op | source)
XLA Modules:
  0.0 123.1 jit_solution(15822050472438909598)
XLA Ops:
  0.6 2.6 %shard_map.102 = (bf16[8,8,1536]{2,1,0:T(8,128)(2,1)}, bf16[384,768]{1,0:T(8,128)(2,1)}, bf16[80,1536]{1,0:T(8,128)(2,1)}) custom-call(bf16[6,1536]{1,0:T(8,128)(2,1)} %weights.1, s32[1,8]{1,0:T(1,128)} %durations.1, bf16[128,1536]{1,0:T(8,128)(2,1)} %bitcast.6, bf16[128,1536]{1,0:T(8,128)(2,1)} %bitcast.1.upstream), custom_call_target="tpu_custom_call" | custom-call | flops 200000000 | bytes 1837088 | tf_op jit(solution)/shard_map/pallas_call | solution.py:418
  3.2 3.8 %collective-permute-start = (bf16[384,768]{1,0:T(8,128)(2,1)}, bf16[384,768]{1,0:T(8,128)(2,1)S(1)}, u32[]{:S(2)}, u32[]{:S(2)}) collective-permute-start(bf16[384,768]{1,0:T(8,128)(2,1)} %get-tuple-element.20), channel_id=1, source_target_pairs={{0,4},{4,0},{1,5},{5,1},{2,6},{6,2},{3,7},{7,3},{8,12},{12,8},{9,1... | collective-permute-start | bytes 1769480 | tf_op jit(solution)/shard_map/ppermute | solution.py:454
  7.1 0.7 collective-permute-start.3
  7.7 8.2 %all-to-all-start = ((bf16[8,8,1536]{2,1,0:T(8,128)(2,1)}), bf16[8,8,1536]{2,1,0:T(8,128)(2,1)S(1)}, u32[]{:S(2)}, u32[]{:S(2)}) async-start(bf16[8,8,1536]{2,1,0:T(8,128)(2,1)} %get-tuple-element.19), calls=%async_computation | async-start | bytes 393216 | tf_op jit(solution)/shard_map/all_to_all | solution.py:453
  15.9 0.0 collective-permute-done.3.slot
  15.9 0.0 copy-start.4
  15.9 0.7 shard_map.104
  16.7 6.1 %collective-permute-start.4 = (bf16[112,768]{1,0:T(8,128)(2,1)S(1)}, bf16[112,768]{1,0:T(8,128)(2,1)S(1)}, u32[]{:S(2)}, u32[]{:S(2)}) collective-permute-start(bf16[112,768]{1,0:T(8,128)(2,1)S(1)} %shard_map.104), channel_id=1, source_target_pairs={{0,4},{4,0},{1,5},{5,1},{2,6},{6,2},{3,7},{7,3},{8,12},{12,8},{9,1... | collective-permute-start | bytes 516104 | tf_op jit(solution)/shard_map/ppermute | solution.py:458
  22.8 1.8 %all-to-all-done.gathered = bf16[8,8,1536]{2,1,0:T(8,128)(2,1)S(1)} async-done(((bf16[8,8,1536]{2,1,0:T(8,128)(2,1)}), bf16[8,8,1536]{2,1,0:T(8,128)(2,1)S(1)}, u32[]{:S(2)}, u32[]{:S(2)}) %all-to-all-start) | async-done | bytes 196640 | tf_op jit(solution)/shard_map/all_to_all | solution.py:453
  24.6 0.0 copy-start.9
  24.6 0.7 copy-done.9
  25.2 2.5 %shard_map.103 = bf16[32,24,896]{2,1,0:T(8,128)(2,1)} custom-call(bf16[8,8,1536]{2,1,0:T(8,128)(2,1)} %copy-done.9), custom_call_target="tpu_custom_call" | custom-call | flops 200000000 | bytes 1572864 | tf_op jit(solution)/shard_map/pallas_call | solution.py:418
  27.7 0.0 copy-start.3
  27.8 10.1 %all-to-all-start.1 = ((bf16[32,24,896]{2,1,0:T(8,128)(2,1)}), bf16[32,24,896]{2,1,0:T(8,128)(2,1)S(1)}, u32[]{:S(2)}, u32[]{:S(2)}) async-start(bf16[32,24,896]{2,1,0:T(8,128)(2,1)} %shard_map.103), calls=%async_computation.1 | async-start | bytes 2752512 | tf_op jit(solution)/shard_map/all_to_all | solution.py:469
  37.9 0.0 collective-permute-done.across
  37.9 0.0 copy-start.2
  37.9 0.3 collective-permute-start.2
  38.2 0.0 collective-permute-done.4.lent
  38.2 0.0 copy-done.4
  38.2 0.0 copy-done.3
  38.2 0.0 copy-start.5
  38.3 0.8 shard_map.105
  39.1 0.0 copy-done.2
  39.1 0.0 copy-done.5
  39.1 0.4 collective-permute-start.5
  39.5 0.2 collective-permute-start.1
  39.7 1.4 %fusion.kernel = f32[32,384]{1,0:T(8,128)} fusion(s32[]{:T(128)S(6)} %select_n.8, bf16[31,1536]{1,0:T(8,128)(2,1)} %param.10), kind=kLoop, calls=%fused_computation.2 | loop fusion | flops 12288 | bytes 144388 | tf_op jit(solution)/shard_map/convert_element_type | solution.py:473
  41.1 0.7 collective-permute-done.1.up_beside
  41.8 0.0 copy-start.8
  41.8 0.0 collective-permute-done.5.beside
  41.8 0.0 copy-start.7
  41.8 0.0 collective-permute-done.2.beyond
  41.8 0.7 copy-done.8
  42.5 0.2 copy-done.7
  42.7 9.6 %shard_map.106 = (f32[560,384]{1,0:T(8,128)}, f32[592,384]{1,0:T(8,128)}, bf16[32,24,896]{2,1,0:T(8,128)(2,1)}) custom-call(bf16[128,1536]{1,0:T(8,128)(2,1)} %bitcast.7, bf16[80,1536]{1,0:T(8,128)(2,1)} %copy-done.4, bf16[384,768]{1,0:T(8,128)(2,1)} %copy-done.2, bf16[112,768]{1,0:T(8,128)(2,1)} %copy-done.5, bf16[2,304,384]{2,1,0:T(8,128)(2,1)} %copy-done.7, ...), custom_call_target="tpu_custom_call" | custom-call | flops 200000000 | bytes 7618560 | tf_op jit(solution)/shard_map/pallas_call | solution.py:418
  52.3 5.8 %all-to-all-done.1.gathered = bf16[32,24,896]{2,1,0:T(8,128)(2,1)S(1)} async-done(((bf16[32,24,896]{2,1,0:T(8,128)(2,1)}), bf16[32,24,896]{2,1,0:T(8,128)(2,1)S(1)}, u32[]{:S(2)}, u32[]{:S(2)}) %all-to-all-start.1) | async-done | bytes 1376288 | tf_op jit(solution)/shard_map/all_to_all | solution.py:469
  58.0 0.0 copy-start
  58.0 1.1 copy-done
  59.1 7.2 %shard_map.107 = (bf16[512,384]{1,0:T(8,128)(2,1)}, bf16[384,1536]{1,0:T(8,128)(2,1)}, bf16[32,24,896]{2,1,0:T(8,128)(2,1)}) custom-call(bf16[32,24,896]{2,1,0:T(8,128)(2,1)} %copy-done, bf16[384,768]{1,0:T(8,128)(2,1)} %constant.34.clone.low, bf16[384,768]{1,0:T(8,128)(2,1)} %constant.35.clone.high, ...), custom_call_target="tpu_custom_call", output_to_operand_aliasing={{2}: (9, {})} | custom-call | flops 200000000 | bytes 10616832 | tf_op jit(solution)/shard_map/pallas_call | solution.py:418
  66.4 5.1 %all-to-all-start.2 = ((bf16[32,24,896]{2,1,0:T(8,128)(2,1)}), bf16[32,24,896]{2,1,0:T(8,128)(2,1)S(1)}, u32[]{:S(2)}, u32[]{:S(2)}) async-start(bf16[32,24,896]{2,1,0:T(8,128)(2,1)} %get-tuple-element.31), calls=%async_computation.2 | async-start | bytes 2752512 | tf_op jit(solution)/shard_map/all_to_all | solution.py:507
  71.5 7.4 %shard_map.108 = (bf16[2,144,384]{2,1,0:T(8,128)(2,1)}, bf16[2,144,384]{2,1,0:T(8,128)(2,1)}) custom-call(bf16[512,384]{1,0:T(8,128)(2,1)} %get-tuple-element.25.grad_conv, bf16[384,1536]{1,0:T(8,128)(2,1)} %get-tuple-element.26.projection, f32[560,384]{1,0:T(8,128)} %get-tuple-element.22.slope, bf16[80,1536]{1,0:T(8,128)(2,1)} %copy-done.4, ...), custom_call_target="tpu_custom_call" | custom-call | flops 200000000 | bytes 3809280 | tf_op jit(solution)/shard_map/pallas_call | solution.py:418
  78.9 0.0 copy-start.6
  78.9 0.3 collective-permute-start.6
  79.3 12.4 %all-to-all-done.2.parts = bf16[32,24,896]{2,1,0:T(8,128)(2,1)S(1)} async-done(((bf16[32,24,896]{2,1,0:T(8,128)(2,1)}), bf16[32,24,896]{2,1,0:T(8,128)(2,1)S(1)}, u32[]{:S(2)}, u32[]{:S(2)}) %all-to-all-start.2) | async-done | bytes 1376288 | tf_op jit(solution)/shard_map/all_to_all | solution.py:507
  91.7 1.5 %shard_map.110 = bf16[8,8,1536]{2,1,0:T(8,128)(2,1)} custom-call(bf16[32,24,896]{2,1,0:T(8,128)(2,1)S(1)} %all-to-all-done.2.parts), custom_call_target="tpu_custom_call" | custom-call | flops 200000000 | bytes 1572864 | tf_op jit(solution)/shard_map/pallas_call | solution.py:418
  93.2 0.0 copy-start.10
  93.2 0.0 copy-start.1
  93.2 3.5 %all-to-all-start.3 = ((bf16[8,8,1536]{2,1,0:T(8,128)(2,1)}), bf16[8,8,1536]{2,1,0:T(8,128)(2,1)S(1)}, u32[]{:S(2)}, u32[]{:S(2)}) async-start(bf16[8,8,1536]{2,1,0:T(8,128)(2,1)} %shard_map.110), calls=%async_computation.3 | async-start | bytes 393216 | tf_op jit(solution)/shard_map/all_to_all | solution.py:515
  96.8 0.0 copy-done.6
  96.8 0.0 collective-permute-done.6.got
  96.9 1.9 %collective-permute-start.7 = (bf16[2,144,384]{2,1,0:T(8,128)(2,1)S(1)}, bf16[2,144,384]{2,1,0:T(8,128)(2,1)S(1)}, u32[]{:S(2)}, u32[]{:S(2)}) collective-permute-start(bf16[2,144,384]{2,1,0:T(8,128)(2,1)S(1)} %pad_maximum_fusion), channel_id=1, source_target_pairs={{0,4},{4,0},{1,5},{5,1},{2,6},{6,2},{3,7},{7,3},{8,12},{12,8},{9,1... | collective-permute-start | bytes 663560 | tf_op jit(solution)/shard_map/ppermute | solution.py:548
  98.7 6.6 %all-to-all-done.3.got = bf16[8,8,1536]{2,1,0:T(8,128)(2,1)S(1)} async-done(((bf16[8,8,1536]{2,1,0:T(8,128)(2,1)}), bf16[8,8,1536]{2,1,0:T(8,128)(2,1)S(1)}, u32[]{:S(2)}, u32[]{:S(2)}) %all-to-all-start.3) | async-done | bytes 196640 | tf_op jit(solution)/shard_map/all_to_all | solution.py:515
  105.3 1.4 %shard_map.111 = (f32[6,1536]{1,0:T(8,128)}, f32[32,1,1536]{2,1,0:T(1,128)}) custom-call(bf16[8,8,1536]{2,1,0:T(8,128)(2,1)S(1)} %all-to-all-done.3.got), custom_call_target="tpu_custom_call" | custom-call | flops 200000000 | bytes 430080 | tf_op jit(solution)/shard_map/pallas_call | solution.py:418
  106.7 6.8 %all-to-all-start.4 = ((f32[32,1,1536]{2,1,0:T(1,128)}), f32[32,1,1536]{2,1,0:T(1,128)S(1)}, u32[]{:S(2)}, u32[]{:S(2)}) async-start(f32[32,1,1536]{2,1,0:T(1,128)} %get-tuple-element.33), calls=%async_computation.4 | async-start | bytes 393216 | tf_op jit(solution)/shard_map/all_to_all | solution.py:523
  113.5 0.0 copy-done.10
  113.6 0.0 collective-permute-done.7.far
  113.6 0.0 copy-done.1
  113.6 1.4 %shard_map.109 = (bf16[128,1536]{1,0:T(8,128)(2,1)}, f32[8,1536]{1,0:T(8,128)}) custom-call(bf16[2,144,384]{2,1,0:T(8,128)(2,1)S(1)} %copy-done.6, bf16[2,144,384]{2,1,0:T(8,128)(2,1)S(1)} %collective-permute-done.6.got, bf16[2,144,384]{2,1,0:T(8,128)(2,1)S(1)} %collective-permute-done.7.far, bf16[32,24,896]{2,1,0:T(8,128)(2,1)S(1)} %copy-done.1, ...), custom_call_target="tpu_custom_call" | custom-call | flops 200000000 | bytes 2486272 | tf_op jit(solution)/shard_map/pallas_call | solution.py:418
  115.0 6.7 %all-to-all-done.4.got = f32[32,1,1536]{2,1,0:T(1,128)S(1)} async-done(((f32[32,1,1536]{2,1,0:T(1,128)}), f32[32,1,1536]{2,1,0:T(1,128)S(1)}, u32[]{:S(2)}, u32[]{:S(2)}) %all-to-all-start.4) | async-done | bytes 196640 | tf_op jit(solution)/shard_map/all_to_all | solution.py:523
  121.7 1.4 %shard_map.112 = f32[31,1536]{1,0:T(8,128)} custom-call(f32[32,1,1536]{2,1,0:T(1,128)S(1)} %all-to-all-done.4.got), custom_call_target="tpu_custom_call" | custom-call | flops 200000000 | bytes 387072 | tf_op jit(solution)/shard_map/pallas_call | solution.py:418
  (6 shorter events, 0.1 us)
Async XLA Ops:
  3.2 34.7 %collective-permute-start = (bf16[384,768]{1,0:T(8,128)(2,1)}, bf16[384,768]{1,0:T(8,128)(2,1)S(1)}, u32[]{:S(2)}, u32[]{:S(2)}) collective-permute-start(bf16[384,768]{1,0:T(8,128)(2,1)} %get-tuple-element.20), channel_id=1, source_target_pairs={{0,4},{4,0},{1,5},{5,1},{2,6},{6,2},{3,7},{7,3},{8,12},{12,8},{9,1... | collective-permute-start | bytes 1769480 | tf_op jit(solution)/shard_map/ppermute | solution.py:454
  7.1 8.9 %collective-permute-start.3 = (bf16[80,1536]{1,0:T(8,128)(2,1)}, bf16[80,1536]{1,0:T(8,128)(2,1)S(1)}, u32[]{:S(2)}, u32[]{:S(2)}) collective-permute-start(bf16[80,1536]{1,0:T(8,128)(2,1)} %get-tuple-element.21), channel_id=1, source_target_pairs={{6,8},{14,16},{22,24},{30,32},{38,40},{46,48},{54,56},{62,64},{70,... | collective-permute-start | bytes 737288 | tf_op jit(solution)/shard_map/ppermute | solution.py:452
  7.7 16.8 %all-to-all-start = ((bf16[8,8,1536]{2,1,0:T(8,128)(2,1)}), bf16[8,8,1536]{2,1,0:T(8,128)(2,1)S(1)}, u32[]{:S(2)}, u32[]{:S(2)}) async-start(bf16[8,8,1536]{2,1,0:T(8,128)(2,1)} %get-tuple-element.19), calls=%async_computation | async-start | bytes 393216 | tf_op jit(solution)/shard_map/all_to_all | solution.py:453
  15.9 22.3 %copy-start.4 = (bf16[80,1536]{1,0:T(8,128)(2,1)}, bf16[80,1536]{1,0:T(8,128)(2,1)S(1)}, u32[]{:S(2)}) copy-start(bf16[80,1536]{1,0:T(8,128)(2,1)S(1)} %collective-permute-done.3.slot) | copy-start | bytes 737284
  16.7 21.6 %collective-permute-start.4 = (bf16[112,768]{1,0:T(8,128)(2,1)S(1)}, bf16[112,768]{1,0:T(8,128)(2,1)S(1)}, u32[]{:S(2)}, u32[]{:S(2)}) collective-permute-start(bf16[112,768]{1,0:T(8,128)(2,1)S(1)} %shard_map.104), channel_id=1, source_target_pairs={{0,4},{4,0},{1,5},{5,1},{2,6},{6,2},{3,7},{7,3},{8,12},{12,8},{9,1... | collective-permute-start | bytes 516104 | tf_op jit(solution)/shard_map/ppermute | solution.py:458
  24.6 0.7 copy-start.9
  27.7 10.5 %copy-start.3 = (bf16[1,128,1536]{2,1,0:T(8,128)(2,1)S(1)}, bf16[1,128,1536]{2,1,0:T(8,128)(2,1)}, u32[]{:S(2)}) copy-start(bf16[1,128,1536]{2,1,0:T(8,128)(2,1)} %param.7) | copy-start | bytes 1179652
  27.8 30.3 %all-to-all-start.1 = ((bf16[32,24,896]{2,1,0:T(8,128)(2,1)}), bf16[32,24,896]{2,1,0:T(8,128)(2,1)S(1)}, u32[]{:S(2)}, u32[]{:S(2)}) async-start(bf16[32,24,896]{2,1,0:T(8,128)(2,1)} %shard_map.103), calls=%async_computation.1 | async-start | bytes 2752512 | tf_op jit(solution)/shard_map/all_to_all | solution.py:469
  37.9 1.2 copy-start.2
  37.9 3.9 %collective-permute-start.2 = (bf16[384,768]{1,0:T(8,128)(2,1)S(1)}, bf16[384,768]{1,0:T(8,128)(2,1)}, u32[]{:S(2)}, u32[]{:S(2)}) collective-permute-start(bf16[384,768]{1,0:T(8,128)(2,1)S(1)} %collective-permute-done.across), channel_id=1, source_target_pairs={{0,2},{2,0},{1,3},{3,1},{4,6},{6,4},{5,7},{7,5},{8,10},{10,8},{9,1... | collective-permute-start | bytes 1769480 | tf_op jit(solution)/shard_map/ppermute | solution.py:456
  38.2 0.9 copy-start.5
  39.1 2.7 %collective-permute-start.5 = (bf16[2,304,384]{2,1,0:T(8,128)(2,1)S(1)}, bf16[2,304,384]{2,1,0:T(8,128)(2,1)S(1)}, u32[]{:S(2)}, u32[]{:S(2)}) collective-permute-start(bf16[2,304,384]{2,1,0:T(8,128)(2,1)S(1)} %shard_map.105), channel_id=1, source_target_pairs={{0,2},{2,0},{1,3},{3,1},{4,6},{6,4},{5,7},{7,5},{8,10},{10,8},{9,1... | collective-permute-start | bytes 1400840 | tf_op jit(solution)/shard_map/ppermute | solution.py:470
  39.5 2.3 %collective-permute-start.1 = (bf16[128,1536]{1,0:T(8,128)(2,1)}, bf16[128,1536]{1,0:T(8,128)(2,1)S(1)}, u32[]{:S(2)}, u32[]{:S(2)}) collective-permute-start(bf16[128,1536]{1,0:T(8,128)(2,1)} %bitcast.1.upstream), channel_id=1, source_target_pairs={{0,2},{2,0},{1,3},{3,1},{4,6},{6,4},{5,7},{7,5},{8,10},{10,8},{9,1... | collective-permute-start | bytes 1179656 | tf_op jit(solution)/shard_map/ppermute | solution.py:455
  41.8 0.7 copy-start.8
  41.8 0.9 copy-start.7
  58.0 1.1 copy-start
  66.4 25.3 %all-to-all-start.2 = ((bf16[32,24,896]{2,1,0:T(8,128)(2,1)}), bf16[32,24,896]{2,1,0:T(8,128)(2,1)S(1)}, u32[]{:S(2)}, u32[]{:S(2)}) async-start(bf16[32,24,896]{2,1,0:T(8,128)(2,1)} %get-tuple-element.31), calls=%async_computation.2 | async-start | bytes 2752512 | tf_op jit(solution)/shard_map/all_to_all | solution.py:507
  78.9 17.8 %copy-start.6 = (bf16[2,144,384]{2,1,0:T(8,128)(2,1)S(1)}, bf16[2,144,384]{2,1,0:T(8,128)(2,1)}, u32[]{:S(2)}) copy-start(bf16[2,144,384]{2,1,0:T(8,128)(2,1)} %get-tuple-element.27.kept) | copy-start | bytes 663556
  78.9 17.8 %collective-permute-start.6 = (bf16[2,144,384]{2,1,0:T(8,128)(2,1)}, bf16[2,144,384]{2,1,0:T(8,128)(2,1)S(1)}, u32[]{:S(2)}, u32[]{:S(2)}) collective-permute-start(bf16[2,144,384]{2,1,0:T(8,128)(2,1)} %get-tuple-element.28), channel_id=1, source_target_pairs={{0,2},{2,0},{1,3},{3,1},{4,6},{6,4},{5,7},{7,5},{8,10},{10,8},{9,1... | collective-permute-start | bytes 663560 | tf_op jit(solution)/shard_map/ppermute | solution.py:544
  93.2 20.4 %copy-start.10 = (s32[1,8]{1,0:T(1,128)S(1)}, s32[1,8]{1,0:T(1,128)}, u32[]{:S(2)}) copy-start(s32[1,8]{1,0:T(1,128)} %durations.1) | copy-start | bytes 100
  93.2 20.4 %copy-start.1 = (bf16[32,24,896]{2,1,0:T(8,128)(2,1)S(1)}, bf16[32,24,896]{2,1,0:T(8,128)(2,1)}, u32[]{:S(2)}) copy-start(bf16[32,24,896]{2,1,0:T(8,128)(2,1)} %copy-done) | copy-start | bytes 4128772
  93.2 12.1 %all-to-all-start.3 = ((bf16[8,8,1536]{2,1,0:T(8,128)(2,1)}), bf16[8,8,1536]{2,1,0:T(8,128)(2,1)S(1)}, u32[]{:S(2)}, u32[]{:S(2)}) async-start(bf16[8,8,1536]{2,1,0:T(8,128)(2,1)} %shard_map.110), calls=%async_computation.3 | async-start | bytes 393216 | tf_op jit(solution)/shard_map/all_to_all | solution.py:515
  96.9 16.7 %collective-permute-start.7 = (bf16[2,144,384]{2,1,0:T(8,128)(2,1)S(1)}, bf16[2,144,384]{2,1,0:T(8,128)(2,1)S(1)}, u32[]{:S(2)}, u32[]{:S(2)}) collective-permute-start(bf16[2,144,384]{2,1,0:T(8,128)(2,1)S(1)} %pad_maximum_fusion), channel_id=1, source_target_pairs={{0,4},{4,0},{1,5},{5,1},{2,6},{6,2},{3,7},{7,3},{8,12},{12,8},{9,1... | collective-permute-start | bytes 663560 | tf_op jit(solution)/shard_map/ppermute | solution.py:548
  106.7 15.0 %all-to-all-start.4 = ((f32[32,1,1536]{2,1,0:T(1,128)}), f32[32,1,1536]{2,1,0:T(1,128)S(1)}, u32[]{:S(2)}, u32[]{:S(2)}) async-start(f32[32,1,1536]{2,1,0:T(1,128)} %get-tuple-element.33), calls=%async_computation.4 | async-start | bytes 393216 | tf_op jit(solution)/shard_map/all_to_all | solution.py:523

commit v6 on v5

--- a/solution.py
+++ b/solution.py
@@ -24,7 +24,7 @@
 WIDE = FRAMES + LEFT_U + EDGE_U
 LONG = FRAMES + SPILL
 SHARE = EDGE_H + 2 * EDGE_U
-HANDED = 128 + EDGE_H + 4 * EDGE_U
+HANDED = EDGE_H + 4 * EDGE_U
 BACK = 128 + SPILL
 SWAP = [(0, 1), (1, 0)]
 BF = jnp.bfloat16
@@ -114,26 +114,35 @@
         rows[at + 12 : at + 12 + BLOCK, :768] = block_z[:BLOCK, 768:]
         note += jnp.broadcast_to(block_z[BLOCK : BLOCK + 1, :EXTRA], (8, EXTRA))
     rows[:, 768:] = jnp.concatenate([note] * (ROWS // 2), axis=0)
+    sent = []
     for q in range(4):
         block[q] = rows[ROWS * q : ROWS * q + ROWS].astype(BF)
-    finish(begin([(block.at[(j // 2) % 4], plane.at[j]) for j in range(MEMBERS)], sems))
-
-
-def relay(hidden, slot, across, lent, beside, v_beside, sems):
+        members = [j for j in range(MEMBERS) if (j // 2) % 4 == q]
+        sent += begin([(block.at[q], plane.at[j]) for j in members], sems.at[pl.ds(8 * q, 8)])
+    finish(sent)
+
+
+def relay(hidden, across, beside, v_beside, sems):
     yh, core = lax.axis_index("yh"), lax.axis_index("core")
     other = pl.ds(pl.multiple_of((yh * 2 + 1 - core) * CHANNELS, 128), CHANNELS)
     part = pl.ds(pl.multiple_of((1 - core) * CHANNELS, 128), CHANNELS)
-    ups = 128 + EDGE_H
+    moves = [(hidden.at[:, other], v_beside.at[0]), (across.at[pl.ds(0, 128), part], v_beside.at[1])]
+    finish(begin(moves, sems))
+    finish(begin([(v_beside, beside)], sems))
+
+
+def relay_edges(slot, lent, beside, v_beside, sems):
+    yh, core = lax.axis_index("yh"), lax.axis_index("core")
+    other = pl.ds(pl.multiple_of((yh * 2 + 1 - core) * CHANNELS, 128), CHANNELS)
+    part = pl.ds(pl.multiple_of((1 - core) * CHANNELS, 128), CHANNELS)
     edge = pl.ds(0, EDGE_H)
     moves = [
-        (hidden.at[:, other], v_beside.at[0, pl.ds(0, 128)]),
-        (slot.at[edge, other], v_beside.at[0, pl.ds(128, EDGE_H)]),
-        (across.at[pl.ds(0, 128), part], v_beside.at[1, pl.ds(0, 128)]),
-        (lent.at[edge, part], v_beside.at[1, pl.ds(128, EDGE_H)]),
+        (slot.at[edge, other], v_beside.at[0, edge]),
+        (lent.at[edge, part], v_beside.at[1, edge]),
     ]
     for i in range(4):
         cut = pl.ds((i % 2) * CHANNELS, CHANNELS)
-        row = pl.ds(ups + EDGE_U * i, EDGE_U)
+        row = pl.ds(EDGE_H + EDGE_U * i, EDGE_U)
         wide = pl.ds(i * CHANNELS, CHANNELS)
         moves.append((slot.at[pl.ds(EDGE_H, EDGE_U), wide], v_beside.at[0, row]))
         moves.append((lent.at[pl.ds(EDGE_H + EDGE_U * (i // 2), EDGE_U), cut], v_beside.at[1, row]))
@@ -152,29 +161,31 @@
 
 
 def convolve(
-    own, slot, across, lent, beside, upstream, up_beside, beyond, kernel, low, high,
+    own, slot, across, lent, beside, edges, upstream, up_beside, beyond, kernel, low, high,
     slope, hidden, parts,
     grads, frames, weights, v_low, v_high, v_slope, v_hidden, v_parts, active, sems,
 ):
     yh, core = lax.axis_index("yh"), lax.axis_index("core")
     part = pl.ds(pl.multiple_of(core * CHANNELS, 128), CHANNELS)
     mine = pl.ds(pl.multiple_of((yh * 2 + core) * CHANNELS, 128), CHANNELS)
-    block = pl.ds(0, 128 + EDGE_H)
+    block, edge = pl.ds(0, 128), pl.ds(0, EDGE_H)
     needed = begin(
         [
             (own.at[:, mine], frames.at[yh * 2 + core, pl.ds(0, 128)]),
             (slot.at[pl.ds(0, EDGE_H), mine], frames.at[yh * 2 + core, pl.ds(128, EDGE_H)]),
             (across.at[pl.ds(0, 128), part], frames.at[(1 - yh) * 2 + core, pl.ds(0, 128)]),
             (lent.at[pl.ds(0, EDGE_H), part], frames.at[(1 - yh) * 2 + core, pl.ds(128, EDGE_H)]),
-            (beside.at[0, block], frames.at[yh * 2 + 1 - core]),
-            (beside.at[1, block], frames.at[(1 - yh) * 2 + 1 - core]),
+            (beside.at[0], frames.at[yh * 2 + 1 - core, block]),
+            (beside.at[1], frames.at[(1 - yh) * 2 + 1 - core, block]),
+            (edges.at[0, edge], frames.at[yh * 2 + 1 - core, pl.ds(128, EDGE_H)]),
+            (edges.at[1, edge], frames.at[(1 - yh) * 2 + 1 - core, pl.ds(128, EDGE_H)]),
             (kernel, weights),
         ],
         sems,
     )
     later = begin(
         group_grads(upstream, across, up_beside, beyond, grads) + [(low, v_low), (high, v_high)],
-        sems.at[pl.ds(8, 8)],
+        sems.at[pl.ds(10, 8)],
     )
     finish(needed)
     v_hidden[:LEFT_H] = frames[0, 128 + EDGE_H - LEFT_H :].astype(F32)
@@ -269,7 +280,7 @@
                         )
             return 0
 
-        lax.fori_loop(0, FRAMES // span, piece, 0)
+        lax.fori_loop(0, FRAMES // span, piece, 0, unroll=True)
     for j in range(MEMBERS):
         rows = [
             jnp.sum(sums[j, :, lanes(tile)], axis=0, keepdims=True)
@@ -288,7 +299,6 @@
     kept, given, v_grad, v_weights, v_slope, ups, weights, wide, total_f, v_kept, v_given, sems,
 ):
     yh, core = lax.axis_index("yh"), lax.axis_index("core")
-    far = 128 + EDGE_H
     edges = [(slot.at[pl.ds(EDGE_H, EDGE_U)], ups.at[yh * 2 + core])]
     for i in range(2):
         edges.append(
@@ -298,7 +308,7 @@
             )
         )
     for i in range(4):
-        row, cut = pl.ds(far + EDGE_U * i, EDGE_U), pl.ds(CHANNELS * i, CHANNELS)
+        row, cut = pl.ds(EDGE_H + EDGE_U * i, EDGE_U), pl.ds(CHANNELS * i, CHANNELS)
         edges.append((beside.at[0, row], ups.at[yh * 2 + 1 - core, :, cut]))
         edges.append((beside.at[1, row], ups.at[(1 - yh) * 2 + 1 - core, :, cut]))
     edges += [
@@ -373,14 +383,13 @@
     finish(out)
 
 
-def pack_z(parts, out, v_parts, v_out, sems):
-    finish(begin([(parts, v_parts)], sems))
+def pack_z(parts, out, sems):
     sums = []
     for q in range(4):
         total = jnp.zeros((ROWS, 896), F32)
         for x in range(4):
             for rep in range(2):
-                total += v_parts[(x * 4 + q) * 2 + rep].astype(F32)
+                total += parts[(x * 4 + q) * 2 + rep].astype(F32)
         sums.append(total)
     taps = [total[:3, 768:] + total[3:6, 768:] for total in sums]
     taps = jnp.concatenate([t[j : j + 1] for t in taps for j in range(3)], axis=1)
@@ -389,37 +398,38 @@
         at = BLOCK * (z % 2)
         halves = [sums[z // 2][at + 12 * side : at + 12 * side + BLOCK, :768] for side in range(2)]
         rows = [jnp.concatenate(halves, axis=1), high, taps - high]
-        v_out[z] = jnp.concatenate(rows, axis=0).astype(BF)
+        out[z] = jnp.concatenate(rows, axis=0).astype(BF)
+
+
+def unpack_z(got, weights, taps, sems):
+    total = got[0].astype(F32)
+    for z in range(1, 8):
+        total += got[z].astype(F32)
+    total = total * (1.0 / math.sqrt(2 * 16384))
+    weights[...] = total[:BLOCK]
+    for peer in range(MEMBERS):
+        taps[peer] = total[6:7] + total[7:8]
+
+
+def arrange(got, out, v_out, sems):
+    for k in range(TAPS):
+        v_out[k : k + 1] = got[k]
     finish(begin([(v_out, out)], sems))
 
 
-def unpack_z(got, weights, taps, v_got, v_weights, v_taps, sems):
-    finish(begin([(got, v_got)], sems))
-    total = v_got[0].astype(F32)
-    for z in range(1, 8):
-        total += v_got[z].astype(F32)
-    total = total * (1.0 / math.sqrt(2 * 16384))
-    v_weights[...] = total[:BLOCK]
-    for peer in range(MEMBERS):
-        v_taps[peer] = total[6:7] + total[7:8]
-    finish(begin([(v_taps, taps), (v_weights, weights)], sems))
-
-
-def arrange(got, out, v_got, v_out, sems):
-    finish(begin([(got, v_got)], sems))
-    for k in range(TAPS):
-        v_out[k : k + 1] = v_got[k]
-    finish(begin([(v_out, out)], sems))
-
-
-def call(kernel, outs, scratch, megabytes, *args, alias=None, flops=200_000_000):
+def call(
+    kernel, outs, scratch, megabytes, *args, alias=None, flops=200_000_000, near=(), near_out=()
+):
+    def space(vmem):
+        return pl.BlockSpec(memory_space=pltpu.VMEM if vmem else pltpu.HBM)
+
     shapes = [jax.ShapeDtypeStruct(shape, dtype) for shape, dtype in outs]
     size = sum(math.prod(s.shape) * s.dtype.itemsize for s in list(args) + shapes)
     return pl.pallas_call(
         kernel,
         out_shape=shapes,
-        in_specs=[pl.BlockSpec(memory_space=pltpu.HBM)] * len(args),
-        out_specs=[pl.BlockSpec(memory_space=pltpu.HBM)] * len(shapes),
+        in_specs=[space(i in near) for i in range(len(args))],
+        out_specs=[space(i in near_out) for i in range(len(shapes))],
         scratch_shapes=[pltpu.VMEM(shape, dtype) for shape, dtype in scratch]
         + [pltpu.SemaphoreType.DMA((48,))],
         input_output_aliases=alias or {},
@@ -464,10 +474,13 @@
         56,
         rows,
     )
+    handed = ((2, 128, CHANNELS), BF)
+    [beside] = call(relay, [handed], [handed], 16, hidden, across, flops=3_000_000_000)
     handed = ((2, HANDED, CHANNELS), BF)
-    [beside] = call(relay, [handed], [handed], 16, hidden, slot, across, lent, flops=30_000_000_000)
+    [edges] = call(relay_edges, [handed], [handed], 16, slot, lent, flops=30_000_000_000)
     rows = lax.all_to_all(plane, PLANE, 0, 0, tiled=True)
     beside = lax.ppermute(beside, "core", SWAP)
+    edges = lax.ppermute(edges, "core", SWAP)
     kernel_f = lax.dynamic_slice_in_dim(
         jnp.pad(conv_kernel, ((0, 1), (0, 0))), quarter * CHANNELS, CHANNELS, 1
     ).astype(F32)
@@ -487,7 +500,7 @@
             sent, slope_f,
         ],
         56,
-        hidden, slot, across, lent, beside, grads, up_beside, beyond, kernel_f, low, high,
+        hidden, slot, across, lent, beside, edges, grads, up_beside, beyond, kernel_f, low, high,
     )
     grad_conv, projection, parts = call(
         backward,
@@ -508,25 +521,30 @@
     [parts] = call(
         pack_z,
         [((8, 8, 1536), BF)],
-        [message, ((8, 8, 1536), BF)],
+        [],
         16,
         parts,
+        near=(0,),
+        near_out=(0,),
     )
     parts = lax.all_to_all(parts, "z", 0, 0, tiled=True)
     weight_grad, taps_all = call(
         unpack_z,
         [((BLOCK, 1536), F32), ((32, 1, 1536), F32)],
-        [((8, 8, 1536), BF), ((BLOCK, 1536), F32), ((32, 1, 1536), F32)],
+        [],
         16,
         parts,
+        near=(0,),
+        near_out=(0, 1),
     )
     taps_all = lax.all_to_all(taps_all, PLANE, 0, 0, tiled=True)
     [kernel_grad] = call(
         arrange,
         [((TAPS, 1536), F32)],
-        [((32, 1, 1536), F32), ((TAPS, 1536), F32)],
+        [((TAPS, 1536), F32)],
         16,
         taps_all,
+        near=(0,),
     )
 
     back = ((2, BACK, CHANNELS), BF)
@@ -539,7 +557,7 @@
             slope_f, ((LONG, CHANNELS), F32), back, back,
         ],
         56,
-        grad_conv, projection, slope, slot, lent, beside, kernel_f,
+        grad_conv, projection, slope, slot, lent, edges, kernel_f,
     )
     got = lax.ppermute(given, "core", SWAP)
     far = jnp.stack(

time: 124 us -> 123 us (level)
    pallas_call x11 -> x12, Pallas kernels: 36.5 us -> 36.3 us  [call(): pl.pallas_call(kernel, out_shape=shapes, in_specs=[space(i in near) for i...]
    unnamed x22 -> x26, local copies, waits for them, and re-layouts: 2.68 us -> 2.62 us
  transfers between devices with their start and end apart: 13 -> 14, of which waited for: 6 -> 6; matrix products, arithmetic and copies ran while one was open for 1% -> 1% of each run, Pallas kernels for 21% -> 21%
where the time goes in v6:
time: 123 us
  starting transfers between devices  47.5 us (39%)
  Pallas kernels  36.3 us (30%)
  waiting for transfers between devices  34.4 us (28%)
  local copies, waits for them, and re-layouts  2.67 us (2%)
    pallas_call x12, Pallas kernels, call(): pl.pallas_call(kernel, out_shape=shapes, in_specs=[space(i in near) for i...  36.3 us
    all_to_all x1, waiting for transfers between devices, body(): parts = lax.all_to_all(parts, PLANE, 0, 0, tiled=True)  12.4 us
    all_to_all x1, starting transfers between devices, body(): rows = lax.all_to_all(plane, PLANE, 0, 0, tiled=True)  9.97 us
    all_to_all x1, starting transfers between devices, body(): rows = lax.all_to_all(rows, 'z', 0, 0, tiled=True)  8.2 us
    all_to_all x1, starting transfers between devices, body(): taps_all = lax.all_to_all(taps_all, PLANE, 0, 0, tiled=True)  6.81 us
    all_to_all x1, waiting for transfers between devices, body(): taps_all = lax.all_to_all(taps_all, PLANE, 0, 0, tiled=True)  6.68 us
    all_to_all x1, waiting for transfers between devices, body(): parts = lax.all_to_all(parts, 'z', 0, 0, tiled=True)  6.59 us
    all_to_all x1, waiting for transfers between devices, body(): rows = lax.all_to_all(plane, PLANE, 0, 0, tiled=True)  6.27 us
  transfers between devices with their start and end apart: 14, of which 6 were waited for; matrix products, arithmetic and copies ran while one was open for 1% of the time, Pallas kernels for 21%

profile of v6, /device:TPU:1, one launch (start us, length us, event | category | flops | bytes accessed | tf_op | source)
XLA Modules:
  0.0 122.6 jit_solution(9840855053105717438)
XLA Ops:
  0.6 0.0 copy-start.7
  0.6 2.6 %shard_map.102 = (bf16[8,8,1536]{2,1,0:T(8,128)(2,1)}, bf16[384,768]{1,0:T(8,128)(2,1)}, bf16[80,1536]{1,0:T(8,128)(2,1)}) custom-call(bf16[6,1536]{1,0:T(8,128)(2,1)} %weights.1, s32[1,8]{1,0:T(1,128)} %durations.1, bf16[128,1536]{1,0:T(8,128)(2,1)} %bitcast.6, bf16[128,1536]{1,0:T(8,128)(2,1)} %bitcast.9), custom_call_target="tpu_custom_call" | custom-call | flops 200000000 | bytes 1837088 | tf_op jit(solution)/shard_map/pallas_call | solution.py:428
  3.3 3.8 %collective-permute-start = (bf16[384,768]{1,0:T(8,128)(2,1)}, bf16[384,768]{1,0:T(8,128)(2,1)S(1)}, u32[]{:S(2)}, u32[]{:S(2)}) collective-permute-start(bf16[384,768]{1,0:T(8,128)(2,1)} %get-tuple-element.20), channel_id=1, source_target_pairs={{0,4},{4,0},{1,5},{5,1},{2,6},{6,2},{3,7},{7,3},{8,12},{12,8},{9,1... | collective-permute-start | bytes 1769480 | tf_op jit(solution)/shard_map/ppermute | solution.py:464
  7.1 0.7 collective-permute-start.3
  7.8 8.2 %all-to-all-start = ((bf16[8,8,1536]{2,1,0:T(8,128)(2,1)}), bf16[8,8,1536]{2,1,0:T(8,128)(2,1)S(1)}, u32[]{:S(2)}, u32[]{:S(2)}) async-start(bf16[8,8,1536]{2,1,0:T(8,128)(2,1)} %get-tuple-element.19), calls=%async_computation | async-start | bytes 393216 | tf_op jit(solution)/shard_map/all_to_all | solution.py:463
  16.0 0.0 collective-permute-done.3.slot
  16.0 0.0 copy-start.4
  16.0 0.7 shard_map.104
  16.7 6.1 %collective-permute-start.4 = (bf16[112,768]{1,0:T(8,128)(2,1)S(1)}, bf16[112,768]{1,0:T(8,128)(2,1)S(1)}, u32[]{:S(2)}, u32[]{:S(2)}) collective-permute-start(bf16[112,768]{1,0:T(8,128)(2,1)S(1)} %shard_map.104), channel_id=1, source_target_pairs={{0,4},{4,0},{1,5},{5,1},{2,6},{6,2},{3,7},{7,3},{8,12},{12,8},{9,1... | collective-permute-start | bytes 516104 | tf_op jit(solution)/shard_map/ppermute | solution.py:468
  22.8 0.0 copy-done.7
  22.8 0.0 collective-permute-start.1
  22.8 1.8 %all-to-all-done.gathered = bf16[8,8,1536]{2,1,0:T(8,128)(2,1)S(1)} async-done(((bf16[8,8,1536]{2,1,0:T(8,128)(2,1)}), bf16[8,8,1536]{2,1,0:T(8,128)(2,1)S(1)}, u32[]{:S(2)}, u32[]{:S(2)}) %all-to-all-start) | async-done | bytes 196640 | tf_op jit(solution)/shard_map/all_to_all | solution.py:463
  24.6 0.0 copy-start.9
  24.6 0.7 copy-done.9
  25.3 2.5 %shard_map.103 = bf16[32,24,896]{2,1,0:T(8,128)(2,1)} custom-call(bf16[8,8,1536]{2,1,0:T(8,128)(2,1)} %copy-done.9), custom_call_target="tpu_custom_call" | custom-call | flops 200000000 | bytes 1572864 | tf_op jit(solution)/shard_map/pallas_call | solution.py:428
  27.8 10.0 %all-to-all-start.1 = ((bf16[32,24,896]{2,1,0:T(8,128)(2,1)}), bf16[32,24,896]{2,1,0:T(8,128)(2,1)S(1)}, u32[]{:S(2)}, u32[]{:S(2)}) async-start(bf16[32,24,896]{2,1,0:T(8,128)(2,1)} %shard_map.103), calls=%async_computation.1 | async-start | bytes 2752512 | tf_op jit(solution)/shard_map/all_to_all | solution.py:481
  37.8 0.0 copy-start.3
  37.8 0.0 collective-permute-done.across
  37.8 0.0 copy-start.2
  37.8 0.3 collective-permute-start.2
  38.1 0.0 collective-permute-done.4.lent
  38.1 0.0 copy-done.4
  38.1 0.0 copy-start.5
  38.1 0.5 shard_map.106
  38.7 0.1 copy-done.5
  38.8 0.0 copy-start.11
  38.8 0.3 collective-permute-start.6
  39.1 0.0 copy-done.2
  39.1 0.0 copy-done.3
  39.1 0.7 shard_map.105
  39.8 0.5 collective-permute-start.5
  40.3 0.0 copy-done.11
  40.3 0.6 fusion.kernel
  40.9 0.0 collective-permute-done.1.up_beside
  40.9 0.0 collective-permute-done.6.edges.beside
  40.9 0.6 collective-permute-done.5.beside
  41.5 0.0 collective-permute-done.2.beyond
  41.5 0.2 copy-done.8
  41.7 0.5 copy-done.10
  42.2 9.5 %shard_map.107 = (f32[560,384]{1,0:T(8,128)}, f32[592,384]{1,0:T(8,128)}, bf16[32,24,896]{2,1,0:T(8,128)(2,1)}) custom-call(bf16[128,1536]{1,0:T(8,128)(2,1)} %bitcast.7, bf16[80,1536]{1,0:T(8,128)(2,1)} %copy-done.4, bf16[384,768]{1,0:T(8,128)(2,1)} %copy-done.2, bf16[112,768]{1,0:T(8,128)(2,1)} %copy-done.5, bf16[2,128,384]{2,1,0:T(8,128)(2,1)} %copy-done.10, ...), custom_call_target="tpu_custom_call" | custom-call | flops 200000000 | bytes 7618560 | tf_op jit(solution)/shard_map/pallas_call | solution.py:428
  51.6 6.3 %all-to-all-done.1.gathered = bf16[32,24,896]{2,1,0:T(8,128)(2,1)S(1)} async-done(((bf16[32,24,896]{2,1,0:T(8,128)(2,1)}), bf16[32,24,896]{2,1,0:T(8,128)(2,1)S(1)}, u32[]{:S(2)}, u32[]{:S(2)}) %all-to-all-start.1) | async-done | bytes 1376288 | tf_op jit(solution)/shard_map/all_to_all | solution.py:481
  57.9 1.1 copy-done
  59.0 7.3 %shard_map.108 = (bf16[512,384]{1,0:T(8,128)(2,1)}, bf16[384,1536]{1,0:T(8,128)(2,1)}, bf16[32,24,896]{2,1,0:T(8,128)(2,1)}) custom-call(bf16[32,24,896]{2,1,0:T(8,128)(2,1)} %copy-done, bf16[384,768]{1,0:T(8,128)(2,1)} %constant.34.clone.low, bf16[384,768]{1,0:T(8,128)(2,1)} %constant.35.clone.high, ...), custom_call_target="tpu_custom_call", output_to_operand_aliasing={{2}: (9, {})} | custom-call | flops 200000000 | bytes 10616832 | tf_op jit(solution)/shard_map/pallas_call | solution.py:428
  66.3 5.1 %all-to-all-start.2 = ((bf16[32,24,896]{2,1,0:T(8,128)(2,1)}), bf16[32,24,896]{2,1,0:T(8,128)(2,1)S(1)}, u32[]{:S(2)}, u32[]{:S(2)}) async-start(bf16[32,24,896]{2,1,0:T(8,128)(2,1)} %get-tuple-element.31), calls=%async_computation.2 | async-start | bytes 2752512 | tf_op jit(solution)/shard_map/all_to_all | solution.py:520
  71.5 7.4 %shard_map.109 = (bf16[2,144,384]{2,1,0:T(8,128)(2,1)}, bf16[2,144,384]{2,1,0:T(8,128)(2,1)}) custom-call(bf16[512,384]{1,0:T(8,128)(2,1)} %get-tuple-element.25.grad_conv, bf16[384,1536]{1,0:T(8,128)(2,1)} %get-tuple-element.26.projection, f32[560,384]{1,0:T(8,128)} %get-tuple-element.22.slope, bf16[80,1536]{1,0:T(8,128)(2,1)} %copy-done.4, ...), custom_call_target="tpu_custom_call" | custom-call | flops 200000000 | bytes 3612672 | tf_op jit(solution)/shard_map/pallas_call | solution.py:428
  78.9 0.0 copy-start.6
  78.9 0.3 collective-permute-start.7
  79.2 12.4 %all-to-all-done.2.parts = bf16[32,24,896]{2,1,0:T(8,128)(2,1)S(1)} async-done(((bf16[32,24,896]{2,1,0:T(8,128)(2,1)}), bf16[32,24,896]{2,1,0:T(8,128)(2,1)S(1)}, u32[]{:S(2)}, u32[]{:S(2)}) %all-to-all-start.2) | async-done | bytes 1376288 | tf_op jit(solution)/shard_map/all_to_all | solution.py:520
  91.6 1.3 %shard_map.111 = bf16[8,8,1536]{2,1,0:T(8,128)(2,1)} custom-call(bf16[32,24,896]{2,1,0:T(8,128)(2,1)S(1)} %all-to-all-done.2.parts), custom_call_target="tpu_custom_call" | custom-call | flops 200000000 | bytes 1572864 | tf_op jit(solution)/shard_map/pallas_call | solution.py:428
  93.0 0.0 copy-start.12
  93.0 0.0 copy-start.1
  93.0 3.5 %all-to-all-start.3 = ((bf16[8,8,1536]{2,1,0:T(8,128)(2,1)}), bf16[8,8,1536]{2,1,0:T(8,128)(2,1)S(1)}, u32[]{:S(2)}, u32[]{:S(2)}) async-start(bf16[8,8,1536]{2,1,0:T(8,128)(2,1)} %shard_map.111), calls=%async_computation.3 | async-start | bytes 393216 | tf_op jit(solution)/shard_map/all_to_all | solution.py:530
  96.5 0.0 copy-done.6
  96.6 0.0 collective-permute-done.7.got
  96.6 1.9 %collective-permute-start.8 = (bf16[2,144,384]{2,1,0:T(8,128)(2,1)S(1)}, bf16[2,144,384]{2,1,0:T(8,128)(2,1)S(1)}, u32[]{:S(2)}, u32[]{:S(2)}) collective-permute-start(bf16[2,144,384]{2,1,0:T(8,128)(2,1)S(1)} %pad_maximum_fusion), channel_id=1, source_target_pairs={{0,4},{4,0},{1,5},{5,1},{2,6},{6,2},{3,7},{7,3},{8,12},{12,8},{9,1... | collective-permute-start | bytes 663560 | tf_op jit(solution)/shard_map/ppermute | solution.py:566
  98.5 6.6 %all-to-all-done.3.got = bf16[8,8,1536]{2,1,0:T(8,128)(2,1)S(1)} async-done(((bf16[8,8,1536]{2,1,0:T(8,128)(2,1)}), bf16[8,8,1536]{2,1,0:T(8,128)(2,1)S(1)}, u32[]{:S(2)}, u32[]{:S(2)}) %all-to-all-start.3) | async-done | bytes 196640 | tf_op jit(solution)/shard_map/all_to_all | solution.py:530
  105.1 1.2 shard_map.112
  106.3 6.8 %all-to-all-start.4 = ((f32[32,1,1536]{2,1,0:T(1,128)}), f32[32,1,1536]{2,1,0:T(1,128)S(1)}, u32[]{:S(2)}, u32[]{:S(2)}) async-start(f32[32,1,1536]{2,1,0:T(1,128)} %get-tuple-element.33), calls=%async_computation.4 | async-start | bytes 393216 | tf_op jit(solution)/shard_map/all_to_all | solution.py:540
  113.1 0.0 copy-done.12
  113.1 0.0 collective-permute-done.8.far
  113.1 0.0 copy-done.1
  113.1 1.4 %shard_map.110 = (bf16[128,1536]{1,0:T(8,128)(2,1)}, f32[8,1536]{1,0:T(8,128)}) custom-call(bf16[2,144,384]{2,1,0:T(8,128)(2,1)S(1)} %copy-done.6, bf16[2,144,384]{2,1,0:T(8,128)(2,1)S(1)} %collective-permute-done.7.got, bf16[2,144,384]{2,1,0:T(8,128)(2,1)S(1)} %collective-permute-done.8.far, bf16[32,24,896]{2,1,0:T(8,128)(2,1)S(1)} %copy-done.1, ...), custom_call_target="tpu_custom_call" | custom-call | flops 200000000 | bytes 2486272 | tf_op jit(solution)/shard_map/pallas_call | solution.py:428
  114.6 6.7 %all-to-all-done.4.got = f32[32,1,1536]{2,1,0:T(1,128)S(1)} async-done(((f32[32,1,1536]{2,1,0:T(1,128)}), f32[32,1,1536]{2,1,0:T(1,128)S(1)}, u32[]{:S(2)}, u32[]{:S(2)}) %all-to-all-start.4) | async-done | bytes 196640 | tf_op jit(solution)/shard_map/all_to_all | solution.py:540
  121.3 1.1 shard_map.113
  (9 shorter events, 0.1 us)
Async XLA Ops:
  0.6 22.2 %copy-start.7 = (bf16[1,128,1536]{2,1,0:T(8,128)(2,1)S(1)}, bf16[1,128,1536]{2,1,0:T(8,128)(2,1)}, u32[]{:S(2)}) copy-start(bf16[1,128,1536]{2,1,0:T(8,128)(2,1)} %param.8) | copy-start | bytes 1179652
  3.3 34.5 %collective-permute-start = (bf16[384,768]{1,0:T(8,128)(2,1)}, bf16[384,768]{1,0:T(8,128)(2,1)S(1)}, u32[]{:S(2)}, u32[]{:S(2)}) collective-permute-start(bf16[384,768]{1,0:T(8,128)(2,1)} %get-tuple-element.20), channel_id=1, source_target_pairs={{0,4},{4,0},{1,5},{5,1},{2,6},{6,2},{3,7},{7,3},{8,12},{12,8},{9,1... | collective-permute-start | bytes 1769480 | tf_op jit(solution)/shard_map/ppermute | solution.py:464
  7.1 8.9 %collective-permute-start.3 = (bf16[80,1536]{1,0:T(8,128)(2,1)}, bf16[80,1536]{1,0:T(8,128)(2,1)S(1)}, u32[]{:S(2)}, u32[]{:S(2)}) collective-permute-start(bf16[80,1536]{1,0:T(8,128)(2,1)} %get-tuple-element.21), channel_id=1, source_target_pairs={{6,8},{14,16},{22,24},{30,32},{38,40},{46,48},{54,56},{62,64},{70,... | collective-permute-start | bytes 737288 | tf_op jit(solution)/shard_map/ppermute | solution.py:462
  7.8 16.8 %all-to-all-start = ((bf16[8,8,1536]{2,1,0:T(8,128)(2,1)}), bf16[8,8,1536]{2,1,0:T(8,128)(2,1)S(1)}, u32[]{:S(2)}, u32[]{:S(2)}) async-start(bf16[8,8,1536]{2,1,0:T(8,128)(2,1)} %get-tuple-element.19), calls=%async_computation | async-start | bytes 393216 | tf_op jit(solution)/shard_map/all_to_all | solution.py:463
  16.0 22.1 %copy-start.4 = (bf16[80,1536]{1,0:T(8,128)(2,1)}, bf16[80,1536]{1,0:T(8,128)(2,1)S(1)}, u32[]{:S(2)}) copy-start(bf16[80,1536]{1,0:T(8,128)(2,1)S(1)} %collective-permute-done.3.slot) | copy-start | bytes 737284
  16.7 21.4 %collective-permute-start.4 = (bf16[112,768]{1,0:T(8,128)(2,1)S(1)}, bf16[112,768]{1,0:T(8,128)(2,1)S(1)}, u32[]{:S(2)}, u32[]{:S(2)}) collective-permute-start(bf16[112,768]{1,0:T(8,128)(2,1)S(1)} %shard_map.104), channel_id=1, source_target_pairs={{0,4},{4,0},{1,5},{5,1},{2,6},{6,2},{3,7},{7,3},{8,12},{12,8},{9,1... | collective-permute-start | bytes 516104 | tf_op jit(solution)/shard_map/ppermute | solution.py:468
  22.8 18.1 %collective-permute-start.1 = (bf16[128,1536]{1,0:T(8,128)(2,1)S(1)}, bf16[128,1536]{1,0:T(8,128)(2,1)S(1)}, u32[]{:S(2)}, u32[]{:S(2)}) collective-permute-start(bf16[128,1536]{1,0:T(8,128)(2,1)S(1)} %bitcast.12), channel_id=1, source_target_pairs={{0,2},{2,0},{1,3},{3,1},{4,6},{6,4},{5,7},{7,5},{8,10},{10,8},{9,1... | collective-permute-start | bytes 1179656 | tf_op jit(solution)/shard_map/ppermute | solution.py:465
  24.6 0.7 copy-start.9
  27.8 30.1 %all-to-all-start.1 = ((bf16[32,24,896]{2,1,0:T(8,128)(2,1)}), bf16[32,24,896]{2,1,0:T(8,128)(2,1)S(1)}, u32[]{:S(2)}, u32[]{:S(2)}) async-start(bf16[32,24,896]{2,1,0:T(8,128)(2,1)} %shard_map.103), calls=%async_computation.1 | async-start | bytes 2752512 | tf_op jit(solution)/shard_map/all_to_all | solution.py:481
  37.8 1.3 %copy-start.3 = (bf16[1,128,1536]{2,1,0:T(8,128)(2,1)S(1)}, bf16[1,128,1536]{2,1,0:T(8,128)(2,1)}, u32[]{:S(2)}) copy-start(bf16[1,128,1536]{2,1,0:T(8,128)(2,1)} %param.7) | copy-start | bytes 1179652
  37.8 1.3 %copy-start.2 = (bf16[384,768]{1,0:T(8,128)(2,1)}, bf16[384,768]{1,0:T(8,128)(2,1)S(1)}, u32[]{:S(2)}) copy-start(bf16[384,768]{1,0:T(8,128)(2,1)S(1)} %collective-permute-done.across) | copy-start | bytes 1769476
  37.8 3.7 %collective-permute-start.2 = (bf16[384,768]{1,0:T(8,128)(2,1)S(1)}, bf16[384,768]{1,0:T(8,128)(2,1)}, u32[]{:S(2)}, u32[]{:S(2)}) collective-permute-start(bf16[384,768]{1,0:T(8,128)(2,1)S(1)} %collective-permute-done.across), channel_id=1, source_target_pairs={{0,2},{2,0},{1,3},{3,1},{4,6},{6,4},{5,7},{7,5},{8,10},{10,8},{9,1... | collective-permute-start | bytes 1769480 | tf_op jit(solution)/shard_map/ppermute | solution.py:466
  38.1 0.7 copy-start.5
  38.8 1.5 %copy-start.11 = (bf16[31,1536]{1,0:T(8,128)(2,1)S(1)}, bf16[31,1536]{1,0:T(8,128)(2,1)}, u32[]{:S(2)}) copy-start(bf16[31,1536]{1,0:T(8,128)(2,1)} %param.10) | copy-start | bytes 285700
  38.8 2.1 %collective-permute-start.6 = (bf16[2,176,384]{2,1,0:T(8,128)(2,1)S(1)}, bf16[2,176,384]{2,1,0:T(8,128)(2,1)}, u32[]{:S(2)}, u32[]{:S(2)}) collective-permute-start(bf16[2,176,384]{2,1,0:T(8,128)(2,1)S(1)} %shard_map.106), channel_id=1, source_target_pairs={{0,2},{2,0},{1,3},{3,1},{4,6},{6,4},{5,7},{7,5},{8,10},{10,8},{9,1... | collective-permute-start | bytes 811016 | tf_op jit(solution)/shard_map/ppermute | solution.py:483
  39.8 1.7 %collective-permute-start.5 = (bf16[2,128,384]{2,1,0:T(8,128)(2,1)S(1)}, bf16[2,128,384]{2,1,0:T(8,128)(2,1)S(1)}, u32[]{:S(2)}, u32[]{:S(2)}) collective-permute-start(bf16[2,128,384]{2,1,0:T(8,128)(2,1)S(1)} %shard_map.105), channel_id=1, source_target_pairs={{0,2},{2,0},{1,3},{3,1},{4,6},{6,4},{5,7},{7,5},{8,10},{10,8},{9,1... | collective-permute-start | bytes 589832 | tf_op jit(solution)/shard_map/ppermute | solution.py:482
  40.9 0.7 copy-start.8
  41.5 0.7 copy-start.10
  57.9 1.1 copy-start
  66.3 25.3 %all-to-all-start.2 = ((bf16[32,24,896]{2,1,0:T(8,128)(2,1)}), bf16[32,24,896]{2,1,0:T(8,128)(2,1)S(1)}, u32[]{:S(2)}, u32[]{:S(2)}) async-start(bf16[32,24,896]{2,1,0:T(8,128)(2,1)} %get-tuple-element.31), calls=%async_computation.2 | async-start | bytes 2752512 | tf_op jit(solution)/shard_map/all_to_all | solution.py:520
  78.9 17.7 %copy-start.6 = (bf16[2,144,384]{2,1,0:T(8,128)(2,1)S(1)}, bf16[2,144,384]{2,1,0:T(8,128)(2,1)}, u32[]{:S(2)}) copy-start(bf16[2,144,384]{2,1,0:T(8,128)(2,1)} %get-tuple-element.27.kept) | copy-start | bytes 663556
  78.9 17.7 %collective-permute-start.7 = (bf16[2,144,384]{2,1,0:T(8,128)(2,1)}, bf16[2,144,384]{2,1,0:T(8,128)(2,1)S(1)}, u32[]{:S(2)}, u32[]{:S(2)}) collective-permute-start(bf16[2,144,384]{2,1,0:T(8,128)(2,1)} %get-tuple-element.28), channel_id=1, source_target_pairs={{0,2},{2,0},{1,3},{3,1},{4,6},{6,4},{5,7},{7,5},{8,10},{10,8},{9,1... | collective-permute-start | bytes 663560 | tf_op jit(solution)/shard_map/ppermute | solution.py:562
  93.0 20.1 %copy-start.12 = (s32[1,8]{1,0:T(1,128)S(1)}, s32[1,8]{1,0:T(1,128)}, u32[]{:S(2)}) copy-start(s32[1,8]{1,0:T(1,128)} %durations.1) | copy-start | bytes 100
  93.0 20.2 %copy-start.1 = (bf16[32,24,896]{2,1,0:T(8,128)(2,1)S(1)}, bf16[32,24,896]{2,1,0:T(8,128)(2,1)}, u32[]{:S(2)}) copy-start(bf16[32,24,896]{2,1,0:T(8,128)(2,1)} %copy-done) | copy-start | bytes 4128772
  93.0 12.1 %all-to-all-start.3 = ((bf16[8,8,1536]{2,1,0:T(8,128)(2,1)}), bf16[8,8,1536]{2,1,0:T(8,128)(2,1)S(1)}, u32[]{:S(2)}, u32[]{:S(2)}) async-start(bf16[8,8,1536]{2,1,0:T(8,128)(2,1)} %shard_map.111), calls=%async_computation.3 | async-start | bytes 393216 | tf_op jit(solution)/shard_map/all_to_all | solution.py:530
  96.6 16.5 %collective-permute-start.8 = (bf16[2,144,384]{2,1,0:T(8,128)(2,1)S(1)}, bf16[2,144,384]{2,1,0:T(8,128)(2,1)S(1)}, u32[]{:S(2)}, u32[]{:S(2)}) collective-permute-start(bf16[2,144,384]{2,1,0:T(8,128)(2,1)S(1)} %pad_maximum_fusion), channel_id=1, source_target_pairs={{0,4},{4,0},{1,5},{5,1},{2,6},{6,2},{3,7},{7,3},{8,12},{12,8},{9,1... | collective-permute-start | bytes 663560 | tf_op jit(solution)/shard_map/ppermute | solution.py:566
  106.3 15.0 %all-to-all-start.4 = ((f32[32,1,1536]{2,1,0:T(1,128)}), f32[32,1,1536]{2,1,0:T(1,128)S(1)}, u32[]{:S(2)}, u32[]{:S(2)}) async-start(f32[32,1,1536]{2,1,0:T(1,128)} %get-tuple-element.33), calls=%async_computation.4 | async-start | bytes 393216 | tf_op jit(solution)/shard_map/all_to_all | solution.py:540

commit v7 on v6

--- a/solution.py
+++ b/solution.py
@@ -16,7 +16,7 @@
 QUARTERS = 4
 BLOCK = 6
 EXTRA = 128
-MEMBERS, ROWS = 32, 24
+MEMBERS, ROWS, LANES = 32, 8, 2304
 MESSAGE = MEMBERS * ROWS
 FRAMES, CHANNELS, TAPS = 512, 384, 31
 EDGE_H, EDGE_U, SPILL = 48, 32, 16
@@ -31,13 +31,16 @@
 F32 = jnp.float32
 
 
-def placement(side):
+def placement(part):
     out = np.zeros((CHANNELS, MESSAGE), np.float32)
     for zl in range(2):
         for member in range(MEMBERS):
             for r in range(BLOCK):
-                row = (zl * MEMBERS + member) * BLOCK + r
-                out[row, member * ROWS + 12 * side + zl * BLOCK + r] = 1
+                row, i = (zl * MEMBERS + member) * BLOCK + r, zl * BLOCK + r
+                if part == 0 and i < ROWS:
+                    out[row, member * ROWS + i] = 1
+                if part > 0 and i >= ROWS:
+                    out[row, member * ROWS + 2 * (i - ROWS) + part - 1] = 1
     return jnp.asarray(out, BF)
 
 
@@ -104,17 +107,23 @@
     finish(begin([(v_out, out)], sems))
 
 
-def pack(gathered, plane, rows, got, block, sems):
+def pack(gathered, plane, note_out, rows, got, block, v_note, sems):
     finish(begin([(gathered, got)], sems))
     note = jnp.zeros((8, EXTRA), F32)
     for z in range(8):
         block_z = got[z].astype(F32)
-        at = ROWS * (z // 2) + BLOCK * (z % 2)
-        rows[at : at + BLOCK, :768] = block_z[:BLOCK, :768]
-        rows[at + 12 : at + 12 + BLOCK, :768] = block_z[:BLOCK, 768:]
+        for r in range(BLOCK):
+            i = BLOCK * (z % 2) + r
+            at = ROWS * (z // 2)
+            if i < ROWS:
+                rows[at + i : at + i + 1, :1536] = block_z[r : r + 1]
+            else:
+                for h in range(2):
+                    to = at + 2 * (i - ROWS) + h
+                    rows[to : to + 1, 1536:] = block_z[r : r + 1, 768 * h : 768 * h + 768]
         note += jnp.broadcast_to(block_z[BLOCK : BLOCK + 1, :EXTRA], (8, EXTRA))
-    rows[:, 768:] = jnp.concatenate([note] * (ROWS // 2), axis=0)
-    sent = []
+    v_note[...] = note
+    sent = begin([(v_note, note_out)], sems.at[pl.ds(32, 1)])
     for q in range(4):
         block[q] = rows[ROWS * q : ROWS * q + ROWS].astype(BF)
         members = [j for j in range(MEMBERS) if (j // 2) % 4 == q]
@@ -161,9 +170,9 @@
 
 
 def convolve(
-    own, slot, across, lent, beside, edges, upstream, up_beside, beyond, kernel, low, high,
+    own, slot, across, lent, beside, edges, upstream, up_beside, beyond, kernel, whole, low, high,
     slope, hidden, parts,
-    grads, frames, weights, v_low, v_high, v_slope, v_hidden, v_parts, active, sems,
+    grads, frames, weights, v_whole, v_low, v_high, v_slope, v_hidden, v_parts, active, sems,
 ):
     yh, core = lax.axis_index("yh"), lax.axis_index("core")
     part = pl.ds(pl.multiple_of(core * CHANNELS, 128), CHANNELS)
@@ -184,8 +193,8 @@
         sems,
     )
     later = begin(
-        group_grads(upstream, across, up_beside, beyond, grads) + [(low, v_low), (high, v_high)],
-        sems.at[pl.ds(10, 8)],
+        group_grads(upstream, across, up_beside, beyond, grads) + [(whole, v_whole), (low, v_low), (high, v_high)],
+        sems.at[pl.ds(10, 9)],
     )
     finish(needed)
     v_hidden[:LEFT_H] = frames[0, 128 + EDGE_H - LEFT_H :].astype(F32)
@@ -214,28 +223,31 @@
     out = begin([(v_slope, slope), (v_hidden, hidden)], sems)
     finish(later)
     acts = active[LEFT_U : LEFT_U + FRAMES].astype(BF)
-    product = jnp.zeros((MESSAGE, 768), F32)
-    for side, spot in enumerate((v_low, v_high)):
+    def outer(spot, cut):
         columns = jnp.dot(acts, spot[...], preferred_element_type=F32).astype(BF)
-        product += lax.dot_general(
+        return lax.dot_general(
             columns,
-            grads[:, :, 768 * side : 768 * side + 768].reshape(FRAMES, 768),
+            grads[:, :, cut].reshape(FRAMES, -1),
             (((0,), (0,)), ((), ())),
             preferred_element_type=F32,
         )
+
+    product = outer(v_whole, slice(0, 1536))
+    halves = outer(v_low, slice(0, 768)) + outer(v_high, slice(768, 1536))
     for j in range(MEMBERS):
-        v_parts[j] = product[ROWS * j : ROWS * j + ROWS].astype(BF)
-    finish(begin([(v_parts, parts.at[:, :, pl.ds(0, 768)])], sems.at[pl.ds(2, 1)]))
+        v_parts[j, :, :1536] = product[ROWS * j : ROWS * j + ROWS].astype(BF)
+        v_parts[j, :, 1536:] = halves[ROWS * j : ROWS * j + ROWS].astype(BF)
+    finish(begin([(v_parts, parts.at[:, :, pl.ds(0, LANES)])], sems.at[pl.ds(2, 1)]))
     finish(out)
 
 
 def backward(
-    gathered, low, high, upstream, across, up_beside, beyond, slope, hidden, parts,
+    gathered, notes, whole, low, high, upstream, across, up_beside, beyond, slope, hidden, parts,
     grad_conv, projection, message,
-    got, v_low, v_high, grads, v_slope, v_hidden, v_grad, v_grad_f, v_taps, sums, v_weights, sems,
+    got, v_note, v_whole, v_low, v_high, grads, v_slope, v_hidden, v_grad, v_grad_f, v_taps, sums, v_weights, sems,
 ):
     needed = begin(
-        [(gathered.at[:, :, pl.ds(0, 768)], got), (low, v_low), (high, v_high)], sems
+        [(gathered, got), (whole, v_whole), (low, v_low), (high, v_high), (notes, v_note)], sems
     )
     later = begin(
         group_grads(upstream, across, up_beside, beyond, grads), sems.at[pl.ds(5, 6)]
@@ -244,11 +256,13 @@
         [(slope.at[pl.ds(LEFT_U, FRAMES)], v_slope), (hidden, v_hidden)], sems.at[pl.ds(13, 2)]
     )
     finish(needed)
-    rows = got[...].reshape(MESSAGE, 768)
+    rows = got[:, :, :1536].reshape(MESSAGE, 1536)
+    halves = got[:, :, 1536:].reshape(MESSAGE, 768)
     for side, spot in enumerate((v_low, v_high)):
-        v_weights[:, 768 * side : 768 * side + 768] = jnp.dot(
-            spot[...], rows, preferred_element_type=F32
-        ).astype(BF)
+        cut = slice(768 * side, 768 * side + 768)
+        value = jnp.dot(v_whole[...], rows[:, cut], preferred_element_type=F32)
+        value += jnp.dot(spot[...], halves, preferred_element_type=F32)
+        v_weights[:, cut] = value.astype(BF)
     finish(later)
     value = lax.dot_general(
         grads[...].reshape(FRAMES, 1536),
@@ -288,9 +302,9 @@
         ]
         rows = jnp.concatenate(rows, axis=0)
         high_part = rows.astype(BF).astype(F32)
-        rows = [high_part, rows - high_part, jnp.zeros((ROWS - 6, 128), F32)]
+        rows = [high_part, rows - high_part, v_note[:1], jnp.zeros((ROWS - 7, 128), F32)]
         v_taps[j] = jnp.concatenate(rows, axis=0).astype(BF)
-    finish(begin([(v_taps, message.at[:, :, pl.ds(768, EXTRA)])], sems.at[pl.ds(3, 1)]))
+    finish(begin([(v_taps, message.at[:, :, pl.ds(LANES, EXTRA)])], sems.at[pl.ds(3, 1)]))
     finish(out)
 
 
@@ -357,7 +371,7 @@
     yh, core = lax.axis_index("yh"), lax.axis_index("core")
     sources = [(kept.at[yh], yh, core), (got.at[yh], yh, 1 - core)]
     sources += [(far.at[0], 1 - yh, core), (far.at[1], 1 - yh, 1 - core)]
-    moves = [(lengths, v_lengths), (gathered.at[:, pl.ds(0, 16), pl.ds(768, EXTRA)], notes)]
+    moves = [(lengths, v_lengths), (gathered.at[:, :, pl.ds(LANES, EXTRA)], notes)]
     for source, a, b in sources:
         cut = pl.ds(pl.multiple_of((a * 2 + b) * CHANNELS, 128), CHANNELS)
         moves.append((source, frames.at[:, cut]))
@@ -370,7 +384,7 @@
     for member in range(MEMBERS):
         block = lane * 16 + member // 2
         earlier = (block < place * 4 + mine) & (lane < 8) & (lax.axis_index("rep") == member % 2)
-        start += jnp.where(earlier, notes[member, :8].astype(F32), 0.0)
+        start += jnp.where(earlier, notes[member, 6:7].astype(F32), 0.0)
     start = jnp.sum(start, axis=1, keepdims=True) - (place * FRAMES + mine * 128).astype(F32)
     gloss_id = lax.broadcasted_iota(jnp.int32, (8, EXTRA), 0)
     length = v_lengths[...]
@@ -386,18 +400,23 @@
 def pack_z(parts, out, sems):
     sums = []
     for q in range(4):
-        total = jnp.zeros((ROWS, 896), F32)
+        total = jnp.zeros((ROWS, LANES + EXTRA), F32)
         for x in range(4):
             for rep in range(2):
                 total += parts[(x * 4 + q) * 2 + rep].astype(F32)
         sums.append(total)
-    taps = [total[:3, 768:] + total[3:6, 768:] for total in sums]
+    taps = [total[:3, LANES:] + total[3:6, LANES:] for total in sums]
     taps = jnp.concatenate([t[j : j + 1] for t in taps for j in range(3)], axis=1)
     high = taps.astype(BF).astype(F32)
     for z in range(8):
-        at = BLOCK * (z % 2)
-        halves = [sums[z // 2][at + 12 * side : at + 12 * side + BLOCK, :768] for side in range(2)]
-        rows = [jnp.concatenate(halves, axis=1), high, taps - high]
+        total = sums[z // 2]
+        rows = [total[:BLOCK, :1536]]
+        if z % 2:
+            rows = [total[BLOCK:, :1536]]
+            for i in range(0, ROWS, 2):
+                halves = [total[i + h : i + h + 1, 1536:LANES] for h in range(2)]
+                rows.append(jnp.concatenate(halves, axis=1))
+        rows += [high, taps - high]
         out[z] = jnp.concatenate(rows, axis=0).astype(BF)
 
 
@@ -465,12 +484,13 @@
     up_beside = lax.ppermute(grads, "core", SWAP)
     beyond = lax.ppermute(across, "core", SWAP)
     [lent] = call(lend, [((SHARE, 768), BF)], [((SHARE, 768), BF)], 16, slot)
-    lent = lax.ppermute(lent, "yh", SWAP)
-    message = ((MEMBERS, ROWS, 768 + EXTRA), BF)
-    [plane] = call(
+    lent = lax.ppermute(lent, GROUP, [(0, 2), (3, 1)])
+    message = ((MEMBERS, ROWS, LANES + EXTRA), BF)
+    note = ((8, EXTRA), F32)
+    plane, notes = call(
         pack,
-        [message],
-        [((4 * ROWS, 768 + EXTRA), F32), ((8, 8, 1536), BF), ((4, ROWS, 768 + EXTRA), BF)],
+        [((MEMBERS, ROWS, LANES), BF), note],
+        [((4 * ROWS, LANES), F32), ((8, 8, 1536), BF), ((4, ROWS, LANES), BF), note],
         56,
         rows,
     )
@@ -485,22 +505,22 @@
         jnp.pad(conv_kernel, ((0, 1), (0, 0))), quarter * CHANNELS, CHANNELS, 1
     ).astype(F32)
     spot = ((CHANNELS, MESSAGE), BF)
-    low, high = placement(0), placement(1)
+    spots = [placement(part) for part in range(3)]
     frames_f = ((FRAMES, CHANNELS), F32)
     wide_f = ((LEFT_H + FRAMES + EDGE_H, CHANNELS), F32)
     slope_f = ((WIDE, CHANNELS), F32)
     all_grads = ((4, 128, 1536), BF)
-    sent = ((MEMBERS, ROWS, 768), BF)
+    sent = ((MEMBERS, ROWS, LANES), BF)
     kernel_shape = ((TAPS + 1, CHANNELS), F32)
     slope, hidden_f, parts = call(
         convolve,
         [slope_f, wide_f, message],
         [
-            all_grads, ((4, 128 + EDGE_H, CHANNELS), BF), kernel_shape, spot, spot, slope_f, wide_f,
+            all_grads, ((4, 128 + EDGE_H, CHANNELS), BF), kernel_shape, spot, spot, spot, slope_f, wide_f,
             sent, slope_f,
         ],
         56,
-        hidden, slot, across, lent, beside, edges, grads, up_beside, beyond, kernel_f, low, high,
+        hidden, slot, across, lent, beside, edges, grads, up_beside, beyond, kernel_f, *spots,
     )
     grad_conv, projection, parts = call(
         backward,
@@ -508,16 +528,16 @@
             ((FRAMES, CHANNELS), BF), ((CHANNELS, 1536), BF), message,
         ],
         [
-            sent, spot, spot, all_grads, frames_f, wide_f, ((FRAMES, CHANNELS), BF), frames_f,
+            sent, note, spot, spot, spot, all_grads, frames_f, wide_f, ((FRAMES, CHANNELS), BF), frames_f,
             ((MEMBERS, ROWS, EXTRA), BF), ((TAPS + 1, 8, CHANNELS), F32),
             ((CHANNELS, 1536), BF),
         ],
         56,
-        rows, low, high, grads, across, up_beside, beyond, slope, hidden_f, parts,
-        alias={9: 2},
-    )
-
-    parts = lax.all_to_all(parts, PLANE, 0, 0, tiled=True)
+        rows, notes, *spots, grads, across, up_beside, beyond, slope, hidden_f, parts,
+        alias={11: 2},
+    )
+
+    summed = parts = lax.all_to_all(parts, PLANE, 0, 0, tiled=True)
     [parts] = call(
         pack_z,
         [((8, 8, 1536), BF)],
@@ -568,11 +588,11 @@
         settle,
         [((128, 1536), BF), ((8, 1536), F32)],
         [
-            ((BACK, 1536), BF), ((MEMBERS, 16, EXTRA), BF), ((8, EXTRA), F32),
+            ((BACK, 1536), BF), ((MEMBERS, ROWS, EXTRA), BF), ((8, EXTRA), F32),
             ((8, 1536), F32),
         ],
         16,
-        kept, got, far, rows, lengths,
+        kept, got, far, summed, lengths,
     )
     return (frame_grad[None], gloss[None], weight_grad, kernel_grad)
 

time: 123 us -> 119 us (0.967)
  waiting for transfers between devices: 34.4 us -> 31.8 us
  starting transfers between devices: 47.5 us -> 46.2 us
    ppermute x1, starting transfers between devices: 6.07 us -> 1.29 us  [body(): lent = lax.ppermute(lent, GROUP, [(0, 2), (3, 1)])]
    ppermute x1, starting transfers between devices: 0.01 us -> 4.26 us  [body(): up_beside = lax.ppermute(grads, 'core', SWAP)]
    all_to_all x1, waiting for transfers between devices: 6.27 us -> 4.32 us  [body(): rows = lax.all_to_all(plane, PLANE, 0, 0, tiled=True)]
    all_to_all x1, waiting for transfers between devices: 12.4 us -> 11.1 us  [body(): summed = parts = lax.all_to_all(parts, PLANE, 0, 0, tiled=True)]
    unnamed x26 -> x24, local copies, waits for them, and re-layouts: 2.62 us -> 3.34 us
where the time goes in v7:
time: 119 us; the launch traced here: 118 us
  starting transfers between devices  46.2 us (39%)
  Pallas kernels  35.3 us (30%)
  waiting for transfers between devices  31.8 us (27%)
  local copies, waits for them, and re-layouts  3.39 us (3%)
    pallas_call x12, Pallas kernels, call(): pl.pallas_call(kernel, out_shape=shapes, in_specs=[space(i in near) for i...  35.3 us
    all_to_all x1, waiting for transfers between devices, body(): summed = parts = lax.all_to_all(parts, PLANE, 0, 0, tiled=True)  11.1 us
    all_to_all x1, starting transfers between devices, body(): rows = lax.all_to_all(plane, PLANE, 0, 0, tiled=True)  9.96 us
    all_to_all x1, starting transfers between devices, body(): rows = lax.all_to_all(rows, 'z', 0, 0, tiled=True)  8.2 us
    all_to_all x1, waiting for transfers between devices, body(): parts = lax.all_to_all(parts, 'z', 0, 0, tiled=True)  6.73 us
    all_to_all x1, waiting for transfers between devices, body(): taps_all = lax.all_to_all(taps_all, PLANE, 0, 0, tiled=True)  6.69 us
    all_to_all x1, starting transfers between devices, body(): taps_all = lax.all_to_all(taps_all, PLANE, 0, 0, tiled=True)  6.53 us
    all_to_all x1, starting transfers between devices, body(): summed = parts = lax.all_to_all(parts, PLANE, 0, 0, tiled=True)  4.96 us
  transfers between devices with their start and end apart: 14, of which 6 were waited for; matrix products, arithmetic and copies ran while one was open for 1% of the time, Pallas kernels for 21%

profile of v7, /device:TPU:1, one launch (start us, length us, event | category | flops | bytes accessed | tf_op | source)
XLA Modules:
  0.0 118.4 jit_solution(6877448500352971927)
XLA Ops:
  0.6 0.0 copy-start.6
  0.6 2.6 %shard_map.111 = (bf16[8,8,1536]{2,1,0:T(8,128)(2,1)}, bf16[384,768]{1,0:T(8,128)(2,1)}, bf16[80,1536]{1,0:T(8,128)(2,1)}) custom-call(bf16[6,1536]{1,0:T(8,128)(2,1)} %weights.1, s32[1,8]{1,0:T(1,128)} %durations.1, bf16[128,1536]{1,0:T(8,128)(2,1)} %bitcast.6, bf16[128,1536]{1,0:T(8,128)(2,1)} %bitcast.9), custom_call_target="tpu_custom_call" | custom-call | flops 200000000 | bytes 1837088 | tf_op jit(solution)/shard_map/pallas_call | solution.py:447
  3.3 3.8 %collective-permute-start = (bf16[384,768]{1,0:T(8,128)(2,1)}, bf16[384,768]{1,0:T(8,128)(2,1)S(1)}, u32[]{:S(2)}, u32[]{:S(2)}) collective-permute-start(bf16[384,768]{1,0:T(8,128)(2,1)} %get-tuple-element.24), channel_id=1, source_target_pairs={{0,4},{4,0},{1,5},{5,1},{2,6},{6,2},{3,7},{7,3},{8,12},{12,8},{9,1... | collective-permute-start | bytes 1769480 | tf_op jit(solution)/shard_map/ppermute | solution.py:483
  7.1 0.7 collective-permute-start.3
  7.8 8.2 %all-to-all-start = ((bf16[8,8,1536]{2,1,0:T(8,128)(2,1)}), bf16[8,8,1536]{2,1,0:T(8,128)(2,1)S(1)}, u32[]{:S(2)}, u32[]{:S(2)}) async-start(bf16[8,8,1536]{2,1,0:T(8,128)(2,1)} %get-tuple-element.21), calls=%async_computation | async-start | bytes 393216 | tf_op jit(solution)/shard_map/all_to_all | solution.py:482
  16.0 0.0 collective-permute-done.3.slot
  16.0 0.0 copy-start.2
  16.0 0.7 shard_map.113
  16.7 1.3 %collective-permute-start.4 = (bf16[112,768]{1,0:T(8,128)(2,1)S(1)}, bf16[112,768]{1,0:T(8,128)(2,1)S(1)}, u32[]{:S(2)}, u32[]{:S(2)}) collective-permute-start(bf16[112,768]{1,0:T(8,128)(2,1)S(1)} %shard_map.113), channel_id=1, source_target_pairs={{0,4},{6,2},{1,5},{7,3},{8,12},{14,10},{9,13},{15,11},{16,20},{22,... | collective-permute-start | bytes 516104 | tf_op jit(solution)/shard_map/ppermute | solution.py:487
  18.0 0.0 copy-done.6
  18.0 4.3 %collective-permute-start.1 = (bf16[128,1536]{1,0:T(8,128)(2,1)S(1)}, bf16[128,1536]{1,0:T(8,128)(2,1)}, u32[]{:S(2)}, u32[]{:S(2)}) collective-permute-start(bf16[128,1536]{1,0:T(8,128)(2,1)S(1)} %bitcast.12), channel_id=1, source_target_pairs={{0,2},{2,0},{1,3},{3,1},{4,6},{6,4},{5,7},{7,5},{8,10},{10,8},{9,1... | collective-permute-start | bytes 1179656 | tf_op jit(solution)/shard_map/ppermute | solution.py:484
  22.3 2.3 %all-to-all-done.gathered = bf16[8,8,1536]{2,1,0:T(8,128)(2,1)S(1)} async-done(((bf16[8,8,1536]{2,1,0:T(8,128)(2,1)}), bf16[8,8,1536]{2,1,0:T(8,128)(2,1)S(1)}, u32[]{:S(2)}, u32[]{:S(2)}) %all-to-all-start) | async-done | bytes 196640 | tf_op jit(solution)/shard_map/all_to_all | solution.py:482
  24.6 0.0 copy-start.8
  24.6 0.7 copy-done.8
  25.3 2.4 %shard_map.112 = (bf16[32,8,2304]{2,1,0:T(8,128)(2,1)}, f32[8,128]{1,0:T(8,128)}) custom-call(bf16[8,8,1536]{2,1,0:T(8,128)(2,1)} %copy-done.8), custom_call_target="tpu_custom_call" | custom-call | flops 200000000 | bytes 1380352 | tf_op jit(solution)/shard_map/pallas_call | solution.py:447
  27.7 10.0 %all-to-all-start.1 = ((bf16[32,8,2304]{2,1,0:T(8,128)(2,1)}), bf16[32,8,2304]{2,1,0:T(8,128)(2,1)S(1)}, u32[]{:S(2)}, u32[]{:S(2)}) async-start(bf16[32,8,2304]{2,1,0:T(8,128)(2,1)} %get-tuple-element.22), calls=%async_computation.1 | async-start | bytes 2359296 | tf_op jit(solution)/shard_map/all_to_all | solution.py:501
  37.7 0.0 copy-start.1
  37.7 0.0 collective-permute-done.across
  37.7 0.0 copy-start
  37.7 0.3 collective-permute-start.2
  38.1 0.0 collective-permute-done.4.lent
  38.1 0.0 copy-done.2
  38.1 0.0 copy-start.3
  38.1 0.5 shard_map.115
  38.6 0.1 copy-done.3
  38.7 0.0 copy-start.10
  38.7 0.3 collective-permute-start.6
  39.0 0.0 copy-done
  39.0 0.0 copy-done.1
  39.0 0.7 shard_map.114
  39.7 0.3 collective-permute-start.5
  40.1 0.0 copy-done.10
  40.1 0.6 fusion.kernel
  40.7 0.0 collective-permute-done.1.up_beside
  40.7 0.0 collective-permute-done.6.edges.beside
  40.7 0.6 collective-permute-done.5.beside
  41.3 0.0 copy-start.9
  41.3 0.0 collective-permute-done.2.beyond
  41.3 0.7 copy-done.9
  41.9 0.0 copy-start.7
  41.9 0.8 copy-done.7
  42.8 9.1 %shard_map.116 = (f32[560,384]{1,0:T(8,128)}, f32[592,384]{1,0:T(8,128)}, bf16[32,8,2432]{2,1,0:T(8,128)(2,1)}) custom-call(bf16[128,1536]{1,0:T(8,128)(2,1)} %bitcast.7, bf16[80,1536]{1,0:T(8,128)(2,1)} %copy-done.2, bf16[384,768]{1,0:T(8,128)(2,1)} %copy-done, bf16[112,768]{1,0:T(8,128)(2,1)} %copy-done.3, bf16[2,128,384]{2,1,0:T(8,128)(2,1)} %copy-done.9, ...), custom_call_target="tpu_custom_call" | custom-call | flops 200000000 | bytes 6897664 | tf_op jit(solution)/shard_map/pallas_call | solution.py:447
  51.9 4.3 %all-to-all-done.1.gathered = bf16[32,8,2304]{2,1,0:T(8,128)(2,1)S(1)} async-done(((bf16[32,8,2304]{2,1,0:T(8,128)(2,1)}), bf16[32,8,2304]{2,1,0:T(8,128)(2,1)S(1)}, u32[]{:S(2)}, u32[]{:S(2)}) %all-to-all-start.1) | async-done | bytes 1179680 | tf_op jit(solution)/shard_map/all_to_all | solution.py:501
  56.2 1.0 copy-done.5
  57.2 6.7 %shard_map.117 = (bf16[512,384]{1,0:T(8,128)(2,1)}, bf16[384,1536]{1,0:T(8,128)(2,1)}, bf16[32,8,2432]{2,1,0:T(8,128)(2,1)}) custom-call(bf16[32,8,2304]{2,1,0:T(8,128)(2,1)} %copy-done.5, f32[8,128]{1,0:T(8,128)} %get-tuple-element.23.notes, bf16[384,256]{1,0:T(8,128)(2,1)} %constant.36.clone.whole, ...), custom_call_target="tpu_custom_call", output_to_operand_aliasing={{2}: (11, {})} | custom-call | flops 200000000 | bytes 9572352 | tf_op jit(solution)/shard_map/pallas_call | solution.py:447
  63.9 5.0 %all-to-all-start.2 = ((bf16[32,8,2432]{2,1,0:T(8,128)(2,1)}), bf16[32,8,2432]{2,1,0:T(8,128)(2,1)S(1)}, u32[]{:S(2)}, u32[]{:S(2)}) async-start(bf16[32,8,2432]{2,1,0:T(8,128)(2,1)} %get-tuple-element.33), calls=%async_computation.2 | async-start | bytes 2490368 | tf_op jit(solution)/shard_map/all_to_all | solution.py:540
  68.9 7.4 %shard_map.118 = (bf16[2,144,384]{2,1,0:T(8,128)(2,1)}, bf16[2,144,384]{2,1,0:T(8,128)(2,1)}) custom-call(bf16[512,384]{1,0:T(8,128)(2,1)} %get-tuple-element.29.grad_conv, bf16[384,1536]{1,0:T(8,128)(2,1)} %get-tuple-element.30.projection, f32[560,384]{1,0:T(8,128)} %get-tuple-element.26.slope, bf16[80,1536]{1,0:T(8,128)(2,1)} %copy-done.2, ...), custom_call_target="tpu_custom_call" | custom-call | flops 200000000 | bytes 3612672 | tf_op jit(solution)/shard_map/pallas_call | solution.py:447
  76.3 0.0 copy-start.4
  76.3 0.6 collective-permute-start.7
  76.9 11.1 %all-to-all-done.2.gathered.parts = bf16[32,8,2432]{2,1,0:T(8,128)(2,1)S(1)} async-done(((bf16[32,8,2432]{2,1,0:T(8,128)(2,1)}), bf16[32,8,2432]{2,1,0:T(8,128)(2,1)S(1)}, u32[]{:S(2)}, u32[]{:S(2)}) %all-to-all-start.2) | async-done | bytes 1245216 | tf_op jit(solution)/shard_map/all_to_all | solution.py:540
  88.0 1.4 %shard_map.120 = bf16[8,8,1536]{2,1,0:T(8,128)(2,1)} custom-call(bf16[32,8,2432]{2,1,0:T(8,128)(2,1)S(1)} %all-to-all-done.2.gathered.parts), custom_call_target="tpu_custom_call" | custom-call | flops 200000000 | bytes 1441792 | tf_op jit(solution)/shard_map/pallas_call | solution.py:447
  89.4 0.0 copy-start.11
  89.4 3.4 %all-to-all-start.3 = ((bf16[8,8,1536]{2,1,0:T(8,128)(2,1)}), bf16[8,8,1536]{2,1,0:T(8,128)(2,1)S(1)}, u32[]{:S(2)}, u32[]{:S(2)}) async-start(bf16[8,8,1536]{2,1,0:T(8,128)(2,1)} %shard_map.120), calls=%async_computation.3 | async-start | bytes 393216 | tf_op jit(solution)/shard_map/all_to_all | solution.py:550
  92.8 0.0 copy-done.4
  92.8 0.0 collective-permute-done.7.got
  92.9 1.6 %collective-permute-start.8 = (bf16[2,144,384]{2,1,0:T(8,128)(2,1)S(1)}, bf16[2,144,384]{2,1,0:T(8,128)(2,1)S(1)}, u32[]{:S(2)}, u32[]{:S(2)}) collective-permute-start(bf16[2,144,384]{2,1,0:T(8,128)(2,1)S(1)} %pad_maximum_fusion), channel_id=1, source_target_pairs={{0,4},{4,0},{1,5},{5,1},{2,6},{6,2},{3,7},{7,3},{8,12},{12,8},{9,1... | collective-permute-start | bytes 663560 | tf_op jit(solution)/shard_map/ppermute | solution.py:586
  94.5 6.7 %all-to-all-done.3.got = bf16[8,8,1536]{2,1,0:T(8,128)(2,1)S(1)} async-done(((bf16[8,8,1536]{2,1,0:T(8,128)(2,1)}), bf16[8,8,1536]{2,1,0:T(8,128)(2,1)S(1)}, u32[]{:S(2)}, u32[]{:S(2)}) %all-to-all-start.3) | async-done | bytes 196640 | tf_op jit(solution)/shard_map/all_to_all | solution.py:550
  101.2 1.2 shard_map.121
  102.4 6.5 %all-to-all-start.4 = ((f32[32,1,1536]{2,1,0:T(1,128)}), f32[32,1,1536]{2,1,0:T(1,128)S(1)}, u32[]{:S(2)}, u32[]{:S(2)}) async-start(f32[32,1,1536]{2,1,0:T(1,128)} %get-tuple-element.37), calls=%async_computation.4 | async-start | bytes 393216 | tf_op jit(solution)/shard_map/all_to_all | solution.py:560
  108.9 0.0 copy-done.11
  109.0 0.0 collective-permute-done.8.far
  109.0 1.4 %shard_map.119 = (bf16[128,1536]{1,0:T(8,128)(2,1)}, f32[8,1536]{1,0:T(8,128)}) custom-call(bf16[2,144,384]{2,1,0:T(8,128)(2,1)S(1)} %copy-done.4, bf16[2,144,384]{2,1,0:T(8,128)(2,1)S(1)} %collective-permute-done.7.got, bf16[2,144,384]{2,1,0:T(8,128)(2,1)S(1)} %collective-permute-done.8.far, bf16[32,8,2432]{2,1,0:T(8,128)(2,1)S(1)} %all-to-all-done.2.gathered.parts, ...), custom_call_target="tpu_custom_call" | custom-call | flops 200000000 | bytes 2355200 | tf_op jit(solution)/shard_map/pallas_call | solution.py:447
  110.4 6.7 %all-to-all-done.4.got = f32[32,1,1536]{2,1,0:T(1,128)S(1)} async-done(((f32[32,1,1536]{2,1,0:T(1,128)}), f32[32,1,1536]{2,1,0:T(1,128)S(1)}, u32[]{:S(2)}, u32[]{:S(2)}) %all-to-all-start.4) | async-done | bytes 196640 | tf_op jit(solution)/shard_map/all_to_all | solution.py:560
  117.1 1.1 shard_map.122
  (7 shorter events, 0.1 us)
Async XLA Ops:
  0.6 17.4 %copy-start.6 = (bf16[1,128,1536]{2,1,0:T(8,128)(2,1)S(1)}, bf16[1,128,1536]{2,1,0:T(8,128)(2,1)}, u32[]{:S(2)}) copy-start(bf16[1,128,1536]{2,1,0:T(8,128)(2,1)} %param.9) | copy-start | bytes 1179652
  3.3 34.4 %collective-permute-start = (bf16[384,768]{1,0:T(8,128)(2,1)}, bf16[384,768]{1,0:T(8,128)(2,1)S(1)}, u32[]{:S(2)}, u32[]{:S(2)}) collective-permute-start(bf16[384,768]{1,0:T(8,128)(2,1)} %get-tuple-element.24), channel_id=1, source_target_pairs={{0,4},{4,0},{1,5},{5,1},{2,6},{6,2},{3,7},{7,3},{8,12},{12,8},{9,1... | collective-permute-start | bytes 1769480 | tf_op jit(solution)/shard_map/ppermute | solution.py:483
  7.1 8.9 %collective-permute-start.3 = (bf16[80,1536]{1,0:T(8,128)(2,1)}, bf16[80,1536]{1,0:T(8,128)(2,1)S(1)}, u32[]{:S(2)}, u32[]{:S(2)}) collective-permute-start(bf16[80,1536]{1,0:T(8,128)(2,1)} %get-tuple-element.25), channel_id=1, source_target_pairs={{6,8},{14,16},{22,24},{30,32},{38,40},{46,48},{54,56},{62,64},{70,... | collective-permute-start | bytes 737288 | tf_op jit(solution)/shard_map/ppermute | solution.py:481
  7.8 16.8 %all-to-all-start = ((bf16[8,8,1536]{2,1,0:T(8,128)(2,1)}), bf16[8,8,1536]{2,1,0:T(8,128)(2,1)S(1)}, u32[]{:S(2)}, u32[]{:S(2)}) async-start(bf16[8,8,1536]{2,1,0:T(8,128)(2,1)} %get-tuple-element.21), calls=%async_computation | async-start | bytes 393216 | tf_op jit(solution)/shard_map/all_to_all | solution.py:482
  16.0 22.1 %copy-start.2 = (bf16[80,1536]{1,0:T(8,128)(2,1)}, bf16[80,1536]{1,0:T(8,128)(2,1)S(1)}, u32[]{:S(2)}) copy-start(bf16[80,1536]{1,0:T(8,128)(2,1)S(1)} %collective-permute-done.3.slot) | copy-start | bytes 737284
  16.7 21.3 %collective-permute-start.4 = (bf16[112,768]{1,0:T(8,128)(2,1)S(1)}, bf16[112,768]{1,0:T(8,128)(2,1)S(1)}, u32[]{:S(2)}, u32[]{:S(2)}) collective-permute-start(bf16[112,768]{1,0:T(8,128)(2,1)S(1)} %shard_map.113), channel_id=1, source_target_pairs={{0,4},{6,2},{1,5},{7,3},{8,12},{14,10},{9,13},{15,11},{16,20},{22,... | collective-permute-start | bytes 516104 | tf_op jit(solution)/shard_map/ppermute | solution.py:487
  18.0 22.7 %collective-permute-start.1 = (bf16[128,1536]{1,0:T(8,128)(2,1)S(1)}, bf16[128,1536]{1,0:T(8,128)(2,1)}, u32[]{:S(2)}, u32[]{:S(2)}) collective-permute-start(bf16[128,1536]{1,0:T(8,128)(2,1)S(1)} %bitcast.12), channel_id=1, source_target_pairs={{0,2},{2,0},{1,3},{3,1},{4,6},{6,4},{5,7},{7,5},{8,10},{10,8},{9,1... | collective-permute-start | bytes 1179656 | tf_op jit(solution)/shard_map/ppermute | solution.py:484
  24.6 0.7 copy-start.8
  27.7 28.4 %all-to-all-start.1 = ((bf16[32,8,2304]{2,1,0:T(8,128)(2,1)}), bf16[32,8,2304]{2,1,0:T(8,128)(2,1)S(1)}, u32[]{:S(2)}, u32[]{:S(2)}) async-start(bf16[32,8,2304]{2,1,0:T(8,128)(2,1)} %get-tuple-element.22), calls=%async_computation.1 | async-start | bytes 2359296 | tf_op jit(solution)/shard_map/all_to_all | solution.py:501
  37.7 1.3 %copy-start.1 = (bf16[1,128,1536]{2,1,0:T(8,128)(2,1)S(1)}, bf16[1,128,1536]{2,1,0:T(8,128)(2,1)}, u32[]{:S(2)}) copy-start(bf16[1,128,1536]{2,1,0:T(8,128)(2,1)} %param.8) | copy-start | bytes 1179652
  37.7 1.3 %copy-start = (bf16[384,768]{1,0:T(8,128)(2,1)}, bf16[384,768]{1,0:T(8,128)(2,1)S(1)}, u32[]{:S(2)}) copy-start(bf16[384,768]{1,0:T(8,128)(2,1)S(1)} %collective-permute-done.across) | copy-start | bytes 1769476
  37.7 3.5 %collective-permute-start.2 = (bf16[384,768]{1,0:T(8,128)(2,1)S(1)}, bf16[384,768]{1,0:T(8,128)(2,1)S(1)}, u32[]{:S(2)}, u32[]{:S(2)}) collective-permute-start(bf16[384,768]{1,0:T(8,128)(2,1)S(1)} %collective-permute-done.across), channel_id=1, source_target_pairs={{0,2},{2,0},{1,3},{3,1},{4,6},{6,4},{5,7},{7,5},{8,10},{10,8},{9,1... | collective-permute-start | bytes 1769480 | tf_op jit(solution)/shard_map/ppermute | solution.py:485
  38.1 0.7 copy-start.3
  38.7 1.3 %copy-start.10 = (bf16[31,1536]{1,0:T(8,128)(2,1)S(1)}, bf16[31,1536]{1,0:T(8,128)(2,1)}, u32[]{:S(2)}) copy-start(bf16[31,1536]{1,0:T(8,128)(2,1)} %param.11) | copy-start | bytes 285700
  38.7 2.0 %collective-permute-start.6 = (bf16[2,176,384]{2,1,0:T(8,128)(2,1)S(1)}, bf16[2,176,384]{2,1,0:T(8,128)(2,1)}, u32[]{:S(2)}, u32[]{:S(2)}) collective-permute-start(bf16[2,176,384]{2,1,0:T(8,128)(2,1)S(1)} %shard_map.115), channel_id=1, source_target_pairs={{0,2},{2,0},{1,3},{3,1},{4,6},{6,4},{5,7},{7,5},{8,10},{10,8},{9,1... | collective-permute-start | bytes 811016 | tf_op jit(solution)/shard_map/ppermute | solution.py:503
  39.7 1.5 %collective-permute-start.5 = (bf16[2,128,384]{2,1,0:T(8,128)(2,1)S(1)}, bf16[2,128,384]{2,1,0:T(8,128)(2,1)S(1)}, u32[]{:S(2)}, u32[]{:S(2)}) collective-permute-start(bf16[2,128,384]{2,1,0:T(8,128)(2,1)S(1)} %shard_map.114), channel_id=1, source_target_pairs={{0,2},{2,0},{1,3},{3,1},{4,6},{6,4},{5,7},{7,5},{8,10},{10,8},{9,1... | collective-permute-start | bytes 589832 | tf_op jit(solution)/shard_map/ppermute | solution.py:502
  41.3 0.7 copy-start.9
  41.9 0.8 copy-start.7
  56.2 1.0 copy-start.5
  63.9 24.1 %all-to-all-start.2 = ((bf16[32,8,2432]{2,1,0:T(8,128)(2,1)}), bf16[32,8,2432]{2,1,0:T(8,128)(2,1)S(1)}, u32[]{:S(2)}, u32[]{:S(2)}) async-start(bf16[32,8,2432]{2,1,0:T(8,128)(2,1)} %get-tuple-element.33), calls=%async_computation.2 | async-start | bytes 2490368 | tf_op jit(solution)/shard_map/all_to_all | solution.py:540
  76.3 16.5 %copy-start.4 = (bf16[2,144,384]{2,1,0:T(8,128)(2,1)S(1)}, bf16[2,144,384]{2,1,0:T(8,128)(2,1)}, u32[]{:S(2)}) copy-start(bf16[2,144,384]{2,1,0:T(8,128)(2,1)} %get-tuple-element.31.kept) | copy-start | bytes 663556
  76.3 16.5 %collective-permute-start.7 = (bf16[2,144,384]{2,1,0:T(8,128)(2,1)}, bf16[2,144,384]{2,1,0:T(8,128)(2,1)S(1)}, u32[]{:S(2)}, u32[]{:S(2)}) collective-permute-start(bf16[2,144,384]{2,1,0:T(8,128)(2,1)} %get-tuple-element.32), channel_id=1, source_target_pairs={{0,2},{2,0},{1,3},{3,1},{4,6},{6,4},{5,7},{7,5},{8,10},{10,8},{9,1... | collective-permute-start | bytes 663560 | tf_op jit(solution)/shard_map/ppermute | solution.py:582
  89.4 19.6 %copy-start.11 = (s32[1,8]{1,0:T(1,128)S(1)}, s32[1,8]{1,0:T(1,128)}, u32[]{:S(2)}) copy-start(s32[1,8]{1,0:T(1,128)} %durations.1) | copy-start | bytes 100
  89.4 11.9 %all-to-all-start.3 = ((bf16[8,8,1536]{2,1,0:T(8,128)(2,1)}), bf16[8,8,1536]{2,1,0:T(8,128)(2,1)S(1)}, u32[]{:S(2)}, u32[]{:S(2)}) async-start(bf16[8,8,1536]{2,1,0:T(8,128)(2,1)} %shard_map.120), calls=%async_computation.3 | async-start | bytes 393216 | tf_op jit(solution)/shard_map/all_to_all | solution.py:550
  92.9 16.1 %collective-permute-start.8 = (bf16[2,144,384]{2,1,0:T(8,128)(2,1)S(1)}, bf16[2,144,384]{2,1,0:T(8,128)(2,1)S(1)}, u32[]{:S(2)}, u32[]{:S(2)}) collective-permute-start(bf16[2,144,384]{2,1,0:T(8,128)(2,1)S(1)} %pad_maximum_fusion), channel_id=1, source_target_pairs={{0,4},{4,0},{1,5},{5,1},{2,6},{6,2},{3,7},{7,3},{8,12},{12,8},{9,1... | collective-permute-start | bytes 663560 | tf_op jit(solution)/shard_map/ppermute | solution.py:586
  102.4 14.7 %all-to-all-start.4 = ((f32[32,1,1536]{2,1,0:T(1,128)}), f32[32,1,1536]{2,1,0:T(1,128)S(1)}, u32[]{:S(2)}, u32[]{:S(2)}) async-start(f32[32,1,1536]{2,1,0:T(1,128)} %get-tuple-element.37), calls=%async_computation.4 | async-start | bytes 393216 | tf_op jit(solution)/shard_map/all_to_all | solution.py:560

commit v8 on v7

--- a/solution.py
+++ b/solution.py
@@ -80,11 +80,16 @@
         sems.at[pl.ds(9, 5)],
     )
     finish(begin([(weights, got), (durations, lengths)], sems))
-    lane = lax.broadcasted_iota(jnp.int32, (1, 1536), 1)
+    lane = lax.broadcasted_iota(jnp.int32, (8, EXTRA), 1)
     total = jnp.sum(lengths[...].astype(F32), axis=1, keepdims=True)
-    note = jnp.where(lane == lax.axis_index("z"), jnp.broadcast_to(total, (1, 1536)), 0.0)
-    rows = [got[...].astype(F32), note, jnp.zeros((1, 1536), F32)]
-    block[...] = jnp.concatenate(rows, axis=0).astype(BF)
+    note = jnp.where(lane == lax.axis_index("z"), jnp.broadcast_to(total, (8, EXTRA)), 0.0)
+    rows = got[...].astype(F32)
+    rest = [
+        jnp.concatenate([rows[3 * i + j : 3 * i + j + 1, 1152:] for j in range(3)], axis=1)
+        for i in range(2)
+    ]
+    rows = jnp.concatenate([rows[:, :1152]] + rest, axis=0)
+    block[...] = jnp.concatenate([rows, note], axis=1).astype(BF)
     sent = begin([(block, out.at[peer]) for peer in range(8)], sems)
     finish(taken)
     finish(begin([(v_share, share), (v_edge, edge)], sems.at[pl.ds(9, 2)]))
@@ -112,6 +117,11 @@
     note = jnp.zeros((8, EXTRA), F32)
     for z in range(8):
         block_z = got[z].astype(F32)
+        rest = [block_z[6 + r // 3, 384 * (r % 3) : 384 * (r % 3) + 384] for r in range(BLOCK)]
+        block_z, spare = (
+            jnp.concatenate([block_z[:BLOCK, :1152], jnp.stack(rest)], axis=1),
+            block_z[:, 1152:],
+        )
         for r in range(BLOCK):
             i = BLOCK * (z % 2) + r
             at = ROWS * (z // 2)
@@ -121,7 +131,7 @@
                 for h in range(2):
                     to = at + 2 * (i - ROWS) + h
                     rows[to : to + 1, 1536:] = block_z[r : r + 1, 768 * h : 768 * h + 768]
-        note += jnp.broadcast_to(block_z[BLOCK : BLOCK + 1, :EXTRA], (8, EXTRA))
+        note += spare
     v_note[...] = note
     sent = begin([(v_note, note_out)], sems.at[pl.ds(32, 1)])
     for q in range(4):
@@ -219,7 +229,7 @@
             active[pl.ds(base, rows), lanes(tile)] = total * sig
             return 0
 
-        lax.fori_loop(0, WIDE // rows, chunk, 0)
+        lax.fori_loop(0, WIDE // rows, chunk, 0, unroll=True)
     out = begin([(v_slope, slope), (v_hidden, hidden)], sems)
     finish(later)
     acts = active[LEFT_U : LEFT_U + FRAMES].astype(BF)
@@ -233,11 +243,15 @@
         )
 
     product = outer(v_whole, slice(0, 1536))
+    for j in range(MEMBERS):
+        v_parts[j, :, :1536] = product[ROWS * j : ROWS * j + ROWS].astype(BF)
+    cut = pl.ds(0, 1536)
+    out += begin([(v_parts.at[:, :, cut], parts.at[:, :, cut])], sems.at[pl.ds(2, 1)])
     halves = outer(v_low, slice(0, 768)) + outer(v_high, slice(768, 1536))
     for j in range(MEMBERS):
-        v_parts[j, :, :1536] = product[ROWS * j : ROWS * j + ROWS].astype(BF)
         v_parts[j, :, 1536:] = halves[ROWS * j : ROWS * j + ROWS].astype(BF)
-    finish(begin([(v_parts, parts.at[:, :, pl.ds(0, LANES)])], sems.at[pl.ds(2, 1)]))
+    cut = pl.ds(1536, LANES - 1536)
+    out += begin([(v_parts.at[:, :, cut], parts.at[:, :, cut])], sems.at[pl.ds(3, 1)])
     finish(out)
 
 
@@ -469,9 +483,9 @@
 
     rows, share, edge = call(
         spread,
-        [((8, 8, 1536), BF), ((384, 768), BF), ((EDGE_H + EDGE_U, 1536), BF)],
-        [
-            ((BLOCK, 1536), BF), ((1, 8), jnp.int32), ((8, 1536), BF), ((384, 768), BF),
+        [((8, 8, 1280), BF), ((384, 768), BF), ((EDGE_H + EDGE_U, 1536), BF)],
+        [
+            ((BLOCK, 1536), BF), ((1, 8), jnp.int32), ((8, 1280), BF), ((384, 768), BF),
             ((EDGE_H + EDGE_U, 1536), BF),
         ],
         56,
@@ -490,7 +504,7 @@
     plane, notes = call(
         pack,
         [((MEMBERS, ROWS, LANES), BF), note],
-        [((4 * ROWS, LANES), F32), ((8, 8, 1536), BF), ((4, ROWS, LANES), BF), note],
+        [((4 * ROWS, LANES), F32), ((8, 8, 1280), BF), ((4, ROWS, LANES), BF), note],
         56,
         rows,
     )

time: 119 us -> 119 us (level)
  Pallas kernels: 35.3 us -> 34 us
    pallas_call x12, Pallas kernels: 35.3 us -> 34 us  [call(): pl.pallas_call(kernel, out_shape=shapes, in_specs=[space(i in near) for i...]
  transfers between devices with their start and end apart: 14 -> 14, of which waited for: 6 -> 6; matrix products, arithmetic and copies ran while one was open for 1% -> 1% of each run, Pallas kernels for 21% -> 20%
where the time goes in v8:
time: 119 us; the launch traced here: 118 us
  starting transfers between devices  46.1 us (39%)
  Pallas kernels  34 us (29%)
  waiting for transfers between devices  32.8 us (28%)
  local copies, waits for them, and re-layouts  3.38 us (3%)
    pallas_call x12, Pallas kernels, call(): pl.pallas_call(kernel, out_shape=shapes, in_specs=[space(i in near) for i...  34 us
    all_to_all x1, waiting for transfers between devices, body(): summed = parts = lax.all_to_all(parts, PLANE, 0, 0, tiled=True)  11.3 us
    all_to_all x1, starting transfers between devices, body(): rows = lax.all_to_all(plane, PLANE, 0, 0, tiled=True)  9.97 us
    all_to_all x1, starting transfers between devices, body(): rows = lax.all_to_all(rows, 'z', 0, 0, tiled=True)  8.2 us
    all_to_all x1, waiting for transfers between devices, body(): parts = lax.all_to_all(parts, 'z', 0, 0, tiled=True)  6.84 us
    all_to_all x1, waiting for transfers between devices, body(): taps_all = lax.all_to_all(taps_all, PLANE, 0, 0, tiled=True)  6.69 us
    all_to_all x1, starting transfers between devices, body(): taps_all = lax.all_to_all(taps_all, PLANE, 0, 0, tiled=True)  6.42 us
    all_to_all x1, waiting for transfers between devices, body(): rows = lax.all_to_all(plane, PLANE, 0, 0, tiled=True)  5.44 us
  transfers between devices with their start and end apart: 14, of which 6 were waited for; matrix products, arithmetic and copies ran while one was open for 1% of the time, Pallas kernels for 20%

profile of v8, /device:TPU:1, one launch (start us, length us, event | category | flops | bytes accessed | tf_op | source)
XLA Modules:
  0.0 118.1 jit_solution(16760268301797279563)
XLA Ops:
  0.6 0.0 copy-start.6
  0.6 2.6 %shard_map.111 = (bf16[8,8,1280]{2,1,0:T(8,128)(2,1)}, bf16[384,768]{1,0:T(8,128)(2,1)}, bf16[80,1536]{1,0:T(8,128)(2,1)}) custom-call(bf16[6,1536]{1,0:T(8,128)(2,1)} %weights.1, s32[1,8]{1,0:T(1,128)} %durations.1, bf16[128,1536]{1,0:T(8,128)(2,1)} %bitcast.6, bf16[128,1536]{1,0:T(8,128)(2,1)} %bitcast.9), custom_call_target="tpu_custom_call" | custom-call | flops 200000000 | bytes 1804320 | tf_op jit(solution)/shard_map/pallas_call | solution.py:461
  3.3 3.8 %collective-permute-start = (bf16[384,768]{1,0:T(8,128)(2,1)}, bf16[384,768]{1,0:T(8,128)(2,1)S(1)}, u32[]{:S(2)}, u32[]{:S(2)}) collective-permute-start(bf16[384,768]{1,0:T(8,128)(2,1)} %get-tuple-element.24), channel_id=1, source_target_pairs={{0,4},{4,0},{1,5},{5,1},{2,6},{6,2},{3,7},{7,3},{8,12},{12,8},{9,1... | collective-permute-start | bytes 1769480 | tf_op jit(solution)/shard_map/ppermute | solution.py:497
  7.1 0.7 collective-permute-start.3
  7.8 8.2 %all-to-all-start = ((bf16[8,8,1280]{2,1,0:T(8,128)(2,1)}), bf16[8,8,1280]{2,1,0:T(8,128)(2,1)S(1)}, u32[]{:S(2)}, u32[]{:S(2)}) async-start(bf16[8,8,1280]{2,1,0:T(8,128)(2,1)} %get-tuple-element.21), calls=%async_computation | async-start | bytes 327680 | tf_op jit(solution)/shard_map/all_to_all | solution.py:496
  16.0 0.0 collective-permute-done.3.slot
  16.0 0.0 copy-start.2
  16.0 0.7 shard_map.113
  16.7 1.3 %collective-permute-start.4 = (bf16[112,768]{1,0:T(8,128)(2,1)S(1)}, bf16[112,768]{1,0:T(8,128)(2,1)S(1)}, u32[]{:S(2)}, u32[]{:S(2)}) collective-permute-start(bf16[112,768]{1,0:T(8,128)(2,1)S(1)} %shard_map.113), channel_id=1, source_target_pairs={{0,4},{6,2},{1,5},{7,3},{8,12},{14,10},{9,13},{15,11},{16,20},{22,... | collective-permute-start | bytes 516104 | tf_op jit(solution)/shard_map/ppermute | solution.py:501
  18.0 0.0 copy-done.6
  18.0 4.3 %collective-permute-start.1 = (bf16[128,1536]{1,0:T(8,128)(2,1)S(1)}, bf16[128,1536]{1,0:T(8,128)(2,1)}, u32[]{:S(2)}, u32[]{:S(2)}) collective-permute-start(bf16[128,1536]{1,0:T(8,128)(2,1)S(1)} %bitcast.12), channel_id=1, source_target_pairs={{0,2},{2,0},{1,3},{3,1},{4,6},{6,4},{5,7},{7,5},{8,10},{10,8},{9,1... | collective-permute-start | bytes 1179656 | tf_op jit(solution)/shard_map/ppermute | solution.py:498
  22.3 2.0 %all-to-all-done.gathered = bf16[8,8,1280]{2,1,0:T(8,128)(2,1)S(1)} async-done(((bf16[8,8,1280]{2,1,0:T(8,128)(2,1)}), bf16[8,8,1280]{2,1,0:T(8,128)(2,1)S(1)}, u32[]{:S(2)}, u32[]{:S(2)}) %all-to-all-start) | async-done | bytes 163872 | tf_op jit(solution)/shard_map/all_to_all | solution.py:496
  24.2 0.0 copy-start.9
  24.2 0.7 copy-done.9
  24.9 2.5 %shard_map.112 = (bf16[32,8,2304]{2,1,0:T(8,128)(2,1)}, f32[8,128]{1,0:T(8,128)}) custom-call(bf16[8,8,1280]{2,1,0:T(8,128)(2,1)} %copy-done.9), custom_call_target="tpu_custom_call" | custom-call | flops 200000000 | bytes 1347584 | tf_op jit(solution)/shard_map/pallas_call | solution.py:461
  27.4 10.0 %all-to-all-start.1 = ((bf16[32,8,2304]{2,1,0:T(8,128)(2,1)}), bf16[32,8,2304]{2,1,0:T(8,128)(2,1)S(1)}, u32[]{:S(2)}, u32[]{:S(2)}) async-start(bf16[32,8,2304]{2,1,0:T(8,128)(2,1)} %get-tuple-element.22), calls=%async_computation.1 | async-start | bytes 2359296 | tf_op jit(solution)/shard_map/all_to_all | solution.py:515
  37.4 0.0 copy-start.1
  37.4 0.0 collective-permute-done.across
  37.4 0.0 copy-start
  37.4 0.3 collective-permute-start.2
  37.7 0.0 collective-permute-done.4.lent
  37.7 0.0 copy-done.2
  37.7 0.0 copy-start.3
  37.7 0.5 shard_map.115
  38.3 0.1 copy-done.3
  38.4 0.0 copy-start.10
  38.4 0.3 collective-permute-start.6
  38.7 0.0 copy-done
  38.7 0.0 copy-done.1
  38.7 0.7 shard_map.114
  39.4 0.5 collective-permute-start.5
  39.9 0.0 copy-done.10
  39.9 0.6 fusion.kernel
  40.5 0.0 collective-permute-done.1.up_beside
  40.5 0.0 collective-permute-done.6.edges.beside
  40.5 0.6 collective-permute-done.5.beside
  41.1 0.0 copy-start.8
  41.1 0.0 collective-permute-done.2.beyond
  41.1 0.7 copy-done.8
  41.8 0.0 copy-start.7
  41.8 0.8 copy-done.7
  42.6 7.8 %shard_map.116 = (f32[560,384]{1,0:T(8,128)}, f32[592,384]{1,0:T(8,128)}, bf16[32,8,2432]{2,1,0:T(8,128)(2,1)}) custom-call(bf16[128,1536]{1,0:T(8,128)(2,1)} %bitcast.7, bf16[80,1536]{1,0:T(8,128)(2,1)} %copy-done.2, bf16[384,768]{1,0:T(8,128)(2,1)} %copy-done, bf16[112,768]{1,0:T(8,128)(2,1)} %copy-done.3, bf16[2,128,384]{2,1,0:T(8,128)(2,1)} %copy-done.8, ...), custom_call_target="tpu_custom_call" | custom-call | flops 200000000 | bytes 6897664 | tf_op jit(solution)/shard_map/pallas_call | solution.py:461
  50.4 5.4 %all-to-all-done.1.gathered = bf16[32,8,2304]{2,1,0:T(8,128)(2,1)S(1)} async-done(((bf16[32,8,2304]{2,1,0:T(8,128)(2,1)}), bf16[32,8,2304]{2,1,0:T(8,128)(2,1)S(1)}, u32[]{:S(2)}, u32[]{:S(2)}) %all-to-all-start.1) | async-done | bytes 1179680 | tf_op jit(solution)/shard_map/all_to_all | solution.py:515
  55.8 1.0 copy-done.5
  56.9 6.7 %shard_map.117 = (bf16[512,384]{1,0:T(8,128)(2,1)}, bf16[384,1536]{1,0:T(8,128)(2,1)}, bf16[32,8,2432]{2,1,0:T(8,128)(2,1)}) custom-call(bf16[32,8,2304]{2,1,0:T(8,128)(2,1)} %copy-done.5, f32[8,128]{1,0:T(8,128)} %get-tuple-element.23.notes, bf16[384,256]{1,0:T(8,128)(2,1)} %constant.36.clone.whole, ...), custom_call_target="tpu_custom_call", output_to_operand_aliasing={{2}: (11, {})} | custom-call | flops 200000000 | bytes 9572352 | tf_op jit(solution)/shard_map/pallas_call | solution.py:461
  63.6 4.9 %all-to-all-start.2 = ((bf16[32,8,2432]{2,1,0:T(8,128)(2,1)}), bf16[32,8,2432]{2,1,0:T(8,128)(2,1)S(1)}, u32[]{:S(2)}, u32[]{:S(2)}) async-start(bf16[32,8,2432]{2,1,0:T(8,128)(2,1)} %get-tuple-element.33), calls=%async_computation.2 | async-start | bytes 2490368 | tf_op jit(solution)/shard_map/all_to_all | solution.py:554
  68.5 7.4 %shard_map.118 = (bf16[2,144,384]{2,1,0:T(8,128)(2,1)}, bf16[2,144,384]{2,1,0:T(8,128)(2,1)}) custom-call(bf16[512,384]{1,0:T(8,128)(2,1)} %get-tuple-element.29.grad_conv, bf16[384,1536]{1,0:T(8,128)(2,1)} %get-tuple-element.30.projection, f32[560,384]{1,0:T(8,128)} %get-tuple-element.26.slope, bf16[80,1536]{1,0:T(8,128)(2,1)} %copy-done.2, ...), custom_call_target="tpu_custom_call" | custom-call | flops 200000000 | bytes 3612672 | tf_op jit(solution)/shard_map/pallas_call | solution.py:461
  75.9 0.0 copy-start.4
  75.9 0.4 collective-permute-start.7
  76.3 11.3 %all-to-all-done.2.gathered.parts = bf16[32,8,2432]{2,1,0:T(8,128)(2,1)S(1)} async-done(((bf16[32,8,2432]{2,1,0:T(8,128)(2,1)}), bf16[32,8,2432]{2,1,0:T(8,128)(2,1)S(1)}, u32[]{:S(2)}, u32[]{:S(2)}) %all-to-all-start.2) | async-done | bytes 1245216 | tf_op jit(solution)/shard_map/all_to_all | solution.py:554
  87.6 1.4 %shard_map.120 = bf16[8,8,1536]{2,1,0:T(8,128)(2,1)} custom-call(bf16[32,8,2432]{2,1,0:T(8,128)(2,1)S(1)} %all-to-all-done.2.gathered.parts), custom_call_target="tpu_custom_call" | custom-call | flops 200000000 | bytes 1441792 | tf_op jit(solution)/shard_map/pallas_call | solution.py:461
  89.0 0.0 copy-start.11
  89.0 3.4 %all-to-all-start.3 = ((bf16[8,8,1536]{2,1,0:T(8,128)(2,1)}), bf16[8,8,1536]{2,1,0:T(8,128)(2,1)S(1)}, u32[]{:S(2)}, u32[]{:S(2)}) async-start(bf16[8,8,1536]{2,1,0:T(8,128)(2,1)} %shard_map.120), calls=%async_computation.3 | async-start | bytes 393216 | tf_op jit(solution)/shard_map/all_to_all | solution.py:564
  92.4 0.0 copy-done.4
  92.5 0.0 collective-permute-done.7.got
  92.5 1.6 %collective-permute-start.8 = (bf16[2,144,384]{2,1,0:T(8,128)(2,1)S(1)}, bf16[2,144,384]{2,1,0:T(8,128)(2,1)S(1)}, u32[]{:S(2)}, u32[]{:S(2)}) collective-permute-start(bf16[2,144,384]{2,1,0:T(8,128)(2,1)S(1)} %pad_maximum_fusion), channel_id=1, source_target_pairs={{0,4},{4,0},{1,5},{5,1},{2,6},{6,2},{3,7},{7,3},{8,12},{12,8},{9,1... | collective-permute-start | bytes 663560 | tf_op jit(solution)/shard_map/ppermute | solution.py:600
  94.1 6.8 %all-to-all-done.3.got = bf16[8,8,1536]{2,1,0:T(8,128)(2,1)S(1)} async-done(((bf16[8,8,1536]{2,1,0:T(8,128)(2,1)}), bf16[8,8,1536]{2,1,0:T(8,128)(2,1)S(1)}, u32[]{:S(2)}, u32[]{:S(2)}) %all-to-all-start.3) | async-done | bytes 196640 | tf_op jit(solution)/shard_map/all_to_all | solution.py:564
  101.0 1.2 shard_map.121
  102.1 6.4 %all-to-all-start.4 = ((f32[32,1,1536]{2,1,0:T(1,128)}), f32[32,1,1536]{2,1,0:T(1,128)S(1)}, u32[]{:S(2)}, u32[]{:S(2)}) async-start(f32[32,1,1536]{2,1,0:T(1,128)} %get-tuple-element.37), calls=%async_computation.4 | async-start | bytes 393216 | tf_op jit(solution)/shard_map/all_to_all | solution.py:574
  108.6 0.0 copy-done.11
  108.6 0.0 collective-permute-done.8.far
  108.6 1.4 %shard_map.119 = (bf16[128,1536]{1,0:T(8,128)(2,1)}, f32[8,1536]{1,0:T(8,128)}) custom-call(bf16[2,144,384]{2,1,0:T(8,128)(2,1)S(1)} %copy-done.4, bf16[2,144,384]{2,1,0:T(8,128)(2,1)S(1)} %collective-permute-done.7.got, bf16[2,144,384]{2,1,0:T(8,128)(2,1)S(1)} %collective-permute-done.8.far, bf16[32,8,2432]{2,1,0:T(8,128)(2,1)S(1)} %all-to-all-done.2.gathered.parts, ...), custom_call_target="tpu_custom_call" | custom-call | flops 200000000 | bytes 2355200 | tf_op jit(solution)/shard_map/pallas_call | solution.py:461
  110.1 6.7 %all-to-all-done.4.got = f32[32,1,1536]{2,1,0:T(1,128)S(1)} async-done(((f32[32,1,1536]{2,1,0:T(1,128)}), f32[32,1,1536]{2,1,0:T(1,128)S(1)}, u32[]{:S(2)}, u32[]{:S(2)}) %all-to-all-start.4) | async-done | bytes 196640 | tf_op jit(solution)/shard_map/all_to_all | solution.py:574
  116.8 1.1 shard_map.122
  (7 shorter events, 0.1 us)
Async XLA Ops:
  0.6 17.4 %copy-start.6 = (bf16[1,128,1536]{2,1,0:T(8,128)(2,1)S(1)}, bf16[1,128,1536]{2,1,0:T(8,128)(2,1)}, u32[]{:S(2)}) copy-start(bf16[1,128,1536]{2,1,0:T(8,128)(2,1)} %param.9) | copy-start | bytes 1179652
  3.3 34.1 %collective-permute-start = (bf16[384,768]{1,0:T(8,128)(2,1)}, bf16[384,768]{1,0:T(8,128)(2,1)S(1)}, u32[]{:S(2)}, u32[]{:S(2)}) collective-permute-start(bf16[384,768]{1,0:T(8,128)(2,1)} %get-tuple-element.24), channel_id=1, source_target_pairs={{0,4},{4,0},{1,5},{5,1},{2,6},{6,2},{3,7},{7,3},{8,12},{12,8},{9,1... | collective-permute-start | bytes 1769480 | tf_op jit(solution)/shard_map/ppermute | solution.py:497
  7.1 8.9 %collective-permute-start.3 = (bf16[80,1536]{1,0:T(8,128)(2,1)}, bf16[80,1536]{1,0:T(8,128)(2,1)S(1)}, u32[]{:S(2)}, u32[]{:S(2)}) collective-permute-start(bf16[80,1536]{1,0:T(8,128)(2,1)} %get-tuple-element.25), channel_id=1, source_target_pairs={{6,8},{14,16},{22,24},{30,32},{38,40},{46,48},{54,56},{62,64},{70,... | collective-permute-start | bytes 737288 | tf_op jit(solution)/shard_map/ppermute | solution.py:495
  7.8 16.5 %all-to-all-start = ((bf16[8,8,1280]{2,1,0:T(8,128)(2,1)}), bf16[8,8,1280]{2,1,0:T(8,128)(2,1)S(1)}, u32[]{:S(2)}, u32[]{:S(2)}) async-start(bf16[8,8,1280]{2,1,0:T(8,128)(2,1)} %get-tuple-element.21), calls=%async_computation | async-start | bytes 327680 | tf_op jit(solution)/shard_map/all_to_all | solution.py:496
  16.0 21.7 %copy-start.2 = (bf16[80,1536]{1,0:T(8,128)(2,1)}, bf16[80,1536]{1,0:T(8,128)(2,1)S(1)}, u32[]{:S(2)}) copy-start(bf16[80,1536]{1,0:T(8,128)(2,1)S(1)} %collective-permute-done.3.slot) | copy-start | bytes 737284
  16.7 21.0 %collective-permute-start.4 = (bf16[112,768]{1,0:T(8,128)(2,1)S(1)}, bf16[112,768]{1,0:T(8,128)(2,1)S(1)}, u32[]{:S(2)}, u32[]{:S(2)}) collective-permute-start(bf16[112,768]{1,0:T(8,128)(2,1)S(1)} %shard_map.113), channel_id=1, source_target_pairs={{0,4},{6,2},{1,5},{7,3},{8,12},{14,10},{9,13},{15,11},{16,20},{22,... | collective-permute-start | bytes 516104 | tf_op jit(solution)/shard_map/ppermute | solution.py:501
  18.0 22.5 %collective-permute-start.1 = (bf16[128,1536]{1,0:T(8,128)(2,1)S(1)}, bf16[128,1536]{1,0:T(8,128)(2,1)}, u32[]{:S(2)}, u32[]{:S(2)}) collective-permute-start(bf16[128,1536]{1,0:T(8,128)(2,1)S(1)} %bitcast.12), channel_id=1, source_target_pairs={{0,2},{2,0},{1,3},{3,1},{4,6},{6,4},{5,7},{7,5},{8,10},{10,8},{9,1... | collective-permute-start | bytes 1179656 | tf_op jit(solution)/shard_map/ppermute | solution.py:498
  24.2 0.7 copy-start.9
  27.4 28.5 %all-to-all-start.1 = ((bf16[32,8,2304]{2,1,0:T(8,128)(2,1)}), bf16[32,8,2304]{2,1,0:T(8,128)(2,1)S(1)}, u32[]{:S(2)}, u32[]{:S(2)}) async-start(bf16[32,8,2304]{2,1,0:T(8,128)(2,1)} %get-tuple-element.22), calls=%async_computation.1 | async-start | bytes 2359296 | tf_op jit(solution)/shard_map/all_to_all | solution.py:515
  37.4 1.3 %copy-start.1 = (bf16[1,128,1536]{2,1,0:T(8,128)(2,1)S(1)}, bf16[1,128,1536]{2,1,0:T(8,128)(2,1)}, u32[]{:S(2)}) copy-start(bf16[1,128,1536]{2,1,0:T(8,128)(2,1)} %param.8) | copy-start | bytes 1179652
  37.4 1.3 %copy-start = (bf16[384,768]{1,0:T(8,128)(2,1)}, bf16[384,768]{1,0:T(8,128)(2,1)S(1)}, u32[]{:S(2)}) copy-start(bf16[384,768]{1,0:T(8,128)(2,1)S(1)} %collective-permute-done.across) | copy-start | bytes 1769476
  37.4 3.7 %collective-permute-start.2 = (bf16[384,768]{1,0:T(8,128)(2,1)S(1)}, bf16[384,768]{1,0:T(8,128)(2,1)S(1)}, u32[]{:S(2)}, u32[]{:S(2)}) collective-permute-start(bf16[384,768]{1,0:T(8,128)(2,1)S(1)} %collective-permute-done.across), channel_id=1, source_target_pairs={{0,2},{2,0},{1,3},{3,1},{4,6},{6,4},{5,7},{7,5},{8,10},{10,8},{9,1... | collective-permute-start | bytes 1769480 | tf_op jit(solution)/shard_map/ppermute | solution.py:499
  37.7 0.7 copy-start.3
  38.4 1.5 %copy-start.10 = (bf16[31,1536]{1,0:T(8,128)(2,1)S(1)}, bf16[31,1536]{1,0:T(8,128)(2,1)}, u32[]{:S(2)}) copy-start(bf16[31,1536]{1,0:T(8,128)(2,1)} %param.11) | copy-start | bytes 285700
  38.4 2.1 %collective-permute-start.6 = (bf16[2,176,384]{2,1,0:T(8,128)(2,1)S(1)}, bf16[2,176,384]{2,1,0:T(8,128)(2,1)}, u32[]{:S(2)}, u32[]{:S(2)}) collective-permute-start(bf16[2,176,384]{2,1,0:T(8,128)(2,1)S(1)} %shard_map.115), channel_id=1, source_target_pairs={{0,2},{2,0},{1,3},{3,1},{4,6},{6,4},{5,7},{7,5},{8,10},{10,8},{9,1... | collective-permute-start | bytes 811016 | tf_op jit(solution)/shard_map/ppermute | solution.py:517
  39.4 1.7 %collective-permute-start.5 = (bf16[2,128,384]{2,1,0:T(8,128)(2,1)S(1)}, bf16[2,128,384]{2,1,0:T(8,128)(2,1)S(1)}, u32[]{:S(2)}, u32[]{:S(2)}) collective-permute-start(bf16[2,128,384]{2,1,0:T(8,128)(2,1)S(1)} %shard_map.114), channel_id=1, source_target_pairs={{0,2},{2,0},{1,3},{3,1},{4,6},{6,4},{5,7},{7,5},{8,10},{10,8},{9,1... | collective-permute-start | bytes 589832 | tf_op jit(solution)/shard_map/ppermute | solution.py:516
  41.1 0.7 copy-start.8
  41.8 0.8 copy-start.7
  55.8 1.0 copy-start.5
  63.6 24.1 %all-to-all-start.2 = ((bf16[32,8,2432]{2,1,0:T(8,128)(2,1)}), bf16[32,8,2432]{2,1,0:T(8,128)(2,1)S(1)}, u32[]{:S(2)}, u32[]{:S(2)}) async-start(bf16[32,8,2432]{2,1,0:T(8,128)(2,1)} %get-tuple-element.33), calls=%async_computation.2 | async-start | bytes 2490368 | tf_op jit(solution)/shard_map/all_to_all | solution.py:554
  75.9 16.5 %copy-start.4 = (bf16[2,144,384]{2,1,0:T(8,128)(2,1)S(1)}, bf16[2,144,384]{2,1,0:T(8,128)(2,1)}, u32[]{:S(2)}) copy-start(bf16[2,144,384]{2,1,0:T(8,128)(2,1)} %get-tuple-element.31.kept) | copy-start | bytes 663556
  75.9 16.5 %collective-permute-start.7 = (bf16[2,144,384]{2,1,0:T(8,128)(2,1)}, bf16[2,144,384]{2,1,0:T(8,128)(2,1)S(1)}, u32[]{:S(2)}, u32[]{:S(2)}) collective-permute-start(bf16[2,144,384]{2,1,0:T(8,128)(2,1)} %get-tuple-element.32), channel_id=1, source_target_pairs={{0,2},{2,0},{1,3},{3,1},{4,6},{6,4},{5,7},{7,5},{8,10},{10,8},{9,1... | collective-permute-start | bytes 663560 | tf_op jit(solution)/shard_map/ppermute | solution.py:596
  89.0 19.6 %copy-start.11 = (s32[1,8]{1,0:T(1,128)S(1)}, s32[1,8]{1,0:T(1,128)}, u32[]{:S(2)}) copy-start(s32[1,8]{1,0:T(1,128)} %durations.1) | copy-start | bytes 100
  89.0 12.0 %all-to-all-start.3 = ((bf16[8,8,1536]{2,1,0:T(8,128)(2,1)}), bf16[8,8,1536]{2,1,0:T(8,128)(2,1)S(1)}, u32[]{:S(2)}, u32[]{:S(2)}) async-start(bf16[8,8,1536]{2,1,0:T(8,128)(2,1)} %shard_map.120), calls=%async_computation.3 | async-start | bytes 393216 | tf_op jit(solution)/shard_map/all_to_all | solution.py:564
  92.5 16.1 %collective-permute-start.8 = (bf16[2,144,384]{2,1,0:T(8,128)(2,1)S(1)}, bf16[2,144,384]{2,1,0:T(8,128)(2,1)S(1)}, u32[]{:S(2)}, u32[]{:S(2)}) collective-permute-start(bf16[2,144,384]{2,1,0:T(8,128)(2,1)S(1)} %pad_maximum_fusion), channel_id=1, source_target_pairs={{0,4},{4,0},{1,5},{5,1},{2,6},{6,2},{3,7},{7,3},{8,12},{12,8},{9,1... | collective-permute-start | bytes 663560 | tf_op jit(solution)/shard_map/ppermute | solution.py:600
  102.1 14.6 %all-to-all-start.4 = ((f32[32,1,1536]{2,1,0:T(1,128)}), f32[32,1,1536]{2,1,0:T(1,128)S(1)}, u32[]{:S(2)}, u32[]{:S(2)}) async-start(f32[32,1,1536]{2,1,0:T(1,128)} %get-tuple-element.37), calls=%async_computation.4 | async-start | bytes 393216 | tf_op jit(solution)/shard_map/all_to_all | solution.py:574

commit v9 on v8

--- a/solution.py
+++ b/solution.py
@@ -112,8 +112,7 @@
     finish(begin([(v_out, out)], sems))
 
 
-def pack(gathered, plane, note_out, rows, got, block, v_note, sems):
-    finish(begin([(gathered, got)], sems))
+def pack(got, plane, note_out, rows, block, v_note, sems):
     note = jnp.zeros((8, EXTRA), F32)
     for z in range(8):
         block_z = got[z].astype(F32)
@@ -504,9 +503,10 @@
     plane, notes = call(
         pack,
         [((MEMBERS, ROWS, LANES), BF), note],
-        [((4 * ROWS, LANES), F32), ((8, 8, 1280), BF), ((4, ROWS, LANES), BF), note],
-        56,
+        [((4 * ROWS, LANES), F32), ((4, ROWS, LANES), BF), note],
+        16,
         rows,
+        near=(0,),
     )
     handed = ((2, 128, CHANNELS), BF)
     [beside] = call(relay, [handed], [handed], 16, hidden, across, flops=3_000_000_000)

time: 119 us -> 118 us (level)
  transfers between devices with their start and end apart: 14 -> 14, of which waited for: 6 -> 6; matrix products, arithmetic and copies ran while one was open for 1% -> 1% of each run, Pallas kernels for 20% -> 19%
where the time goes in v9:
time: 118 us; the launch traced here: 117 us
  starting transfers between devices  46.1 us (39%)
  Pallas kernels  33.1 us (28%)
  waiting for transfers between devices  32.8 us (28%)
  local copies, waits for them, and re-layouts  3.3 us (3%)
    pallas_call x12, Pallas kernels, call(): pl.pallas_call(kernel, out_shape=shapes, in_specs=[space(i in near) for i...  33.1 us
    all_to_all x1, waiting for transfers between devices, body(): summed = parts = lax.all_to_all(parts, PLANE, 0, 0, tiled=True)  11.3 us
    all_to_all x1, starting transfers between devices, body(): rows = lax.all_to_all(plane, PLANE, 0, 0, tiled=True)  9.96 us
    all_to_all x1, starting transfers between devices, body(): rows = lax.all_to_all(rows, 'z', 0, 0, tiled=True)  8.2 us
    all_to_all x1, waiting for transfers between devices, body(): parts = lax.all_to_all(parts, 'z', 0, 0, tiled=True)  6.85 us
    all_to_all x1, waiting for transfers between devices, body(): taps_all = lax.all_to_all(taps_all, PLANE, 0, 0, tiled=True)  6.69 us
    all_to_all x1, starting transfers between devices, body(): taps_all = lax.all_to_all(taps_all, PLANE, 0, 0, tiled=True)  6.41 us
    all_to_all x1, waiting for transfers between devices, body(): rows = lax.all_to_all(plane, PLANE, 0, 0, tiled=True)  5.44 us
  transfers between devices with their start and end apart: 14, of which 6 were waited for; matrix products, arithmetic and copies ran while one was open for 1% of the time, Pallas kernels for 19%

profile of v9, /device:TPU:1, one launch (start us, length us, event | category | flops | bytes accessed | tf_op | source)
XLA Modules:
  0.0 117.1 jit_solution(897745313812473478)
XLA Ops:
  0.6 0.0 copy-start.7
  0.6 2.6 %shard_map.111 = (bf16[8,8,1280]{2,1,0:T(8,128)(2,1)}, bf16[384,768]{1,0:T(8,128)(2,1)}, bf16[80,1536]{1,0:T(8,128)(2,1)}) custom-call(bf16[6,1536]{1,0:T(8,128)(2,1)} %weights.1, s32[1,8]{1,0:T(1,128)} %durations.1, bf16[128,1536]{1,0:T(8,128)(2,1)} %bitcast.6, bf16[128,1536]{1,0:T(8,128)(2,1)} %bitcast.9), custom_call_target="tpu_custom_call" | custom-call | flops 200000000 | bytes 1804320 | tf_op jit(solution)/shard_map/pallas_call | solution.py:460
  3.3 3.8 %collective-permute-start = (bf16[384,768]{1,0:T(8,128)(2,1)}, bf16[384,768]{1,0:T(8,128)(2,1)S(1)}, u32[]{:S(2)}, u32[]{:S(2)}) collective-permute-start(bf16[384,768]{1,0:T(8,128)(2,1)} %get-tuple-element.24), channel_id=1, source_target_pairs={{0,4},{4,0},{1,5},{5,1},{2,6},{6,2},{3,7},{7,3},{8,12},{12,8},{9,1... | collective-permute-start | bytes 1769480 | tf_op jit(solution)/shard_map/ppermute | solution.py:496
  7.1 0.7 collective-permute-start.3
  7.8 8.2 %all-to-all-start = ((bf16[8,8,1280]{2,1,0:T(8,128)(2,1)}), bf16[8,8,1280]{2,1,0:T(8,128)(2,1)S(1)}, u32[]{:S(2)}, u32[]{:S(2)}) async-start(bf16[8,8,1280]{2,1,0:T(8,128)(2,1)} %get-tuple-element.21), calls=%async_computation | async-start | bytes 327680 | tf_op jit(solution)/shard_map/all_to_all | solution.py:495
  16.0 0.0 collective-permute-done.3.slot
  16.0 0.0 copy-start.2
  16.0 0.7 shard_map.113
  16.7 1.3 %collective-permute-start.4 = (bf16[112,768]{1,0:T(8,128)(2,1)S(1)}, bf16[112,768]{1,0:T(8,128)(2,1)S(1)}, u32[]{:S(2)}, u32[]{:S(2)}) collective-permute-start(bf16[112,768]{1,0:T(8,128)(2,1)S(1)} %shard_map.113), channel_id=1, source_target_pairs={{0,4},{6,2},{1,5},{7,3},{8,12},{14,10},{9,13},{15,11},{16,20},{22,... | collective-permute-start | bytes 516104 | tf_op jit(solution)/shard_map/ppermute | solution.py:500
  18.0 0.0 copy-done.7
  18.0 4.3 %collective-permute-start.1 = (bf16[128,1536]{1,0:T(8,128)(2,1)S(1)}, bf16[128,1536]{1,0:T(8,128)(2,1)}, u32[]{:S(2)}, u32[]{:S(2)}) collective-permute-start(bf16[128,1536]{1,0:T(8,128)(2,1)S(1)} %bitcast.12), channel_id=1, source_target_pairs={{0,2},{2,0},{1,3},{3,1},{4,6},{6,4},{5,7},{7,5},{8,10},{10,8},{9,1... | collective-permute-start | bytes 1179656 | tf_op jit(solution)/shard_map/ppermute | solution.py:497
  22.3 2.0 %all-to-all-done.got = bf16[8,8,1280]{2,1,0:T(8,128)(2,1)S(1)} async-done(((bf16[8,8,1280]{2,1,0:T(8,128)(2,1)}), bf16[8,8,1280]{2,1,0:T(8,128)(2,1)S(1)}, u32[]{:S(2)}, u32[]{:S(2)}) %all-to-all-start) | async-done | bytes 163872 | tf_op jit(solution)/shard_map/all_to_all | solution.py:495
  24.2 1.6 %shard_map.112 = (bf16[32,8,2304]{2,1,0:T(8,128)(2,1)}, f32[8,128]{1,0:T(8,128)S(1)}) custom-call(bf16[8,8,1280]{2,1,0:T(8,128)(2,1)S(1)} %all-to-all-done.got), custom_call_target="tpu_custom_call" | custom-call | flops 200000000 | bytes 1347584 | tf_op jit(solution)/shard_map/pallas_call | solution.py:460
  25.8 0.0 copy-start.5
  25.8 0.6 copy-done.5
  26.4 10.0 %all-to-all-start.1 = ((bf16[32,8,2304]{2,1,0:T(8,128)(2,1)}), bf16[32,8,2304]{2,1,0:T(8,128)(2,1)S(1)}, u32[]{:S(2)}, u32[]{:S(2)}) async-start(bf16[32,8,2304]{2,1,0:T(8,128)(2,1)} %get-tuple-element.22), calls=%async_computation.1 | async-start | bytes 2359296 | tf_op jit(solution)/shard_map/all_to_all | solution.py:515
  36.4 0.0 copy-start.1
  36.4 0.0 collective-permute-done.across
  36.4 0.0 copy-start
  36.4 0.3 collective-permute-start.2
  36.8 0.0 collective-permute-done.4.lent
  36.8 0.0 copy-done.2
  36.8 0.0 copy-start.3
  36.8 0.5 shard_map.115
  37.3 0.1 copy-done.3
  37.4 0.0 copy-start.10
  37.4 0.3 collective-permute-start.6
  37.7 0.0 copy-done
  37.7 0.0 copy-done.1
  37.7 0.7 shard_map.114
  38.4 0.5 collective-permute-start.5
  38.9 0.0 copy-done.10
  38.9 0.6 fusion.kernel
  39.6 0.0 collective-permute-done.1.up_beside
  39.6 0.0 collective-permute-done.6.edges.beside
  39.6 0.6 collective-permute-done.5.beside
  40.1 0.0 copy-start.9
  40.1 0.0 collective-permute-done.2.beyond
  40.1 0.7 copy-done.9
  40.8 0.0 copy-start.8
  40.8 0.8 copy-done.8
  41.6 7.8 %shard_map.116 = (f32[560,384]{1,0:T(8,128)}, f32[592,384]{1,0:T(8,128)}, bf16[32,8,2432]{2,1,0:T(8,128)(2,1)}) custom-call(bf16[128,1536]{1,0:T(8,128)(2,1)} %bitcast.7, bf16[80,1536]{1,0:T(8,128)(2,1)} %copy-done.2, bf16[384,768]{1,0:T(8,128)(2,1)} %copy-done, bf16[112,768]{1,0:T(8,128)(2,1)} %copy-done.3, bf16[2,128,384]{2,1,0:T(8,128)(2,1)} %copy-done.9, ...), custom_call_target="tpu_custom_call" | custom-call | flops 200000000 | bytes 6897664 | tf_op jit(solution)/shard_map/pallas_call | solution.py:460
  49.4 5.4 %all-to-all-done.1.gathered = bf16[32,8,2304]{2,1,0:T(8,128)(2,1)S(1)} async-done(((bf16[32,8,2304]{2,1,0:T(8,128)(2,1)}), bf16[32,8,2304]{2,1,0:T(8,128)(2,1)S(1)}, u32[]{:S(2)}, u32[]{:S(2)}) %all-to-all-start.1) | async-done | bytes 1179680 | tf_op jit(solution)/shard_map/all_to_all | solution.py:515
  54.9 1.0 copy-done.6
  55.9 6.7 %shard_map.117 = (bf16[512,384]{1,0:T(8,128)(2,1)}, bf16[384,1536]{1,0:T(8,128)(2,1)}, bf16[32,8,2432]{2,1,0:T(8,128)(2,1)}) custom-call(bf16[32,8,2304]{2,1,0:T(8,128)(2,1)} %copy-done.6, f32[8,128]{1,0:T(8,128)} %copy-done.5, bf16[384,256]{1,0:T(8,128)(2,1)} %constant.36.clone.whole, ...), custom_call_target="tpu_custom_call", output_to_operand_aliasing={{2}: (11, {})} | custom-call | flops 200000000 | bytes 9572352 | tf_op jit(solution)/shard_map/pallas_call | solution.py:460
  62.6 4.9 %all-to-all-start.2 = ((bf16[32,8,2432]{2,1,0:T(8,128)(2,1)}), bf16[32,8,2432]{2,1,0:T(8,128)(2,1)S(1)}, u32[]{:S(2)}, u32[]{:S(2)}) async-start(bf16[32,8,2432]{2,1,0:T(8,128)(2,1)} %get-tuple-element.33), calls=%async_computation.2 | async-start | bytes 2490368 | tf_op jit(solution)/shard_map/all_to_all | solution.py:554
  67.5 7.4 %shard_map.118 = (bf16[2,144,384]{2,1,0:T(8,128)(2,1)}, bf16[2,144,384]{2,1,0:T(8,128)(2,1)}) custom-call(bf16[512,384]{1,0:T(8,128)(2,1)} %get-tuple-element.29.grad_conv, bf16[384,1536]{1,0:T(8,128)(2,1)} %get-tuple-element.30.projection, f32[560,384]{1,0:T(8,128)} %get-tuple-element.26.slope, bf16[80,1536]{1,0:T(8,128)(2,1)} %copy-done.2, ...), custom_call_target="tpu_custom_call" | custom-call | flops 200000000 | bytes 3612672 | tf_op jit(solution)/shard_map/pallas_call | solution.py:460
  75.0 0.0 copy-start.4
  75.0 0.4 collective-permute-start.7
  75.4 11.3 %all-to-all-done.2.gathered.parts = bf16[32,8,2432]{2,1,0:T(8,128)(2,1)S(1)} async-done(((bf16[32,8,2432]{2,1,0:T(8,128)(2,1)}), bf16[32,8,2432]{2,1,0:T(8,128)(2,1)S(1)}, u32[]{:S(2)}, u32[]{:S(2)}) %all-to-all-start.2) | async-done | bytes 1245216 | tf_op jit(solution)/shard_map/all_to_all | solution.py:554
  86.7 1.4 %shard_map.120 = bf16[8,8,1536]{2,1,0:T(8,128)(2,1)} custom-call(bf16[32,8,2432]{2,1,0:T(8,128)(2,1)S(1)} %all-to-all-done.2.gathered.parts), custom_call_target="tpu_custom_call" | custom-call | flops 200000000 | bytes 1441792 | tf_op jit(solution)/shard_map/pallas_call | solution.py:460
  88.1 0.0 copy-start.11
  88.1 3.4 %all-to-all-start.3 = ((bf16[8,8,1536]{2,1,0:T(8,128)(2,1)}), bf16[8,8,1536]{2,1,0:T(8,128)(2,1)S(1)}, u32[]{:S(2)}, u32[]{:S(2)}) async-start(bf16[8,8,1536]{2,1,0:T(8,128)(2,1)} %shard_map.120), calls=%async_computation.3 | async-start | bytes 393216 | tf_op jit(solution)/shard_map/all_to_all | solution.py:564
  91.5 0.0 copy-done.4
  91.5 0.0 collective-permute-done.7.got
  91.6 1.6 %collective-permute-start.8 = (bf16[2,144,384]{2,1,0:T(8,128)(2,1)S(1)}, bf16[2,144,384]{2,1,0:T(8,128)(2,1)S(1)}, u32[]{:S(2)}, u32[]{:S(2)}) collective-permute-start(bf16[2,144,384]{2,1,0:T(8,128)(2,1)S(1)} %pad_maximum_fusion), channel_id=1, source_target_pairs={{0,4},{4,0},{1,5},{5,1},{2,6},{6,2},{3,7},{7,3},{8,12},{12,8},{9,1... | collective-permute-start | bytes 663560 | tf_op jit(solution)/shard_map/ppermute | solution.py:600
  93.2 6.9 %all-to-all-done.3.got = bf16[8,8,1536]{2,1,0:T(8,128)(2,1)S(1)} async-done(((bf16[8,8,1536]{2,1,0:T(8,128)(2,1)}), bf16[8,8,1536]{2,1,0:T(8,128)(2,1)S(1)}, u32[]{:S(2)}, u32[]{:S(2)}) %all-to-all-start.3) | async-done | bytes 196640 | tf_op jit(solution)/shard_map/all_to_all | solution.py:564
  100.0 1.2 shard_map.121
  101.2 6.4 %all-to-all-start.4 = ((f32[32,1,1536]{2,1,0:T(1,128)}), f32[32,1,1536]{2,1,0:T(1,128)S(1)}, u32[]{:S(2)}, u32[]{:S(2)}) async-start(f32[32,1,1536]{2,1,0:T(1,128)} %get-tuple-element.37), calls=%async_computation.4 | async-start | bytes 393216 | tf_op jit(solution)/shard_map/all_to_all | solution.py:574
  107.6 0.0 copy-done.11
  107.7 0.0 collective-permute-done.8.far
  107.7 1.4 %shard_map.119 = (bf16[128,1536]{1,0:T(8,128)(2,1)}, f32[8,1536]{1,0:T(8,128)}) custom-call(bf16[2,144,384]{2,1,0:T(8,128)(2,1)S(1)} %copy-done.4, bf16[2,144,384]{2,1,0:T(8,128)(2,1)S(1)} %collective-permute-done.7.got, bf16[2,144,384]{2,1,0:T(8,128)(2,1)S(1)} %collective-permute-done.8.far, bf16[32,8,2432]{2,1,0:T(8,128)(2,1)S(1)} %all-to-all-done.2.gathered.parts, ...), custom_call_target="tpu_custom_call" | custom-call | flops 200000000 | bytes 2355200 | tf_op jit(solution)/shard_map/pallas_call | solution.py:460
  109.1 6.7 %all-to-all-done.4.got = f32[32,1,1536]{2,1,0:T(1,128)S(1)} async-done(((f32[32,1,1536]{2,1,0:T(1,128)}), f32[32,1,1536]{2,1,0:T(1,128)S(1)}, u32[]{:S(2)}, u32[]{:S(2)}) %all-to-all-start.4) | async-done | bytes 196640 | tf_op jit(solution)/shard_map/all_to_all | solution.py:574
  115.8 1.1 shard_map.122
  (7 shorter events, 0.1 us)
Async XLA Ops:
  0.6 17.4 %copy-start.7 = (bf16[1,128,1536]{2,1,0:T(8,128)(2,1)S(1)}, bf16[1,128,1536]{2,1,0:T(8,128)(2,1)}, u32[]{:S(2)}) copy-start(bf16[1,128,1536]{2,1,0:T(8,128)(2,1)} %param.9) | copy-start | bytes 1179652
  3.3 33.1 %collective-permute-start = (bf16[384,768]{1,0:T(8,128)(2,1)}, bf16[384,768]{1,0:T(8,128)(2,1)S(1)}, u32[]{:S(2)}, u32[]{:S(2)}) collective-permute-start(bf16[384,768]{1,0:T(8,128)(2,1)} %get-tuple-element.24), channel_id=1, source_target_pairs={{0,4},{4,0},{1,5},{5,1},{2,6},{6,2},{3,7},{7,3},{8,12},{12,8},{9,1... | collective-permute-start | bytes 1769480 | tf_op jit(solution)/shard_map/ppermute | solution.py:496
  7.1 8.9 %collective-permute-start.3 = (bf16[80,1536]{1,0:T(8,128)(2,1)}, bf16[80,1536]{1,0:T(8,128)(2,1)S(1)}, u32[]{:S(2)}, u32[]{:S(2)}) collective-permute-start(bf16[80,1536]{1,0:T(8,128)(2,1)} %get-tuple-element.25), channel_id=1, source_target_pairs={{6,8},{14,16},{22,24},{30,32},{38,40},{46,48},{54,56},{62,64},{70,... | collective-permute-start | bytes 737288 | tf_op jit(solution)/shard_map/ppermute | solution.py:494
  7.8 16.5 %all-to-all-start = ((bf16[8,8,1280]{2,1,0:T(8,128)(2,1)}), bf16[8,8,1280]{2,1,0:T(8,128)(2,1)S(1)}, u32[]{:S(2)}, u32[]{:S(2)}) async-start(bf16[8,8,1280]{2,1,0:T(8,128)(2,1)} %get-tuple-element.21), calls=%async_computation | async-start | bytes 327680 | tf_op jit(solution)/shard_map/all_to_all | solution.py:495
  16.0 20.8 %copy-start.2 = (bf16[80,1536]{1,0:T(8,128)(2,1)}, bf16[80,1536]{1,0:T(8,128)(2,1)S(1)}, u32[]{:S(2)}) copy-start(bf16[80,1536]{1,0:T(8,128)(2,1)S(1)} %collective-permute-done.3.slot) | copy-start | bytes 737284
  16.7 20.1 %collective-permute-start.4 = (bf16[112,768]{1,0:T(8,128)(2,1)S(1)}, bf16[112,768]{1,0:T(8,128)(2,1)S(1)}, u32[]{:S(2)}, u32[]{:S(2)}) collective-permute-start(bf16[112,768]{1,0:T(8,128)(2,1)S(1)} %shard_map.113), channel_id=1, source_target_pairs={{0,4},{6,2},{1,5},{7,3},{8,12},{14,10},{9,13},{15,11},{16,20},{22,... | collective-permute-start | bytes 516104 | tf_op jit(solution)/shard_map/ppermute | solution.py:500
  18.0 21.5 %collective-permute-start.1 = (bf16[128,1536]{1,0:T(8,128)(2,1)S(1)}, bf16[128,1536]{1,0:T(8,128)(2,1)}, u32[]{:S(2)}, u32[]{:S(2)}) collective-permute-start(bf16[128,1536]{1,0:T(8,128)(2,1)S(1)} %bitcast.12), channel_id=1, source_target_pairs={{0,2},{2,0},{1,3},{3,1},{4,6},{6,4},{5,7},{7,5},{8,10},{10,8},{9,1... | collective-permute-start | bytes 1179656 | tf_op jit(solution)/shard_map/ppermute | solution.py:497
  25.8 0.6 copy-start.5
  26.4 28.4 %all-to-all-start.1 = ((bf16[32,8,2304]{2,1,0:T(8,128)(2,1)}), bf16[32,8,2304]{2,1,0:T(8,128)(2,1)S(1)}, u32[]{:S(2)}, u32[]{:S(2)}) async-start(bf16[32,8,2304]{2,1,0:T(8,128)(2,1)} %get-tuple-element.22), calls=%async_computation.1 | async-start | bytes 2359296 | tf_op jit(solution)/shard_map/all_to_all | solution.py:515
  36.4 1.3 %copy-start.1 = (bf16[1,128,1536]{2,1,0:T(8,128)(2,1)S(1)}, bf16[1,128,1536]{2,1,0:T(8,128)(2,1)}, u32[]{:S(2)}) copy-start(bf16[1,128,1536]{2,1,0:T(8,128)(2,1)} %param.8) | copy-start | bytes 1179652
  36.4 1.3 %copy-start = (bf16[384,768]{1,0:T(8,128)(2,1)}, bf16[384,768]{1,0:T(8,128)(2,1)S(1)}, u32[]{:S(2)}) copy-start(bf16[384,768]{1,0:T(8,128)(2,1)S(1)} %collective-permute-done.across) | copy-start | bytes 1769476
  36.4 3.7 %collective-permute-start.2 = (bf16[384,768]{1,0:T(8,128)(2,1)S(1)}, bf16[384,768]{1,0:T(8,128)(2,1)S(1)}, u32[]{:S(2)}, u32[]{:S(2)}) collective-permute-start(bf16[384,768]{1,0:T(8,128)(2,1)S(1)} %collective-permute-done.across), channel_id=1, source_target_pairs={{0,2},{2,0},{1,3},{3,1},{4,6},{6,4},{5,7},{7,5},{8,10},{10,8},{9,1... | collective-permute-start | bytes 1769480 | tf_op jit(solution)/shard_map/ppermute | solution.py:498
  36.8 0.7 copy-start.3
  37.4 1.5 %copy-start.10 = (bf16[31,1536]{1,0:T(8,128)(2,1)S(1)}, bf16[31,1536]{1,0:T(8,128)(2,1)}, u32[]{:S(2)}) copy-start(bf16[31,1536]{1,0:T(8,128)(2,1)} %param.11) | copy-start | bytes 285700
  37.4 2.1 %collective-permute-start.6 = (bf16[2,176,384]{2,1,0:T(8,128)(2,1)S(1)}, bf16[2,176,384]{2,1,0:T(8,128)(2,1)}, u32[]{:S(2)}, u32[]{:S(2)}) collective-permute-start(bf16[2,176,384]{2,1,0:T(8,128)(2,1)S(1)} %shard_map.115), channel_id=1, source_target_pairs={{0,2},{2,0},{1,3},{3,1},{4,6},{6,4},{5,7},{7,5},{8,10},{10,8},{9,1... | collective-permute-start | bytes 811016 | tf_op jit(solution)/shard_map/ppermute | solution.py:517
  38.4 1.7 %collective-permute-start.5 = (bf16[2,128,384]{2,1,0:T(8,128)(2,1)S(1)}, bf16[2,128,384]{2,1,0:T(8,128)(2,1)S(1)}, u32[]{:S(2)}, u32[]{:S(2)}) collective-permute-start(bf16[2,128,384]{2,1,0:T(8,128)(2,1)S(1)} %shard_map.114), channel_id=1, source_target_pairs={{0,2},{2,0},{1,3},{3,1},{4,6},{6,4},{5,7},{7,5},{8,10},{10,8},{9,1... | collective-permute-start | bytes 589832 | tf_op jit(solution)/shard_map/ppermute | solution.py:516
  40.1 0.7 copy-start.9
  40.8 0.8 copy-start.8
  54.9 1.0 copy-start.6
  62.6 24.1 %all-to-all-start.2 = ((bf16[32,8,2432]{2,1,0:T(8,128)(2,1)}), bf16[32,8,2432]{2,1,0:T(8,128)(2,1)S(1)}, u32[]{:S(2)}, u32[]{:S(2)}) async-start(bf16[32,8,2432]{2,1,0:T(8,128)(2,1)} %get-tuple-element.33), calls=%async_computation.2 | async-start | bytes 2490368 | tf_op jit(solution)/shard_map/all_to_all | solution.py:554
  75.0 16.5 %copy-start.4 = (bf16[2,144,384]{2,1,0:T(8,128)(2,1)S(1)}, bf16[2,144,384]{2,1,0:T(8,128)(2,1)}, u32[]{:S(2)}) copy-start(bf16[2,144,384]{2,1,0:T(8,128)(2,1)} %get-tuple-element.31.kept) | copy-start | bytes 663556
  75.0 16.5 %collective-permute-start.7 = (bf16[2,144,384]{2,1,0:T(8,128)(2,1)}, bf16[2,144,384]{2,1,0:T(8,128)(2,1)S(1)}, u32[]{:S(2)}, u32[]{:S(2)}) collective-permute-start(bf16[2,144,384]{2,1,0:T(8,128)(2,1)} %get-tuple-element.32), channel_id=1, source_target_pairs={{0,2},{2,0},{1,3},{3,1},{4,6},{6,4},{5,7},{7,5},{8,10},{10,8},{9,1... | collective-permute-start | bytes 663560 | tf_op jit(solution)/shard_map/ppermute | solution.py:596
  88.1 19.6 %copy-start.11 = (s32[1,8]{1,0:T(1,128)S(1)}, s32[1,8]{1,0:T(1,128)}, u32[]{:S(2)}) copy-start(s32[1,8]{1,0:T(1,128)} %durations.1) | copy-start | bytes 100
  88.1 12.0 %all-to-all-start.3 = ((bf16[8,8,1536]{2,1,0:T(8,128)(2,1)}), bf16[8,8,1536]{2,1,0:T(8,128)(2,1)S(1)}, u32[]{:S(2)}, u32[]{:S(2)}) async-start(bf16[8,8,1536]{2,1,0:T(8,128)(2,1)} %shard_map.120), calls=%async_computation.3 | async-start | bytes 393216 | tf_op jit(solution)/shard_map/all_to_all | solution.py:564
  91.6 16.1 %collective-permute-start.8 = (bf16[2,144,384]{2,1,0:T(8,128)(2,1)S(1)}, bf16[2,144,384]{2,1,0:T(8,128)(2,1)S(1)}, u32[]{:S(2)}, u32[]{:S(2)}) collective-permute-start(bf16[2,144,384]{2,1,0:T(8,128)(2,1)S(1)} %pad_maximum_fusion), channel_id=1, source_target_pairs={{0,4},{4,0},{1,5},{5,1},{2,6},{6,2},{3,7},{7,3},{8,12},{12,8},{9,1... | collective-permute-start | bytes 663560 | tf_op jit(solution)/shard_map/ppermute | solution.py:600
  101.2 14.6 %all-to-all-start.4 = ((f32[32,1,1536]{2,1,0:T(1,128)}), f32[32,1,1536]{2,1,0:T(1,128)S(1)}, u32[]{:S(2)}, u32[]{:S(2)}) async-start(f32[32,1,1536]{2,1,0:T(1,128)} %get-tuple-element.37), calls=%async_computation.4 | async-start | bytes 393216 | tf_op jit(solution)/shard_map/all_to_all | solution.py:574

commit v10 on v9

--- a/solution.py
+++ b/solution.py
@@ -262,13 +262,13 @@
     needed = begin(
         [(gathered, got), (whole, v_whole), (low, v_low), (high, v_high), (notes, v_note)], sems
     )
+    finish(needed)
     later = begin(
         group_grads(upstream, across, up_beside, beyond, grads), sems.at[pl.ds(5, 6)]
     )
     last = begin(
         [(slope.at[pl.ds(LEFT_U, FRAMES)], v_slope), (hidden, v_hidden)], sems.at[pl.ds(13, 2)]
     )
-    finish(needed)
     rows = got[:, :, :1536].reshape(MESSAGE, 1536)
     halves = got[:, :, 1536:].reshape(MESSAGE, 768)
     for side, spot in enumerate((v_low, v_high)):

time: 118 us -> 118 us (level)
  no operation moved by 1% of the time
where the time goes in v10:
time: 118 us
  starting transfers between devices  46.1 us (39%)
  Pallas kernels  33.7 us (29%)
  waiting for transfers between devices  32.8 us (28%)
  local copies, waits for them, and re-layouts  3.3 us (3%)
    pallas_call x12, Pallas kernels, call(): pl.pallas_call(kernel, out_shape=shapes, in_specs=[space(i in near) for i...  33.7 us
    all_to_all x1, waiting for transfers between devices, body(): summed = parts = lax.all_to_all(parts, PLANE, 0, 0, tiled=True)  11.3 us
    all_to_all x1, starting transfers between devices, body(): rows = lax.all_to_all(plane, PLANE, 0, 0, tiled=True)  9.96 us
    all_to_all x1, starting transfers between devices, body(): rows = lax.all_to_all(rows, 'z', 0, 0, tiled=True)  8.2 us
    all_to_all x1, waiting for transfers between devices, body(): parts = lax.all_to_all(parts, 'z', 0, 0, tiled=True)  6.85 us
    all_to_all x1, waiting for transfers between devices, body(): taps_all = lax.all_to_all(taps_all, PLANE, 0, 0, tiled=True)  6.69 us
    all_to_all x1, starting transfers between devices, body(): taps_all = lax.all_to_all(taps_all, PLANE, 0, 0, tiled=True)  6.41 us
    all_to_all x1, waiting for transfers between devices, body(): rows = lax.all_to_all(plane, PLANE, 0, 0, tiled=True)  5.44 us
  transfers between devices with their start and end apart: 14, of which 6 were waited for; matrix products, arithmetic and copies ran while one was open for 1% of the time, Pallas kernels for 19%

profile of v10, /device:TPU:1, one launch (start us, length us, event | category | flops | bytes accessed | tf_op | source)
XLA Modules:
  0.0 117.7 jit_solution(922705872781338717)
XLA Ops:
  0.6 0.0 copy-start.7
  0.6 2.6 %shard_map.111 = (bf16[8,8,1280]{2,1,0:T(8,128)(2,1)}, bf16[384,768]{1,0:T(8,128)(2,1)}, bf16[80,1536]{1,0:T(8,128)(2,1)}) custom-call(bf16[6,1536]{1,0:T(8,128)(2,1)} %weights.1, s32[1,8]{1,0:T(1,128)} %durations.1, bf16[128,1536]{1,0:T(8,128)(2,1)} %bitcast.6, bf16[128,1536]{1,0:T(8,128)(2,1)} %bitcast.9), custom_call_target="tpu_custom_call" | custom-call | flops 200000000 | bytes 1804320 | tf_op jit(solution)/shard_map/pallas_call | solution.py:460
  3.3 3.8 %collective-permute-start = (bf16[384,768]{1,0:T(8,128)(2,1)}, bf16[384,768]{1,0:T(8,128)(2,1)S(1)}, u32[]{:S(2)}, u32[]{:S(2)}) collective-permute-start(bf16[384,768]{1,0:T(8,128)(2,1)} %get-tuple-element.24), channel_id=1, source_target_pairs={{0,4},{4,0},{1,5},{5,1},{2,6},{6,2},{3,7},{7,3},{8,12},{12,8},{9,1... | collective-permute-start | bytes 1769480 | tf_op jit(solution)/shard_map/ppermute | solution.py:496
  7.1 0.7 collective-permute-start.3
  7.8 8.2 %all-to-all-start = ((bf16[8,8,1280]{2,1,0:T(8,128)(2,1)}), bf16[8,8,1280]{2,1,0:T(8,128)(2,1)S(1)}, u32[]{:S(2)}, u32[]{:S(2)}) async-start(bf16[8,8,1280]{2,1,0:T(8,128)(2,1)} %get-tuple-element.21), calls=%async_computation | async-start | bytes 327680 | tf_op jit(solution)/shard_map/all_to_all | solution.py:495
  16.0 0.0 collective-permute-done.3.slot
  16.0 0.0 copy-start.2
  16.0 0.7 shard_map.113
  16.7 1.3 %collective-permute-start.4 = (bf16[112,768]{1,0:T(8,128)(2,1)S(1)}, bf16[112,768]{1,0:T(8,128)(2,1)S(1)}, u32[]{:S(2)}, u32[]{:S(2)}) collective-permute-start(bf16[112,768]{1,0:T(8,128)(2,1)S(1)} %shard_map.113), channel_id=1, source_target_pairs={{0,4},{6,2},{1,5},{7,3},{8,12},{14,10},{9,13},{15,11},{16,20},{22,... | collective-permute-start | bytes 516104 | tf_op jit(solution)/shard_map/ppermute | solution.py:500
  18.0 0.0 copy-done.7
  18.0 4.3 %collective-permute-start.1 = (bf16[128,1536]{1,0:T(8,128)(2,1)S(1)}, bf16[128,1536]{1,0:T(8,128)(2,1)}, u32[]{:S(2)}, u32[]{:S(2)}) collective-permute-start(bf16[128,1536]{1,0:T(8,128)(2,1)S(1)} %bitcast.12), channel_id=1, source_target_pairs={{0,2},{2,0},{1,3},{3,1},{4,6},{6,4},{5,7},{7,5},{8,10},{10,8},{9,1... | collective-permute-start | bytes 1179656 | tf_op jit(solution)/shard_map/ppermute | solution.py:497
  22.3 2.0 %all-to-all-done.got = bf16[8,8,1280]{2,1,0:T(8,128)(2,1)S(1)} async-done(((bf16[8,8,1280]{2,1,0:T(8,128)(2,1)}), bf16[8,8,1280]{2,1,0:T(8,128)(2,1)S(1)}, u32[]{:S(2)}, u32[]{:S(2)}) %all-to-all-start) | async-done | bytes 163872 | tf_op jit(solution)/shard_map/all_to_all | solution.py:495
  24.2 1.6 %shard_map.112 = (bf16[32,8,2304]{2,1,0:T(8,128)(2,1)}, f32[8,128]{1,0:T(8,128)S(1)}) custom-call(bf16[8,8,1280]{2,1,0:T(8,128)(2,1)S(1)} %all-to-all-done.got), custom_call_target="tpu_custom_call" | custom-call | flops 200000000 | bytes 1347584 | tf_op jit(solution)/shard_map/pallas_call | solution.py:460
  25.8 0.0 copy-start.5
  25.8 0.6 copy-done.5
  26.4 10.0 %all-to-all-start.1 = ((bf16[32,8,2304]{2,1,0:T(8,128)(2,1)}), bf16[32,8,2304]{2,1,0:T(8,128)(2,1)S(1)}, u32[]{:S(2)}, u32[]{:S(2)}) async-start(bf16[32,8,2304]{2,1,0:T(8,128)(2,1)} %get-tuple-element.22), calls=%async_computation.1 | async-start | bytes 2359296 | tf_op jit(solution)/shard_map/all_to_all | solution.py:515
  36.4 0.0 copy-start.1
  36.4 0.0 collective-permute-done.across
  36.4 0.0 copy-start
  36.4 0.3 collective-permute-start.2
  36.8 0.0 collective-permute-done.4.lent
  36.8 0.0 copy-done.2
  36.8 0.0 copy-start.3
  36.8 0.5 shard_map.115
  37.3 0.1 copy-done.3
  37.4 0.0 copy-start.10
  37.4 0.3 collective-permute-start.6
  37.7 0.0 copy-done
  37.7 0.0 copy-done.1
  37.7 0.7 shard_map.114
  38.4 0.5 collective-permute-start.5
  38.9 0.0 copy-done.10
  38.9 0.6 fusion.kernel
  39.6 0.0 collective-permute-done.1.up_beside
  39.6 0.0 collective-permute-done.6.edges.beside
  39.6 0.6 collective-permute-done.5.beside
  40.1 0.0 copy-start.9
  40.1 0.0 collective-permute-done.2.beyond
  40.1 0.7 copy-done.9
  40.8 0.0 copy-start.8
  40.8 0.8 copy-done.8
  41.6 7.8 %shard_map.116 = (f32[560,384]{1,0:T(8,128)}, f32[592,384]{1,0:T(8,128)}, bf16[32,8,2432]{2,1,0:T(8,128)(2,1)}) custom-call(bf16[128,1536]{1,0:T(8,128)(2,1)} %bitcast.7, bf16[80,1536]{1,0:T(8,128)(2,1)} %copy-done.2, bf16[384,768]{1,0:T(8,128)(2,1)} %copy-done, bf16[112,768]{1,0:T(8,128)(2,1)} %copy-done.3, bf16[2,128,384]{2,1,0:T(8,128)(2,1)} %copy-done.9, ...), custom_call_target="tpu_custom_call" | custom-call | flops 200000000 | bytes 6897664 | tf_op jit(solution)/shard_map/pallas_call | solution.py:460
  49.4 5.4 %all-to-all-done.1.gathered = bf16[32,8,2304]{2,1,0:T(8,128)(2,1)S(1)} async-done(((bf16[32,8,2304]{2,1,0:T(8,128)(2,1)}), bf16[32,8,2304]{2,1,0:T(8,128)(2,1)S(1)}, u32[]{:S(2)}, u32[]{:S(2)}) %all-to-all-start.1) | async-done | bytes 1179680 | tf_op jit(solution)/shard_map/all_to_all | solution.py:515
  54.9 1.0 copy-done.6
  55.9 7.3 %shard_map.117 = (bf16[512,384]{1,0:T(8,128)(2,1)}, bf16[384,1536]{1,0:T(8,128)(2,1)}, bf16[32,8,2432]{2,1,0:T(8,128)(2,1)}) custom-call(bf16[32,8,2304]{2,1,0:T(8,128)(2,1)} %copy-done.6, f32[8,128]{1,0:T(8,128)} %copy-done.5, bf16[384,256]{1,0:T(8,128)(2,1)} %constant.36.clone.whole, ...), custom_call_target="tpu_custom_call", output_to_operand_aliasing={{2}: (11, {})} | custom-call | flops 200000000 | bytes 9572352 | tf_op jit(solution)/shard_map/pallas_call | solution.py:460
  63.2 4.9 %all-to-all-start.2 = ((bf16[32,8,2432]{2,1,0:T(8,128)(2,1)}), bf16[32,8,2432]{2,1,0:T(8,128)(2,1)S(1)}, u32[]{:S(2)}, u32[]{:S(2)}) async-start(bf16[32,8,2432]{2,1,0:T(8,128)(2,1)} %get-tuple-element.33), calls=%async_computation.2 | async-start | bytes 2490368 | tf_op jit(solution)/shard_map/all_to_all | solution.py:554
  68.1 7.4 %shard_map.118 = (bf16[2,144,384]{2,1,0:T(8,128)(2,1)}, bf16[2,144,384]{2,1,0:T(8,128)(2,1)}) custom-call(bf16[512,384]{1,0:T(8,128)(2,1)} %get-tuple-element.29.grad_conv, bf16[384,1536]{1,0:T(8,128)(2,1)} %get-tuple-element.30.projection, f32[560,384]{1,0:T(8,128)} %get-tuple-element.26.slope, bf16[80,1536]{1,0:T(8,128)(2,1)} %copy-done.2, ...), custom_call_target="tpu_custom_call" | custom-call | flops 200000000 | bytes 3612672 | tf_op jit(solution)/shard_map/pallas_call | solution.py:460
  75.5 0.0 copy-start.4
  75.5 0.4 collective-permute-start.7
  76.0 11.3 %all-to-all-done.2.gathered.parts = bf16[32,8,2432]{2,1,0:T(8,128)(2,1)S(1)} async-done(((bf16[32,8,2432]{2,1,0:T(8,128)(2,1)}), bf16[32,8,2432]{2,1,0:T(8,128)(2,1)S(1)}, u32[]{:S(2)}, u32[]{:S(2)}) %all-to-all-start.2) | async-done | bytes 1245216 | tf_op jit(solution)/shard_map/all_to_all | solution.py:554
  87.3 1.4 %shard_map.120 = bf16[8,8,1536]{2,1,0:T(8,128)(2,1)} custom-call(bf16[32,8,2432]{2,1,0:T(8,128)(2,1)S(1)} %all-to-all-done.2.gathered.parts), custom_call_target="tpu_custom_call" | custom-call | flops 200000000 | bytes 1441792 | tf_op jit(solution)/shard_map/pallas_call | solution.py:460
  88.6 0.0 copy-start.11
  88.6 3.4 %all-to-all-start.3 = ((bf16[8,8,1536]{2,1,0:T(8,128)(2,1)}), bf16[8,8,1536]{2,1,0:T(8,128)(2,1)S(1)}, u32[]{:S(2)}, u32[]{:S(2)}) async-start(bf16[8,8,1536]{2,1,0:T(8,128)(2,1)} %shard_map.120), calls=%async_computation.3 | async-start | bytes 393216 | tf_op jit(solution)/shard_map/all_to_all | solution.py:564
  92.1 0.0 copy-done.4
  92.1 0.0 collective-permute-done.7.got
  92.2 1.6 %collective-permute-start.8 = (bf16[2,144,384]{2,1,0:T(8,128)(2,1)S(1)}, bf16[2,144,384]{2,1,0:T(8,128)(2,1)S(1)}, u32[]{:S(2)}, u32[]{:S(2)}) collective-permute-start(bf16[2,144,384]{2,1,0:T(8,128)(2,1)S(1)} %pad_maximum_fusion), channel_id=1, source_target_pairs={{0,4},{4,0},{1,5},{5,1},{2,6},{6,2},{3,7},{7,3},{8,12},{12,8},{9,1... | collective-permute-start | bytes 663560 | tf_op jit(solution)/shard_map/ppermute | solution.py:600
  93.8 6.9 %all-to-all-done.3.got = bf16[8,8,1536]{2,1,0:T(8,128)(2,1)S(1)} async-done(((bf16[8,8,1536]{2,1,0:T(8,128)(2,1)}), bf16[8,8,1536]{2,1,0:T(8,128)(2,1)S(1)}, u32[]{:S(2)}, u32[]{:S(2)}) %all-to-all-start.3) | async-done | bytes 196640 | tf_op jit(solution)/shard_map/all_to_all | solution.py:564
  100.6 1.2 shard_map.121
  101.8 6.4 %all-to-all-start.4 = ((f32[32,1,1536]{2,1,0:T(1,128)}), f32[32,1,1536]{2,1,0:T(1,128)S(1)}, u32[]{:S(2)}, u32[]{:S(2)}) async-start(f32[32,1,1536]{2,1,0:T(1,128)} %get-tuple-element.37), calls=%async_computation.4 | async-start | bytes 393216 | tf_op jit(solution)/shard_map/all_to_all | solution.py:574
  108.2 0.0 copy-done.11
  108.2 0.0 collective-permute-done.8.far
  108.3 1.4 %shard_map.119 = (bf16[128,1536]{1,0:T(8,128)(2,1)}, f32[8,1536]{1,0:T(8,128)}) custom-call(bf16[2,144,384]{2,1,0:T(8,128)(2,1)S(1)} %copy-done.4, bf16[2,144,384]{2,1,0:T(8,128)(2,1)S(1)} %collective-permute-done.7.got, bf16[2,144,384]{2,1,0:T(8,128)(2,1)S(1)} %collective-permute-done.8.far, bf16[32,8,2432]{2,1,0:T(8,128)(2,1)S(1)} %all-to-all-done.2.gathered.parts, ...), custom_call_target="tpu_custom_call" | custom-call | flops 200000000 | bytes 2355200 | tf_op jit(solution)/shard_map/pallas_call | solution.py:460
  109.7 6.7 %all-to-all-done.4.got = f32[32,1,1536]{2,1,0:T(1,128)S(1)} async-done(((f32[32,1,1536]{2,1,0:T(1,128)}), f32[32,1,1536]{2,1,0:T(1,128)S(1)}, u32[]{:S(2)}, u32[]{:S(2)}) %all-to-all-start.4) | async-done | bytes 196640 | tf_op jit(solution)/shard_map/all_to_all | solution.py:574
  116.4 1.1 shard_map.122
  (7 shorter events, 0.1 us)
Async XLA Ops:
  0.6 17.4 %copy-start.7 = (bf16[1,128,1536]{2,1,0:T(8,128)(2,1)S(1)}, bf16[1,128,1536]{2,1,0:T(8,128)(2,1)}, u32[]{:S(2)}) copy-start(bf16[1,128,1536]{2,1,0:T(8,128)(2,1)} %param.9) | copy-start | bytes 1179652
  3.3 33.1 %collective-permute-start = (bf16[384,768]{1,0:T(8,128)(2,1)}, bf16[384,768]{1,0:T(8,128)(2,1)S(1)}, u32[]{:S(2)}, u32[]{:S(2)}) collective-permute-start(bf16[384,768]{1,0:T(8,128)(2,1)} %get-tuple-element.24), channel_id=1, source_target_pairs={{0,4},{4,0},{1,5},{5,1},{2,6},{6,2},{3,7},{7,3},{8,12},{12,8},{9,1... | collective-permute-start | bytes 1769480 | tf_op jit(solution)/shard_map/ppermute | solution.py:496
  7.1 8.9 %collective-permute-start.3 = (bf16[80,1536]{1,0:T(8,128)(2,1)}, bf16[80,1536]{1,0:T(8,128)(2,1)S(1)}, u32[]{:S(2)}, u32[]{:S(2)}) collective-permute-start(bf16[80,1536]{1,0:T(8,128)(2,1)} %get-tuple-element.25), channel_id=1, source_target_pairs={{6,8},{14,16},{22,24},{30,32},{38,40},{46,48},{54,56},{62,64},{70,... | collective-permute-start | bytes 737288 | tf_op jit(solution)/shard_map/ppermute | solution.py:494
  7.8 16.5 %all-to-all-start = ((bf16[8,8,1280]{2,1,0:T(8,128)(2,1)}), bf16[8,8,1280]{2,1,0:T(8,128)(2,1)S(1)}, u32[]{:S(2)}, u32[]{:S(2)}) async-start(bf16[8,8,1280]{2,1,0:T(8,128)(2,1)} %get-tuple-element.21), calls=%async_computation | async-start | bytes 327680 | tf_op jit(solution)/shard_map/all_to_all | solution.py:495
  16.0 20.8 %copy-start.2 = (bf16[80,1536]{1,0:T(8,128)(2,1)}, bf16[80,1536]{1,0:T(8,128)(2,1)S(1)}, u32[]{:S(2)}) copy-start(bf16[80,1536]{1,0:T(8,128)(2,1)S(1)} %collective-permute-done.3.slot) | copy-start | bytes 737284
  16.7 20.1 %collective-permute-start.4 = (bf16[112,768]{1,0:T(8,128)(2,1)S(1)}, bf16[112,768]{1,0:T(8,128)(2,1)S(1)}, u32[]{:S(2)}, u32[]{:S(2)}) collective-permute-start(bf16[112,768]{1,0:T(8,128)(2,1)S(1)} %shard_map.113), channel_id=1, source_target_pairs={{0,4},{6,2},{1,5},{7,3},{8,12},{14,10},{9,13},{15,11},{16,20},{22,... | collective-permute-start | bytes 516104 | tf_op jit(solution)/shard_map/ppermute | solution.py:500
  18.0 21.5 %collective-permute-start.1 = (bf16[128,1536]{1,0:T(8,128)(2,1)S(1)}, bf16[128,1536]{1,0:T(8,128)(2,1)}, u32[]{:S(2)}, u32[]{:S(2)}) collective-permute-start(bf16[128,1536]{1,0:T(8,128)(2,1)S(1)} %bitcast.12), channel_id=1, source_target_pairs={{0,2},{2,0},{1,3},{3,1},{4,6},{6,4},{5,7},{7,5},{8,10},{10,8},{9,1... | collective-permute-start | bytes 1179656 | tf_op jit(solution)/shard_map/ppermute | solution.py:497
  25.8 0.6 copy-start.5
  26.4 28.4 %all-to-all-start.1 = ((bf16[32,8,2304]{2,1,0:T(8,128)(2,1)}), bf16[32,8,2304]{2,1,0:T(8,128)(2,1)S(1)}, u32[]{:S(2)}, u32[]{:S(2)}) async-start(bf16[32,8,2304]{2,1,0:T(8,128)(2,1)} %get-tuple-element.22), calls=%async_computation.1 | async-start | bytes 2359296 | tf_op jit(solution)/shard_map/all_to_all | solution.py:515
  36.4 1.3 %copy-start.1 = (bf16[1,128,1536]{2,1,0:T(8,128)(2,1)S(1)}, bf16[1,128,1536]{2,1,0:T(8,128)(2,1)}, u32[]{:S(2)}) copy-start(bf16[1,128,1536]{2,1,0:T(8,128)(2,1)} %param.8) | copy-start | bytes 1179652
  36.4 1.3 %copy-start = (bf16[384,768]{1,0:T(8,128)(2,1)}, bf16[384,768]{1,0:T(8,128)(2,1)S(1)}, u32[]{:S(2)}) copy-start(bf16[384,768]{1,0:T(8,128)(2,1)S(1)} %collective-permute-done.across) | copy-start | bytes 1769476
  36.4 3.7 %collective-permute-start.2 = (bf16[384,768]{1,0:T(8,128)(2,1)S(1)}, bf16[384,768]{1,0:T(8,128)(2,1)S(1)}, u32[]{:S(2)}, u32[]{:S(2)}) collective-permute-start(bf16[384,768]{1,0:T(8,128)(2,1)S(1)} %collective-permute-done.across), channel_id=1, source_target_pairs={{0,2},{2,0},{1,3},{3,1},{4,6},{6,4},{5,7},{7,5},{8,10},{10,8},{9,1... | collective-permute-start | bytes 1769480 | tf_op jit(solution)/shard_map/ppermute | solution.py:498
  36.8 0.7 copy-start.3
  37.4 1.5 %copy-start.10 = (bf16[31,1536]{1,0:T(8,128)(2,1)S(1)}, bf16[31,1536]{1,0:T(8,128)(2,1)}, u32[]{:S(2)}) copy-start(bf16[31,1536]{1,0:T(8,128)(2,1)} %param.11) | copy-start | bytes 285700
  37.4 2.1 %collective-permute-start.6 = (bf16[2,176,384]{2,1,0:T(8,128)(2,1)S(1)}, bf16[2,176,384]{2,1,0:T(8,128)(2,1)}, u32[]{:S(2)}, u32[]{:S(2)}) collective-permute-start(bf16[2,176,384]{2,1,0:T(8,128)(2,1)S(1)} %shard_map.115), channel_id=1, source_target_pairs={{0,2},{2,0},{1,3},{3,1},{4,6},{6,4},{5,7},{7,5},{8,10},{10,8},{9,1... | collective-permute-start | bytes 811016 | tf_op jit(solution)/shard_map/ppermute | solution.py:517
  38.4 1.7 %collective-permute-start.5 = (bf16[2,128,384]{2,1,0:T(8,128)(2,1)S(1)}, bf16[2,128,384]{2,1,0:T(8,128)(2,1)S(1)}, u32[]{:S(2)}, u32[]{:S(2)}) collective-permute-start(bf16[2,128,384]{2,1,0:T(8,128)(2,1)S(1)} %shard_map.114), channel_id=1, source_target_pairs={{0,2},{2,0},{1,3},{3,1},{4,6},{6,4},{5,7},{7,5},{8,10},{10,8},{9,1... | collective-permute-start | bytes 589832 | tf_op jit(solution)/shard_map/ppermute | solution.py:516
  40.1 0.7 copy-start.9
  40.8 0.8 copy-start.8
  54.9 1.0 copy-start.6
  63.2 24.1 %all-to-all-start.2 = ((bf16[32,8,2432]{2,1,0:T(8,128)(2,1)}), bf16[32,8,2432]{2,1,0:T(8,128)(2,1)S(1)}, u32[]{:S(2)}, u32[]{:S(2)}) async-start(bf16[32,8,2432]{2,1,0:T(8,128)(2,1)} %get-tuple-element.33), calls=%async_computation.2 | async-start | bytes 2490368 | tf_op jit(solution)/shard_map/all_to_all | solution.py:554
  75.5 16.5 %copy-start.4 = (bf16[2,144,384]{2,1,0:T(8,128)(2,1)S(1)}, bf16[2,144,384]{2,1,0:T(8,128)(2,1)}, u32[]{:S(2)}) copy-start(bf16[2,144,384]{2,1,0:T(8,128)(2,1)} %get-tuple-element.31.kept) | copy-start | bytes 663556
  75.5 16.5 %collective-permute-start.7 = (bf16[2,144,384]{2,1,0:T(8,128)(2,1)}, bf16[2,144,384]{2,1,0:T(8,128)(2,1)S(1)}, u32[]{:S(2)}, u32[]{:S(2)}) collective-permute-start(bf16[2,144,384]{2,1,0:T(8,128)(2,1)} %get-tuple-element.32), channel_id=1, source_target_pairs={{0,2},{2,0},{1,3},{3,1},{4,6},{6,4},{5,7},{7,5},{8,10},{10,8},{9,1... | collective-permute-start | bytes 663560 | tf_op jit(solution)/shard_map/ppermute | solution.py:596
  88.6 19.6 %copy-start.11 = (s32[1,8]{1,0:T(1,128)S(1)}, s32[1,8]{1,0:T(1,128)}, u32[]{:S(2)}) copy-start(s32[1,8]{1,0:T(1,128)} %durations.1) | copy-start | bytes 100
  88.6 12.0 %all-to-all-start.3 = ((bf16[8,8,1536]{2,1,0:T(8,128)(2,1)}), bf16[8,8,1536]{2,1,0:T(8,128)(2,1)S(1)}, u32[]{:S(2)}, u32[]{:S(2)}) async-start(bf16[8,8,1536]{2,1,0:T(8,128)(2,1)} %shard_map.120), calls=%async_computation.3 | async-start | bytes 393216 | tf_op jit(solution)/shard_map/all_to_all | solution.py:564
  92.2 16.1 %collective-permute-start.8 = (bf16[2,144,384]{2,1,0:T(8,128)(2,1)S(1)}, bf16[2,144,384]{2,1,0:T(8,128)(2,1)S(1)}, u32[]{:S(2)}, u32[]{:S(2)}) collective-permute-start(bf16[2,144,384]{2,1,0:T(8,128)(2,1)S(1)} %pad_maximum_fusion), channel_id=1, source_target_pairs={{0,4},{4,0},{1,5},{5,1},{2,6},{6,2},{3,7},{7,3},{8,12},{12,8},{9,1... | collective-permute-start | bytes 663560 | tf_op jit(solution)/shard_map/ppermute | solution.py:600
  101.8 14.6 %all-to-all-start.4 = ((f32[32,1,1536]{2,1,0:T(1,128)}), f32[32,1,1536]{2,1,0:T(1,128)S(1)}, u32[]{:S(2)}, u32[]{:S(2)}) async-start(f32[32,1,1536]{2,1,0:T(1,128)} %get-tuple-element.37), calls=%async_computation.4 | async-start | bytes 393216 | tf_op jit(solution)/shard_map/all_to_all | solution.py:574
